TPU v7x, 32 devices: a whole 2x2x4 slice. The times are simulated.
32 devices in a mesh: shard: 8 (over z, y), grp: 4 (over x, core).
Axes of the slice: x: 2, y: 2, z: 4, core: 2. Of those that a mesh axis runs over, the one named last changes fastest.
Arguments:
- entity_table: float32 [131072, 400], P(('shard', 'grp')), may hold values from -1.5 to 1.5
- rel_diag: float32 [64, 400], replicated, may hold values from 0.25 to 1.75
- src_ids: int32 [64000], P(('shard', 'grp')), may hold values from 0 to 131071, as said below
- dst_ids: int32 [64000], P(('shard', 'grp')), may hold values from 0 to 131071, as said below
- rel_ids: int32 [64000], P(('shard', 'grp')), may hold values from 0 to 63
- neg_ids: int32 [16, 1000], P('shard'), may hold values from 0 to 131071, as said below
Outputs:
- entity_grad: float32 [131072, 400], P(('shard', 'grp'))
Inputs may be any that keep to these rules, and one draw needn't show every extreme that they name: `src_ids`: entity e is held by device e // 4096 of shard+grp. Among the sources and destinations of the 2000 edges of one device (aligned blocks of 2000 edges), at most 250 are held by any one device; in every draw one device holds exactly 250 of those of every block. `dst_ids`: drawn together with src_ids, under the bound stated there. `neg_ids`: for a shard index s and a column block g (columns g * 250 to (g + 1) * 250 - 1), the entries of rows s * 2 to (s + 1) * 2 - 1 in that block name at most 31 entities held by any one device; in every draw one device holds exactly 31 of those of every such block. A whole row set s thus names at most 124 of one device's entities, reached.
All inputs are finite; a program needn't handle non-finite values.
Results may differ from a plain program's by a relative error of at most 0.0037.
Values may be sent and summed in bfloat16 or wider, within the bound.
No kernel may reach another device: no remote copies, remote signals or barrier semaphores. Data moves between devices by JAX's collectives and lax.ppermute only.
A program may use at most 192 MiB of HBM per device.

v0:
```python
import jax
import jax.numpy as jnp
from jax import lax
from jax.sharding import PartitionSpec as P


def slot_of(owner, devices, capacity):
    member = (owner[:, None] == jnp.arange(devices, dtype=jnp.int32)[None, :]).astype(jnp.int32)
    position = jnp.sum((jnp.cumsum(member, axis=0) - member) * member, axis=1)
    return owner * capacity + position


def body(entity_table, rel_diag, src_ids, dst_ids, rel_ids, neg_ids):
    rows_dev, feature = entity_table.shape
    sharers = lax.axis_size("grp")
    shards = lax.axis_size("shard")
    devices = shards * sharers
    spans, neg_count = neg_ids.shape
    edge_count = src_ids.shape[0]
    block_len = edge_count // spans
    edge_cap = 4 * edge_count // devices
    part_width = neg_count // sharers
    base_cap = 2 * spans * part_width // devices
    endpoints = jnp.concatenate([src_ids, dst_ids])
    edge_owner = endpoints // rows_dev
    edge_slot = slot_of(edge_owner, devices, edge_cap)
    edge_req = (
        jnp.zeros((devices * edge_cap,), jnp.int32)
        .at[edge_slot]
        .set(endpoints - edge_owner * rows_dev)
    )
    edge_req = edge_req.reshape(devices, edge_cap)
    own_ids = lax.dynamic_slice_in_dim(
        neg_ids, lax.axis_index("grp") * part_width, part_width, 1
    ).reshape(-1)
    neg_owner = own_ids // rows_dev
    neg_slot = slot_of(neg_owner, devices, base_cap)
    negative_request_list = (
        jnp.zeros((devices * base_cap,), jnp.int32).at[neg_slot].set(own_ids - neg_owner * rows_dev)
    )
    negative_request_list = negative_request_list.reshape(devices, base_cap)
    got_edge, got_neg = (
        lax.all_to_all(edge_req, ("shard", "grp"), split_axis=0, concat_axis=0, tiled=True),
        lax.all_to_all(
            negative_request_list, ("shard", "grp"), split_axis=0, concat_axis=0, tiled=True
        ),
    )
    got_edge = got_edge.reshape(-1)
    got_neg = got_neg.reshape(-1)
    look_edge = entity_table[got_edge].astype(jnp.bfloat16)
    look_neg = entity_table[got_neg].astype(jnp.bfloat16)
    back_edge, back_neg = (
        lax.all_to_all(
            look_edge.reshape(devices, edge_cap, feature),
            ("shard", "grp"),
            split_axis=0,
            concat_axis=0,
            tiled=True,
        ),
        lax.all_to_all(
            look_neg.reshape(devices, base_cap, feature),
            ("shard", "grp"),
            split_axis=0,
            concat_axis=0,
            tiled=True,
        ),
    )
    back_edge = back_edge.reshape(-1, feature)
    back_neg = back_neg.reshape(-1, feature)
    end_rows = back_edge[edge_slot]
    source = end_rows[:edge_count].astype(jnp.float32).reshape(spans, block_len, feature)
    target = end_rows[edge_count:].astype(jnp.float32).reshape(spans, block_len, feature)
    negative_samples = lax.all_gather(
        back_neg[neg_slot].reshape(spans, part_width, feature), "grp", axis=1, tiled=True
    )
    nrel = rel_diag.shape[0]
    rel_onehot = (rel_ids[:, None] == jnp.arange(nrel, dtype=jnp.int32)[None, :]).astype(
        jnp.float32
    )
    relation = jnp.dot(rel_onehot, rel_diag, precision=lax.Precision.HIGHEST).reshape(
        spans, block_len, feature
    )
    positive = jnp.sum(source * relation * target, axis=-1)
    query_vector = (source * relation).astype(jnp.bfloat16)
    logit_scores = jnp.einsum(
        "vpa,voa->vpo", query_vector, negative_samples, preferred_element_type=jnp.float32
    )
    sample_weight = jax.nn.sigmoid(logit_scores).astype(jnp.bfloat16)
    pos_weight = -jax.nn.sigmoid(-positive)
    gathered_rows = jnp.einsum(
        "gmz,gzu->gmu", sample_weight, negative_samples, preferred_element_type=jnp.float32
    )
    source_grad = pos_weight[..., None] * relation * target + relation * gathered_rows
    target_grad = pos_weight[..., None] * source * relation
    summed = lax.psum_scatter(
        jnp.einsum(
            "eri,era->iea", sample_weight, query_vector, preferred_element_type=jnp.float32
        ).reshape(part_width * lax.axis_size("grp"), spans * feature),
        "grp",
        scatter_dimension=0,
        tiled=True,
    )
    negative_row_gradient = (
        summed.reshape(part_width, spans, feature).transpose(1, 0, 2).reshape(-1, feature)
    )
    edge_grads = jnp.concatenate(
        [source_grad.reshape(-1, feature), target_grad.reshape(-1, feature)]
    )
    edge_buffer = (
        jnp.zeros((devices * edge_cap, feature), jnp.float32).at[edge_slot].set(edge_grads)
    )
    neg_buffer = (
        jnp.zeros((devices * base_cap, feature), jnp.float32)
        .at[neg_slot]
        .set(negative_row_gradient)
    )
    recv_edge, recv_neg = (
        lax.all_to_all(
            edge_buffer.reshape(devices, edge_cap, feature),
            ("shard", "grp"),
            split_axis=0,
            concat_axis=0,
            tiled=True,
        ),
        lax.all_to_all(
            neg_buffer.reshape(devices, base_cap, feature),
            ("shard", "grp"),
            split_axis=0,
            concat_axis=0,
            tiled=True,
        ),
    )
    entity_grad = jnp.zeros((rows_dev, feature), jnp.float32)
    entity_grad = entity_grad.at[got_edge].add(recv_edge.reshape(-1, feature))
    entity_grad = entity_grad.at[got_neg].add(recv_neg.reshape(-1, feature))
    return entity_grad


def solution(mesh):
    placed = (
        P(("shard", "grp"), None),
        P(),
        P(("shard", "grp")),
        P(("shard", "grp")),
        P(("shard", "grp")),
        P("shard", None),
    )
    return jax.shard_map(
        body, mesh=mesh, in_specs=placed, out_specs=P(("shard", "grp"), None), check_vma=False
    )
```

profile of v0, /device:TPU:0, one launch (start us, length us, event | category | flops | bytes accessed | tf_op | source)
XLA Modules:
  0.0 978.5 jit_solution(8867862509591265403)
XLA Ops:
  6.5 0.8 constant_dynamic-slice_fusion.1
  7.6 1.2 reduce-window.16
  9.1 2.9 scatter_custom_fusion.1
  12.1 0.7 all_to_all.27
  12.8 7.3 all-to-all-start.2
  20.1 0.8 multiply_subtract_fusion
  21.1 9.2 reduce-window.14
  30.3 0.8 slice_reduce_fusion
  32.1 19.3 %scatter_custom_fusion = s32[8000]{0:T(1024)S(1)} fusion(s32[4000]{0:T(1024)S(1)} %bitcast.68, s32[4000]{0:T(1024)S(1)} %get-tuple-element.7, s32[]{:T(128)} %constant.24.clone.1), kind=kCustom, calls=%fused_computation.65 | custom fusion | bytes 32004 | tf_op jit(solution)/shard_map/scatter | solution.py:30
  51.5 0.8 all_to_all.24
  52.2 6.9 copy.87
  59.1 5.8 all-to-all-start
  65.5 0.7 reduce.11
  66.3 6.8 gather_fusion.2
  73.2 1.3 convert_element_type.43
  74.5 6.0 all-to-all-start.3
  80.9 26.6 %gather_fusion = bf16[8000,400]{1,0:T(8,128)(2,1)} fusion(bf16[4096,400]{1,0:T(8,128)(2,1)} %copy.87, s32[8192]{0:T(1024)S(1)} %pad_clamp_fusion), kind=kCustom, calls=%fused_computation | custom fusion | bytes 12832000 | tf_op jit(solution)/shard_map/gather | solution.py:50
  107.6 10.5 %copy.88 = bf16[8000,400]{0,1:T(8,128)(2,1)} copy(bf16[8000,400]{1,0:T(8,128)(2,1)} %gather_fusion) | data formatting | bytes 12800000 | tf_op jit(solution)/shard_map/gather | solution.py:50
  118.1 22.9 %convert_element_type.37 = bf16[32,250,400]{1,0,2:T(8,128)(2,1)} reshape(bf16[8000,400]{0,1:T(8,128)(2,1)} %copy.88) | data formatting | bytes 12800000 | tf_op jit(solution)/shard_map/convert_element_type | solution.py:50
  141.0 9.3 copy.89
  150.3 6.1 all-to-all-start.1
  156.9 2.1 gather_fusion.3
  159.2 1.3 copy.103
  160.9 54.7 %all-gather.2.cloned.1.call-done = bf16[2,1000,400]{2,0,1:T(2,128)(2,1)} async-done(((bf16[2,250,400]{2,0,1:T(2,128)(2,1)}), bf16[2,1000,400]{2,0,1:T(2,128)(2,1)}) %all-gather.2.cloned.1.call-update) | async-done | bytes 1600016 | tf_op jit(solution)/shard_map/all_gather | solution.py:73
  215.6 6.2 copy.104
  221.7 81.5 %all-to-all-done.1 = bf16[32,250,400]{1,2,0:T(8,128)(2,1)} async-done(((bf16[32,250,400]{1,2,0:T(8,128)(2,1)}), bf16[32,250,400]{1,2,0:T(8,128)(2,1)}, u32[]{:S(2)}, u32[]{:S(2)}) %all-to-all-start.1) | async-done | bytes 6400032 | tf_op jit(solution)/shard_map/all_to_all | solution.py:53
  303.3 10.6 %copy.116 = bf16[32,250,400]{2,1,0:T(8,128)(2,1)} copy(bf16[32,250,400]{1,2,0:T(8,128)(2,1)} %all-to-all-done.1) | data formatting | bytes 12800000 | tf_op jit(solution)/shard_map/reshape | solution.py:68
  313.9 10.5 %reshape.557 = bf16[8000,400]{1,0:T(8,128)(2,1)} reshape(bf16[32,250,400]{2,1,0:T(8,128)(2,1)} %copy.116) | data formatting | bytes 12800000 | tf_op jit(solution)/shard_map/reshape | solution.py:68
  324.4 21.8 %gather_fusion.1 = bf16[4000,400]{1,0:T(8,128)(2,1)} fusion(bf16[8000,400]{1,0:T(8,128)(2,1)} %reshape.557, s32[4096]{0:T(1024)S(1)} %pad_clamp_fusion.1), kind=kCustom, calls=%fused_computation.1 | custom fusion | bytes 6416000 | tf_op jit(solution)/shard_map/gather | solution.py:70
  346.2 3.8 fusion.23
  350.0 2.3 copy.129
  352.2 2.8 copy.128
  355.0 1.2 copy-done.2
  356.2 4.7 reshape.459
  361.0 3.8 multiply_reduce_fusion
  364.8 5.0 reshape.457
  369.8 4.8 fusion.4
  374.5 3.4 divide_convert_fusion
  378.0 3.7 fusion.24
  383.5 65.7 %all-reduce.5.cloned.1.call-done = f32[1000,800]{0,1:T(8,128)} async-done(((f32[1000,800]{0,1:T(8,128)}), f32[1000,800]{0,1:T(8,128)}) %all-reduce.5.cloned.1.call-update) | async-done | bytes 3200016
  449.3 2.5 constant_dynamic-slice_fusion
  451.8 2.5 copy.122
  454.2 2.3 reshape.561
  456.5 4.3 scatter_custom_fusion.4
  460.8 2.9 reshape.473
  463.7 5.0 all-to-all-start.5
  468.8 6.0 reshape.458
  474.8 8.0 fusion.5
  482.8 4.2 copy.107
  487.0 6.1 reshape.467
  493.1 2.1 multiply_multiply_fusion
  495.5 4.2 pad_maximum_fusion
  499.7 8.4 copy.108
  508.1 27.8 %scatter_custom_fusion.2 = f32[8000,400]{1,0:T(8,128)} fusion(s32[4000]{0:T(1024)S(1)} %bitcast.70, f32[4000,400]{1,0:T(8,128)} %copy.108, f32[]{:T(128)} %constant.23.clone.1), kind=kCustom, calls=%fused_computation.11 | custom fusion | bytes 12800512 | tf_op jit(solution)/shard_map/scatter | solution.py:110
  535.9 14.0 %reshape.559 = f32[32,250,400]{2,1,0:T(8,128)} reshape(f32[8000,400]{1,0:T(8,128)} %scatter_custom_fusion.2) | data formatting | bytes 25600000 | tf_op jit(solution)/shard_map/reshape | solution.py:119
  549.9 16.3 %copy.110 = f32[32,250,400]{1,2,0:T(8,128)} copy(f32[32,250,400]{2,1,0:T(8,128)} %reshape.559) | data formatting | bytes 25600000 | tf_op jit(solution)/shard_map/reshape | solution.py:119
  566.2 6.1 all-to-all-start.4
  572.3 1.7 reshape.553
  574.0 288.8 %all-to-all-done.4 = f32[32,250,400]{1,2,0:T(8,128)} async-done(((f32[32,250,400]{1,2,0:T(8,128)}), f32[32,250,400]{1,2,0:T(8,128)}, u32[]{:S(2)}, u32[]{:S(2)}) %all-to-all-start.4) | async-done | bytes 12800032 | tf_op jit(solution)/shard_map/all_to_all | solution.py:118
  862.8 15.8 %copy.121 = f32[32,250,400]{2,1,0:T(8,128)} copy(f32[32,250,400]{1,2,0:T(8,128)} %all-to-all-done.4) | data formatting | bytes 25600000 | tf_op jit(solution)/shard_map/reshape | solution.py:134
  878.6 13.9 %reshape.560 = f32[8000,400]{1,0:T(8,128)} reshape(f32[32,250,400]{2,1,0:T(8,128)} %copy.121) | data formatting | bytes 25600000 | tf_op jit(solution)/shard_map/reshape | solution.py:134
  892.5 56.8 %scatter_custom_fusion.3 = f32[4096,400]{1,0:T(8,128)} fusion(s32[8000]{0:T(1024)} %copy-done.6, f32[8000,400]{1,0:T(8,128)} %reshape.560, f32[]{:T(128)} %constant.23.clone.1), kind=kCustom, calls=%fused_computation.14 | custom fusion | flops 3200000 | bytes 6554112 | tf_op jit(solution)/shard_map/scatter-add | solution.py:134
  949.3 13.6 %scatter_fusion = f32[4096,400]{1,0:T(8,128)} fusion(f32[4096,400]{1,0:T(8,128)} %scatter_custom_fusion.3, s32[992]{0:T(1024)S(1)} %bitcast.72, f32[992,400]{1,0:T(8,128)S(1)} %reshape.553), kind=kCustom, calls=%fused_computation.9 | custom fusion | flops 396800 | bytes 4765568 | tf_op jit(solution)/shard_map/scatter-add | solution.py:135
  962.8 8.6 copy.115
  (67 shorter events, 5.5 us)
Async XLA Ops:
  6.5 354.4 %copy-start = (f32[64,400]{1,0:T(8,128)S(1)}, f32[64,400]{1,0:T(8,128)}, u32[]{:S(2)}) copy-start(f32[64,400]{1,0:T(8,128)} %param.7) | copy-start | bytes 307204
  8.7 23.2 %copy-start.9 = (s32[2000]{0:T(1024)S(1)}, s32[2000]{0:T(1024)}, u32[]{:S(2)}) copy-start(s32[2000]{0:T(1024)} %param.9) | copy-start | bytes 24004
  8.7 23.3 %copy-start.10 = (s32[2000]{0:T(1024)S(1)}, s32[2000]{0:T(1024)}, u32[]{:S(2)}) copy-start(s32[2000]{0:T(1024)} %param.8) | copy-start | bytes 24004
  12.8 46.4 %all-to-all-start.2 = ((s32[32,1,31]{2,1,0:T(1,128)}), s32[32,1,31]{2,1,0:T(1,128)S(1)}, u32[]{:S(2)}, u32[]{:S(2)}) async-start(s32[32,1,31]{2,1,0:T(1,128)} %bitcast.8), calls=%async_computation.2 | async-start | bytes 32768 | tf_op jit(solution)/shard_map/all_to_all | solution.py:44
  59.1 15.4 %all-to-all-start = ((s32[32,1,250]{2,1,0:T(1,128)}), s32[32,1,250]{2,1,0:T(1,128)S(1)}, u32[]{:S(2)}, u32[]{:S(2)}) async-start(s32[32,1,250]{2,1,0:T(1,128)} %all_to_all.24), calls=%async_computation | async-start | bytes 65536 | tf_op jit(solution)/shard_map/all_to_all | solution.py:43
  66.3 6.9 copy-start.7
  74.5 75.7 %all-to-all-start.3 = ((bf16[32,31,400]{2,1,0:T(8,128)(2,1)}), bf16[32,31,400]{2,1,0:T(8,128)(2,1)S(1)}, u32[]{:S(2)}, u32[]{:S(2)}) async-start(bf16[32,31,400]{2,1,0:T(8,128)(2,1)} %convert_element_type.43), calls=%async_computation.3 | async-start | bytes 2097152 | tf_op jit(solution)/shard_map/all_to_all | solution.py:60
  80.9 26.7 %copy-start.6 = (s32[8000]{0:T(1024)}, s32[8000]{0:T(1024)S(1)}, u32[]{:S(2)}) copy-start(s32[8000]{0:T(1024)S(1)} %fusion.14) | copy-start | bytes 96004
  150.3 153.0 %all-to-all-start.1 = ((bf16[32,250,400]{1,2,0:T(8,128)(2,1)}), bf16[32,250,400]{1,2,0:T(8,128)(2,1)}, u32[]{:S(2)}, u32[]{:S(2)}) async-start(bf16[32,250,400]{1,2,0:T(8,128)(2,1)} %copy.89), calls=%async_computation.1 | async-start | bytes 13107200 | tf_op jit(solution)/shard_map/all_to_all | solution.py:53
  156.4 59.2 %all-gather.2.cloned.1.call-start = ((), (), s32[]{:S(2)}) async-start(), calls=%async_computation.6 | async-start | bytes 2560000 | tf_op jit(solution)/shard_map/all_gather | solution.py:73
  160.6 288.7 %all-reduce.5.cloned.1.call-start = ((), (), s32[]{:S(2)}) async-start(), calls=%async_computation.7 | async-start | bytes 6553600
  355.0 1.2 copy-start.2
  356.2 4.8 copy-start.11
  369.7 4.8 copy-start.4
  378.0 3.7 copy-start.5
  381.6 0.7 copy-start.12
  463.7 102.5 %all-to-all-start.5 = ((f32[32,31,400]{2,1,0:T(8,128)}), f32[32,31,400]{2,1,0:T(8,128)}, u32[]{:S(2)}, u32[]{:S(2)}) async-start(f32[32,31,400]{2,1,0:T(8,128)} %reshape.473), calls=%async_computation.5 | async-start | bytes 4194304 | tf_op jit(solution)/shard_map/all_to_all | solution.py:125
  493.1 2.4 copy-start.3
  566.2 296.6 %all-to-all-start.4 = ((f32[32,250,400]{1,2,0:T(8,128)}), f32[32,250,400]{1,2,0:T(8,128)}, u32[]{:S(2)}, u32[]{:S(2)}) async-start(f32[32,250,400]{1,2,0:T(8,128)} %copy.110), calls=%async_computation.4 | async-start | bytes 26214400 | tf_op jit(solution)/shard_map/all_to_all | solution.py:118
  892.5 56.8 %copy-start.8 = (s32[992,1]{0,1:T(1,128)S(1)}, s32[992,1]{0,1:T(1,128)}, u32[]{:S(2)}) copy-start(s32[992,1]{0,1:T(1,128)} %copy-done.7) | copy-start | bytes 11908
  962.8 8.6 copy-start.1
Sparse Core Ops, SparseCore 0:
  160.7 54.8 all-gather.1
  381.8 67.4 all-reduce.4
where the time goes:
time: 987 us; the launch traced here: 979 us
  waiting for transfers between devices  491 us (50%)
  local copies, waits for them, and re-layouts  323 us (33%)
  other arithmetic  94.4 us (10%)
  starting transfers between devices  36.6 us (4%)
  matrix products  18.8 us (2%)
  between operations  14.7 us (1%)
    all_to_all x1, waiting for transfers between devices, body(): lax.all_to_all(edge_buffer.reshape(devices, edge_cap, feature), ('shard',...  289 us
    all_to_all x1, waiting for transfers between devices, body(): lax.all_to_all(look_edge.reshape(devices, edge_cap, feature), ('shard', '...  81.5 us
    unnamed x3, waiting for transfers between devices  65.8 us
    scatter-add x1, other arithmetic, body(): entity_grad = entity_grad.at[got_edge].add(recv_edge.reshape(-1, feature))  56.8 us
    all_gather x1, waiting for transfers between devices, body(): lax.all_gather(back_neg[neg_slot].reshape(spans, part_width, feature), 'g...  54.7 us
    gather x2, local copies, waits for them, and re-layouts, body(): look_edge = entity_table[got_edge].astype(jnp.bfloat16)  37.1 us
    convert_element_type x2, local copies, waits for them, and re-layouts, body(): look_edge = entity_table[got_edge].astype(jnp.bfloat16)  32.2 us
    reshape x2, local copies, waits for them, and re-layouts, body(): edge_buffer.reshape(devices, edge_cap, feature)  30.3 us
  transfers between devices with their start and end apart: 8, of which 4 were waited for; matrix products, arithmetic and copies ran while one was open for 23% of the time, Pallas kernels for 0%

commit v1 on v0

v1 whole, which is shorter than its diff:
```python
import functools

import jax
import jax.numpy as jnp
from jax import lax
from jax.experimental import pallas as pl
from jax.experimental.pallas import tpu as pltpu
from jax.sharding import PartitionSpec as P

LANES = 128
VMEM_BYTES = 56 << 20
F32 = jnp.float32
BF16 = jnp.bfloat16
NN = (((1,), (0,)), ((), ()))
NT = (((1,), (1,)), ((), ()))
TN = (((0,), (0,)), ((), ()))


def round_up(value, unit):
    return -(-value // unit) * unit


def dot(left, right, dims):
    return lax.dot_general(left, right, dims, preferred_element_type=F32)


def one_hot(rows, row, base=0):
    places = lax.broadcasted_iota(jnp.int32, (rows, row.shape[1]), 0) + base
    return jnp.where(places == row, 1.0, 0.0).astype(BF16)


def call(kernel, name, flops, nbytes, **kwargs):
    return pl.pallas_call(
        kernel,
        name=name,
        compiler_params=pltpu.CompilerParams(vmem_limit_bytes=VMEM_BYTES),
        cost_estimate=pl.CostEstimate(flops=flops, bytes_accessed=nbytes, transcendentals=0),
        **kwargs,
    )


def slots_kernel(ids_ref, req_ref, *slot_refs, rows_dev, devices):
    segments, width = ids_ref.shape
    chunks = len(slot_refs)
    upper = jnp.where(
        lax.broadcasted_iota(jnp.int32, (LANES, LANES), 0)
        < lax.broadcasted_iota(jnp.int32, (LANES, LANES), 1),
        1.0,
        0.0,
    ).astype(BF16)
    owners = lax.broadcasted_iota(jnp.int32, (devices, LANES), 0)
    taken = jnp.zeros((devices, 1), F32)
    sums = [[jnp.zeros((devices, LANES), F32) for _ in range(2)] for _ in range(chunks)]
    for segment in range(segments):
        for start in range(0, width, LANES):
            ids = ids_ref[segment : segment + 1, start : start + LANES]
            valid = ids >= 0
            owner = jnp.where(valid, ids // rows_dev, -1)
            code = jnp.where(valid, ids - owner * rows_dev + 1, 0)
            member = jnp.where(owners == owner, 1.0, 0.0)
            before = dot(member.astype(BF16), upper, NN) + taken
            taken = taken + jnp.sum(member, axis=1, keepdims=True)
            rank = jnp.sum(before * member, axis=0, keepdims=True).astype(jnp.int32)
            high = (member * (code // 64).astype(F32)).astype(BF16)
            low = (member * (code % 64).astype(F32)).astype(BF16)
            for chunk in range(chunks):
                place = rank - chunk * LANES
                inside = valid & (place >= 0) & (place < LANES)
                slot_refs[chunk][segment : segment + 1, start : start + LANES] = jnp.where(
                    inside, owner * LANES + place, -1
                )
                hot = one_hot(LANES, jnp.where(inside, place, -1))
                sums[chunk][0] += dot(high, hot, NT)
                sums[chunk][1] += dot(low, hot, NT)
    for chunk in range(chunks):
        value = 64.0 * sums[chunk][0] + sums[chunk][1]
        req_ref[:, chunk * LANES : (chunk + 1) * LANES] = value.astype(jnp.int32) - 1


def make_slots(ids, rows_dev, devices, chunks):
    shape = ids.shape
    return call(
        functools.partial(slots_kernel, rows_dev=rows_dev, devices=devices),
        "slots",
        4 * devices * LANES * ids.size,
        8 * ids.size,
        out_shape=[jax.ShapeDtypeStruct((devices, chunks * LANES), jnp.int32)]
        + [jax.ShapeDtypeStruct(shape, jnp.int32)] * chunks,
    )(ids)


def gather_kernel(table_ref, req_ref, out_ref, *, group):
    first = pl.program_id(0) * group
    row = jnp.concatenate([req_ref[pl.ds(first + i, 1), :] for i in range(group)], axis=1)
    rows = dot(table_ref[...], one_hot(table_ref.shape[1], row), NN).astype(BF16)
    for i in range(group):
        out_ref[i] = rows[:, i * LANES : (i + 1) * LANES]


def gather(table, requests):
    feature, rows_dev = table.shape
    devices = requests.shape[0]
    group = 4
    slots = devices * LANES
    return call(
        functools.partial(gather_kernel, group=group),
        "gather_rows",
        2 * feature * rows_dev * slots,
        2 * feature * (rows_dev + slots),
        grid=(devices // group,),
        in_specs=[
            pl.BlockSpec((feature, rows_dev), lambda i: (0, 0)),
            pl.BlockSpec((devices, LANES), lambda i: (0, 0)),
        ],
        out_specs=pl.BlockSpec((group, feature, LANES), lambda i: (i, 0, 0)),
        out_shape=jax.ShapeDtypeStruct((devices, feature, LANES), BF16),
    )(table, requests)


def gather_neg_kernel(table_ref, req_ref, out_ref, *, cap):
    devices = req_ref.shape[0]
    row = jnp.concatenate([req_ref[d : d + 1, :cap] for d in range(devices)], axis=1)
    rows = dot(table_ref[...], one_hot(table_ref.shape[1], row), NN)
    out_ref[...] = rows.T.astype(BF16)


def gather_neg(table, requests, cap):
    feature, rows_dev = table.shape
    slots = requests.shape[0] * cap
    return call(
        functools.partial(gather_neg_kernel, cap=cap),
        "gather_negatives",
        2 * feature * rows_dev * slots,
        2 * feature * (rows_dev + slots),
        out_shape=jax.ShapeDtypeStruct((slots, feature), BF16),
    )(table, requests)


def neg_slot_row(slot, cap):
    return jnp.where(slot >= 0, (slot // LANES) * cap + slot % LANES, -1)


def spread_neg_kernel(back_ref, slot_ref, out_ref, *, cap):
    parts, width = slot_ref.shape
    for part in range(parts):
        row = neg_slot_row(slot_ref[part : part + 1, :], cap)
        hot = one_hot(back_ref.shape[0], row)
        out_ref[part] = dot(hot, back_ref[...], TN).astype(BF16)


def spread_neg(back, slot, cap):
    parts, width = slot.shape
    return call(
        functools.partial(spread_neg_kernel, cap=cap),
        "spread_negatives",
        2 * back.size * slot.size,
        2 * back.size,
        out_shape=jax.ShapeDtypeStruct((parts, width, back.shape[1]), BF16),
    )(back, slot)


def collect_neg_kernel(grad_ref, slot_ref, out_ref, *, cap):
    parts, width = slot_ref.shape
    total = jnp.zeros(out_ref.shape, F32)
    for part in range(parts):
        value = grad_ref[0, part].astype(F32)
        for sharer in range(1, grad_ref.shape[0]):
            value = value + grad_ref[sharer, part].astype(F32)
        row = neg_slot_row(slot_ref[part : part + 1, :], cap)
        total = total + dot(one_hot(out_ref.shape[0], row), value.astype(BF16), NN)
    out_ref[...] = total.astype(BF16)


def collect_neg(grads, slot, cap, devices):
    feature = grads.shape[-1]
    return call(
        functools.partial(collect_neg_kernel, cap=cap),
        "collect_negatives",
        2 * devices * cap * feature * slot.size,
        4 * grads.size,
        out_shape=jax.ShapeDtypeStruct((devices * cap, feature), BF16),
    )(grads, slot)


def spread_kernel(*refs, first):
    if first:
        back_ref, slot_ref, out_ref, flat = refs
    else:
        back_ref, slot_ref, so_far_ref, out_ref, flat = refs

    @pl.when(pl.program_id(0) == 0)
    def _():
        for d in range(back_ref.shape[0]):
            flat[:, d * LANES : (d + 1) * LANES] = back_ref[d]

    row = slot_ref[...].reshape(1, slot_ref.shape[-1])
    rows = dot(flat[...], one_hot(flat.shape[1], row), NN)
    if not first:
        rows = rows + so_far_ref[...].astype(F32)
    out_ref[...] = rows.astype(BF16)


def spread(back, slot, so_far):
    devices, feature, _ = back.shape
    segments, width = slot.shape
    tile = 512 if devices * LANES <= 4096 else 128
    steps = width // tile
    slots = devices * LANES
    rows_spec = pl.BlockSpec((feature, tile), lambda i: (0, i))
    return call(
        functools.partial(spread_kernel, first=so_far is None),
        "spread_rows",
        2 * feature * slots * slot.size,
        2 * feature * (slots + slot.size),
        grid=(segments * steps,),
        in_specs=[
            pl.BlockSpec((devices, feature, LANES), lambda i: (0, 0, 0)),
            pl.BlockSpec((1, 1, tile), lambda i: (i // steps, 0, i % steps)),
        ]
        + ([] if so_far is None else [rows_spec]),
        out_specs=rows_spec,
        out_shape=jax.ShapeDtypeStruct((feature, slot.size), BF16),
        scratch_shapes=[pltpu.VMEM((feature, slots), BF16)],
    )(back, slot.reshape(segments, 1, width), *([] if so_far is None else [so_far]))


def edges_kernel(
    src_ref, dst_ref, rel_ids_ref, rel_ref, neg_ref, src_grad_ref, dst_grad_ref, neg_grad_ref, sums
):
    step = pl.program_id(1)
    parts, _, part, feature = neg_ref.shape
    negatives = neg_ref[...].reshape(parts * part, feature)
    nrel = rel_ref.shape[1]
    hot = one_hot(nrel, rel_ids_ref[...].reshape(1, rel_ids_ref.shape[-1]))
    table = rel_ref[...]
    relation = jnp.zeros(src_ref.shape, F32)
    for _ in range(3):
        piece = table.astype(BF16)
        relation = relation + dot(piece, hot, NN)
        table = table - piece.astype(F32)
    source = src_ref[...].astype(F32)
    target = dst_ref[...].astype(F32)
    product = source * relation
    positive = jnp.sum(product * target, axis=0, keepdims=True)
    pos_weight = -jax.nn.sigmoid(-positive)
    query = product.astype(BF16)
    weight = jax.nn.sigmoid(dot(negatives, query, NN)).astype(BF16)
    gathered = dot(negatives, weight, TN)
    src_grad_ref[...] = (relation * (pos_weight * target + gathered)).astype(BF16)
    dst_grad_ref[...] = (pos_weight * product).astype(BF16)
    neg_grad = dot(weight, query, NT)

    @pl.when(step == 0)
    def _():
        sums[...] = neg_grad

    @pl.when(step != 0)
    def _():
        sums[...] += neg_grad

    @pl.when(step == pl.num_programs(1) - 1)
    def _():
        neg_grad_ref[...] = sums[...].astype(BF16).reshape(neg_grad_ref.shape)


def edges(rows, rel_ids, relations, negatives):
    feature, endpoints = rows.shape
    parts, spans, part, _ = negatives.shape
    width = rel_ids.shape[1]
    tile = 512
    steps = width // tile
    blocks = spans * steps
    edge_spec = pl.BlockSpec((feature, tile), lambda b, i: (0, b * steps + i))
    flops = 6 * feature * parts * part * spans * width
    src_grad, dst_grad, neg_grad = call(
        edges_kernel,
        "edges",
        flops,
        2 * (2 * rows.size + 2 * negatives.size),
        grid=(spans, steps),
        in_specs=[
            edge_spec,
            pl.BlockSpec((feature, tile), lambda b, i: (0, blocks + b * steps + i)),
            pl.BlockSpec((1, 1, tile), lambda b, i: (b, 0, i)),
            pl.BlockSpec(relations.shape, lambda b, i: (0, 0)),
            pl.BlockSpec((parts, 1, part, feature), lambda b, i: (0, b, 0, 0)),
        ],
        out_specs=[
            edge_spec,
            edge_spec,
            pl.BlockSpec((parts, 1, part, feature), lambda b, i: (0, b, 0, 0)),
        ],
        out_shape=[
            jax.ShapeDtypeStruct((feature, endpoints // 2), BF16),
            jax.ShapeDtypeStruct((feature, endpoints // 2), BF16),
            jax.ShapeDtypeStruct(negatives.shape, BF16),
        ],
        scratch_shapes=[pltpu.VMEM((parts * part, feature), F32)],
    )(rows, rows, rel_ids.reshape(spans, 1, width), relations, negatives)
    return src_grad, dst_grad, neg_grad


def collect_kernel(src_ref, dst_ref, slot_ref, out_ref, *, group):
    segments, width = slot_ref.shape
    base = pl.program_id(0) * group * LANES
    total = jnp.zeros((src_ref.shape[0], group * LANES), F32)
    for segment in range(segments):
        grads = src_ref if segment < segments // 2 else dst_ref
        start = segment % (segments // 2) * width
        hot = one_hot(group * LANES, slot_ref[segment : segment + 1, :], base)
        total = total + dot(grads[:, start : start + width], hot, NT)
    total = total.astype(BF16)
    for i in range(group):
        out_ref[i] = total[:, i * LANES : (i + 1) * LANES]


def collect(src_grad, dst_grad, slot, devices):
    feature = src_grad.shape[0]
    group = 4
    slots = devices * LANES
    whole = pl.BlockSpec(src_grad.shape, lambda i: (0, 0))
    return call(
        functools.partial(collect_kernel, group=group),
        "collect_grads",
        2 * feature * slots * slot.size,
        2 * feature * (slots + slot.size),
        grid=(devices // group,),
        in_specs=[whole, whole, pl.BlockSpec(slot.shape, lambda i: (0, 0))],
        out_specs=pl.BlockSpec((group, feature, LANES), lambda i: (i, 0, 0)),
        out_shape=jax.ShapeDtypeStruct((devices, feature, LANES), BF16),
    )(src_grad, dst_grad, slot)


def add_kernel(*refs, rows, cap, with_neg, first):
    refs = list(refs)
    recv_ref, req_ref = refs[:2]
    refs = refs[2:]
    if with_neg:
        neg_ref, neg_req_ref = refs[:2]
        refs = refs[2:]
    if not first:
        so_far_ref = refs.pop(0)
    out_ref, flat = refs[:2]
    devices = recv_ref.shape[0]
    step = pl.program_id(0)

    @pl.when(step == 0)
    def _():
        for d in range(devices):
            flat[:, d * LANES : (d + 1) * LANES] = recv_ref[d]

    base = step * rows
    row = jnp.concatenate([req_ref[d : d + 1, :] for d in range(devices)], axis=1)
    total = dot(flat[...], one_hot(rows, row, base), NT)
    if with_neg:
        row = jnp.concatenate([neg_req_ref[d : d + 1, :cap] for d in range(devices)], axis=1)
        total = total + dot(neg_ref[...].astype(F32).T.astype(BF16), one_hot(rows, row, base), NT)
    if not first:
        total = total + so_far_ref[...]
    out_ref[...] = total


def add_rows(recv, requests, so_far, neg, neg_requests, cap, rows_dev):
    devices, feature, _ = recv.shape
    rows = 512 if devices * LANES <= 4096 else 128
    slots = devices * LANES
    with_neg = neg is not None
    whole_req = pl.BlockSpec((devices, LANES), lambda i: (0, 0))
    rows_spec = pl.BlockSpec((feature, rows), lambda i: (0, i))
    operands = [recv, requests]
    specs = [pl.BlockSpec((devices, feature, LANES), lambda i: (0, 0, 0)), whole_req]
    if with_neg:
        operands += [neg, neg_requests]
        specs += [pl.BlockSpec(neg.shape, lambda i: (0, 0)), whole_req]
    if so_far is not None:
        operands.append(so_far)
        specs.append(rows_spec)
    return call(
        functools.partial(
            add_kernel, rows=rows, cap=cap, with_neg=with_neg, first=so_far is None
        ),
        "add_grads",
        2 * feature * slots * rows_dev,
        2 * feature * slots + 8 * feature * rows_dev,
        grid=(rows_dev // rows,),
        in_specs=specs,
        out_specs=rows_spec,
        out_shape=jax.ShapeDtypeStruct((feature, rows_dev), F32),
        scratch_shapes=[pltpu.VMEM((feature, slots), BF16)],
    )(*operands)


def exchange(value, axes=("shard", "grp")):
    return lax.all_to_all(value, axes, split_axis=0, concat_axis=0, tiled=True)


def pad_lanes(value, width, fill):
    return jnp.pad(value, ((0, 0), (0, width - value.shape[1])), constant_values=fill)


def body(entity_table, rel_diag, src_ids, dst_ids, rel_ids, neg_ids):
    rows_dev, feature = entity_table.shape
    sharers = lax.axis_size("grp")
    devices = lax.axis_size("shard") * sharers
    spans, neg_count = neg_ids.shape
    edge_count = src_ids.shape[0]
    block_len = edge_count // spans
    edge_cap = 4 * edge_count // devices
    chunks = round_up(edge_cap, LANES) // LANES
    part_width = neg_count // sharers
    neg_cap = round_up(2 * spans * part_width // devices, 16)
    width = round_up(block_len, 512)
    part = round_up(part_width, LANES)

    table = entity_table.T.astype(BF16)
    own_ids = lax.dynamic_slice_in_dim(
        neg_ids, lax.axis_index("grp") * part_width, part_width, 1
    )
    ends = jnp.concatenate(
        [src_ids.reshape(spans, block_len), dst_ids.reshape(spans, block_len)]
    )
    edge_req, *edge_slots = make_slots(pad_lanes(ends, width, -1), rows_dev, devices, chunks)
    neg_req, neg_slot = make_slots(pad_lanes(own_ids, part, -1), rows_dev, devices, 1)
    rel_rows = pad_lanes(rel_ids.reshape(spans, block_len), width, -1)

    asked = exchange(jnp.concatenate([edge_req, neg_req], axis=1))
    edge_asked = [asked[:, c * LANES : (c + 1) * LANES] for c in range(chunks)]
    neg_asked = asked[:, chunks * LANES :]

    neg_rows = gather_neg(table, neg_asked, neg_cap)
    neg_back = exchange(neg_rows.reshape(devices, neg_cap, feature))
    edge_back = [exchange(gather(table, edge_asked[c])) for c in range(chunks)]

    own_neg = spread_neg(neg_back.reshape(devices * neg_cap, feature), neg_slot, neg_cap)
    negatives = lax.all_gather(own_neg, "grp", axis=0, tiled=False)
    rows = None
    for c in range(chunks):
        rows = spread(edge_back[c], edge_slots[c], rows)
    src_grad, dst_grad, neg_grad = edges(rows, rel_rows, rel_diag.T, negatives)

    edge_recv = [exchange(collect(src_grad, dst_grad, edge_slots[c], devices)) for c in range(chunks)]
    neg_parts = exchange(neg_grad, "grp")
    neg_out = collect_neg(neg_parts, neg_slot, neg_cap, devices)
    neg_recv = exchange(neg_out.reshape(devices, neg_cap, feature))
    grad = None
    for c in range(chunks):
        last = c == chunks - 1
        grad = add_rows(
            edge_recv[c],
            edge_asked[c],
            grad,
            neg_recv.reshape(devices * neg_cap, feature) if last else None,
            neg_asked if last else None,
            neg_cap,
            rows_dev,
        )
    return grad.T


def solution(mesh):
    placed = (
        P(("shard", "grp"), None),
        P(),
        P(("shard", "grp")),
        P(("shard", "grp")),
        P(("shard", "grp")),
        P("shard", None),
    )
    return jax.shard_map(
        body, mesh=mesh, in_specs=placed, out_specs=P(("shard", "grp"), None), check_vma=False
    )
```

time: 987 us -> 514 us (0.52)
  local copies, waits for them, and re-layouts: 323 us -> 21.3 us
  waiting for transfers between devices: 491 us -> 230 us
  Pallas kernels: 0 us -> 189 us
  other arithmetic: 94.4 us -> 5.83 us
  blocking collectives: 0 us -> 23.2 us
  matrix products: 18.8 us -> 0 us
    pallas_call x0 -> x14, Pallas kernels: none -> 189 us  [the longest x2 42.7 us: add_rows(): call(functools.partial(add_kernel, rows=rows, cap=cap, with_neg=with_neg,...]
    all_to_all x6 -> x7, waiting for transfers between devices: 370 us -> 197 us  [exchange(): return lax.all_to_all(value, axes, split_axis=0, concat_axis=0, tiled=True)]
    reshape x21 -> x6, local copies, waits for them, and re-layouts: 115 us -> 3.47 us  [the longest x2 1.23 us: spread(): slot.reshape(segments, 1, width)]
    scatter-add x2 -> x0, other arithmetic: 70.3 us -> none  [the longest x1 56.8 us: body(): entity_grad = entity_grad.at[got_edge].add(recv_edge.reshape(-1, feature))]
    gather x5 -> x0, local copies, waits for them, and re-layouts: 67.9 us -> none  [the longest x2 37.1 us: body(): look_edge = entity_table[got_edge].astype(jnp.bfloat16)]
    unnamed x3 -> x1, waiting for transfers between devices: 65.8 us -> 0.02 us
    scatter x4 -> x0, local copies, waits for them, and re-layouts: 54.3 us -> none  [the longest x1 27.8 us: body(): jnp.zeros((devices * edge_cap, feature), jnp.float32).at[edge_slot]]
    convert_element_type x3 -> x0, local copies, waits for them, and re-layouts: 33.6 us -> none  [the longest x2 32.2 us: body(): look_edge = entity_table[got_edge].astype(jnp.bfloat16)]
  transfers between devices with their start and end apart: 8 -> 8, of which waited for: 4 -> 8; matrix products, arithmetic and copies ran while one was open for 23% -> 3% of each run, Pallas kernels for 0% -> 22%
where the time goes in v1:
time: 514 us; the launch traced here: 513 us
  waiting for transfers between devices  230 us (45%)
  Pallas kernels  189 us (37%)
  starting transfers between devices  29.7 us (6%)
  blocking collectives  23.2 us (5%)
  local copies, waits for them, and re-layouts  21.3 us (4%)
  between operations  13.5 us (3%)
  other arithmetic  5.83 us (1%)
    all_to_all x7, waiting for transfers between devices, exchange(): return lax.all_to_all(value, axes, split_axis=0, concat_axis=0, tiled=True)  197 us
    pallas_call x2, Pallas kernels, add_rows(): call(functools.partial(add_kernel, rows=rows, cap=cap, with_neg=with_neg,...  42.7 us
    pallas_call x2, Pallas kernels, spread(): call(functools.partial(spread_kernel, first=so_far is None), 'spread_rows...  38.3 us
    pallas_call x2, Pallas kernels, gather(): call(functools.partial(gather_kernel, group=group), 'gather_rows', 2 * fe...  35.9 us
    pallas_call x2, Pallas kernels, collect(): call(functools.partial(collect_kernel, group=group), 'collect_grads', 2 *...  35.9 us
    all_gather x1, waiting for transfers between devices, body(): negatives = lax.all_gather(own_neg, 'grp', axis=0, tiled=False)  33.1 us
    all_to_all x7, starting transfers between devices, exchange(): return lax.all_to_all(value, axes, split_axis=0, concat_axis=0, tiled=True)  29.5 us
    all_to_all x1, blocking collectives, exchange(): return lax.all_to_all(value, axes, split_axis=0, concat_axis=0, tiled=True)  23.2 us
  transfers between devices with their start and end apart: 8, of which 8 were waited for; matrix products, arithmetic and copies ran while one was open for 3% of the time, Pallas kernels for 22%

profile of v1, /device:TPU:0, one launch (start us, length us, event | category | flops | bytes accessed | tf_op | source)
XLA Modules:
  0.0 512.8 jit_solution(4541022210018629987)
XLA Ops:
  6.5 0.0 copy-start
  6.5 0.8 reshape.32
  7.3 0.8 reshape.33
  8.1 0.0 copy-done
  8.1 0.1 constant_dynamic-slice_fusion
  8.2 0.6 pad.13.ids_ref
  8.8 0.6 pad.12.ids_ref
  9.4 2.0 slots.3
  11.4 8.3 %slots.2 = (s32[32,256]{1,0:T(8,128)}, s32[4,1024]{1,0:T(4,128)}, s32[4,1024]{1,0:T(4,128)}) custom-call(s32[4,1024]{1,0:T(4,128)} %pad.12.ids_ref), custom_call_target="tpu_custom_call" | custom-call | flops 67108864 | bytes 32768 | tf_op jit(solution)/shard_map/slots/pallas_call | solution.py:82
  19.7 0.8 add_bitcast_fusion
  20.5 0.7 copy.8
  21.1 7.3 %all-to-all-start = ((s32[32,1,384]{2,1,0:T(1,128)}), s32[32,1,384]{2,1,0:T(1,128)S(1)}, u32[]{:S(2)}, u32[]{:S(2)}) async-start(s32[32,1,384]{2,1,0:T(1,128)} %copy.8), calls=%async_computation | async-start | bytes 98304 | tf_op jit(solution)/shard_map/all_to_all | solution.py:394
  28.4 5.0 convert_bitcast_fusion.table_ref
  33.5 2.3 all-to-all-done
  35.8 0.6 fusion
  36.4 6.7 %gather_negatives.1 = bf16[1024,400]{1,0:T(8,128)(2,1)} custom-call(bf16[400,4096]{1,0:T(8,128)(2,1)} %convert_bitcast_fusion.table_ref, s32[32,128]{1,0:T(8,128)} %get-tuple-element.21.req_ref.refs_3_), custom_call_target="tpu_custom_call" | custom-call | flops 3355443200 | bytes 4096000 | tf_op jit(solution)/shard_map/gather_negatives/pallas_call | solution.py:130
  43.1 3.5 all-to-all-start.3
  46.6 18.0 %gather_rows.3 = bf16[32,400,128]{2,1,0:T(8,128)(2,1)} custom-call(bf16[400,4096]{1,0:T(8,128)(2,1)} %convert_bitcast_fusion.table_ref, s32[32,128]{1,0:T(8,128)} %get-tuple-element.22.req_ref.refs_1_), custom_call_target="tpu_custom_call" | custom-call | flops 13421772800 | bytes 6553600 | tf_op jit(solution)/shard_map/gather_rows/pallas_call | solution.py:105
  64.6 8.3 %all-to-all-done.3 = bf16[32,32,400]{2,1,0:T(8,128)(2,1)S(1)} async-done(((bf16[32,32,400]{2,1,0:T(8,128)(2,1)}), bf16[32,32,400]{2,1,0:T(8,128)(2,1)S(1)}, u32[]{:S(2)}, u32[]{:S(2)}) %all-to-all-start.3) | async-done | bytes 819232 | tf_op jit(solution)/shard_map/all_to_all | solution.py:394
  72.9 0.0 copy-start.2
  72.9 1.0 copy-done.2
  73.8 3.7 all-to-all-start.2
  77.6 17.9 %gather_rows.2 = bf16[32,400,128]{2,1,0:T(8,128)(2,1)} custom-call(bf16[400,4096]{1,0:T(8,128)(2,1)} %convert_bitcast_fusion.table_ref, s32[32,128]{1,0:T(8,128)} %get-tuple-element.23.req_ref.refs_1_), custom_call_target="tpu_custom_call" | custom-call | flops 13421772800 | bytes 6553600 | tf_op jit(solution)/shard_map/gather_rows/pallas_call | solution.py:105
  95.5 0.0 copy-start.9
  95.5 0.0 copy-start.7
  95.5 56.3 %all-to-all-done.2.refs_0_ = bf16[32,400,128]{2,1,0:T(8,128)(2,1)} async-done(((bf16[32,400,128]{2,1,0:T(8,128)(2,1)}), bf16[32,400,128]{2,1,0:T(8,128)(2,1)}, u32[]{:S(2)}, u32[]{:S(2)}) %all-to-all-start.2) | async-done | bytes 3276832 | tf_op jit(solution)/shard_map/all_to_all | solution.py:394
  151.8 3.9 all-to-all-start.1
  155.8 0.2 all-gather.3.cloned.1.call-start
  156.0 2.8 spread_negatives.1
  158.8 2.0 copy.10
  160.8 0.0 all-gather.3.cloned.1.call-update
  160.8 0.0 copy-done.9
  160.9 0.1 reshape.36
  160.9 0.6 reshape.37.rel_ids_ref
  161.5 0.0 copy-done.7
  161.5 0.6 reshape.34.refs_1_
  162.2 0.0 copy-done.8
  162.2 0.6 reshape.35.refs_1_
  162.8 0.0 copy-done.6
  162.8 0.8 copy.9
  163.6 33.1 %all-gather.3.cloned.1.call-done = bf16[8,256,400]{1,2,0:T(8,128)(2,1)} async-done(((bf16[2,256,400]{1,2,0:T(8,128)(2,1)}), bf16[8,256,400]{1,2,0:T(8,128)(2,1)}) %all-gather.3.cloned.1.call-update) | async-done | bytes 1638416 | tf_op jit(solution)/shard_map/all_gather | solution.py:435
  196.7 3.7 copy.11
  200.4 19.1 %spread_rows.2.refs_2_ = bf16[400,4096]{1,0:T(8,128)(2,1)} custom-call(bf16[32,400,128]{2,1,0:T(8,128)(2,1)} %all-to-all-done.2.refs_0_, s32[4,1,1024]{2,1,0:T(1,128)} %reshape.35.refs_1_), custom_call_target="tpu_custom_call" | custom-call | flops 13421772800 | bytes 6553600 | tf_op jit(solution)/shard_map/spread_rows/pallas_call | solution.py:210
  219.4 10.7 %all-to-all-done.1.refs_0_ = bf16[32,400,128]{2,1,0:T(8,128)(2,1)S(1)} async-done(((bf16[32,400,128]{2,1,0:T(8,128)(2,1)}), bf16[32,400,128]{2,1,0:T(8,128)(2,1)S(1)}, u32[]{:S(2)}, u32[]{:S(2)}) %all-to-all-start.1) | async-done | bytes 3276832 | tf_op jit(solution)/shard_map/all_to_all | solution.py:394
  230.2 1.7 copy-done.3
  231.9 19.3 %spread_rows.3.src_ref.dst_ref = bf16[400,4096]{1,0:T(8,128)(2,1)} custom-call(bf16[32,400,128]{2,1,0:T(8,128)(2,1)} %copy-done.3, s32[4,1,1024]{2,1,0:T(1,128)} %reshape.34.refs_1_, bf16[400,4096]{1,0:T(8,128)(2,1)} %spread_rows.2.refs_2_), custom_call_target="tpu_custom_call" | custom-call | flops 13421772800 | bytes 6553600 | tf_op jit(solution)/shard_map/spread_rows/pallas_call | solution.py:210
  251.1 12.9 %edges.1 = (bf16[400,2048]{1,0:T(8,128)(2,1)}, bf16[400,2048]{1,0:T(8,128)(2,1)}, bf16[4,2,256,400]{3,2,1,0:T(8,128)(2,1)}) custom-call(bf16[400,4096]{1,0:T(8,128)(2,1)} %spread_rows.3.src_ref.dst_ref, bf16[400,4096]{1,0:T(8,128)(2,1)} %spread_rows.3.src_ref.dst_ref, s32[2,1,1024]{2,1,0:T(1,128)} %reshape.37.rel_ids_ref, f32[400,64]{1,0:T(8,128)} %bitcast.19, ...), custom_call_target="tpu_custom_call" | custom-call | flops 5033164800 | bytes 9830400 | tf_op jit(solution)/shard_map/edges/pallas_call | solution.py:275
  264.0 2.8 copy.12
  266.8 23.2 %all_to_all.47 = bf16[4,2,256,400]{2,3,1,0:T(8,128)(2,1)S(1)} all-to-all(bf16[4,2,256,400]{2,3,1,0:T(8,128)(2,1)S(1)} %copy.12), channel_id=1, replica_groups=mesh['shard'=8,'grp'=4] {'grp'}, dimensions={0} | all-to-all | bytes 3276800 | tf_op jit(solution)/shard_map/all_to_all | solution.py:394
  290.0 2.3 copy.13.grad_ref
  292.3 3.4 collect_negatives.1
  295.7 3.0 all-to-all-start.6
  298.8 18.0 %collect_grads.3 = bf16[32,400,128]{2,1,0:T(8,128)(2,1)} custom-call(bf16[400,2048]{1,0:T(8,128)(2,1)} %get-tuple-element.18.src_ref, bf16[400,2048]{1,0:T(8,128)(2,1)} %get-tuple-element.19.dst_ref, s32[4,1024]{1,0:T(4,128)} %get-tuple-element.16.slot_ref), custom_call_target="tpu_custom_call" | custom-call | flops 13421772800 | bytes 6553600 | tf_op jit(solution)/shard_map/collect_grads/pallas_call | solution.py:322
  316.7 8.3 %all-to-all-done.6 = bf16[32,32,400]{2,1,0:T(8,128)(2,1)S(1)} async-done(((bf16[32,32,400]{2,1,0:T(8,128)(2,1)}), bf16[32,32,400]{2,1,0:T(8,128)(2,1)S(1)}, u32[]{:S(2)}, u32[]{:S(2)}) %all-to-all-start.6) | async-done | bytes 819232 | tf_op jit(solution)/shard_map/all_to_all | solution.py:394
  325.0 1.0 copy-done.5
  326.0 3.6 all-to-all-start.7
  329.6 17.9 %collect_grads.2 = bf16[32,400,128]{2,1,0:T(8,128)(2,1)} custom-call(bf16[400,2048]{1,0:T(8,128)(2,1)} %get-tuple-element.18.src_ref, bf16[400,2048]{1,0:T(8,128)(2,1)} %get-tuple-element.19.dst_ref, s32[4,1024]{1,0:T(4,128)} %get-tuple-element.15.slot_ref), custom_call_target="tpu_custom_call" | custom-call | flops 13421772800 | bytes 6553600 | tf_op jit(solution)/shard_map/collect_grads/pallas_call | solution.py:322
  347.5 56.3 %all-to-all-done.7.refs_0_ = bf16[32,400,128]{2,1,0:T(8,128)(2,1)S(1)} async-done(((bf16[32,400,128]{2,1,0:T(8,128)(2,1)}), bf16[32,400,128]{2,1,0:T(8,128)(2,1)S(1)}, u32[]{:S(2)}, u32[]{:S(2)}) %all-to-all-start.7) | async-done | bytes 3276832 | tf_op jit(solution)/shard_map/all_to_all | solution.py:394
  403.8 4.3 all-to-all-start.4
  408.1 0.0 copy-done.4
  408.1 19.0 %add_grads.2.refs_4_ = f32[400,4096]{1,0:T(8,128)} custom-call(bf16[32,400,128]{2,1,0:T(8,128)(2,1)} %copy-done.4, s32[32,128]{1,0:T(8,128)} %get-tuple-element.22.req_ref.refs_1_), custom_call_target="tpu_custom_call" | custom-call | flops 13421772800 | bytes 16384000 | tf_op jit(solution)/shard_map/add_grads/pallas_call | solution.py:378
  427.2 55.1 %all-to-all-done.4.refs_0_ = bf16[32,400,128]{2,1,0:T(8,128)(2,1)} async-done(((bf16[32,400,128]{2,1,0:T(8,128)(2,1)}), bf16[32,400,128]{2,1,0:T(8,128)(2,1)}, u32[]{:S(2)}, u32[]{:S(2)}) %all-to-all-start.4) | async-done | bytes 3276832 | tf_op jit(solution)/shard_map/all_to_all | solution.py:394
  482.3 23.7 %add_grads.3 = f32[400,4096]{1,0:T(8,128)} custom-call(bf16[32,400,128]{2,1,0:T(8,128)(2,1)} %all-to-all-done.4.refs_0_, s32[32,128]{1,0:T(8,128)} %get-tuple-element.23.req_ref.refs_1_, bf16[1024,400]{1,0:T(8,128)(2,1)} %bitcast.17, s32[32,128]{1,0:T(8,128)} %get-tuple-element.21.req_ref.refs_3_, f32[400,4096]{1,0:T(8,128)} %add_grads.2.refs_4_), custom_call_target="tpu_custom_call" | custom-call | flops 13421772800 | bytes 16384000 | tf_op jit(solution)/shard_map/add_grads/pallas_call | solution.py:378
  506.0 0.0 copy-done.1
  (9 shorter events, 0.0 us)
Async XLA Ops:
  6.5 1.6 copy-start
  21.1 14.6 %all-to-all-start = ((s32[32,1,384]{2,1,0:T(1,128)}), s32[32,1,384]{2,1,0:T(1,128)S(1)}, u32[]{:S(2)}, u32[]{:S(2)}) async-start(s32[32,1,384]{2,1,0:T(1,128)} %copy.8), calls=%async_computation | async-start | bytes 98304 | tf_op jit(solution)/shard_map/all_to_all | solution.py:394
  43.1 29.8 %all-to-all-start.3 = ((bf16[32,32,400]{2,1,0:T(8,128)(2,1)}), bf16[32,32,400]{2,1,0:T(8,128)(2,1)S(1)}, u32[]{:S(2)}, u32[]{:S(2)}) async-start(bf16[32,32,400]{2,1,0:T(8,128)(2,1)} %bitcast.18), calls=%async_computation.3 | async-start | bytes 2097152 | tf_op jit(solution)/shard_map/all_to_all | solution.py:394
  72.9 1.0 copy-start.2
  73.8 78.0 %all-to-all-start.2 = ((bf16[32,400,128]{2,1,0:T(8,128)(2,1)}), bf16[32,400,128]{2,1,0:T(8,128)(2,1)}, u32[]{:S(2)}, u32[]{:S(2)}) async-start(bf16[32,400,128]{2,1,0:T(8,128)(2,1)} %gather_rows.3), calls=%async_computation.2 | async-start | bytes 6553600 | tf_op jit(solution)/shard_map/all_to_all | solution.py:394
  95.5 65.3 %copy-start.9 = (s32[2000]{0:T(1024)S(1)}, s32[2000]{0:T(1024)}, u32[]{:S(2)}) copy-start(s32[2000]{0:T(1024)} %param.10) | copy-start | bytes 24004
  95.5 66.0 %copy-start.7 = (s32[4,1024]{1,0:T(4,128)S(1)}, s32[4,1024]{1,0:T(4,128)}, u32[]{:S(2)}) copy-start(s32[4,1024]{1,0:T(4,128)} %get-tuple-element.15.slot_ref) | copy-start | bytes 49156
  95.5 66.6 %copy-start.8 = (s32[4,1024]{1,0:T(4,128)S(1)}, s32[4,1024]{1,0:T(4,128)}, u32[]{:S(2)}) copy-start(s32[4,1024]{1,0:T(4,128)} %get-tuple-element.16.slot_ref) | copy-start | bytes 49156
  95.5 67.2 %copy-start.6 = (f32[64,400]{1,0:T(8,128)S(1)}, f32[64,400]{1,0:T(8,128)}, u32[]{:S(2)}) copy-start(f32[64,400]{1,0:T(8,128)} %param.7) | copy-start | bytes 307204
  151.8 78.3 %all-to-all-start.1 = ((bf16[32,400,128]{2,1,0:T(8,128)(2,1)}), bf16[32,400,128]{2,1,0:T(8,128)(2,1)S(1)}, u32[]{:S(2)}, u32[]{:S(2)}) async-start(bf16[32,400,128]{2,1,0:T(8,128)(2,1)} %gather_rows.2), calls=%async_computation.1 | async-start | bytes 6553600 | tf_op jit(solution)/shard_map/all_to_all | solution.py:394
  155.8 40.9 %all-gather.3.cloned.1.call-start = ((), (), s32[]{:S(2)}) async-start(), calls=%async_computation.8 | async-start | bytes 2048000 | tf_op jit(solution)/shard_map/all_gather | solution.py:435
  230.1 1.7 copy-start.3
  295.7 29.3 %all-to-all-start.6 = ((bf16[32,32,400]{2,1,0:T(8,128)(2,1)}), bf16[32,32,400]{2,1,0:T(8,128)(2,1)S(1)}, u32[]{:S(2)}, u32[]{:S(2)}) async-start(bf16[32,32,400]{2,1,0:T(8,128)(2,1)} %bitcast.15), calls=%async_computation.6 | async-start | bytes 2097152 | tf_op jit(solution)/shard_map/all_to_all | solution.py:394
  325.0 1.0 copy-start.5
  326.0 77.9 %all-to-all-start.7 = ((bf16[32,400,128]{2,1,0:T(8,128)(2,1)}), bf16[32,400,128]{2,1,0:T(8,128)(2,1)S(1)}, u32[]{:S(2)}, u32[]{:S(2)}) async-start(bf16[32,400,128]{2,1,0:T(8,128)(2,1)} %collect_grads.3), calls=%async_computation.7 | async-start | bytes 6553600 | tf_op jit(solution)/shard_map/all_to_all | solution.py:394
  403.8 4.3 copy-start.4
  403.8 78.4 %all-to-all-start.4 = ((bf16[32,400,128]{2,1,0:T(8,128)(2,1)}), bf16[32,400,128]{2,1,0:T(8,128)(2,1)}, u32[]{:S(2)}, u32[]{:S(2)}) async-start(bf16[32,400,128]{2,1,0:T(8,128)(2,1)} %collect_grads.2), calls=%async_computation.4 | async-start | bytes 6553600 | tf_op jit(solution)/shard_map/all_to_all | solution.py:394
  482.3 23.7 %copy-start.1 = (s32[2,1000]{1,0:T(2,128)S(1)}, s32[2,1000]{1,0:T(2,128)}, u32[]{:S(2)}) copy-start(s32[2,1000]{1,0:T(2,128)} %param.11) | copy-start | bytes 24004
Sparse Core Ops, SparseCore 0:
  161.0 35.6 all-gather.2

commit v2 on v1

v2 whole, which is shorter than its diff:
```python
import functools

import jax
import jax.numpy as jnp
from jax import lax
from jax.experimental import pallas as pl
from jax.experimental.pallas import tpu as pltpu
from jax.sharding import PartitionSpec as P

LANES = 128
POOL = 48
VMEM_BYTES = 56 << 20
F32 = jnp.float32
BF16 = jnp.bfloat16
NN = (((1,), (0,)), ((), ()))
NT = (((1,), (1,)), ((), ()))
TN = (((0,), (0,)), ((), ()))


def round_up(value, unit):
    return -(-value // unit) * unit


def dot(left, right, dims):
    return lax.dot_general(left, right, dims, preferred_element_type=F32)


def one_hot(rows, row, base=0):
    places = lax.broadcasted_iota(jnp.int32, (rows, row.shape[1]), 0) + base
    return jnp.where(places == row, 1.0, 0.0).astype(BF16)


def call(kernel, name, flops, nbytes, **kwargs):
    return pl.pallas_call(
        kernel,
        name=name,
        compiler_params=pltpu.CompilerParams(vmem_limit_bytes=VMEM_BYTES),
        cost_estimate=pl.CostEstimate(flops=flops, bytes_accessed=nbytes, transcendentals=0),
        **kwargs,
    )


def ranks(members, mixer):
    groups = members[0].shape[0]
    both = dot(jnp.concatenate(members, axis=0).astype(BF16), mixer, NN)
    taken = jnp.zeros((groups, LANES), F32)
    found = []
    for i, member in enumerate(members):
        chunk = both[i * groups : (i + 1) * groups]
        found.append(jnp.sum((chunk[:, :LANES] + taken) * member, axis=0, keepdims=True))
        taken = taken + chunk[:, LANES:]
    return [rank.astype(jnp.int32) for rank in found], taken


def fill(members, codes, places, count):
    groups = members[0].shape[0]
    high = [m * (c // LANES).astype(F32) for m, c in zip(members, codes)]
    low = [m * (c % LANES).astype(F32) for m, c in zip(members, codes)]
    left = jnp.concatenate(
        [jnp.concatenate(high, axis=1), jnp.concatenate(low, axis=1)], axis=0
    ).astype(BF16)
    sums = dot(left, one_hot(count, jnp.concatenate(places, axis=1)), NT)
    return (LANES * sums[:groups] + sums[groups:]).astype(jnp.int32) - 1


def slots_kernel(ends_ref, own_ref, *refs, rows_dev, devices, sharers, chunks, neg_cap):
    msg_ref = refs[0]
    slot_refs = refs[1 : 1 + chunks]
    pool_ref = refs[1 + chunks] if chunks > 1 else None
    neg_ref = refs[-1]
    row = lax.broadcasted_iota(jnp.int32, (LANES, 2 * LANES), 0)
    lane = lax.broadcasted_iota(jnp.int32, (LANES, 2 * LANES), 1)
    mixer = jnp.where(row < lane, 1.0, 0.0).astype(BF16)
    owners = lax.broadcasted_iota(jnp.int32, (devices, LANES), 0)

    def prepare(ids_ref):
        where, holder, codes, members = [], [], [], []
        for segment in range(ids_ref.shape[0]):
            for start in range(0, ids_ref.shape[1], LANES):
                ids = ids_ref[segment : segment + 1, start : start + LANES]
                owner = jnp.where(ids >= 0, ids // rows_dev, -1)
                where.append((slice(segment, segment + 1), slice(start, start + LANES)))
                holder.append(owner)
                codes.append(jnp.where(ids >= 0, ids - owner * rows_dev + 1, 0))
                members.append(jnp.where(owners == owner, 1.0, 0.0))
        found, _ = ranks(members, mixer)
        return where, holder, codes, members, found

    where, holder, codes, members, found = prepare(ends_ref)
    for chunk in range(chunks):
        places = []
        for at, owner, rank in zip(where, holder, found):
            place = rank - chunk * LANES
            place = jnp.where((owner >= 0) & (place >= 0) & (place < LANES), place, -1)
            slot_refs[chunk][at] = jnp.where(place >= 0, owner * LANES + place, -1)
            places.append(place)
        msg_ref[:, chunk * LANES : (chunk + 1) * LANES] = fill(members, codes, places, LANES)
    offset = chunks * LANES
    flag = jnp.full((1, 1), -1, jnp.int32)
    if chunks > 1:
        shards = devices // sharers
        room = sharers * POOL
        shard_rows = lax.broadcasted_iota(jnp.int32, (shards, LANES), 0)
        spilled, spill_codes = [], []
        for owner, code, rank in zip(holder, codes, found):
            shard = jnp.where(rank >= LANES, owner // sharers, -1)
            spilled.append(jnp.where(shard_rows == shard, 1.0, 0.0))
            spill_codes.append(code + (owner % sharers) * rows_dev)
        pooled, taken = ranks(spilled, mixer)
        places = []
        for at, owner, rank, place in zip(where, holder, found, pooled):
            inside = (owner >= 0) & (rank >= LANES) & (place < room)
            pool_ref[at] = jnp.where(inside, owner // sharers * room + place, -1)
            places.append(jnp.where(inside, place, -1))
        listed = fill(spilled, spill_codes, places, 2 * LANES)
        for shard in range(shards):
            msg_ref[shard * sharers : (shard + 1) * sharers, offset : offset + 2 * LANES] = (
                jnp.broadcast_to(listed[shard : shard + 1], (sharers, 2 * LANES))
            )
        offset += 2 * LANES
        most = jnp.max(jnp.max(taken, axis=1, keepdims=True), axis=0, keepdims=True)
        flag = jnp.where(most > room, 1, -1)

    where, holder, codes, members, found = prepare(own_ref)
    for at, owner, rank in zip(where, holder, found):
        neg_ref[at] = jnp.where(owner >= 0, owner * neg_cap + rank, -1)
    places = [jnp.where(owner >= 0, rank, -1) for owner, rank in zip(holder, found)]
    listed = fill(members, codes, places, LANES)
    lanes = lax.broadcasted_iota(jnp.int32, listed.shape, 1)
    msg_ref[:, offset:] = jnp.where(lanes == LANES - 1, flag, listed)


def make_slots(ends, own, rows_dev, devices, sharers, chunks, neg_cap):
    pooled = chunks > 1
    width = (chunks + 1 + 2 * pooled) * LANES
    return call(
        functools.partial(
            slots_kernel,
            rows_dev=rows_dev,
            devices=devices,
            sharers=sharers,
            chunks=chunks,
            neg_cap=neg_cap,
        ),
        "slots",
        16 * devices * LANES * ends.size,
        8 * ends.size,
        out_shape=[jax.ShapeDtypeStruct((devices, width), jnp.int32)]
        + [jax.ShapeDtypeStruct(ends.shape, jnp.int32)] * (chunks + pooled)
        + [jax.ShapeDtypeStruct(own.shape, jnp.int32)],
    )(ends, own)


def pack(out_ref, at, start, rows):
    count, feature = rows.shape
    full = round_up(feature, LANES)
    rows = jnp.concatenate([rows, jnp.zeros((count, full - feature), rows.dtype)], axis=1)
    for piece in range(full // LANES):
        out_ref[at, start + piece * count : start + (piece + 1) * count, :] = rows[
            :, piece * LANES : (piece + 1) * LANES
        ].astype(out_ref.dtype)


def unpack(in_ref, at, start, count, flat_ref, to):
    for piece in range(flat_ref.shape[1] // LANES):
        flat_ref[to : to + count, piece * LANES : (piece + 1) * LANES] = in_ref[
            at, start + piece * count : start + (piece + 1) * count, :
        ]


def gather_kernel(table_ref, *refs, group, neg_cap):
    feature, rows_dev = table_ref.shape
    first = pl.program_id(0) * group
    req_ref, out_ref = refs[0], refs[-1]
    row = [req_ref[pl.ds(first + i, 1), :] for i in range(group)]
    if neg_cap:
        row += [refs[1][pl.ds(first + i, 1), :neg_cap] for i in range(group)]
    rows = dot(table_ref[...], one_hot(rows_dev, jnp.concatenate(row, axis=1)), NN)
    start = out_ref.shape[1] - feature
    for i in range(group):
        out_ref[i, start:] = rows[:, i * LANES : (i + 1) * LANES].astype(BF16)
    if neg_cap:
        neg = rows[:, group * LANES :].T
        for i in range(group):
            pack(out_ref, i, 0, neg[i * neg_cap : (i + 1) * neg_cap])


def gather(table, requests, neg_requests=None, neg_cap=0):
    feature, rows_dev = table.shape
    devices = requests.shape[0]
    group = 4
    height = feature + neg_cap * (round_up(feature, LANES) // LANES)
    slots = devices * (LANES + neg_cap)
    whole = pl.BlockSpec((devices, LANES), lambda i: (0, 0))
    return call(
        functools.partial(gather_kernel, group=group, neg_cap=neg_cap),
        "gather_rows",
        2 * feature * rows_dev * slots,
        2 * feature * (rows_dev + slots),
        grid=(devices // group,),
        in_specs=[pl.BlockSpec((feature, rows_dev), lambda i: (0, 0)), whole]
        + ([whole] if neg_cap else []),
        out_specs=pl.BlockSpec((group, height, LANES), lambda i: (i, 0, 0)),
        out_shape=jax.ShapeDtypeStruct((devices, height, LANES), BF16),
    )(table, requests, *([neg_requests] if neg_cap else []))


def gather_pool_kernel(table_ref, req_ref, out_ref, *, group):
    rows_dev = table_ref.shape[1]
    row = req_ref[...].reshape(1, group * POOL)
    rows = dot(table_ref[...], one_hot(rows_dev, row), NN).T
    for i in range(group):
        pack(out_ref, i, 0, rows[i * POOL : (i + 1) * POOL])


def gather_pool(table, requests, devices):
    feature, rows_dev = table.shape
    relays = requests.shape[0]
    group = 8
    steps = devices // group
    height = POOL * (round_up(feature, LANES) // LANES)
    return call(
        functools.partial(gather_pool_kernel, group=group),
        "gather_pool",
        2 * feature * rows_dev * requests.size,
        2 * feature * (rows_dev + requests.size),
        grid=(relays * steps,),
        in_specs=[
            pl.BlockSpec((feature, rows_dev), lambda i: (0, 0)),
            pl.BlockSpec((1, 1, group * POOL), lambda i: (i, 0, 0)),
        ],
        out_specs=pl.BlockSpec((group, height, LANES), lambda i: (i, 0, 0)),
        out_shape=jax.ShapeDtypeStruct((relays * devices, height, LANES), BF16),
    )(table, requests.reshape(relays * steps, 1, group * POOL))


def spread_neg_kernel(back_ref, slot_ref, out_ref, flat, *, cap):
    parts = slot_ref.shape[0]
    feature = out_ref.shape[-1]
    devices = back_ref.shape[0]
    for d in range(devices):
        unpack(back_ref, d, 0, cap, flat, d * cap)
    for part in range(parts):
        hot = one_hot(devices * cap, slot_ref[part : part + 1, :])
        out_ref[part] = dot(hot, flat[...], TN)[:, :feature].astype(BF16)


def spread_neg(back, slot, cap, feature):
    devices = back.shape[0]
    parts, width = slot.shape
    full = round_up(feature, LANES)
    height = cap * full // LANES
    return call(
        functools.partial(spread_neg_kernel, cap=cap),
        "spread_negatives",
        2 * devices * cap * full * slot.size,
        2 * devices * cap * full,
        grid=(1,),
        in_specs=[
            pl.BlockSpec((devices, height, LANES), lambda i: (0, 0, 0)),
            pl.BlockSpec(slot.shape, lambda i: (0, 0)),
        ],
        out_specs=pl.BlockSpec((parts, width, feature), lambda i: (0, 0, 0)),
        out_shape=jax.ShapeDtypeStruct((parts, width, feature), BF16),
        scratch_shapes=[pltpu.VMEM((devices * cap, full), BF16)],
    )(back, slot)


def spread_kernel(*refs, first, pooled):
    back_ref, slot_ref = refs[:2]
    so_far_ref = None if first else refs[2]
    out_ref, flat = refs[2 + (not first) :][:2]
    devices = back_ref.shape[0]
    feature = flat.shape[0]

    @pl.when(pl.program_id(0) == 0)
    def _():
        if pooled:
            for d in range(devices):
                unpack(back_ref, d, 0, POOL, refs[-1], d * POOL)
            flat[...] = refs[-1][...].astype(F32).T[:feature].astype(BF16)
        else:
            start = back_ref.shape[1] - feature
            for d in range(devices):
                flat[:, d * LANES : (d + 1) * LANES] = back_ref[d, start:]

    row = slot_ref[...].reshape(1, slot_ref.shape[-1])
    rows = dot(flat[...], one_hot(flat.shape[1], row), NN)
    if not first:
        rows = rows + so_far_ref[...].astype(F32)
    out_ref[...] = rows.astype(BF16)


def spread(back, slot, so_far, feature, pooled=False):
    devices = back.shape[0]
    segments, width = slot.shape
    slots = devices * (POOL if pooled else LANES)
    tile = 512 if slots <= 4096 else 128
    steps = width // tile
    rows_spec = pl.BlockSpec((feature, tile), lambda i: (0, i))
    extra = [] if so_far is None else [so_far]
    scratch = [pltpu.VMEM((feature, slots), BF16)]
    if pooled:
        scratch.append(pltpu.VMEM((slots, round_up(feature, LANES)), BF16))
    return call(
        functools.partial(spread_kernel, first=so_far is None, pooled=pooled),
        "spread_pool" if pooled else "spread_rows",
        2 * feature * slots * slot.size,
        2 * feature * (slots + slot.size),
        grid=(segments * steps,),
        in_specs=[
            pl.BlockSpec(back.shape, lambda i: (0, 0, 0)),
            pl.BlockSpec((1, 1, tile), lambda i: (i // steps, 0, i % steps)),
        ]
        + [rows_spec] * len(extra),
        out_specs=rows_spec,
        out_shape=jax.ShapeDtypeStruct((feature, slot.size), BF16),
        scratch_shapes=scratch,
    )(back, slot.reshape(segments, 1, width), *extra)


def edges_kernel(
    src_ref, dst_ref, rel_ids_ref, rel_ref, neg_ref, src_grad_ref, dst_grad_ref, neg_grad_ref, sums
):
    step = pl.program_id(1)
    parts, _, part, feature = neg_ref.shape
    negatives = neg_ref[...].reshape(parts * part, feature)
    nrel = rel_ref.shape[1]
    hot = one_hot(nrel, rel_ids_ref[...].reshape(1, rel_ids_ref.shape[-1]))
    table = rel_ref[...]
    relation = jnp.zeros(src_ref.shape, F32)
    for _ in range(3):
        piece = table.astype(BF16)
        relation = relation + dot(piece, hot, NN)
        table = table - piece.astype(F32)
    source = src_ref[...].astype(F32)
    target = dst_ref[...].astype(F32)
    product = source * relation
    positive = jnp.sum(product * target, axis=0, keepdims=True)
    pos_weight = -jax.nn.sigmoid(-positive)
    query = product.astype(BF16)
    weight = jax.nn.sigmoid(dot(negatives, query, NN)).astype(BF16)
    gathered = dot(negatives, weight, TN)
    src_grad_ref[...] = (relation * (pos_weight * target + gathered)).astype(BF16)
    dst_grad_ref[...] = (pos_weight * product).astype(BF16)
    neg_grad = dot(weight, query, NT)

    @pl.when(step == 0)
    def _():
        sums[...] = neg_grad

    @pl.when(step != 0)
    def _():
        sums[...] += neg_grad

    @pl.when(step == pl.num_programs(1) - 1)
    def _():
        neg_grad_ref[...] = sums[...].reshape(neg_grad_ref.shape)


def edges(rows, rel_ids, relations, negatives):
    feature, endpoints = rows.shape
    parts, spans, part, _ = negatives.shape
    width = rel_ids.shape[1]
    tile = 512
    steps = width // tile
    blocks = spans * steps
    edge_spec = pl.BlockSpec((feature, tile), lambda b, i: (0, b * steps + i))
    flops = 6 * feature * parts * part * spans * width
    src_grad, dst_grad, neg_grad = call(
        edges_kernel,
        "edges",
        flops,
        2 * (2 * rows.size + 2 * negatives.size),
        grid=(spans, steps),
        in_specs=[
            edge_spec,
            pl.BlockSpec((feature, tile), lambda b, i: (0, blocks + b * steps + i)),
            pl.BlockSpec((1, 1, tile), lambda b, i: (b, 0, i)),
            pl.BlockSpec(relations.shape, lambda b, i: (0, 0)),
            pl.BlockSpec((parts, 1, part, feature), lambda b, i: (0, b, 0, 0)),
        ],
        out_specs=[
            edge_spec,
            edge_spec,
            pl.BlockSpec((parts, 1, part, feature), lambda b, i: (0, b, 0, 0)),
        ],
        out_shape=[
            jax.ShapeDtypeStruct((feature, endpoints // 2), BF16),
            jax.ShapeDtypeStruct((feature, endpoints // 2), BF16),
            jax.ShapeDtypeStruct(negatives.shape, F32),
        ],
        scratch_shapes=[pltpu.VMEM((parts * part, feature), F32)],
    )(rows, rows, rel_ids.reshape(spans, 1, width), relations, negatives)
    return src_grad, dst_grad, neg_grad


def collect_kernel(src_ref, dst_ref, slot_ref, *refs, group, neg_cap):
    segments, width = slot_ref.shape
    feature = src_ref.shape[0]
    out_ref = refs[-1]
    step = pl.program_id(0)
    total = jnp.zeros((feature, group * LANES), F32)
    for segment in range(segments):
        grads = src_ref if segment < segments // 2 else dst_ref
        start = segment % (segments // 2) * width
        hot = one_hot(group * LANES, slot_ref[segment : segment + 1, :], step * group * LANES)
        total = total + dot(grads[:, start : start + width], hot, NT)
    total = total.astype(BF16)
    first = out_ref.shape[1] - feature
    for i in range(group):
        out_ref[i, first:] = total[:, i * LANES : (i + 1) * LANES]
    if neg_cap:
        neg_grad_ref, neg_slot_ref = refs[:2]
        rows = jnp.zeros((group * neg_cap, feature), F32)
        for part in range(neg_slot_ref.shape[0]):
            row = neg_slot_ref[part : part + 1, :]
            hot = one_hot(group * neg_cap, row, step * group * neg_cap)
            rows = rows + dot(hot, neg_grad_ref[part].astype(BF16), NN)
        for i in range(group):
            pack(out_ref, i, 0, rows[i * neg_cap : (i + 1) * neg_cap])


def collect(src_grad, dst_grad, slot, devices, neg_grad=None, neg_slot=None, neg_cap=0):
    feature = src_grad.shape[0]
    group = 4
    slots = devices * LANES
    height = feature + neg_cap * (round_up(feature, LANES) // LANES)
    whole = pl.BlockSpec(src_grad.shape, lambda i: (0, 0))
    operands = [src_grad, dst_grad, slot]
    specs = [whole, whole, pl.BlockSpec(slot.shape, lambda i: (0, 0))]
    if neg_cap:
        operands += [neg_grad, neg_slot]
        specs += [
            pl.BlockSpec(neg_grad.shape, lambda i: (0, 0, 0)),
            pl.BlockSpec(neg_slot.shape, lambda i: (0, 0)),
        ]
    return call(
        functools.partial(collect_kernel, group=group, neg_cap=neg_cap),
        "collect_grads",
        2 * feature * slots * slot.size,
        2 * feature * (slots + slot.size),
        grid=(devices // group,),
        in_specs=specs,
        out_specs=pl.BlockSpec((group, height, LANES), lambda i: (i, 0, 0)),
        out_shape=jax.ShapeDtypeStruct((devices, height, LANES), BF16),
    )(*operands)


def collect_pool_kernel(src_ref, dst_ref, slot_ref, out_ref, *, group):
    segments, width = slot_ref.shape
    count = group * POOL
    rows = jnp.zeros((count, src_ref.shape[0]), F32)
    for segment in range(segments):
        grads = src_ref if segment < segments // 2 else dst_ref
        start = segment % (segments // 2) * width
        hot = one_hot(count, slot_ref[segment : segment + 1, :], pl.program_id(0) * count)
        rows = rows + dot(hot, grads[:, start : start + width], NT)
    for i in range(group):
        pack(out_ref, i, 0, rows[i * POOL : (i + 1) * POOL])


def collect_pool(src_grad, dst_grad, slot, devices):
    feature = src_grad.shape[0]
    group = 8
    slots = devices * POOL
    height = POOL * (round_up(feature, LANES) // LANES)
    whole = pl.BlockSpec(src_grad.shape, lambda i: (0, 0))
    return call(
        functools.partial(collect_pool_kernel, group=group),
        "collect_pool",
        2 * feature * slots * slot.size,
        2 * feature * (slots + slot.size),
        grid=(devices // group,),
        in_specs=[whole, whole, pl.BlockSpec(slot.shape, lambda i: (0, 0))],
        out_specs=pl.BlockSpec((group, height, LANES), lambda i: (i, 0, 0)),
        out_shape=jax.ShapeDtypeStruct((devices, height, LANES), BF16),
    )(src_grad, dst_grad, slot)


def add_kernel(*refs, rows, neg_cap, first):
    refs = list(refs)
    recv_ref, req_ref = refs[:2]
    refs = refs[2:]
    if neg_cap:
        neg_req_ref = refs.pop(0)
        neg_rows, neg_flat = refs[-2:]
    if not first:
        so_far_ref = refs.pop(0)
    out_ref, flat = refs[:2]
    devices = recv_ref.shape[0]
    feature = flat.shape[0]
    step = pl.program_id(0)

    @pl.when(step == 0)
    def _():
        start = recv_ref.shape[1] - feature
        for d in range(devices):
            flat[:, d * LANES : (d + 1) * LANES] = recv_ref[d, start:]
        if neg_cap:
            for d in range(devices):
                unpack(recv_ref, d, 0, neg_cap, neg_rows, d * neg_cap)
            neg_flat[...] = neg_rows[...].astype(F32).T[:feature].astype(BF16)

    base = step * rows
    row = jnp.concatenate([req_ref[d : d + 1, :] for d in range(devices)], axis=1)
    total = dot(flat[...], one_hot(rows, row, base), NT)
    if neg_cap:
        row = jnp.concatenate([neg_req_ref[d : d + 1, :neg_cap] for d in range(devices)], axis=1)
        total = total + dot(neg_flat[...], one_hot(rows, row, base), NT)
    if not first:
        total = total + so_far_ref[...]
    out_ref[...] = total


def add_rows(recv, requests, so_far, feature, rows_dev, neg_requests=None, neg_cap=0):
    devices = recv.shape[0]
    rows = 512 if devices * LANES <= 4096 else 128
    slots = devices * LANES
    full = round_up(feature, LANES)
    whole_req = pl.BlockSpec((devices, LANES), lambda i: (0, 0))
    rows_spec = pl.BlockSpec((feature, rows), lambda i: (0, i))
    operands = [recv, requests]
    specs = [pl.BlockSpec(recv.shape, lambda i: (0, 0, 0)), whole_req]
    scratch = [pltpu.VMEM((feature, slots), BF16)]
    if neg_cap:
        operands.append(neg_requests)
        specs.append(whole_req)
        scratch += [
            pltpu.VMEM((devices * neg_cap, full), BF16),
            pltpu.VMEM((feature, devices * neg_cap), BF16),
        ]
    if so_far is not None:
        operands.append(so_far)
        specs.append(rows_spec)
    return call(
        functools.partial(add_kernel, rows=rows, neg_cap=neg_cap, first=so_far is None),
        "add_grads",
        2 * feature * slots * rows_dev,
        2 * feature * slots + 8 * feature * rows_dev,
        grid=(rows_dev // rows,),
        in_specs=specs,
        out_specs=rows_spec,
        out_shape=jax.ShapeDtypeStruct((feature, rows_dev), F32),
        scratch_shapes=scratch,
    )(*operands)


def add_pool_kernel(recv_ref, req_ref, out_ref, packed, flat, *, rows):
    feature = flat.shape[0]
    count = packed.shape[0]
    per_relay = count // POOL
    step = pl.program_id(0)

    @pl.when(step == 0)
    def _():
        for relay in range(recv_ref.shape[0] // per_relay):
            for d in range(per_relay):
                unpack(recv_ref, relay * per_relay + d, 0, POOL, packed, d * POOL)
            flat[:, relay * count : (relay + 1) * count] = (
                packed[...].astype(F32).T[:feature].astype(BF16)
            )

    out_ref[...] = dot(flat[...], one_hot(rows, req_ref[...], step * rows), NT)


def add_pool(recv, requests, devices, feature, rows_dev):
    rows = 512
    full = round_up(feature, LANES)
    return call(
        functools.partial(add_pool_kernel, rows=rows),
        "add_pool",
        2 * feature * requests.size * rows_dev,
        2 * feature * requests.size + 4 * feature * rows_dev,
        grid=(rows_dev // rows,),
        in_specs=[
            pl.BlockSpec(recv.shape, lambda i: (0, 0, 0)),
            pl.BlockSpec((1, requests.size), lambda i: (0, 0)),
        ],
        out_specs=pl.BlockSpec((feature, rows), lambda i: (0, i)),
        out_shape=jax.ShapeDtypeStruct((feature, rows_dev), F32),
        scratch_shapes=[
            pltpu.VMEM((devices * POOL, full), BF16),
            pltpu.VMEM((feature, requests.size), BF16),
        ],
    )(recv, requests.reshape(1, -1))


def exchange(value):
    return lax.all_to_all(value, ("shard", "grp"), split_axis=0, concat_axis=0, tiled=True)


def swap(value, bit):
    sharers = lax.axis_size("grp")
    return lax.ppermute(value, "grp", [(i, i ^ bit) for i in range(sharers)])


def sharer_order(sharers):
    order, bit = [0], sharers // 2
    while bit:
        order += [k ^ bit for k in order]
        bit //= 2
    return order


def share_out(value):
    bit = lax.axis_size("grp") // 2
    while bit:
        value = jnp.concatenate([value, swap(value, bit)])
        bit //= 2
    return value


def add_up(value, sent=None):
    sharers = lax.axis_size("grp")
    bit = 1
    while bit < sharers:
        half = value.shape[0] // 2
        away = value[half:]
        if bit > 1 and sent is not None:
            away = away.astype(sent)
        value = value[:half] + swap(away, bit).astype(value.dtype)
        bit *= 2
    return value


def pad_lanes(value, width, fill):
    return jnp.pad(value, ((0, 0), (0, width - value.shape[1])), constant_values=fill)


def body(entity_table, rel_diag, src_ids, dst_ids, rel_ids, neg_ids):
    rows_dev, feature = entity_table.shape
    sharers = lax.axis_size("grp")
    devices = lax.axis_size("shard") * sharers
    spans, neg_count = neg_ids.shape
    edge_count = src_ids.shape[0]
    block_len = edge_count // spans
    edge_cap = 4 * edge_count // devices
    chunks = round_up(edge_cap, LANES) // LANES
    part_width = neg_count // sharers
    neg_cap = round_up(2 * spans * part_width // devices, 16)
    width = round_up(block_len, 512)
    part = round_up(part_width, LANES)
    me = lax.axis_index("grp")

    table = entity_table.T.astype(BF16)
    relations = rel_diag.T
    own_ids = lax.dynamic_slice_in_dim(neg_ids, me * part_width, part_width, 1)
    ends = jnp.concatenate(
        [src_ids.reshape(spans, block_len), dst_ids.reshape(spans, block_len)]
    )
    message, *slots = make_slots(
        pad_lanes(ends, width, -1),
        pad_lanes(own_ids, part, -1),
        rows_dev,
        devices,
        sharers,
        chunks,
        neg_cap,
    )
    neg_slot = slots[-1]
    rel_rows = pad_lanes(rel_ids.reshape(spans, block_len), width, -1)
    asked = exchange(message)
    direct = [asked[:, c * LANES : (c + 1) * LANES] for c in range(chunks)]
    neg_asked = asked[:, -LANES:]

    def chunked():
        back = [exchange(gather(table, direct[0], neg_asked, neg_cap))]
        back += [exchange(gather(table, direct[c])) for c in range(1, chunks)]
        negatives = share_out(spread_neg(back[0], neg_slot, neg_cap, feature)[None])
        rows = None
        for c in range(chunks):
            rows = spread(back[c], slots[c], rows, feature)
        src_grad, dst_grad, neg_grad = edges(rows, rel_rows, relations, negatives)
        grad = None
        for c in range(1, chunks):
            sent = exchange(collect(src_grad, dst_grad, slots[c], devices))
            grad = add_rows(sent, direct[c], grad, feature, rows_dev)
        neg_sum = add_up(neg_grad, BF16)[0]
        sent = exchange(
            collect(src_grad, dst_grad, slots[0], devices, neg_sum, neg_slot, neg_cap)
        )
        return add_rows(sent, direct[0], grad, feature, rows_dev, neg_asked, neg_cap)

    def pooled():
        start = chunks * LANES
        listed = asked[:, start : start + sharers * POOL].reshape(devices, sharers, POOL)
        listed = listed.transpose(1, 0, 2).reshape(sharers, devices * POOL) - me * rows_dev
        listed = listed[me ^ jnp.array(sharer_order(sharers), jnp.int32)]
        back = exchange(gather(table, direct[0], neg_asked, neg_cap))
        held = gather_pool(table, listed, devices)
        relayed = add_up(held.reshape(sharers, devices, *held.shape[1:]))[0]
        negatives = share_out(spread_neg(back, neg_slot, neg_cap, feature)[None])
        rows = spread(back, slots[0], None, feature)
        rows = spread(exchange(relayed), slots[chunks], rows, feature, True)
        src_grad, dst_grad, neg_grad = edges(rows, rel_rows, relations, negatives)
        pool = share_out(exchange(collect_pool(src_grad, dst_grad, slots[chunks], devices)))
        neg_sum = add_up(neg_grad, BF16)[0]
        sent = exchange(
            collect(src_grad, dst_grad, slots[0], devices, neg_sum, neg_slot, neg_cap)
        )
        grad = add_pool(pool, listed, devices, feature, rows_dev)
        return add_rows(sent, direct[0], grad, feature, rows_dev, neg_asked, neg_cap)

    if chunks == 1:
        return chunked().T
    fits = jnp.max(neg_asked[:, -1]) < 0
    return lax.cond(fits, pooled, chunked).T


def solution(mesh):
    placed = (
        P(("shard", "grp"), None),
        P(),
        P(("shard", "grp")),
        P(("shard", "grp")),
        P(("shard", "grp")),
        P("shard", None),
    )
    return jax.shard_map(
        body, mesh=mesh, in_specs=placed, out_specs=P(("shard", "grp"), None), check_vma=False
    )
```

time: 514 us -> 460 us (0.89)
  the two profiles are of different devices: /device:TPU:0 before, /device:TPU:17 now
where the time goes in v2:
time: 460 us; the launch traced here: 454 us
  Pallas kernels  187 us (41%)
  waiting for transfers between devices  184 us (40%)
  starting transfers between devices  37.6 us (8%)
  local copies, waits for them, and re-layouts  21.6 us (5%)
  other arithmetic  16.4 us (4%)
  loops' own time  5.51 us (1%)
    ppermute x8, waiting for transfers between devices, swap(): return lax.ppermute(value, 'grp', [(i, i ^ bit) for i in range(sharers)])  184 us
    pallas_call x1, Pallas kernels, gather_pool(): call(functools.partial(gather_pool_kernel, group=group), 'gather_pool', 2...  33.5 us
    pallas_call x2, Pallas kernels, spread(): call(functools.partial(spread_kernel, first=so_far is None, pooled=pooled...  29.9 us
    all_to_all x5, starting transfers between devices, exchange(): lax.all_to_all(value, ('shard', 'grp'), split_axis=0, concat_axis=0, tile...  28.1 us
    pallas_call x1, Pallas kernels, add_pool(): call(functools.partial(add_pool_kernel, rows=rows), 'add_pool', 2 * featu...  28.1 us
    pallas_call x1, Pallas kernels, add_rows(): call(functools.partial(add_kernel, rows=rows, neg_cap=neg_cap, first=so_f...  23.9 us
    pallas_call x1, Pallas kernels, gather(): call(functools.partial(gather_kernel, group=group, neg_cap=neg_cap), 'gat...  23.7 us
    pallas_call x1, Pallas kernels, collect(): call(functools.partial(collect_kernel, group=group, neg_cap=neg_cap), 'co...  18.8 us
  transfers between devices with their start and end apart: 13, of which 6 were waited for; matrix products, arithmetic and copies ran while one was open for 6% of the time, Pallas kernels for 27%

profile of v2, /device:TPU:17, one launch (start us, length us, event | category | flops | bytes accessed | tf_op | source)
XLA Modules:
  0.0 453.8 jit_solution(11863983394863257999)
XLA Ops:
  0.0 0.8 reshape.45
  0.8 0.8 reshape.44
  1.6 0.6 pad.12.ends_ref
  2.2 0.1 constant_dynamic-slice_fusion
  2.3 0.6 pad.13.own_ref
  2.9 3.5 slots.1
  6.4 1.6 copy.20
  8.0 6.3 %all-to-all-start.8 = ((s32[32,1,640]{2,1,0:T(1,128)}), s32[32,1,640]{2,1,0:T(1,128)S(1)}, u32[]{:S(2)}, u32[]{:S(2)}) async-start(s32[32,1,640]{2,1,0:T(1,128)} %copy.20), calls=%async_computation.8 | async-start | bytes 163840 | tf_op jit(solution)/shard_map/all_to_all | solution.py:590
  14.2 3.3 convert_bitcast_fusion
  17.6 0.1 reshape.46
  17.7 1.7 copy.21
  19.4 0.7 slice_reduce_fusion
  20.7 432.0 %conditional.1 = (f32[400,4096]{1,0:T(8,128)}) conditional(s32[]{:T(128)} %convert_element_type.17, (s32[32,640]{1,0:T(8,128)S(1)}, bf16[400,4096]{1,0:T(8,128)(2,1)S(1)}, s32[4,1024]{1,0:T(4,128)S(1)}, s32[32,128]{1,0:T(8,128)S(1)}, s32[32,128]{1,0:T(8,128)S(1)}, /*index=5*/s32[4,1024]{1,0:T(4,128)S(1)}, s32[2,1024]{1,0:T(2,128)S(1)}, ...), branch_computations={%region_1.2_spmd, %region_2.3_spmd} | conditional | flops 116302528512 | bytes 240112544 | solution.py:708
  25.8 23.7 %gather_rows.5 = bf16[32,528,128]{2,1,0:T(8,128)(2,1)} custom-call(bf16[400,4096]{1,0:T(8,128)(2,1)S(1)} %get-tuple-element.61.table_ref, s32[32,128]{1,0:T(8,128)S(1)} %get-tuple-element.66.refs_0_.refs_1_, s32[32,128]{1,0:T(8,128)S(1)} %get-tuple-element.67.refs_1_.refs_2_), custom_call_target="tpu_custom_call" | custom-call | flops 16777216000 | bytes 7372800 | tf_op jit(solution)/shard_map/cond/branch_1_fun/gather_rows/pallas_call | solution.py:195
  49.5 6.1 %all-to-all-start.5 = ((bf16[32,528,128]{2,1,0:T(8,128)(2,1)}), bf16[32,528,128]{2,1,0:T(8,128)(2,1)}, u32[]{:S(2)}, u32[]{:S(2)}) async-start(bf16[32,528,128]{2,1,0:T(8,128)(2,1)} %gather_rows.5), calls=%async_computation.5 | async-start | bytes 8650752 | tf_op jit(solution)/shard_map/cond/branch_1_fun/all_to_all | solution.py:590
  55.6 0.1 sub.12
  55.7 0.1 sub.14
  55.9 0.6 gather_fusion
  56.5 0.6 reshape.36.req_ref
  57.1 33.5 %gather_pool.1 = bf16[128,192,128]{2,1,0:T(8,128)(2,1)} custom-call(bf16[400,4096]{1,0:T(8,128)(2,1)S(1)} %get-tuple-element.61.table_ref, s32[16,1,384]{2,1,0:T(1,128)} %reshape.36.req_ref), custom_call_target="tpu_custom_call" | custom-call | flops 20132659200 | bytes 8192000 | tf_op jit(solution)/shard_map/cond/branch_1_fun/gather_pool/pallas_call | solution.py:222
  90.6 3.3 fusion.3
  93.9 0.4 collective-permute-start.4
  94.3 5.3 %collective-permute-done.4 = bf16[2,32,192,128]{3,2,1,0:T(8,128)(2,1)S(1)} collective-permute-done((bf16[2,32,192,128]{3,2,1,0:T(8,128)(2,1)S(1)}, bf16[2,32,192,128]{3,2,1,0:T(8,128)(2,1)S(1)}, u32[]{:S(2)}, u32[]{:S(2)}) %collective-permute-start.4) | collective-permute-done | bytes 3145760 | tf_op jit(solution)/shard_map/cond/branch_1_fun/ppermute | solution.py:595
  99.6 1.2 add.19
  100.8 0.1 slice.71
  100.9 1.3 collective-permute-start.5
  102.1 50.4 %collective-permute-done.5 = bf16[1,32,192,128]{3,2,1,0:T(8,128)(2,1)S(1)} collective-permute-done((bf16[1,32,192,128]{3,2,1,0:T(8,128)(2,1)S(1)}, bf16[1,32,192,128]{3,2,1,0:T(8,128)(2,1)S(1)}, u32[]{:S(2)}, u32[]{:S(2)}) %collective-permute-start.5) | collective-permute-done | bytes 1572896 | tf_op jit(solution)/shard_map/cond/branch_1_fun/ppermute | solution.py:595
  152.5 1.3 fusion.1
  153.8 5.8 %all-to-all-start.4 = ((bf16[32,192,128]{2,1,0:T(8,128)(2,1)}), bf16[32,192,128]{2,1,0:T(8,128)(2,1)}, u32[]{:S(2)}, u32[]{:S(2)}) async-start(bf16[32,192,128]{2,1,0:T(8,128)(2,1)} %fusion.1), calls=%async_computation.4 | async-start | bytes 3145728 | tf_op jit(solution)/shard_map/cond/branch_1_fun/all_to_all | solution.py:590
  159.6 2.8 spread_negatives.3
  162.4 1.2 collective-permute-start.6
  163.6 0.6 reshape.37.refs_1_
  164.2 0.6 reshape.38.refs_1_
  164.9 0.6 reshape.39.rel_ids_ref
  165.5 22.7 %collective-permute-done.6 = bf16[1,2,256,400]{3,2,1,0:T(8,128)(2,1)S(1)} collective-permute-done((bf16[1,2,256,400]{3,2,1,0:T(8,128)(2,1)}, bf16[1,2,256,400]{3,2,1,0:T(8,128)(2,1)S(1)}, u32[]{:S(2)}, u32[]{:S(2)}) %collective-permute-start.6) | collective-permute-done | bytes 409632 | tf_op jit(solution)/shard_map/cond/branch_1_fun/ppermute | solution.py:595
  188.1 1.2 pad_maximum_fusion.5
  189.3 0.5 copy.16
  189.8 0.9 collective-permute-start.7
  190.7 19.3 %spread_rows.5.refs_2_ = bf16[400,4096]{1,0:T(8,128)(2,1)} custom-call(bf16[32,528,128]{2,1,0:T(8,128)(2,1)} %all-to-all-done.5.refs_0_.back_ref, s32[4,1,1024]{2,1,0:T(1,128)} %reshape.38.refs_1_), custom_call_target="tpu_custom_call" | custom-call | flops 13421772800 | bytes 6553600 | tf_op jit(solution)/shard_map/cond/branch_1_fun/spread_rows/pallas_call | solution.py:305
  210.1 10.6 %spread_pool.1.src_ref.dst_ref = bf16[400,4096]{1,0:T(8,128)(2,1)} custom-call(bf16[32,192,128]{2,1,0:T(8,128)(2,1)} %all-to-all-done.4.refs_0_, s32[4,1,1024]{2,1,0:T(1,128)} %reshape.37.refs_1_, bf16[400,4096]{1,0:T(8,128)(2,1)} %spread_rows.5.refs_2_), custom_call_target="tpu_custom_call" | custom-call | flops 5033164800 | bytes 4505600 | tf_op jit(solution)/shard_map/cond/branch_1_fun/spread_pool/pallas_call | solution.py:305
  220.7 1.5 copy.17
  222.2 1.6 pad_maximum_fusion.4.neg_ref
  223.8 13.3 %edges.3 = (bf16[400,2048]{1,0:T(8,128)(2,1)}, bf16[400,2048]{1,0:T(8,128)(2,1)}, f32[4,2,256,400]{3,2,1,0:T(8,128)}) custom-call(bf16[400,4096]{1,0:T(8,128)(2,1)} %spread_pool.1.src_ref.dst_ref, bf16[400,4096]{1,0:T(8,128)(2,1)} %spread_pool.1.src_ref.dst_ref, s32[2,1,1024]{2,1,0:T(1,128)} %reshape.39.rel_ids_ref, f32[400,64]{1,0:T(8,128)S(1)} %copy-done.5, ...), custom_call_target="tpu_custom_call" | custom-call | flops 5033164800 | bytes 9830400 | tf_op jit(solution)/shard_map/cond/branch_1_fun/edges/pallas_call | solution.py:370
  237.0 1.8 slice.55
  238.8 1.7 copy.18
  240.6 10.0 %collect_pool.1 = bf16[32,192,128]{2,1,0:T(8,128)(2,1)} custom-call(bf16[400,2048]{1,0:T(8,128)(2,1)} %get-tuple-element.72.src_ref, bf16[400,2048]{1,0:T(8,128)(2,1)} %get-tuple-element.73.dst_ref, s32[4,1024]{1,0:T(4,128)S(1)} %copy-done.7), custom_call_target="tpu_custom_call" | custom-call | flops 5033164800 | bytes 4505600 | tf_op jit(solution)/shard_map/cond/branch_1_fun/collect_pool/pallas_call | solution.py:469
  250.5 4.6 %all-to-all-start.7 = ((bf16[32,192,128]{2,1,0:T(8,128)(2,1)}), bf16[32,192,128]{2,1,0:T(8,128)(2,1)S(1)}, u32[]{:S(2)}, u32[]{:S(2)}) async-start(bf16[32,192,128]{2,1,0:T(8,128)(2,1)} %collect_pool.1), calls=%async_computation.7 | async-start | bytes 3145728 | tf_op jit(solution)/shard_map/cond/branch_1_fun/all_to_all | solution.py:590
  255.1 1.8 copy.19
  256.9 2.7 slice_add_fusion.2
  259.7 1.2 collective-permute-start.9
  261.0 22.7 %collective-permute-done.9 = bf16[1,2,256,400]{3,2,1,0:T(8,128)(2,1)S(1)} collective-permute-done((bf16[1,2,256,400]{3,2,1,0:T(8,128)(2,1)S(1)}, bf16[1,2,256,400]{3,2,1,0:T(8,128)(2,1)S(1)}, u32[]{:S(2)}, u32[]{:S(2)}) %collective-permute-start.9) | collective-permute-done | bytes 409632 | tf_op jit(solution)/shard_map/cond/branch_1_fun/ppermute | solution.py:595
  283.7 1.1 fusion.2.refs_0_
  284.8 18.8 %collect_grads.5 = bf16[32,528,128]{2,1,0:T(8,128)(2,1)} custom-call(bf16[400,2048]{1,0:T(8,128)(2,1)} %get-tuple-element.72.src_ref, bf16[400,2048]{1,0:T(8,128)(2,1)} %get-tuple-element.73.dst_ref, s32[4,1024]{1,0:T(4,128)S(1)} %get-tuple-element.68.slot_ref, f32[2,256,400]{2,1,0:T(8,128)} %fusion.2.refs_0_, s32[2,256]{1,0:T(2,128)S(1)} %copy-done.13), custom_call_target="tpu_custom_call" | custom-call | flops 13421772800 | bytes 6553600 | tf_op jit(solution)/shard_map/cond/branch_1_fun/collect_grads/pallas_call | solution.py:438
  303.6 5.5 %all-to-all-start.6 = ((bf16[32,528,128]{2,1,0:T(8,128)(2,1)}), bf16[32,528,128]{2,1,0:T(8,128)(2,1)}, u32[]{:S(2)}, u32[]{:S(2)}) async-start(bf16[32,528,128]{2,1,0:T(8,128)(2,1)} %collect_grads.5), calls=%async_computation.6 | async-start | bytes 8650752 | tf_op jit(solution)/shard_map/cond/branch_1_fun/all_to_all | solution.py:590
  309.1 1.2 collective-permute-start.10
  310.3 78.4 %collective-permute-done.10 = bf16[32,192,128]{2,1,0:T(8,128)(2,1)S(1)} collective-permute-done((bf16[32,192,128]{2,1,0:T(8,128)(2,1)S(1)}, bf16[32,192,128]{2,1,0:T(8,128)(2,1)S(1)}, u32[]{:S(2)}, u32[]{:S(2)}) %collective-permute-start.10) | collective-permute-done | bytes 1572896 | tf_op jit(solution)/shard_map/cond/branch_1_fun/ppermute | solution.py:595
  388.7 0.3 pad_maximum_fusion.3
  389.0 3.1 collective-permute-start.11
  392.1 0.6 copy.23
  392.7 4.7 %collective-permute-done.11 = bf16[64,192,128]{2,1,0:T(8,128)(2,1)S(1)} collective-permute-done((bf16[64,192,128]{2,1,0:T(8,128)(2,1)S(1)}, bf16[64,192,128]{2,1,0:T(8,128)(2,1)S(1)}, u32[]{:S(2)}, u32[]{:S(2)}) %collective-permute-start.11) | collective-permute-done | bytes 3145760 | tf_op jit(solution)/shard_map/cond/branch_1_fun/ppermute | solution.py:595
  397.4 3.0 pad_maximum_fusion.2.recv_ref
  400.4 28.1 %add_pool.1.refs_3_ = f32[400,4096]{1,0:T(8,128)} custom-call(bf16[128,192,128]{2,1,0:T(8,128)(2,1)} %pad_maximum_fusion.2.recv_ref, s32[1,6144]{1,0:T(1,128)} %bitcast.41), custom_call_target="tpu_custom_call" | custom-call | flops 20132659200 | bytes 11468800 | tf_op jit(solution)/shard_map/cond/branch_1_fun/add_pool/pallas_call | solution.py:570
  428.5 23.9 %add_grads.5 = f32[400,4096]{1,0:T(8,128)} custom-call(bf16[32,528,128]{2,1,0:T(8,128)(2,1)} %all-to-all-done.6.refs_0_, s32[32,128]{1,0:T(8,128)S(1)} %copy-done.11, s32[32,128]{1,0:T(8,128)S(1)} %copy-done.9, f32[400,4096]{1,0:T(8,128)} %add_pool.1.refs_3_), custom_call_target="tpu_custom_call" | custom-call | flops 13421772800 | bytes 16384000 | tf_op jit(solution)/shard_map/cond/branch_1_fun/add_grads/pallas_call | solution.py:536
  452.7 0.7 copy-done.1
  (44 shorter events, 0.3 us)
Async XLA Ops:
  0.0 2.2 copy-start
  8.0 11.4 %all-to-all-start.8 = ((s32[32,1,640]{2,1,0:T(1,128)}), s32[32,1,640]{2,1,0:T(1,128)S(1)}, u32[]{:S(2)}, u32[]{:S(2)}) async-start(s32[32,1,640]{2,1,0:T(1,128)} %copy.20), calls=%async_computation.8 | async-start | bytes 163840 | tf_op jit(solution)/shard_map/all_to_all | solution.py:590
  14.2 3.3 copy-start.14
  25.8 23.8 %copy-start.8 = (s32[32,128]{1,0:T(8,128)}, s32[32,128]{1,0:T(8,128)S(1)}, u32[]{:S(2)}) copy-start(s32[32,128]{1,0:T(8,128)S(1)} %get-tuple-element.67.refs_1_.refs_2_) | copy-start | bytes 49156 | tf_op jit(solution)/shard_map/cond
  25.8 23.8 %copy-start.10 = (s32[32,128]{1,0:T(8,128)}, s32[32,128]{1,0:T(8,128)S(1)}, u32[]{:S(2)}) copy-start(s32[32,128]{1,0:T(8,128)S(1)} %get-tuple-element.66.refs_0_.refs_1_) | copy-start | bytes 49156 | tf_op jit(solution)/shard_map/cond
  25.8 133.8 %copy-start.12 = (s32[2,256]{1,0:T(2,128)}, s32[2,256]{1,0:T(2,128)S(1)}, u32[]{:S(2)}) copy-start(s32[2,256]{1,0:T(2,128)S(1)} %get-tuple-element.71.slot_ref.refs_1_) | copy-start | bytes 6148 | tf_op jit(solution)/shard_map/cond
  25.8 137.8 %copy-start.6 = (s32[4,1024]{1,0:T(4,128)}, s32[4,1024]{1,0:T(4,128)S(1)}, u32[]{:S(2)}) copy-start(s32[4,1024]{1,0:T(4,128)S(1)} %get-tuple-element.65.slot_ref) | copy-start | bytes 49156 | tf_op jit(solution)/shard_map/cond
  49.5 6.3 %copy-start.15 = (s32[4]{0:T(128)S(1)}, s32[4]{0:T(128)}, u32[]{:S(2)}) copy-start(s32[4]{0:T(128)} %constant.22.clone.1) | copy-start | bytes 52 | tf_op jit(solution)/shard_map/cond
  49.5 104.3 %all-to-all-start.5 = ((bf16[32,528,128]{2,1,0:T(8,128)(2,1)}), bf16[32,528,128]{2,1,0:T(8,128)(2,1)}, u32[]{:S(2)}, u32[]{:S(2)}) async-start(bf16[32,528,128]{2,1,0:T(8,128)(2,1)} %gather_rows.5), calls=%async_computation.5 | async-start | bytes 8650752 | tf_op jit(solution)/shard_map/cond/branch_1_fun/all_to_all | solution.py:590
  93.9 5.7 %collective-permute-start.4 = (bf16[2,32,192,128]{3,2,1,0:T(8,128)(2,1)S(1)}, bf16[2,32,192,128]{3,2,1,0:T(8,128)(2,1)S(1)}, u32[]{:S(2)}, u32[]{:S(2)}) collective-permute-start(bf16[2,32,192,128]{3,2,1,0:T(8,128)(2,1)S(1)} %bitcast.31), channel_id=1, source_target_pairs={{0,1},{1,0},{2,3},{3,2},{4,5},{5,4},{6,7},{7,6},{8,9},{9,8},{10,11... | collective-permute-start | bytes 9437192 | tf_op jit(solution)/shard_map/cond/branch_1_fun/ppermute | solution.py:595
  100.9 51.6 %collective-permute-start.5 = (bf16[1,32,192,128]{3,2,1,0:T(8,128)(2,1)S(1)}, bf16[1,32,192,128]{3,2,1,0:T(8,128)(2,1)S(1)}, u32[]{:S(2)}, u32[]{:S(2)}) collective-permute-start(bf16[1,32,192,128]{3,2,1,0:T(8,128)(2,1)S(1)} %slice.71), channel_id=1, source_target_pairs={{0,2},{1,3},{2,0},{3,1},{4,6},{5,7},{6,4},{7,5},{8,10},{9,11},{10,... | collective-permute-start | bytes 4718600 | tf_op jit(solution)/shard_map/cond/branch_1_fun/ppermute | solution.py:595
  153.8 56.2 %all-to-all-start.4 = ((bf16[32,192,128]{2,1,0:T(8,128)(2,1)}), bf16[32,192,128]{2,1,0:T(8,128)(2,1)}, u32[]{:S(2)}, u32[]{:S(2)}) async-start(bf16[32,192,128]{2,1,0:T(8,128)(2,1)} %fusion.1), calls=%async_computation.4 | async-start | bytes 3145728 | tf_op jit(solution)/shard_map/cond/branch_1_fun/all_to_all | solution.py:590
  162.4 25.7 %collective-permute-start.6 = (bf16[1,2,256,400]{3,2,1,0:T(8,128)(2,1)}, bf16[1,2,256,400]{3,2,1,0:T(8,128)(2,1)S(1)}, u32[]{:S(2)}, u32[]{:S(2)}) collective-permute-start(bf16[1,2,256,400]{3,2,1,0:T(8,128)(2,1)} %bitcast.25), channel_id=1, source_target_pairs={{0,2},{1,3},{2,0},{3,1},{4,6},{5,7},{6,4},{7,5},{8,10},{9,11},{10,... | collective-permute-start | bytes 1228808 | tf_op jit(solution)/shard_map/cond/branch_1_fun/ppermute | solution.py:595
  189.8 30.9 %collective-permute-start.7 = (bf16[2,2,256,400]{2,3,1,0:T(8,128)(2,1)S(1)}, bf16[2,2,256,400]{2,3,1,0:T(8,128)(2,1)}, u32[]{:S(2)}, u32[]{:S(2)}) collective-permute-start(bf16[2,2,256,400]{2,3,1,0:T(8,128)(2,1)S(1)} %copy.16), channel_id=1, source_target_pairs={{0,1},{1,0},{2,3},{3,2},{4,5},{5,4},{6,7},{7,6},{8,9},{9,8},{10,11... | collective-permute-start | bytes 2457608 | tf_op jit(solution)/shard_map/cond/branch_1_fun/ppermute | solution.py:595
  210.1 12.1 %copy-start.2 = (bf16[2,256,400]{2,1,0:T(8,128)(2,1)S(1)}, bf16[2,256,400]{2,1,0:T(8,128)(2,1)}, u32[]{:S(2)}) copy-start(bf16[2,256,400]{2,1,0:T(8,128)(2,1)} %spread_negatives.3) | copy-start | bytes 1228804 | tf_op jit(solution)/shard_map/cond
  220.7 3.1 copy-start.5
  237.0 3.5 copy-start.7
  240.5 14.6 %collective-permute-start.8 = (f32[2,2,256,400]{2,3,1,0:T(8,128)}, f32[2,2,256,400]{2,3,1,0:T(8,128)S(1)}, u32[]{:S(2)}, u32[]{:S(2)}) collective-permute-start(f32[2,2,256,400]{2,3,1,0:T(8,128)} %copy.18), channel_id=1, source_target_pairs={{0,1},{1,0},{2,3},{3,2},{4,5},{5,4},{6,7},{7,6},{8,9},{9,8},{10,11... | collective-permute-start | bytes 4915208 | tf_op jit(solution)/shard_map/cond/branch_1_fun/ppermute | solution.py:595
  250.5 53.1 %all-to-all-start.7 = ((bf16[32,192,128]{2,1,0:T(8,128)(2,1)}), bf16[32,192,128]{2,1,0:T(8,128)(2,1)S(1)}, u32[]{:S(2)}, u32[]{:S(2)}) async-start(bf16[32,192,128]{2,1,0:T(8,128)(2,1)} %collect_pool.1), calls=%async_computation.7 | async-start | bytes 3145728 | tf_op jit(solution)/shard_map/cond/branch_1_fun/all_to_all | solution.py:590
  259.6 25.2 %copy-start.13 = (s32[2,256]{1,0:T(2,128)S(1)}, s32[2,256]{1,0:T(2,128)}, u32[]{:S(2)}) copy-start(s32[2,256]{1,0:T(2,128)} %copy-done.12) | copy-start | bytes 6148 | tf_op jit(solution)/shard_map/cond
  259.7 24.0 %collective-permute-start.9 = (bf16[1,2,256,400]{3,2,1,0:T(8,128)(2,1)S(1)}, bf16[1,2,256,400]{3,2,1,0:T(8,128)(2,1)S(1)}, u32[]{:S(2)}, u32[]{:S(2)}) collective-permute-start(bf16[1,2,256,400]{3,2,1,0:T(8,128)(2,1)S(1)} %slice.93), channel_id=1, source_target_pairs={{0,2},{1,3},{2,0},{3,1},{4,6},{5,7},{6,4},{7,5},{8,10},{9,11},{10,... | collective-permute-start | bytes 1228808 | tf_op jit(solution)/shard_map/cond/branch_1_fun/ppermute | solution.py:595
  303.6 124.9 %all-to-all-start.6 = ((bf16[32,528,128]{2,1,0:T(8,128)(2,1)}), bf16[32,528,128]{2,1,0:T(8,128)(2,1)}, u32[]{:S(2)}, u32[]{:S(2)}) async-start(bf16[32,528,128]{2,1,0:T(8,128)(2,1)} %collect_grads.5), calls=%async_computation.6 | async-start | bytes 8650752 | tf_op jit(solution)/shard_map/cond/branch_1_fun/all_to_all | solution.py:590
  309.1 79.6 %collective-permute-start.10 = (bf16[32,192,128]{2,1,0:T(8,128)(2,1)S(1)}, bf16[32,192,128]{2,1,0:T(8,128)(2,1)S(1)}, u32[]{:S(2)}, u32[]{:S(2)}) collective-permute-start(bf16[32,192,128]{2,1,0:T(8,128)(2,1)S(1)} %all-to-all-done.7), channel_id=1, source_target_pairs={{0,2},{1,3},{2,0},{3,1},{4,6},{5,7},{6,4},{7,5},{8,10},{9,11},{10,... | collective-permute-start | bytes 4718600 | tf_op jit(solution)/shard_map/cond/branch_1_fun/ppermute | solution.py:595
  389.0 8.4 %collective-permute-start.11 = (bf16[64,192,128]{2,1,0:T(8,128)(2,1)S(1)}, bf16[64,192,128]{2,1,0:T(8,128)(2,1)S(1)}, u32[]{:S(2)}, u32[]{:S(2)}) collective-permute-start(bf16[64,192,128]{2,1,0:T(8,128)(2,1)S(1)} %pad_maximum_fusion.3), channel_id=1, source_target_pairs={{0,1},{1,0},{2,3},{3,2},{4,5},{5,4},{6,7},{7,6},{8,9},{9,8},{10,11... | collective-permute-start | bytes 9437192 | tf_op jit(solution)/shard_map/cond/branch_1_fun/ppermute | solution.py:595
  400.4 28.1 %copy-start.9 = (s32[32,128]{1,0:T(8,128)S(1)}, s32[32,128]{1,0:T(8,128)}, u32[]{:S(2)}) copy-start(s32[32,128]{1,0:T(8,128)} %copy-done.8) | copy-start | bytes 49156 | tf_op jit(solution)/shard_map/cond
  400.4 28.1 %copy-start.11 = (s32[32,128]{1,0:T(8,128)S(1)}, s32[32,128]{1,0:T(8,128)}, u32[]{:S(2)}) copy-start(s32[32,128]{1,0:T(8,128)} %copy-done.10) | copy-start | bytes 49156 | tf_op jit(solution)/shard_map/cond
  452.7 0.7 copy-start.1

commit v3 on v2

--- a/solution.py
+++ b/solution.py
@@ -215,7 +215,6 @@
 
 def gather_pool(table, requests, devices):
     feature, rows_dev = table.shape
-    relays = requests.shape[0]
     group = 8
     steps = devices // group
     height = POOL * (round_up(feature, LANES) // LANES)
@@ -224,14 +223,14 @@
         "gather_pool",
         2 * feature * rows_dev * requests.size,
         2 * feature * (rows_dev + requests.size),
-        grid=(relays * steps,),
+        grid=(steps,),
         in_specs=[
             pl.BlockSpec((feature, rows_dev), lambda i: (0, 0)),
             pl.BlockSpec((1, 1, group * POOL), lambda i: (i, 0, 0)),
         ],
         out_specs=pl.BlockSpec((group, height, LANES), lambda i: (i, 0, 0)),
-        out_shape=jax.ShapeDtypeStruct((relays * devices, height, LANES), BF16),
-    )(table, requests.reshape(relays * steps, 1, group * POOL))
+        out_shape=jax.ShapeDtypeStruct((devices, height, LANES), BF16),
+    )(table, requests.reshape(steps, 1, group * POOL))
 
 
 def spread_neg_kernel(back_ref, slot_ref, out_ref, flat, *, cap):
@@ -319,14 +318,22 @@
     )(back, slot.reshape(segments, 1, width), *extra)
 
 
-def edges_kernel(
-    src_ref, dst_ref, rel_ids_ref, rel_ref, neg_ref, src_grad_ref, dst_grad_ref, neg_grad_ref, sums
-):
+def edges_kernel(*refs, parts):
+    src_ref, dst_ref, rel_ids_ref, rel_ref = refs[:4]
+    neg_refs = refs[4 : 4 + parts]
+    src_grad_ref, dst_grad_ref = refs[4 + parts : 6 + parts]
+    neg_grad_refs = refs[6 + parts : 6 + 2 * parts]
+    negatives, turned, sums = refs[6 + 2 * parts :]
     step = pl.program_id(1)
-    parts, _, part, feature = neg_ref.shape
-    negatives = neg_ref[...].reshape(parts * part, feature)
-    nrel = rel_ref.shape[1]
-    hot = one_hot(nrel, rel_ids_ref[...].reshape(1, rel_ids_ref.shape[-1]))
+    part = neg_refs[0].shape[1]
+
+    @pl.when(step == 0)
+    def _():
+        for k in range(parts):
+            negatives[k * part : (k + 1) * part] = neg_refs[k][0]
+        turned[...] = negatives[...].astype(F32).T.astype(BF16)
+
+    hot = one_hot(rel_ref.shape[1], rel_ids_ref[...].reshape(1, rel_ids_ref.shape[-1]))
     table = rel_ref[...]
     relation = jnp.zeros(src_ref.shape, F32)
     for _ in range(3):
@@ -339,8 +346,8 @@
     positive = jnp.sum(product * target, axis=0, keepdims=True)
     pos_weight = -jax.nn.sigmoid(-positive)
     query = product.astype(BF16)
-    weight = jax.nn.sigmoid(dot(negatives, query, NN)).astype(BF16)
-    gathered = dot(negatives, weight, TN)
+    weight = jax.nn.sigmoid(dot(negatives[...], query, NN)).astype(BF16)
+    gathered = dot(turned[...], weight, NN)
     src_grad_ref[...] = (relation * (pos_weight * target + gathered)).astype(BF16)
     dst_grad_ref[...] = (pos_weight * product).astype(BF16)
     neg_grad = dot(weight, query, NT)
@@ -355,50 +362,48 @@
 
     @pl.when(step == pl.num_programs(1) - 1)
     def _():
-        neg_grad_ref[...] = sums[...].reshape(neg_grad_ref.shape)
+        for k in range(parts):
+            neg_grad_refs[k][0] = sums[k * part : (k + 1) * part].astype(BF16)
 
 
 def edges(rows, rel_ids, relations, negatives):
     feature, endpoints = rows.shape
-    parts, spans, part, _ = negatives.shape
+    parts = len(negatives)
+    spans, part, _ = negatives[0].shape
     width = rel_ids.shape[1]
     tile = 512
     steps = width // tile
     blocks = spans * steps
     edge_spec = pl.BlockSpec((feature, tile), lambda b, i: (0, b * steps + i))
-    flops = 6 * feature * parts * part * spans * width
-    src_grad, dst_grad, neg_grad = call(
-        edges_kernel,
+    neg_spec = pl.BlockSpec((1, part, feature), lambda b, i: (b, 0, 0))
+    src_grad, dst_grad, *neg_grads = call(
+        functools.partial(edges_kernel, parts=parts),
         "edges",
-        flops,
-        2 * (2 * rows.size + 2 * negatives.size),
+        6 * feature * parts * part * spans * width,
+        4 * (rows.size + parts * negatives[0].size),
         grid=(spans, steps),
         in_specs=[
             edge_spec,
             pl.BlockSpec((feature, tile), lambda b, i: (0, blocks + b * steps + i)),
             pl.BlockSpec((1, 1, tile), lambda b, i: (b, 0, i)),
             pl.BlockSpec(relations.shape, lambda b, i: (0, 0)),
-            pl.BlockSpec((parts, 1, part, feature), lambda b, i: (0, b, 0, 0)),
+        ]
+        + [neg_spec] * parts,
+        out_specs=[edge_spec, edge_spec] + [neg_spec] * parts,
+        out_shape=[jax.ShapeDtypeStruct((feature, endpoints // 2), BF16)] * 2
+        + [jax.ShapeDtypeStruct((spans, part, feature), BF16)] * parts,
+        scratch_shapes=[
+            pltpu.VMEM((parts * part, feature), BF16),
+            pltpu.VMEM((feature, parts * part), BF16),
+            pltpu.VMEM((parts * part, feature), F32),
         ],
-        out_specs=[
-            edge_spec,
-            edge_spec,
-            pl.BlockSpec((parts, 1, part, feature), lambda b, i: (0, b, 0, 0)),
-        ],
-        out_shape=[
-            jax.ShapeDtypeStruct((feature, endpoints // 2), BF16),
-            jax.ShapeDtypeStruct((feature, endpoints // 2), BF16),
-            jax.ShapeDtypeStruct(negatives.shape, F32),
-        ],
-        scratch_shapes=[pltpu.VMEM((parts * part, feature), F32)],
-    )(rows, rows, rel_ids.reshape(spans, 1, width), relations, negatives)
-    return src_grad, dst_grad, neg_grad
-
-
-def collect_kernel(src_ref, dst_ref, slot_ref, *refs, group, neg_cap):
+    )(rows, rows, rel_ids.reshape(spans, 1, width), relations, *negatives)
+    return src_grad, dst_grad, neg_grads
+
+
+def collect_kernel(src_ref, dst_ref, slot_ref, out_ref, *, group):
     segments, width = slot_ref.shape
     feature = src_ref.shape[0]
-    out_ref = refs[-1]
     step = pl.program_id(0)
     total = jnp.zeros((feature, group * LANES), F32)
     for segment in range(segments):
@@ -410,41 +415,66 @@
     first = out_ref.shape[1] - feature
     for i in range(group):
         out_ref[i, first:] = total[:, i * LANES : (i + 1) * LANES]
-    if neg_cap:
-        neg_grad_ref, neg_slot_ref = refs[:2]
-        rows = jnp.zeros((group * neg_cap, feature), F32)
-        for part in range(neg_slot_ref.shape[0]):
-            row = neg_slot_ref[part : part + 1, :]
-            hot = one_hot(group * neg_cap, row, step * group * neg_cap)
-            rows = rows + dot(hot, neg_grad_ref[part].astype(BF16), NN)
-        for i in range(group):
-            pack(out_ref, i, 0, rows[i * neg_cap : (i + 1) * neg_cap])
-
-
-def collect(src_grad, dst_grad, slot, devices, neg_grad=None, neg_slot=None, neg_cap=0):
+
+
+def collect(src_grad, dst_grad, slot, devices, neg_cap=0):
     feature = src_grad.shape[0]
     group = 4
     slots = devices * LANES
     height = feature + neg_cap * (round_up(feature, LANES) // LANES)
     whole = pl.BlockSpec(src_grad.shape, lambda i: (0, 0))
-    operands = [src_grad, dst_grad, slot]
-    specs = [whole, whole, pl.BlockSpec(slot.shape, lambda i: (0, 0))]
-    if neg_cap:
-        operands += [neg_grad, neg_slot]
-        specs += [
-            pl.BlockSpec(neg_grad.shape, lambda i: (0, 0, 0)),
-            pl.BlockSpec(neg_slot.shape, lambda i: (0, 0)),
-        ]
-    return call(
-        functools.partial(collect_kernel, group=group, neg_cap=neg_cap),
+    return call(
+        functools.partial(collect_kernel, group=group),
         "collect_grads",
         2 * feature * slots * slot.size,
         2 * feature * (slots + slot.size),
         grid=(devices // group,),
-        in_specs=specs,
+        in_specs=[whole, whole, pl.BlockSpec(slot.shape, lambda i: (0, 0))],
         out_specs=pl.BlockSpec((group, height, LANES), lambda i: (i, 0, 0)),
         out_shape=jax.ShapeDtypeStruct((devices, height, LANES), BF16),
-    )(*operands)
+    )(src_grad, dst_grad, slot)
+
+
+def collect_neg_kernel(sent_ref, slot_ref, *refs, group, cap):
+    grad_refs, out_ref, sums = refs[:-2], refs[-2], refs[-1]
+    step = pl.program_id(0)
+
+    @pl.when(step == 0)
+    def _():
+        total = grad_refs[0][...].astype(F32)
+        for grad_ref in grad_refs[1:]:
+            total = total + grad_ref[...].astype(F32)
+        sums[...] = total.astype(BF16)
+
+    rows = jnp.zeros((group * cap, sums.shape[-1]), F32)
+    for part in range(slot_ref.shape[0]):
+        hot = one_hot(group * cap, slot_ref[part : part + 1, :], step * group * cap)
+        rows = rows + dot(hot, sums[part], NN)
+    for i in range(group):
+        pack(out_ref, i, 0, rows[i * cap : (i + 1) * cap])
+
+
+def collect_neg(sent, slot, grads, cap):
+    devices = sent.shape[0]
+    feature = grads[0].shape[-1]
+    group = 16
+    height = cap * (round_up(feature, LANES) // LANES)
+    return call(
+        functools.partial(collect_neg_kernel, group=group, cap=cap),
+        "collect_negatives",
+        2 * devices * cap * feature * slot.size,
+        4 * len(grads) * grads[0].size,
+        grid=(devices // group,),
+        in_specs=[
+            pl.BlockSpec(memory_space=pl.ANY),
+            pl.BlockSpec(slot.shape, lambda i: (0, 0)),
+        ]
+        + [pl.BlockSpec(grads[0].shape, lambda i: (0, 0, 0))] * len(grads),
+        out_specs=pl.BlockSpec((group, height, LANES), lambda i: (i, 0, 0)),
+        out_shape=jax.ShapeDtypeStruct(sent.shape, BF16),
+        scratch_shapes=[pltpu.VMEM(grads[0].shape, BF16)],
+        input_output_aliases={0: 0},
+    )(sent, slot, *grads)
 
 
 def collect_pool_kernel(src_ref, dst_ref, slot_ref, out_ref, *, group):
@@ -546,44 +576,52 @@
     )(*operands)
 
 
-def add_pool_kernel(recv_ref, req_ref, out_ref, packed, flat, *, rows):
+def add_pool_kernel(*refs, rows, relays):
+    recv_refs = refs[:relays]
+    req_ref = refs[relays]
+    so_far_ref = refs[relays + 1] if len(refs) == relays + 5 else None
+    out_ref, packed, flat = refs[-3:]
     feature = flat.shape[0]
     count = packed.shape[0]
-    per_relay = count // POOL
     step = pl.program_id(0)
 
     @pl.when(step == 0)
     def _():
-        for relay in range(recv_ref.shape[0] // per_relay):
-            for d in range(per_relay):
-                unpack(recv_ref, relay * per_relay + d, 0, POOL, packed, d * POOL)
+        for relay in range(relays):
+            for d in range(count // POOL):
+                unpack(recv_refs[relay], d, 0, POOL, packed, d * POOL)
             flat[:, relay * count : (relay + 1) * count] = (
                 packed[...].astype(F32).T[:feature].astype(BF16)
             )
 
-    out_ref[...] = dot(flat[...], one_hot(rows, req_ref[...], step * rows), NT)
-
-
-def add_pool(recv, requests, devices, feature, rows_dev):
+    total = dot(flat[...], one_hot(rows, req_ref[...], step * rows), NT)
+    if so_far_ref is not None:
+        total = total + so_far_ref[...]
+    out_ref[...] = total
+
+
+def add_pool(recv, requests, so_far, feature, rows_dev):
     rows = 512
-    full = round_up(feature, LANES)
-    return call(
-        functools.partial(add_pool_kernel, rows=rows),
+    devices, height, _ = recv[0].shape
+    slots = len(recv) * devices * POOL
+    rows_spec = pl.BlockSpec((feature, rows), lambda i: (0, i))
+    extra = [] if so_far is None else [so_far]
+    return call(
+        functools.partial(add_pool_kernel, rows=rows, relays=len(recv)),
         "add_pool",
-        2 * feature * requests.size * rows_dev,
-        2 * feature * requests.size + 4 * feature * rows_dev,
+        2 * feature * slots * rows_dev,
+        2 * feature * slots + 4 * feature * rows_dev,
         grid=(rows_dev // rows,),
-        in_specs=[
-            pl.BlockSpec(recv.shape, lambda i: (0, 0, 0)),
-            pl.BlockSpec((1, requests.size), lambda i: (0, 0)),
-        ],
-        out_specs=pl.BlockSpec((feature, rows), lambda i: (0, i)),
+        in_specs=[pl.BlockSpec(recv[0].shape, lambda i: (0, 0, 0))] * len(recv)
+        + [pl.BlockSpec((1, slots), lambda i: (0, 0))]
+        + [rows_spec] * len(extra),
+        out_specs=rows_spec,
         out_shape=jax.ShapeDtypeStruct((feature, rows_dev), F32),
         scratch_shapes=[
-            pltpu.VMEM((devices * POOL, full), BF16),
-            pltpu.VMEM((feature, requests.size), BF16),
+            pltpu.VMEM((devices * POOL, round_up(feature, LANES)), BF16),
+            pltpu.VMEM((feature, slots), BF16),
         ],
-    )(recv, requests.reshape(1, -1))
+    )(*recv, requests.reshape(1, slots), *extra)
 
 
 def exchange(value):
@@ -595,33 +633,12 @@
     return lax.ppermute(value, "grp", [(i, i ^ bit) for i in range(sharers)])
 
 
-def sharer_order(sharers):
-    order, bit = [0], sharers // 2
-    while bit:
-        order += [k ^ bit for k in order]
-        bit //= 2
-    return order
-
-
 def share_out(value):
-    bit = lax.axis_size("grp") // 2
-    while bit:
-        value = jnp.concatenate([value, swap(value, bit)])
-        bit //= 2
-    return value
-
-
-def add_up(value, sent=None):
-    sharers = lax.axis_size("grp")
-    bit = 1
-    while bit < sharers:
-        half = value.shape[0] // 2
-        away = value[half:]
-        if bit > 1 and sent is not None:
-            away = away.astype(sent)
-        value = value[:half] + swap(away, bit).astype(value.dtype)
-        bit *= 2
-    return value
+    return [value] + [swap(value, k) for k in range(1, lax.axis_size("grp"))]
+
+
+def trade(blocks):
+    return blocks[:1] + [swap(block, k) for k, block in enumerate(blocks) if k]
 
 
 def pad_lanes(value, width, fill):
@@ -664,45 +681,53 @@
     direct = [asked[:, c * LANES : (c + 1) * LANES] for c in range(chunks)]
     neg_asked = asked[:, -LANES:]
 
+    def negatives_of(back):
+        return share_out(spread_neg(back, neg_slot, neg_cap, feature))
+
+    def direct_sent(src_grad, dst_grad, neg_grads):
+        sent = collect(src_grad, dst_grad, slots[0], devices, neg_cap)
+        return exchange(collect_neg(sent, neg_slot, trade(neg_grads), neg_cap))
+
     def chunked():
         back = [exchange(gather(table, direct[0], neg_asked, neg_cap))]
         back += [exchange(gather(table, direct[c])) for c in range(1, chunks)]
-        negatives = share_out(spread_neg(back[0], neg_slot, neg_cap, feature)[None])
+        negatives = negatives_of(back[0])
         rows = None
         for c in range(chunks):
             rows = spread(back[c], slots[c], rows, feature)
-        src_grad, dst_grad, neg_grad = edges(rows, rel_rows, relations, negatives)
+        src_grad, dst_grad, neg_grads = edges(rows, rel_rows, relations, negatives)
         grad = None
         for c in range(1, chunks):
             sent = exchange(collect(src_grad, dst_grad, slots[c], devices))
             grad = add_rows(sent, direct[c], grad, feature, rows_dev)
-        neg_sum = add_up(neg_grad, BF16)[0]
-        sent = exchange(
-            collect(src_grad, dst_grad, slots[0], devices, neg_sum, neg_slot, neg_cap)
-        )
+        sent = direct_sent(src_grad, dst_grad, neg_grads)
         return add_rows(sent, direct[0], grad, feature, rows_dev, neg_asked, neg_cap)
 
     def pooled():
         start = chunks * LANES
         listed = asked[:, start : start + sharers * POOL].reshape(devices, sharers, POOL)
         listed = listed.transpose(1, 0, 2).reshape(sharers, devices * POOL) - me * rows_dev
-        listed = listed[me ^ jnp.array(sharer_order(sharers), jnp.int32)]
+        listed = listed[me ^ jnp.arange(sharers, dtype=jnp.int32)]
         back = exchange(gather(table, direct[0], neg_asked, neg_cap))
-        held = gather_pool(table, listed, devices)
-        relayed = add_up(held.reshape(sharers, devices, *held.shape[1:]))[0]
-        negatives = share_out(spread_neg(back, neg_slot, neg_cap, feature)[None])
+        far = gather_pool(table, listed[2], devices) + swap(
+            gather_pool(table, listed[3], devices), 1
+        )
+        far = swap(far, 2)
+        near = gather_pool(table, listed[0], devices) + swap(
+            gather_pool(table, listed[1], devices), 1
+        )
+        negatives = negatives_of(back)
         rows = spread(back, slots[0], None, feature)
-        rows = spread(exchange(relayed), slots[chunks], rows, feature, True)
-        src_grad, dst_grad, neg_grad = edges(rows, rel_rows, relations, negatives)
-        pool = share_out(exchange(collect_pool(src_grad, dst_grad, slots[chunks], devices)))
-        neg_sum = add_up(neg_grad, BF16)[0]
-        sent = exchange(
-            collect(src_grad, dst_grad, slots[0], devices, neg_sum, neg_slot, neg_cap)
-        )
-        grad = add_pool(pool, listed, devices, feature, rows_dev)
+        rows = spread(exchange(near + far), slots[chunks], rows, feature, True)
+        src_grad, dst_grad, neg_grads = edges(rows, rel_rows, relations, negatives)
+        near = exchange(collect_pool(src_grad, dst_grad, slots[chunks], devices))
+        far = swap(near, 2)
+        sent = direct_sent(src_grad, dst_grad, neg_grads)
+        grad = add_pool([near, swap(near, 1)], listed[:2], None, feature, rows_dev)
+        grad = add_pool([far, swap(far, 1)], listed[2:], grad, feature, rows_dev)
         return add_rows(sent, direct[0], grad, feature, rows_dev, neg_asked, neg_cap)
 
-    if chunks == 1:
+    if chunks == 1 or sharers != 4:
         return chunked().T
     fits = jnp.max(neg_asked[:, -1]) < 0
     return lax.cond(fits, pooled, chunked).T

time: 460 us -> 438 us (0.952)
  waiting for transfers between devices: 184 us -> 157 us
  Pallas kernels: 187 us -> 199 us
  other arithmetic: 16.4 us -> 9.05 us
  local copies, waits for them, and re-layouts: 21.6 us -> 16.7 us
    ppermute x8 -> x12, waiting for transfers between devices: 184 us -> 143 us  [swap(): return lax.ppermute(value, 'grp', [(i, i ^ bit) for i in range(sharers)])]
    all_to_all x5, waiting for transfers between devices: 0.01 us -> 14.2 us  [exchange(): lax.all_to_all(value, ('shard', 'grp'), split_axis=0, concat_axis=0, tile...]
    pallas_call x3 -> x5, Pallas kernels: 60.1 us -> 67.1 us  [the longest x2 32.3 us: add_pool(): call(functools.partial(add_pool_kernel, rows=rows, relays=len(recv)), 'ad...]
    slice x5 -> x1, local copies, waits for them, and re-layouts: 6.92 us -> 0.62 us  [pooled(): listed[1]]
    concatenate x4 -> x0, other arithmetic: 6.08 us -> none  [share_out(): value = jnp.concatenate([value, swap(value, bit)])]
    cond x23 -> x39, local copies, waits for them, and re-layouts: 0.67 us -> 6.54 us
    pallas_call x1 -> x4, Pallas kernels: 33.5 us -> 37.8 us  [gather_pool(): call(functools.partial(gather_pool_kernel, group=group), 'gather_pool', 2...]
    ppermute x8 -> x12, starting transfers between devices: 9.5 us -> 11.1 us  [swap(): return lax.ppermute(value, 'grp', [(i, i ^ bit) for i in range(sharers)])]
  transfers between devices with their start and end apart: 13 -> 17, of which waited for: 6 -> 6; matrix products, arithmetic and copies ran while one was open for 6% -> 3% of each run, Pallas kernels for 27% -> 29%
where the time goes in v3:
time: 438 us; the launch traced here: 432 us
  Pallas kernels  199 us (45%)
  waiting for transfers between devices  157 us (36%)
  starting transfers between devices  41.5 us (9%)
  local copies, waits for them, and re-layouts  16.7 us (4%)
  other arithmetic  9.05 us (2%)
  loops' own time  7.56 us (2%)
    ppermute x12, waiting for transfers between devices, swap(): return lax.ppermute(value, 'grp', [(i, i ^ bit) for i in range(sharers)])  143 us
    pallas_call x4, Pallas kernels, gather_pool(): call(functools.partial(gather_pool_kernel, group=group), 'gather_pool', 2...  37.8 us
    pallas_call x2, Pallas kernels, add_pool(): call(functools.partial(add_pool_kernel, rows=rows, relays=len(recv)), 'ad...  32.3 us
    all_to_all x5, starting transfers between devices, exchange(): lax.all_to_all(value, ('shard', 'grp'), split_axis=0, concat_axis=0, tile...  30.4 us
    pallas_call x2, Pallas kernels, spread(): call(functools.partial(spread_kernel, first=so_far is None, pooled=pooled...  29.9 us
    pallas_call x1, Pallas kernels, add_rows(): call(functools.partial(add_kernel, rows=rows, neg_cap=neg_cap, first=so_f...  23.9 us
    pallas_call x1, Pallas kernels, gather(): call(functools.partial(gather_kernel, group=group, neg_cap=neg_cap), 'gat...  23.7 us
    pallas_call x1, Pallas kernels, collect(): call(functools.partial(collect_kernel, group=group), 'collect_grads', 2 *...  17.9 us
  transfers between devices with their start and end apart: 17, of which 6 were waited for; matrix products, arithmetic and copies ran while one was open for 3% of the time, Pallas kernels for 29%

profile of v3, /device:TPU:17, one launch (start us, length us, event | category | flops | bytes accessed | tf_op | source)
XLA Modules:
  0.0 431.6 jit_solution(14055914233373942856)
XLA Ops:
  0.0 0.8 reshape.57
  0.8 0.8 reshape.58
  1.6 0.6 pad.13.own_ref
  2.3 0.6 pad.12.ends_ref
  2.9 3.5 slots.1
  6.4 1.6 copy.12
  8.0 6.3 %all-to-all-start.8 = ((s32[32,1,640]{2,1,0:T(1,128)}), s32[32,1,640]{2,1,0:T(1,128)S(1)}, u32[]{:S(2)}, u32[]{:S(2)}) async-start(s32[32,1,640]{2,1,0:T(1,128)} %copy.12), calls=%async_computation.8 | async-start | bytes 163840 | tf_op jit(solution)/shard_map/all_to_all | solution.py:628
  14.2 3.3 convert_bitcast_fusion
  17.7 1.7 copy.13
  19.4 0.7 slice_reduce_fusion
  20.8 409.7 %conditional.1 = (f32[400,4096]{1,0:T(8,128)}) conditional(s32[]{:T(128)} %convert_element_type.9, (s32[32,640]{1,0:T(8,128)S(1)}, bf16[400,4096]{1,0:T(8,128)(2,1)S(1)}, s32[4,1024]{1,0:T(4,128)S(1)}, s32[32,128]{1,0:T(8,128)S(1)}, s32[32,128]{1,0:T(8,128)S(1)}, /*index=5*/s32[4,1024]{1,0:T(4,128)S(1)}, s32[2,1024]{1,0:T(2,128)S(1)}, ...), branch_computations={%region_1.2_spmd, %region_2.3_spmd} | conditional | flops 116719091712 | bytes 235771040 | solution.py:733
  27.9 23.7 %gather_rows.5 = bf16[32,528,128]{2,1,0:T(8,128)(2,1)} custom-call(bf16[400,4096]{1,0:T(8,128)(2,1)S(1)} %get-tuple-element.62.table_ref, s32[32,128]{1,0:T(8,128)S(1)} %get-tuple-element.66.refs_0_.refs_1_, s32[32,128]{1,0:T(8,128)S(1)} %get-tuple-element.67.refs_1_.refs_2_), custom_call_target="tpu_custom_call" | custom-call | flops 16777216000 | bytes 7372800 | tf_op jit(solution)/shard_map/cond/branch_1_fun/gather_rows/pallas_call | solution.py:195
  51.6 5.9 %all-to-all-start.5 = ((bf16[32,528,128]{2,1,0:T(8,128)(2,1)}), bf16[32,528,128]{2,1,0:T(8,128)(2,1)}, u32[]{:S(2)}, u32[]{:S(2)}) async-start(bf16[32,528,128]{2,1,0:T(8,128)(2,1)} %gather_rows.5), calls=%async_computation.5 | async-start | bytes 8650752 | tf_op jit(solution)/shard_map/cond/branch_1_fun/all_to_all | solution.py:628
  57.8 0.6 gather_fusion
  58.4 0.6 fusion.1
  59.0 9.5 %gather_pool.7 = bf16[32,192,128]{2,1,0:T(8,128)(2,1)} custom-call(bf16[400,4096]{1,0:T(8,128)(2,1)S(1)} %get-tuple-element.62.table_ref, s32[4,1,384]{2,1,0:T(1,128)} %bitcast.38), custom_call_target="tpu_custom_call" | custom-call | flops 5033164800 | bytes 4505600 | tf_op jit(solution)/shard_map/cond/branch_1_fun/gather_pool/pallas_call | solution.py:221
  68.5 0.4 collective-permute-start.7
  68.8 9.4 %gather_pool.5 = bf16[32,192,128]{2,1,0:T(8,128)(2,1)} custom-call(bf16[400,4096]{1,0:T(8,128)(2,1)S(1)} %get-tuple-element.62.table_ref, s32[4,1,384]{2,1,0:T(1,128)} %bitcast.37), custom_call_target="tpu_custom_call" | custom-call | flops 5033164800 | bytes 4505600 | tf_op jit(solution)/shard_map/cond/branch_1_fun/gather_pool/pallas_call | solution.py:221
  78.2 0.2 collective-permute-start.6
  78.4 9.5 %gather_pool.6 = bf16[32,192,128]{2,1,0:T(8,128)(2,1)} custom-call(bf16[400,4096]{1,0:T(8,128)(2,1)S(1)} %get-tuple-element.62.table_ref, s32[4,1,384]{2,1,0:T(1,128)} %bitcast.36), custom_call_target="tpu_custom_call" | custom-call | flops 5033164800 | bytes 4505600 | tf_op jit(solution)/shard_map/cond/branch_1_fun/gather_pool/pallas_call | solution.py:221
  87.8 2.0 add.19
  89.8 1.3 collective-permute-start.8
  91.1 9.5 %gather_pool.4 = bf16[32,192,128]{2,1,0:T(8,128)(2,1)} custom-call(bf16[400,4096]{1,0:T(8,128)(2,1)S(1)} %get-tuple-element.62.table_ref, s32[4,1,384]{2,1,0:T(1,128)} %bitcast.35), custom_call_target="tpu_custom_call" | custom-call | flops 5033164800 | bytes 4505600 | tf_op jit(solution)/shard_map/cond/branch_1_fun/gather_pool/pallas_call | solution.py:221
  100.6 43.4 %collective-permute-done.8 = bf16[32,192,128]{2,1,0:T(8,128)(2,1)S(1)} collective-permute-done((bf16[32,192,128]{2,1,0:T(8,128)(2,1)S(1)}, bf16[32,192,128]{2,1,0:T(8,128)(2,1)S(1)}, u32[]{:S(2)}, u32[]{:S(2)}) %collective-permute-start.8) | collective-permute-done | bytes 1572896 | tf_op jit(solution)/shard_map/cond/branch_1_fun/ppermute | solution.py:633
  144.0 3.0 add_add_fusion
  147.0 4.2 all-to-all-done.5.refs_0_.back_ref
  151.2 7.4 %all-to-all-start.4 = ((bf16[32,192,128]{2,1,0:T(8,128)(2,1)}), bf16[32,192,128]{2,1,0:T(8,128)(2,1)S(1)}, u32[]{:S(2)}, u32[]{:S(2)}) async-start(bf16[32,192,128]{2,1,0:T(8,128)(2,1)} %add_add_fusion), calls=%async_computation.4 | async-start | bytes 3145728 | tf_op jit(solution)/shard_map/cond/branch_1_fun/all_to_all | solution.py:628
  158.6 0.6 reshape.51.refs_2_
  159.2 0.6 reshape.49.refs_1_
  159.8 0.6 reshape.50.refs_1_
  160.4 2.8 spread_negatives.3.refs_4_
  163.2 1.4 collective-permute-start.11
  164.7 0.3 collective-permute-start.10
  165.0 0.4 collective-permute-start.9
  165.4 19.3 %spread_rows.5.refs_2_ = bf16[400,4096]{1,0:T(8,128)(2,1)} custom-call(bf16[32,528,128]{2,1,0:T(8,128)(2,1)} %all-to-all-done.5.refs_0_.back_ref, s32[4,1,1024]{2,1,0:T(1,128)} %reshape.50.refs_1_), custom_call_target="tpu_custom_call" | custom-call | flops 13421772800 | bytes 6553600 | tf_op jit(solution)/shard_map/cond/branch_1_fun/spread_rows/pallas_call | solution.py:304
  184.7 10.0 %all-to-all-done.4.refs_0_ = bf16[32,192,128]{2,1,0:T(8,128)(2,1)S(1)} async-done(((bf16[32,192,128]{2,1,0:T(8,128)(2,1)}), bf16[32,192,128]{2,1,0:T(8,128)(2,1)S(1)}, u32[]{:S(2)}, u32[]{:S(2)}) %all-to-all-start.4) | async-done | bytes 1572896 | tf_op jit(solution)/shard_map/cond/branch_1_fun/all_to_all | solution.py:628
  194.7 1.2 copy-done.5
  195.9 10.6 %spread_pool.1.refs_0_.refs_1_ = bf16[400,4096]{1,0:T(8,128)(2,1)} custom-call(bf16[32,192,128]{2,1,0:T(8,128)(2,1)} %copy-done.5, s32[4,1,1024]{2,1,0:T(1,128)} %reshape.49.refs_1_, bf16[400,4096]{1,0:T(8,128)(2,1)} %spread_rows.5.refs_2_), custom_call_target="tpu_custom_call" | custom-call | flops 5033164800 | bytes 4505600 | tf_op jit(solution)/shard_map/cond/branch_1_fun/spread_pool/pallas_call | solution.py:304
  206.6 0.8 copy-done.26
  207.3 0.2 copy-done.28
  207.5 13.4 %edges.3 = (bf16[400,2048]{1,0:T(8,128)(2,1)}, bf16[400,2048]{1,0:T(8,128)(2,1)}, bf16[2,256,400]{2,1,0:T(8,128)(2,1)}, bf16[2,256,400]{2,1,0:T(8,128)(2,1)}, bf...) custom-call(bf16[400,4096]{1,0:T(8,128)(2,1)} %spread_pool.1.refs_0_.refs_1_, ...), custom_call_target="tpu_custom_call" | custom-call | flops 5033164800 | bytes 9830400 | tf_op jit(solution)/shard_map/cond/branch_1_fun/edges/pallas_call | solution.py:379
  221.0 10.1 %collect_pool.1 = bf16[32,192,128]{2,1,0:T(8,128)(2,1)} custom-call(bf16[400,2048]{1,0:T(8,128)(2,1)} %get-tuple-element.72.src_ref, bf16[400,2048]{1,0:T(8,128)(2,1)} %get-tuple-element.73.dst_ref, s32[4,1024]{1,0:T(4,128)S(1)} %get-tuple-element.65.slot_ref), custom_call_target="tpu_custom_call" | custom-call | flops 5033164800 | bytes 4505600 | tf_op jit(solution)/shard_map/cond/branch_1_fun/collect_pool/pallas_call | solution.py:499
  231.1 5.3 %all-to-all-start.7 = ((bf16[32,192,128]{2,1,0:T(8,128)(2,1)}), bf16[32,192,128]{2,1,0:T(8,128)(2,1)S(1)}, u32[]{:S(2)}, u32[]{:S(2)}) async-start(bf16[32,192,128]{2,1,0:T(8,128)(2,1)} %collect_pool.1), calls=%async_computation.7 | async-start | bytes 3145728 | tf_op jit(solution)/shard_map/cond/branch_1_fun/all_to_all | solution.py:628
  236.3 0.4 collective-permute-start.12
  236.8 1.2 collective-permute-start.13
  238.0 0.6 collective-permute-start.14
  238.6 17.9 %collect_grads.5.sent_ref = bf16[32,528,128]{2,1,0:T(8,128)(2,1)} custom-call(bf16[400,2048]{1,0:T(8,128)(2,1)} %get-tuple-element.72.src_ref, bf16[400,2048]{1,0:T(8,128)(2,1)} %get-tuple-element.73.dst_ref, s32[4,1024]{1,0:T(4,128)S(1)} %get-tuple-element.68.slot_ref), custom_call_target="tpu_custom_call" | custom-call | flops 13421772800 | bytes 6553600 | tf_op jit(solution)/shard_map/cond/branch_1_fun/collect_grads/pallas_call | solution.py:426
  256.5 8.4 %collective-permute-done.13.refs_2_ = bf16[2,256,400]{2,1,0:T(8,128)(2,1)S(1)} collective-permute-done((bf16[2,256,400]{2,1,0:T(8,128)(2,1)S(1)}, bf16[2,256,400]{2,1,0:T(8,128)(2,1)S(1)}, u32[]{:S(2)}, u32[]{:S(2)}) %collective-permute-start.13) | collective-permute-done | bytes 409632 | tf_op jit(solution)/shard_map/cond/branch_1_fun/ppermute | solution.py:633
  264.9 13.0 %collective-permute-done.14.refs_3_ = bf16[2,256,400]{2,1,0:T(8,128)(2,1)S(1)} collective-permute-done((bf16[2,256,400]{2,1,0:T(8,128)(2,1)S(1)}, bf16[2,256,400]{2,1,0:T(8,128)(2,1)S(1)}, u32[]{:S(2)}, u32[]{:S(2)}) %collective-permute-start.14) | collective-permute-done | bytes 409632 | tf_op jit(solution)/shard_map/cond/branch_1_fun/ppermute | solution.py:633
  277.9 0.8 copy-done.11
  278.7 3.5 collect_negatives.3
  282.2 5.6 %all-to-all-start.6 = ((bf16[32,528,128]{2,1,0:T(8,128)(2,1)}), bf16[32,528,128]{2,1,0:T(8,128)(2,1)}, u32[]{:S(2)}, u32[]{:S(2)}) async-start(bf16[32,528,128]{2,1,0:T(8,128)(2,1)} %collect_negatives.3), calls=%async_computation.6 | async-start | bytes 8650752 | tf_op jit(solution)/shard_map/cond/branch_1_fun/all_to_all | solution.py:628
  287.8 1.2 collective-permute-start.15
  289.0 0.6 collective-permute-start.17
  289.7 77.7 %collective-permute-done.15.refs_0_ = bf16[32,192,128]{2,1,0:T(8,128)(2,1)S(1)} collective-permute-done((bf16[32,192,128]{2,1,0:T(8,128)(2,1)S(1)}, bf16[32,192,128]{2,1,0:T(8,128)(2,1)S(1)}, u32[]{:S(2)}, u32[]{:S(2)}) %collective-permute-start.15) | collective-permute-done | bytes 1572896 | tf_op jit(solution)/shard_map/cond/branch_1_fun/ppermute | solution.py:633
  367.4 3.1 collective-permute-start.16
  370.5 0.6 copy.16
  371.1 0.6 copy.15
  371.7 1.2 copy-done.24
  372.9 15.9 %add_pool.2.refs_3_ = f32[400,4096]{1,0:T(8,128)} custom-call(bf16[32,192,128]{2,1,0:T(8,128)(2,1)} %copy-done.4, bf16[32,192,128]{2,1,0:T(8,128)(2,1)} %copy-done.24, s32[1,3072]{1,0:T(1,128)} %bitcast.34), custom_call_target="tpu_custom_call" | custom-call | flops 10066329600 | bytes 9011200 | tf_op jit(solution)/shard_map/cond/branch_1_fun/add_pool/pallas_call | solution.py:609
  388.8 1.2 copy-done.25
  389.9 16.4 %add_pool.3.refs_3_ = f32[400,4096]{1,0:T(8,128)} custom-call(bf16[32,192,128]{2,1,0:T(8,128)(2,1)} %copy-done.23, bf16[32,192,128]{2,1,0:T(8,128)(2,1)} %copy-done.25, s32[1,3072]{1,0:T(1,128)} %bitcast.33, f32[400,4096]{1,0:T(8,128)} %add_pool.2.refs_3_), custom_call_target="tpu_custom_call" | custom-call | flops 10066329600 | bytes 9011200 | tf_op jit(solution)/shard_map/cond/branch_1_fun/add_pool/pallas_call | solution.py:609
  406.3 23.9 %add_grads.5 = f32[400,4096]{1,0:T(8,128)} custom-call(bf16[32,528,128]{2,1,0:T(8,128)(2,1)} %all-to-all-done.6.refs_0_, s32[32,128]{1,0:T(8,128)S(1)} %copy-done.21, s32[32,128]{1,0:T(8,128)S(1)} %copy-done.17, f32[400,4096]{1,0:T(8,128)} %add_pool.3.refs_3_), custom_call_target="tpu_custom_call" | custom-call | flops 13421772800 | bytes 16384000 | tf_op jit(solution)/shard_map/cond/branch_1_fun/add_grads/pallas_call | solution.py:566
  430.5 0.7 copy-done.1
  (59 shorter events, 0.5 us)
Async XLA Ops:
  0.0 1.6 copy-start
  8.0 11.4 %all-to-all-start.8 = ((s32[32,1,640]{2,1,0:T(1,128)}), s32[32,1,640]{2,1,0:T(1,128)S(1)}, u32[]{:S(2)}, u32[]{:S(2)}) async-start(s32[32,1,640]{2,1,0:T(1,128)} %copy.12), calls=%async_computation.8 | async-start | bytes 163840 | tf_op jit(solution)/shard_map/all_to_all | solution.py:628
  14.2 3.3 copy-start.22
  27.9 23.7 %copy-start.16 = (s32[32,128]{1,0:T(8,128)}, s32[32,128]{1,0:T(8,128)S(1)}, u32[]{:S(2)}) copy-start(s32[32,128]{1,0:T(8,128)S(1)} %get-tuple-element.67.refs_1_.refs_2_) | copy-start | bytes 49156 | tf_op jit(solution)/shard_map/cond
  27.9 23.7 %copy-start.20 = (s32[32,128]{1,0:T(8,128)}, s32[32,128]{1,0:T(8,128)S(1)}, u32[]{:S(2)}) copy-start(s32[32,128]{1,0:T(8,128)S(1)} %get-tuple-element.66.refs_0_.refs_1_) | copy-start | bytes 49156 | tf_op jit(solution)/shard_map/cond
  51.6 99.6 %all-to-all-start.5 = ((bf16[32,528,128]{2,1,0:T(8,128)(2,1)}), bf16[32,528,128]{2,1,0:T(8,128)(2,1)}, u32[]{:S(2)}, u32[]{:S(2)}) async-start(bf16[32,528,128]{2,1,0:T(8,128)(2,1)} %gather_rows.5), calls=%async_computation.5 | async-start | bytes 8650752 | tf_op jit(solution)/shard_map/cond/branch_1_fun/all_to_all | solution.py:628
  68.5 19.4 %collective-permute-start.7 = (bf16[32,192,128]{2,1,0:T(8,128)(2,1)}, bf16[32,192,128]{2,1,0:T(8,128)(2,1)S(1)}, u32[]{:S(2)}, u32[]{:S(2)}) collective-permute-start(bf16[32,192,128]{2,1,0:T(8,128)(2,1)} %gather_pool.7), channel_id=1, source_target_pairs={{0,1},{1,0},{2,3},{3,2},{4,5},{5,4},{6,7},{7,6},{8,9},{9,8},{10,11... | collective-permute-start | bytes 4718600 | tf_op jit(solution)/shard_map/cond/branch_1_fun/ppermute | solution.py:633
  78.2 22.4 %collective-permute-start.6 = (bf16[32,192,128]{2,1,0:T(8,128)(2,1)}, bf16[32,192,128]{2,1,0:T(8,128)(2,1)S(1)}, u32[]{:S(2)}, u32[]{:S(2)}) collective-permute-start(bf16[32,192,128]{2,1,0:T(8,128)(2,1)} %gather_pool.5), channel_id=1, source_target_pairs={{0,1},{1,0},{2,3},{3,2},{4,5},{5,4},{6,7},{7,6},{8,9},{9,8},{10,11... | collective-permute-start | bytes 4718600 | tf_op jit(solution)/shard_map/cond/branch_1_fun/ppermute | solution.py:633
  89.8 54.1 %collective-permute-start.8 = (bf16[32,192,128]{2,1,0:T(8,128)(2,1)S(1)}, bf16[32,192,128]{2,1,0:T(8,128)(2,1)S(1)}, u32[]{:S(2)}, u32[]{:S(2)}) collective-permute-start(bf16[32,192,128]{2,1,0:T(8,128)(2,1)S(1)} %add.19), channel_id=1, source_target_pairs={{0,2},{1,3},{2,0},{3,1},{4,6},{5,7},{6,4},{7,5},{8,10},{9,11},{10,... | collective-permute-start | bytes 4718600 | tf_op jit(solution)/shard_map/cond/branch_1_fun/ppermute | solution.py:633
  151.2 43.6 %all-to-all-start.4 = ((bf16[32,192,128]{2,1,0:T(8,128)(2,1)}), bf16[32,192,128]{2,1,0:T(8,128)(2,1)S(1)}, u32[]{:S(2)}, u32[]{:S(2)}) async-start(bf16[32,192,128]{2,1,0:T(8,128)(2,1)} %add_add_fusion), calls=%async_computation.4 | async-start | bytes 3145728 | tf_op jit(solution)/shard_map/cond/branch_1_fun/all_to_all | solution.py:628
  163.2 43.3 %collective-permute-start.11 = (bf16[2,256,400]{2,1,0:T(8,128)(2,1)}, bf16[2,256,400]{2,1,0:T(8,128)(2,1)S(1)}, u32[]{:S(2)}, u32[]{:S(2)}) collective-permute-start(bf16[2,256,400]{2,1,0:T(8,128)(2,1)} %spread_negatives.3.refs_4_), channel_id=1, source_target_pairs={{0,3},{1,2},{2,1},{3,0},{4,7},{5,6},{6,5},{7,4},{8,11},{9,10},{10,... | collective-permute-start | bytes 1228808 | tf_op jit(solution)/shard_map/cond/branch_1_fun/ppermute | solution.py:633
  164.7 41.9 %collective-permute-start.10 = (bf16[2,256,400]{2,1,0:T(8,128)(2,1)}, bf16[2,256,400]{2,1,0:T(8,128)(2,1)S(1)}, u32[]{:S(2)}, u32[]{:S(2)}) collective-permute-start(bf16[2,256,400]{2,1,0:T(8,128)(2,1)} %spread_negatives.3.refs_4_), channel_id=1, source_target_pairs={{0,2},{1,3},{2,0},{3,1},{4,6},{5,7},{6,4},{7,5},{8,10},{9,11},{10,... | collective-permute-start | bytes 1228808 | tf_op jit(solution)/shard_map/cond/branch_1_fun/ppermute | solution.py:633
  165.0 41.6 %collective-permute-start.9 = (bf16[2,256,400]{2,1,0:T(8,128)(2,1)}, bf16[2,256,400]{2,1,0:T(8,128)(2,1)}, u32[]{:S(2)}, u32[]{:S(2)}) collective-permute-start(bf16[2,256,400]{2,1,0:T(8,128)(2,1)} %spread_negatives.3.refs_4_), channel_id=1, source_target_pairs={{0,1},{1,0},{2,3},{3,2},{4,5},{5,4},{6,7},{7,6},{8,9},{9,8},{10,11... | collective-permute-start | bytes 1228808 | tf_op jit(solution)/shard_map/cond/branch_1_fun/ppermute | solution.py:633
  184.7 22.8 %copy-start.13 = (f32[400,64]{1,0:T(8,128)S(1)}, f32[400,64]{1,0:T(8,128)}, u32[]{:S(2)}) copy-start(f32[400,64]{1,0:T(8,128)} %get-tuple-element.70.refs_3_) | copy-start | bytes 307204 | tf_op jit(solution)/shard_map/cond
  194.7 1.2 copy-start.5
  206.5 0.8 copy-start.26
  206.5 1.0 copy-start.28
  220.9 15.4 %copy-start.30 = (bf16[2,256,400]{2,1,0:T(8,128)(2,1)S(1)}, bf16[2,256,400]{2,1,0:T(8,128)(2,1)}, u32[]{:S(2)}) copy-start(bf16[2,256,400]{2,1,0:T(8,128)(2,1)} %get-tuple-element.75) | copy-start | bytes 1228804 | tf_op jit(solution)/shard_map/cond
  220.9 15.8 %copy-start.29 = (bf16[2,256,400]{2,1,0:T(8,128)(2,1)S(1)}, bf16[2,256,400]{2,1,0:T(8,128)(2,1)}, u32[]{:S(2)}) copy-start(bf16[2,256,400]{2,1,0:T(8,128)(2,1)} %get-tuple-element.76) | copy-start | bytes 1228804 | tf_op jit(solution)/shard_map/cond
  221.0 17.0 %copy-start.27 = (bf16[2,256,400]{2,1,0:T(8,128)(2,1)S(1)}, bf16[2,256,400]{2,1,0:T(8,128)(2,1)}, u32[]{:S(2)}) copy-start(bf16[2,256,400]{2,1,0:T(8,128)(2,1)} %get-tuple-element.77) | copy-start | bytes 1228804 | tf_op jit(solution)/shard_map/cond
  231.1 51.1 %all-to-all-start.7 = ((bf16[32,192,128]{2,1,0:T(8,128)(2,1)}), bf16[32,192,128]{2,1,0:T(8,128)(2,1)S(1)}, u32[]{:S(2)}, u32[]{:S(2)}) async-start(bf16[32,192,128]{2,1,0:T(8,128)(2,1)} %collect_pool.1), calls=%async_computation.7 | async-start | bytes 3145728 | tf_op jit(solution)/shard_map/cond/branch_1_fun/all_to_all | solution.py:628
  236.3 20.2 %collective-permute-start.12 = (bf16[2,256,400]{2,1,0:T(8,128)(2,1)S(1)}, bf16[2,256,400]{2,1,0:T(8,128)(2,1)S(1)}, u32[]{:S(2)}, u32[]{:S(2)}) collective-permute-start(bf16[2,256,400]{2,1,0:T(8,128)(2,1)S(1)} %copy-done.30), channel_id=1, source_target_pairs={{0,1},{1,0},{2,3},{3,2},{4,5},{5,4},{6,7},{7,6},{8,9},{9,8},{10,11... | collective-permute-start | bytes 1228808 | tf_op jit(solution)/shard_map/cond/branch_1_fun/ppermute | solution.py:633
  236.8 28.1 %collective-permute-start.13 = (bf16[2,256,400]{2,1,0:T(8,128)(2,1)S(1)}, bf16[2,256,400]{2,1,0:T(8,128)(2,1)S(1)}, u32[]{:S(2)}, u32[]{:S(2)}) collective-permute-start(bf16[2,256,400]{2,1,0:T(8,128)(2,1)S(1)} %copy-done.29), channel_id=1, source_target_pairs={{0,2},{1,3},{2,0},{3,1},{4,6},{5,7},{6,4},{7,5},{8,10},{9,11},{10,... | collective-permute-start | bytes 1228808 | tf_op jit(solution)/shard_map/cond/branch_1_fun/ppermute | solution.py:633
  238.0 39.9 %collective-permute-start.14 = (bf16[2,256,400]{2,1,0:T(8,128)(2,1)S(1)}, bf16[2,256,400]{2,1,0:T(8,128)(2,1)S(1)}, u32[]{:S(2)}, u32[]{:S(2)}) collective-permute-start(bf16[2,256,400]{2,1,0:T(8,128)(2,1)S(1)} %copy-done.27), channel_id=1, source_target_pairs={{0,3},{1,2},{2,1},{3,0},{4,7},{5,6},{6,5},{7,4},{8,11},{9,10},{10,... | collective-permute-start | bytes 1228808 | tf_op jit(solution)/shard_map/cond/branch_1_fun/ppermute | solution.py:633
  256.5 21.4 %copy-start.7 = (bf16[2,256,400]{2,1,0:T(8,128)(2,1)}, bf16[2,256,400]{2,1,0:T(8,128)(2,1)S(1)}, u32[]{:S(2)}) copy-start(bf16[2,256,400]{2,1,0:T(8,128)(2,1)S(1)} %collective-permute-done.12.refs_1_) | copy-start | bytes 1228804 | tf_op jit(solution)/shard_map/cond
  264.9 13.0 %copy-start.9 = (bf16[2,256,400]{2,1,0:T(8,128)(2,1)}, bf16[2,256,400]{2,1,0:T(8,128)(2,1)S(1)}, u32[]{:S(2)}) copy-start(bf16[2,256,400]{2,1,0:T(8,128)(2,1)S(1)} %collective-permute-done.13.refs_2_) | copy-start | bytes 1228804 | tf_op jit(solution)/shard_map/cond
  277.9 0.8 copy-start.11
  282.2 6.8 %copy-start.4 = (bf16[32,192,128]{2,1,0:T(8,128)(2,1)}, bf16[32,192,128]{2,1,0:T(8,128)(2,1)S(1)}, u32[]{:S(2)}) copy-start(bf16[32,192,128]{2,1,0:T(8,128)(2,1)S(1)} %all-to-all-done.7.refs_0_) | copy-start | bytes 4718596 | tf_op jit(solution)/shard_map/cond
  282.2 124.1 %all-to-all-start.6 = ((bf16[32,528,128]{2,1,0:T(8,128)(2,1)}), bf16[32,528,128]{2,1,0:T(8,128)(2,1)}, u32[]{:S(2)}, u32[]{:S(2)}) async-start(bf16[32,528,128]{2,1,0:T(8,128)(2,1)} %collect_negatives.3), calls=%async_computation.6 | async-start | bytes 8650752 | tf_op jit(solution)/shard_map/cond/branch_1_fun/all_to_all | solution.py:628
  287.8 79.6 %collective-permute-start.15 = (bf16[32,192,128]{2,1,0:T(8,128)(2,1)S(1)}, bf16[32,192,128]{2,1,0:T(8,128)(2,1)S(1)}, u32[]{:S(2)}, u32[]{:S(2)}) collective-permute-start(bf16[32,192,128]{2,1,0:T(8,128)(2,1)S(1)} %all-to-all-done.7.refs_0_), channel_id=1, source_target_pairs={{0,2},{1,3},{2,0},{3,1},{4,6},{5,7},{6,4},{7,5},{8,10},{9,11},{10,... | collective-permute-start | bytes 4718600 | tf_op jit(solution)/shard_map/cond/branch_1_fun/ppermute | solution.py:633
  289.0 82.7 %collective-permute-start.17 = (bf16[32,192,128]{2,1,0:T(8,128)(2,1)S(1)}, bf16[32,192,128]{2,1,0:T(8,128)(2,1)S(1)}, u32[]{:S(2)}, u32[]{:S(2)}) collective-permute-start(bf16[32,192,128]{2,1,0:T(8,128)(2,1)S(1)} %all-to-all-done.7.refs_0_), channel_id=1, source_target_pairs={{0,1},{1,0},{2,3},{3,2},{4,5},{5,4},{6,7},{7,6},{8,9},{9,8},{10,11... | collective-permute-start | bytes 4718600 | tf_op jit(solution)/shard_map/cond/branch_1_fun/ppermute | solution.py:633
  367.4 21.3 %copy-start.23 = (bf16[32,192,128]{2,1,0:T(8,128)(2,1)}, bf16[32,192,128]{2,1,0:T(8,128)(2,1)S(1)}, u32[]{:S(2)}) copy-start(bf16[32,192,128]{2,1,0:T(8,128)(2,1)S(1)} %collective-permute-done.15.refs_0_) | copy-start | bytes 4718596 | tf_op jit(solution)/shard_map/cond
  367.4 21.3 %collective-permute-start.16 = (bf16[32,192,128]{2,1,0:T(8,128)(2,1)S(1)}, bf16[32,192,128]{2,1,0:T(8,128)(2,1)S(1)}, u32[]{:S(2)}, u32[]{:S(2)}) collective-permute-start(bf16[32,192,128]{2,1,0:T(8,128)(2,1)S(1)} %collective-permute-done.15.refs_0_), channel_id=1, source_target_pairs={{0,1},{1,0},{2,3},{3,2},{4,5},{5,4},{6,7},{7,6},{8,9},{9,8},{10,11... | collective-permute-start | bytes 4718600 | tf_op jit(solution)/shard_map/cond/branch_1_fun/ppermute | solution.py:633
  371.7 1.2 copy-start.24
  388.7 1.2 copy-start.25
  389.9 16.4 %copy-start.17 = (s32[32,128]{1,0:T(8,128)S(1)}, s32[32,128]{1,0:T(8,128)}, u32[]{:S(2)}) copy-start(s32[32,128]{1,0:T(8,128)} %copy-done.16) | copy-start | bytes 49156 | tf_op jit(solution)/shard_map/cond
  389.9 16.4 %copy-start.21 = (s32[32,128]{1,0:T(8,128)S(1)}, s32[32,128]{1,0:T(8,128)}, u32[]{:S(2)}) copy-start(s32[32,128]{1,0:T(8,128)} %copy-done.20) | copy-start | bytes 49156 | tf_op jit(solution)/shard_map/cond
  430.5 0.7 copy-start.1

commit v4 on v3

--- a/solution.py
+++ b/solution.py
@@ -8,7 +8,8 @@
 from jax.sharding import PartitionSpec as P
 
 LANES = 128
-POOL = 48
+POOL = 80
+RELAYS = 2
 VMEM_BYTES = 56 << 20
 F32 = jnp.float32
 BF16 = jnp.bfloat16
@@ -63,7 +64,7 @@
     return (LANES * sums[:groups] + sums[groups:]).astype(jnp.int32) - 1
 
 
-def slots_kernel(ends_ref, own_ref, *refs, rows_dev, devices, sharers, chunks, neg_cap):
+def slots_kernel(ends_ref, own_ref, *refs, rows_dev, devices, chunks, neg_cap):
     msg_ref = refs[0]
     slot_refs = refs[1 : 1 + chunks]
     pool_ref = refs[1 + chunks] if chunks > 1 else None
@@ -98,24 +99,24 @@
     offset = chunks * LANES
     flag = jnp.full((1, 1), -1, jnp.int32)
     if chunks > 1:
-        shards = devices // sharers
-        room = sharers * POOL
-        shard_rows = lax.broadcasted_iota(jnp.int32, (shards, LANES), 0)
+        chips = devices // RELAYS
+        room = RELAYS * POOL
+        chip_rows = lax.broadcasted_iota(jnp.int32, (chips, LANES), 0)
         spilled, spill_codes = [], []
         for owner, code, rank in zip(holder, codes, found):
-            shard = jnp.where(rank >= LANES, owner // sharers, -1)
-            spilled.append(jnp.where(shard_rows == shard, 1.0, 0.0))
-            spill_codes.append(code + (owner % sharers) * rows_dev)
+            chip = jnp.where(rank >= LANES, owner // RELAYS, -1)
+            spilled.append(jnp.where(chip_rows == chip, 1.0, 0.0))
+            spill_codes.append(code + (owner % RELAYS) * rows_dev)
         pooled, taken = ranks(spilled, mixer)
         places = []
         for at, owner, rank, place in zip(where, holder, found, pooled):
             inside = (owner >= 0) & (rank >= LANES) & (place < room)
-            pool_ref[at] = jnp.where(inside, owner // sharers * room + place, -1)
+            pool_ref[at] = jnp.where(inside, owner // RELAYS * room + place, -1)
             places.append(jnp.where(inside, place, -1))
         listed = fill(spilled, spill_codes, places, 2 * LANES)
-        for shard in range(shards):
-            msg_ref[shard * sharers : (shard + 1) * sharers, offset : offset + 2 * LANES] = (
-                jnp.broadcast_to(listed[shard : shard + 1], (sharers, 2 * LANES))
+        for chip in range(chips):
+            msg_ref[chip * RELAYS : (chip + 1) * RELAYS, offset : offset + 2 * LANES] = (
+                jnp.broadcast_to(listed[chip : chip + 1], (RELAYS, 2 * LANES))
             )
         offset += 2 * LANES
         most = jnp.max(jnp.max(taken, axis=1, keepdims=True), axis=0, keepdims=True)
@@ -130,7 +131,7 @@
     msg_ref[:, offset:] = jnp.where(lanes == LANES - 1, flag, listed)
 
 
-def make_slots(ends, own, rows_dev, devices, sharers, chunks, neg_cap):
+def make_slots(ends, own, rows_dev, devices, chunks, neg_cap):
     pooled = chunks > 1
     width = (chunks + 1 + 2 * pooled) * LANES
     return call(
@@ -138,7 +139,6 @@
             slots_kernel,
             rows_dev=rows_dev,
             devices=devices,
-            sharers=sharers,
             chunks=chunks,
             neg_cap=neg_cap,
         ),
@@ -151,21 +151,51 @@
     )(ends, own)
 
 
-def pack(out_ref, at, start, rows):
+def packed_height(count, feature):
+    return feature // LANES * count + feature % LANES
+
+
+def pack(out_ref, at, start, rows, tail):
     count, feature = rows.shape
-    full = round_up(feature, LANES)
-    rows = jnp.concatenate([rows, jnp.zeros((count, full - feature), rows.dtype)], axis=1)
-    for piece in range(full // LANES):
+    for piece in range(feature // LANES):
         out_ref[at, start + piece * count : start + (piece + 1) * count, :] = rows[
             :, piece * LANES : (piece + 1) * LANES
         ].astype(out_ref.dtype)
-
-
-def unpack(in_ref, at, start, count, flat_ref, to):
-    for piece in range(flat_ref.shape[1] // LANES):
-        flat_ref[to : to + count, piece * LANES : (piece + 1) * LANES] = in_ref[
-            at, start + piece * count : start + (piece + 1) * count, :
-        ]
+    tail = jnp.concatenate([tail, jnp.zeros((tail.shape[0], LANES - count), tail.dtype)], axis=1)
+    end = start + packed_height(count, feature)
+    out_ref[at, end - tail.shape[0] : end, :] = tail.astype(out_ref.dtype)
+
+
+def pack_all(out_ref, start, count, rows, turned):
+    feature = rows.shape[1]
+    first = feature // LANES * LANES
+    for i in range(out_ref.shape[0]):
+        at = slice(i * count, (i + 1) * count)
+        pack(out_ref, i, start, rows[at], turned[first:, at])
+
+
+def unpack_all(in_ref, start, count, rows_ref, flat_ref):
+    feature = flat_ref.shape[0]
+    pieces = feature // LANES
+    end = start + packed_height(count, feature)
+    devices = in_ref.shape[0]
+    for d in range(devices):
+        for piece in range(pieces):
+            rows_ref[d * count : (d + 1) * count, piece * LANES : (piece + 1) * LANES] = in_ref[
+                d, start + piece * count : start + (piece + 1) * count, :
+            ]
+    tails = [
+        in_ref[d, end - feature % LANES : end, :].astype(F32)[:, :count] for d in range(devices)
+    ]
+    flat_ref[: pieces * LANES] = rows_ref[...].astype(F32).T.astype(BF16)
+    flat_ref[pieces * LANES :] = jnp.concatenate(tails, axis=1).astype(BF16)
+
+
+def unpack_scratch(devices, count, feature):
+    return [
+        pltpu.VMEM((devices * count, feature // LANES * LANES), BF16),
+        pltpu.VMEM((feature, devices * count), BF16),
+    ]
 
 
 def gather_kernel(table_ref, *refs, group, neg_cap):
@@ -180,16 +210,15 @@
     for i in range(group):
         out_ref[i, start:] = rows[:, i * LANES : (i + 1) * LANES].astype(BF16)
     if neg_cap:
-        neg = rows[:, group * LANES :].T
-        for i in range(group):
-            pack(out_ref, i, 0, neg[i * neg_cap : (i + 1) * neg_cap])
+        neg = rows[:, group * LANES :]
+        pack_all(out_ref, 0, neg_cap, neg.T, neg)
 
 
 def gather(table, requests, neg_requests=None, neg_cap=0):
     feature, rows_dev = table.shape
     devices = requests.shape[0]
     group = 4
-    height = feature + neg_cap * (round_up(feature, LANES) // LANES)
+    height = feature + (packed_height(neg_cap, feature) if neg_cap else 0)
     slots = devices * (LANES + neg_cap)
     whole = pl.BlockSpec((devices, LANES), lambda i: (0, 0))
     return call(
@@ -208,16 +237,15 @@
 def gather_pool_kernel(table_ref, req_ref, out_ref, *, group):
     rows_dev = table_ref.shape[1]
     row = req_ref[...].reshape(1, group * POOL)
-    rows = dot(table_ref[...], one_hot(rows_dev, row), NN).T
-    for i in range(group):
-        pack(out_ref, i, 0, rows[i * POOL : (i + 1) * POOL])
+    rows = dot(table_ref[...], one_hot(rows_dev, row), NN)
+    pack_all(out_ref, 0, POOL, rows.T, rows)
 
 
 def gather_pool(table, requests, devices):
     feature, rows_dev = table.shape
     group = 8
     steps = devices // group
-    height = POOL * (round_up(feature, LANES) // LANES)
+    height = packed_height(POOL, feature)
     return call(
         functools.partial(gather_pool_kernel, group=group),
         "gather_pool",
@@ -233,27 +261,22 @@
     )(table, requests.reshape(steps, 1, group * POOL))
 
 
-def spread_neg_kernel(back_ref, slot_ref, out_ref, flat, *, cap):
-    parts = slot_ref.shape[0]
-    feature = out_ref.shape[-1]
-    devices = back_ref.shape[0]
-    for d in range(devices):
-        unpack(back_ref, d, 0, cap, flat, d * cap)
-    for part in range(parts):
-        hot = one_hot(devices * cap, slot_ref[part : part + 1, :])
-        out_ref[part] = dot(hot, flat[...], TN)[:, :feature].astype(BF16)
+def spread_neg_kernel(back_ref, slot_ref, out_ref, rows, flat, *, cap):
+    unpack_all(back_ref, 0, cap, rows, flat)
+    for part in range(slot_ref.shape[0]):
+        hot = one_hot(flat.shape[1], slot_ref[part : part + 1, :])
+        out_ref[part] = dot(flat[...], hot, NN).T.astype(BF16)
 
 
 def spread_neg(back, slot, cap, feature):
     devices = back.shape[0]
     parts, width = slot.shape
-    full = round_up(feature, LANES)
-    height = cap * full // LANES
+    height = packed_height(cap, feature)
     return call(
         functools.partial(spread_neg_kernel, cap=cap),
         "spread_negatives",
-        2 * devices * cap * full * slot.size,
-        2 * devices * cap * full,
+        2 * devices * cap * feature * slot.size,
+        2 * devices * cap * feature,
         grid=(1,),
         in_specs=[
             pl.BlockSpec((devices, height, LANES), lambda i: (0, 0, 0)),
@@ -261,23 +284,21 @@
         ],
         out_specs=pl.BlockSpec((parts, width, feature), lambda i: (0, 0, 0)),
         out_shape=jax.ShapeDtypeStruct((parts, width, feature), BF16),
-        scratch_shapes=[pltpu.VMEM((devices * cap, full), BF16)],
+        scratch_shapes=unpack_scratch(devices, cap, feature),
     )(back, slot)
 
 
 def spread_kernel(*refs, first, pooled):
     back_ref, slot_ref = refs[:2]
     so_far_ref = None if first else refs[2]
-    out_ref, flat = refs[2 + (not first) :][:2]
+    out_ref, flat = refs[2 + (not first)], refs[-1]
     devices = back_ref.shape[0]
     feature = flat.shape[0]
 
     @pl.when(pl.program_id(0) == 0)
     def _():
         if pooled:
-            for d in range(devices):
-                unpack(back_ref, d, 0, POOL, refs[-1], d * POOL)
-            flat[...] = refs[-1][...].astype(F32).T[:feature].astype(BF16)
+            unpack_all(back_ref, 0, POOL, refs[-2], flat)
         else:
             start = back_ref.shape[1] - feature
             for d in range(devices):
@@ -298,9 +319,10 @@
     steps = width // tile
     rows_spec = pl.BlockSpec((feature, tile), lambda i: (0, i))
     extra = [] if so_far is None else [so_far]
-    scratch = [pltpu.VMEM((feature, slots), BF16)]
     if pooled:
-        scratch.append(pltpu.VMEM((slots, round_up(feature, LANES)), BF16))
+        scratch = unpack_scratch(devices, POOL, feature)
+    else:
+        scratch = [pltpu.VMEM((feature, slots), BF16)]
     return call(
         functools.partial(spread_kernel, first=so_far is None, pooled=pooled),
         "spread_pool" if pooled else "spread_rows",
@@ -421,7 +443,7 @@
     feature = src_grad.shape[0]
     group = 4
     slots = devices * LANES
-    height = feature + neg_cap * (round_up(feature, LANES) // LANES)
+    height = feature + (packed_height(neg_cap, feature) if neg_cap else 0)
     whole = pl.BlockSpec(src_grad.shape, lambda i: (0, 0))
     return call(
         functools.partial(collect_kernel, group=group),
@@ -450,15 +472,14 @@
     for part in range(slot_ref.shape[0]):
         hot = one_hot(group * cap, slot_ref[part : part + 1, :], step * group * cap)
         rows = rows + dot(hot, sums[part], NN)
-    for i in range(group):
-        pack(out_ref, i, 0, rows[i * cap : (i + 1) * cap])
+    pack_all(out_ref, 0, cap, rows, rows.T)
 
 
 def collect_neg(sent, slot, grads, cap):
     devices = sent.shape[0]
     feature = grads[0].shape[-1]
     group = 16
-    height = cap * (round_up(feature, LANES) // LANES)
+    height = packed_height(cap, feature)
     return call(
         functools.partial(collect_neg_kernel, group=group, cap=cap),
         "collect_negatives",
@@ -486,15 +507,14 @@
         start = segment % (segments // 2) * width
         hot = one_hot(count, slot_ref[segment : segment + 1, :], pl.program_id(0) * count)
         rows = rows + dot(hot, grads[:, start : start + width], NT)
-    for i in range(group):
-        pack(out_ref, i, 0, rows[i * POOL : (i + 1) * POOL])
+    pack_all(out_ref, 0, POOL, rows, rows.T)
 
 
 def collect_pool(src_grad, dst_grad, slot, devices):
     feature = src_grad.shape[0]
     group = 8
     slots = devices * POOL
-    height = POOL * (round_up(feature, LANES) // LANES)
+    height = packed_height(POOL, feature)
     whole = pl.BlockSpec(src_grad.shape, lambda i: (0, 0))
     return call(
         functools.partial(collect_pool_kernel, group=group),
@@ -528,9 +548,7 @@
         for d in range(devices):
             flat[:, d * LANES : (d + 1) * LANES] = recv_ref[d, start:]
         if neg_cap:
-            for d in range(devices):
-                unpack(recv_ref, d, 0, neg_cap, neg_rows, d * neg_cap)
-            neg_flat[...] = neg_rows[...].astype(F32).T[:feature].astype(BF16)
+            unpack_all(recv_ref, 0, neg_cap, neg_rows, neg_flat)
 
     base = step * rows
     row = jnp.concatenate([req_ref[d : d + 1, :] for d in range(devices)], axis=1)
@@ -547,7 +565,6 @@
     devices = recv.shape[0]
     rows = 512 if devices * LANES <= 4096 else 128
     slots = devices * LANES
-    full = round_up(feature, LANES)
     whole_req = pl.BlockSpec((devices, LANES), lambda i: (0, 0))
     rows_spec = pl.BlockSpec((feature, rows), lambda i: (0, i))
     operands = [recv, requests]
@@ -556,10 +573,7 @@
     if neg_cap:
         operands.append(neg_requests)
         specs.append(whole_req)
-        scratch += [
-            pltpu.VMEM((devices * neg_cap, full), BF16),
-            pltpu.VMEM((feature, devices * neg_cap), BF16),
-        ]
+        scratch += unpack_scratch(devices, neg_cap, feature)
     if so_far is not None:
         operands.append(so_far)
         specs.append(rows_spec)
@@ -576,52 +590,36 @@
     )(*operands)
 
 
-def add_pool_kernel(*refs, rows, relays):
-    recv_refs = refs[:relays]
-    req_ref = refs[relays]
-    so_far_ref = refs[relays + 1] if len(refs) == relays + 5 else None
-    out_ref, packed, flat = refs[-3:]
-    feature = flat.shape[0]
-    count = packed.shape[0]
+def add_pool_kernel(near_ref, far_ref, near_req_ref, far_req_ref, out_ref, packed, *flats, rows):
     step = pl.program_id(0)
 
     @pl.when(step == 0)
     def _():
-        for relay in range(relays):
-            for d in range(count // POOL):
-                unpack(recv_refs[relay], d, 0, POOL, packed, d * POOL)
-            flat[:, relay * count : (relay + 1) * count] = (
-                packed[...].astype(F32).T[:feature].astype(BF16)
-            )
-
-    total = dot(flat[...], one_hot(rows, req_ref[...], step * rows), NT)
-    if so_far_ref is not None:
-        total = total + so_far_ref[...]
-    out_ref[...] = total
-
-
-def add_pool(recv, requests, so_far, feature, rows_dev):
+        for recv_ref, flat in zip((near_ref, far_ref), flats):
+            unpack_all(recv_ref, 0, POOL, packed, flat)
+
+    total = dot(flats[0][...], one_hot(rows, near_req_ref[...], step * rows), NT)
+    out_ref[...] = total + dot(flats[1][...], one_hot(rows, far_req_ref[...], step * rows), NT)
+
+
+def add_pool(near, far, requests, feature, rows_dev):
     rows = 512
-    devices, height, _ = recv[0].shape
-    slots = len(recv) * devices * POOL
-    rows_spec = pl.BlockSpec((feature, rows), lambda i: (0, i))
-    extra = [] if so_far is None else [so_far]
-    return call(
-        functools.partial(add_pool_kernel, rows=rows, relays=len(recv)),
+    devices = near.shape[0]
+    slots = devices * POOL
+    recv_spec = pl.BlockSpec(near.shape, lambda i: (0, 0, 0))
+    req_spec = pl.BlockSpec((1, slots), lambda i: (0, 0))
+    packed, flat = unpack_scratch(devices, POOL, feature)
+    return call(
+        functools.partial(add_pool_kernel, rows=rows),
         "add_pool",
-        2 * feature * slots * rows_dev,
-        2 * feature * slots + 4 * feature * rows_dev,
+        4 * feature * slots * rows_dev,
+        4 * feature * slots + 4 * feature * rows_dev,
         grid=(rows_dev // rows,),
-        in_specs=[pl.BlockSpec(recv[0].shape, lambda i: (0, 0, 0))] * len(recv)
-        + [pl.BlockSpec((1, slots), lambda i: (0, 0))]
-        + [rows_spec] * len(extra),
-        out_specs=rows_spec,
+        in_specs=[recv_spec, recv_spec, req_spec, req_spec],
+        out_specs=pl.BlockSpec((feature, rows), lambda i: (0, i)),
         out_shape=jax.ShapeDtypeStruct((feature, rows_dev), F32),
-        scratch_shapes=[
-            pltpu.VMEM((devices * POOL, round_up(feature, LANES)), BF16),
-            pltpu.VMEM((feature, slots), BF16),
-        ],
-    )(*recv, requests.reshape(1, slots), *extra)
+        scratch_shapes=[packed, flat, flat],
+    )(near, far, requests[0][None], requests[1][None])
 
 
 def exchange(value):
@@ -671,7 +669,6 @@
         pad_lanes(own_ids, part, -1),
         rows_dev,
         devices,
-        sharers,
         chunks,
         neg_cap,
     )
@@ -705,29 +702,23 @@
 
     def pooled():
         start = chunks * LANES
-        listed = asked[:, start : start + sharers * POOL].reshape(devices, sharers, POOL)
-        listed = listed.transpose(1, 0, 2).reshape(sharers, devices * POOL) - me * rows_dev
-        listed = listed[me ^ jnp.arange(sharers, dtype=jnp.int32)]
+        core = me % RELAYS
+        listed = asked[:, start : start + RELAYS * POOL].reshape(devices, RELAYS, POOL)
+        listed = listed.transpose(1, 0, 2).reshape(RELAYS, devices * POOL) - core * rows_dev
+        listed = [jnp.where(core == k, listed[0], listed[1]) for k in range(RELAYS)]
         back = exchange(gather(table, direct[0], neg_asked, neg_cap))
-        far = gather_pool(table, listed[2], devices) + swap(
-            gather_pool(table, listed[3], devices), 1
-        )
-        far = swap(far, 2)
-        near = gather_pool(table, listed[0], devices) + swap(
-            gather_pool(table, listed[1], devices), 1
-        )
+        far = swap(gather_pool(table, listed[1], devices), 1)
+        relayed = gather_pool(table, listed[0], devices) + far
         negatives = negatives_of(back)
         rows = spread(back, slots[0], None, feature)
-        rows = spread(exchange(near + far), slots[chunks], rows, feature, True)
+        rows = spread(exchange(relayed), slots[chunks], rows, feature, True)
         src_grad, dst_grad, neg_grads = edges(rows, rel_rows, relations, negatives)
         near = exchange(collect_pool(src_grad, dst_grad, slots[chunks], devices))
-        far = swap(near, 2)
         sent = direct_sent(src_grad, dst_grad, neg_grads)
-        grad = add_pool([near, swap(near, 1)], listed[:2], None, feature, rows_dev)
-        grad = add_pool([far, swap(far, 1)], listed[2:], grad, feature, rows_dev)
+        grad = add_pool(near, swap(near, 1), listed, feature, rows_dev)
         return add_rows(sent, direct[0], grad, feature, rows_dev, neg_asked, neg_cap)
 
-    if chunks == 1 or sharers != 4:
+    if chunks == 1 or sharers % RELAYS:
         return chunked().T
     fits = jnp.max(neg_asked[:, -1]) < 0
     return lax.cond(fits, pooled, chunked).T

time: 438 us -> 435 us (level)
  the two profiles are of different devices: /device:TPU:17 before, /device:TPU:0 now
where the time goes in v4:
time: 435 us; the launch traced here: 429 us
  Pallas kernels  186 us (43%)
  waiting for transfers between devices  184 us (42%)
  starting transfers between devices  28.8 us (7%)
  local copies, waits for them, and re-layouts  14.5 us (3%)
  other arithmetic  8.52 us (2%)
  loops' own time  6.63 us (2%)
    all_to_all x5, waiting for transfers between devices, exchange(): lax.all_to_all(value, ('shard', 'grp'), split_axis=0, concat_axis=0, tile...  154 us
    pallas_call x2, Pallas kernels, spread(): call(functools.partial(spread_kernel, first=so_far is None, pooled=pooled...  32.6 us
    ppermute x8, waiting for transfers between devices, swap(): return lax.ppermute(value, 'grp', [(i, i ^ bit) for i in range(sharers)])  29.9 us
    pallas_call x2, Pallas kernels, gather_pool(): call(functools.partial(gather_pool_kernel, group=group), 'gather_pool', 2...  25.7 us
    all_to_all x5, starting transfers between devices, exchange(): lax.all_to_all(value, ('shard', 'grp'), split_axis=0, concat_axis=0, tile...  24.2 us
    pallas_call x1, Pallas kernels, add_rows(): call(functools.partial(add_kernel, rows=rows, neg_cap=neg_cap, first=so_f...  23.9 us
    pallas_call x1, Pallas kernels, gather(): call(functools.partial(gather_kernel, group=group, neg_cap=neg_cap), 'gat...  23.6 us
    pallas_call x1, Pallas kernels, add_pool(): call(functools.partial(add_pool_kernel, rows=rows), 'add_pool', 4 * featu...  23.4 us
  transfers between devices with their start and end apart: 13, of which 7 were waited for; matrix products, arithmetic and copies ran while one was open for 3% of the time, Pallas kernels for 25%

profile of v4, /device:TPU:0, one launch (start us, length us, event | category | flops | bytes accessed | tf_op | source)
XLA Modules:
  0.0 428.8 jit_solution(15826571276709641108)
XLA Ops:
  0.0 0.8 reshape.87
  0.8 0.8 reshape.88
  1.6 0.1 constant_dynamic-slice_fusion
  1.6 0.6 pad.13.own_ref
  2.3 0.6 pad.12.ends_ref
  2.9 3.6 slots.1
  6.5 1.6 copy.12
  8.1 7.3 %all-to-all-start.8 = ((s32[32,1,640]{2,1,0:T(1,128)}), s32[32,1,640]{2,1,0:T(1,128)S(1)}, u32[]{:S(2)}, u32[]{:S(2)}) async-start(s32[32,1,640]{2,1,0:T(1,128)} %copy.12), calls=%async_computation.8 | async-start | bytes 163840 | tf_op jit(solution)/shard_map/all_to_all | solution.py:626
  15.4 0.0 copy-start.22
  15.4 3.3 convert_bitcast_fusion
  18.8 0.1 reshape.89
  18.9 1.7 copy.13
  20.6 2.4 all-to-all-done.8
  23.0 0.7 slice_reduce_fusion
  24.4 403.3 %conditional.1 = (f32[400,4096]{1,0:T(8,128)}) conditional(s32[]{:T(128)} %convert_element_type.9, (s32[32,640]{1,0:T(8,128)S(1)}, bf16[400,4096]{1,0:T(8,128)(2,1)S(1)}, s32[4,1024]{1,0:T(4,128)S(1)}, s32[32,128]{1,0:T(8,128)S(1)}, s32[32,128]{1,0:T(8,128)S(1)}, /*index=5*/s32[4,1024]{1,0:T(4,128)S(1)}, s32[2,1024]{1,0:T(2,128)S(1)}, ...), branch_computations={%region_1.2_spmd, %region_2.3_spmd} | conditional | flops 116601651200 | bytes 180995008 | solution.py:724
  30.7 23.6 %gather_rows.5 = bf16[32,512,128]{2,1,0:T(8,128)(2,1)} custom-call(bf16[400,4096]{1,0:T(8,128)(2,1)S(1)} %get-tuple-element.62.table_ref, s32[32,128]{1,0:T(8,128)S(1)} %get-tuple-element.66.refs_0_.refs_1_, s32[32,128]{1,0:T(8,128)S(1)} %get-tuple-element.67.refs_1_.refs_2_), custom_call_target="tpu_custom_call" | custom-call | flops 16777216000 | bytes 7372800 | tf_op jit(solution)/shard_map/cond/branch_1_fun/gather_rows/pallas_call | solution.py:224
  54.3 3.6 all-to-all-start.5
  57.9 0.1 sub.11
  58.0 0.7 select_n.50.req_ref
  58.7 12.9 %gather_pool.3 = bf16[32,256,128]{2,1,0:T(8,128)(2,1)} custom-call(bf16[400,4096]{1,0:T(8,128)(2,1)S(1)} %get-tuple-element.62.table_ref, s32[4,1,640]{2,1,0:T(1,128)} %select_n.50.req_ref), custom_call_target="tpu_custom_call" | custom-call | flops 8388608000 | bytes 5324800 | tf_op jit(solution)/shard_map/cond/branch_1_fun/gather_pool/pallas_call | solution.py:249
  71.5 0.1 collective-permute-start.6
  71.7 0.7 select_n.47.req_ref
  72.4 12.8 %gather_pool.2 = bf16[32,256,128]{2,1,0:T(8,128)(2,1)} custom-call(bf16[400,4096]{1,0:T(8,128)(2,1)S(1)} %get-tuple-element.62.table_ref, s32[4,1,640]{2,1,0:T(1,128)} %select_n.47.req_ref), custom_call_target="tpu_custom_call" | custom-call | flops 8388608000 | bytes 5324800 | tf_op jit(solution)/shard_map/cond/branch_1_fun/gather_pool/pallas_call | solution.py:249
  85.2 0.0 collective-permute-done.6
  85.2 4.5 %add.8 = bf16[32,256,128]{2,1,0:T(8,128)(2,1)} add(bf16[32,256,128]{2,1,0:T(8,128)(2,1)} %gather_pool.2, bf16[32,256,128]{2,1,0:T(8,128)(2,1)} %collective-permute-done.6) | non-fusion elementwise | flops 1048576 | bytes 6291456 | tf_op jit(solution)/shard_map/cond/branch_1_fun/add | solution.py:711
  89.6 62.1 %all-to-all-done.5.refs_0_.back_ref = bf16[32,512,128]{2,1,0:T(8,128)(2,1)} async-done(((bf16[32,512,128]{2,1,0:T(8,128)(2,1)}), bf16[32,512,128]{2,1,0:T(8,128)(2,1)}, u32[]{:S(2)}, u32[]{:S(2)}) %all-to-all-start.5) | async-done | bytes 4194336 | tf_op jit(solution)/shard_map/cond/branch_1_fun/all_to_all | solution.py:626
  151.7 4.1 all-to-all-start.4
  155.8 0.6 reshape.83.refs_2_
  156.4 0.6 reshape.81.refs_1_
  157.0 0.6 reshape.82.refs_1_
  157.7 2.9 spread_negatives.3.refs_4_
  160.5 1.6 collective-permute-start.9
  162.2 0.4 collective-permute-start.8
  162.5 0.0 collective-permute-start.7
  162.5 19.3 %spread_rows.5.refs_2_ = bf16[400,4096]{1,0:T(8,128)(2,1)} custom-call(bf16[32,512,128]{2,1,0:T(8,128)(2,1)} %all-to-all-done.5.refs_0_.back_ref, s32[4,1,1024]{2,1,0:T(1,128)} %reshape.82.refs_1_), custom_call_target="tpu_custom_call" | custom-call | flops 13421772800 | bytes 6553600 | tf_op jit(solution)/shard_map/cond/branch_1_fun/spread_rows/pallas_call | solution.py:326
  181.8 23.1 %all-to-all-done.4.refs_0_ = bf16[32,256,128]{2,1,0:T(8,128)(2,1)S(1)} async-done(((bf16[32,256,128]{2,1,0:T(8,128)(2,1)}), bf16[32,256,128]{2,1,0:T(8,128)(2,1)S(1)}, u32[]{:S(2)}, u32[]{:S(2)}) %all-to-all-start.4) | async-done | bytes 2097184 | tf_op jit(solution)/shard_map/cond/branch_1_fun/all_to_all | solution.py:626
  204.9 1.3 copy-done.5
  206.2 13.3 %spread_pool.1.refs_0_.refs_1_ = bf16[400,4096]{1,0:T(8,128)(2,1)} custom-call(bf16[32,256,128]{2,1,0:T(8,128)(2,1)} %copy-done.5, s32[4,1,1024]{2,1,0:T(1,128)} %reshape.81.refs_1_, bf16[400,4096]{1,0:T(8,128)(2,1)} %spread_rows.5.refs_2_), custom_call_target="tpu_custom_call" | custom-call | flops 8388608000 | bytes 5324800 | tf_op jit(solution)/shard_map/cond/branch_1_fun/spread_pool/pallas_call | solution.py:326
  219.5 0.0 collective-permute-done.9.refs_7_
  219.6 0.0 collective-permute-done.8.refs_6_
  219.6 0.0 collective-permute-done.7.refs_5_
  219.6 0.8 copy-done.23
  220.3 13.5 %edges.3 = (bf16[400,2048]{1,0:T(8,128)(2,1)}, bf16[400,2048]{1,0:T(8,128)(2,1)}, bf16[2,256,400]{2,1,0:T(8,128)(2,1)}, bf16[2,256,400]{2,1,0:T(8,128)(2,1)}, bf...) custom-call(bf16[400,4096]{1,0:T(8,128)(2,1)} %spread_pool.1.refs_0_.refs_1_, ...), custom_call_target="tpu_custom_call" | custom-call | flops 5033164800 | bytes 9830400 | tf_op jit(solution)/shard_map/cond/branch_1_fun/edges/pallas_call | solution.py:401
  233.9 14.7 %collect_pool.1 = bf16[32,256,128]{2,1,0:T(8,128)(2,1)} custom-call(bf16[400,2048]{1,0:T(8,128)(2,1)} %get-tuple-element.72.src_ref, bf16[400,2048]{1,0:T(8,128)(2,1)} %get-tuple-element.73.dst_ref, s32[4,1024]{1,0:T(4,128)S(1)} %get-tuple-element.65.slot_ref), custom_call_target="tpu_custom_call" | custom-call | flops 8388608000 | bytes 5324800 | tf_op jit(solution)/shard_map/cond/branch_1_fun/collect_pool/pallas_call | solution.py:519
  248.6 3.9 all-to-all-start.7
  252.5 0.3 collective-permute-start.10
  252.8 1.7 collective-permute-start.11
  254.5 0.0 collective-permute-start.12
  254.5 17.9 %collect_grads.5.sent_ref = bf16[32,512,128]{2,1,0:T(8,128)(2,1)} custom-call(bf16[400,2048]{1,0:T(8,128)(2,1)} %get-tuple-element.72.src_ref, bf16[400,2048]{1,0:T(8,128)(2,1)} %get-tuple-element.73.dst_ref, s32[4,1024]{1,0:T(4,128)S(1)} %get-tuple-element.68.slot_ref), custom_call_target="tpu_custom_call" | custom-call | flops 13421772800 | bytes 6553600 | tf_op jit(solution)/shard_map/cond/branch_1_fun/collect_grads/pallas_call | solution.py:448
  272.5 0.0 collective-permute-done.10.refs_1_
  272.5 14.3 %collective-permute-done.11.refs_2_ = bf16[2,256,400]{2,1,0:T(8,128)(2,1)S(1)} collective-permute-done((bf16[2,256,400]{2,1,0:T(8,128)(2,1)S(1)}, bf16[2,256,400]{2,1,0:T(8,128)(2,1)S(1)}, u32[]{:S(2)}, u32[]{:S(2)}) %collective-permute-start.11) | collective-permute-done | bytes 409632 | tf_op jit(solution)/shard_map/cond/branch_1_fun/ppermute | solution.py:631
  286.7 13.1 %collective-permute-done.12.refs_3_ = bf16[2,256,400]{2,1,0:T(8,128)(2,1)S(1)} collective-permute-done((bf16[2,256,400]{2,1,0:T(8,128)(2,1)S(1)}, bf16[2,256,400]{2,1,0:T(8,128)(2,1)S(1)}, u32[]{:S(2)}, u32[]{:S(2)}) %collective-permute-start.12) | collective-permute-done | bytes 409632 | tf_op jit(solution)/shard_map/cond/branch_1_fun/ppermute | solution.py:631
  299.8 0.8 copy-done.11
  300.6 3.7 collect_negatives.3
  304.3 5.3 %all-to-all-start.6 = ((bf16[32,512,128]{2,1,0:T(8,128)(2,1)}), bf16[32,512,128]{2,1,0:T(8,128)(2,1)}, u32[]{:S(2)}, u32[]{:S(2)}) async-start(bf16[32,512,128]{2,1,0:T(8,128)(2,1)} %collect_negatives.3), calls=%async_computation.6 | async-start | bytes 8388608 | tf_op jit(solution)/shard_map/cond/branch_1_fun/all_to_all | solution.py:626
  309.7 0.4 collective-permute-start.13
  310.1 0.7 select_n.52.far_req_ref
  310.8 0.7 select_n.51.near_req_ref
  311.5 2.6 collective-permute-done.13.far_ref
  314.1 23.4 %add_pool.1.refs_3_ = f32[400,4096]{1,0:T(8,128)} custom-call(bf16[32,256,128]{2,1,0:T(8,128)(2,1)} %copy-done.4, bf16[32,256,128]{2,1,0:T(8,128)(2,1)} %collective-permute-done.13.far_ref, s32[1,2560]{1,0:T(1,128)} %select_n.51.near_req_ref, s32[1,2560]{1,0:T(1,128)} %select_n.52.far_req_ref), custom_call_target="tpu_custom_call" | custom-call | flops 16777216000 | bytes 10649600 | tf_op jit(solution)/shard_map/cond/branch_1_fun/add_pool/pallas_call | solution.py:612
  337.5 66.1 %all-to-all-done.6.refs_0_ = bf16[32,512,128]{2,1,0:T(8,128)(2,1)} async-done(((bf16[32,512,128]{2,1,0:T(8,128)(2,1)}), bf16[32,512,128]{2,1,0:T(8,128)(2,1)}, u32[]{:S(2)}, u32[]{:S(2)}) %all-to-all-start.6) | async-done | bytes 4194336 | tf_op jit(solution)/shard_map/cond/branch_1_fun/all_to_all | solution.py:626
  403.6 23.9 %add_grads.5 = f32[400,4096]{1,0:T(8,128)} custom-call(bf16[32,512,128]{2,1,0:T(8,128)(2,1)} %all-to-all-done.6.refs_0_, s32[32,128]{1,0:T(8,128)S(1)} %copy-done.21, s32[32,128]{1,0:T(8,128)S(1)} %copy-done.17, f32[400,4096]{1,0:T(8,128)} %add_pool.1.refs_3_), custom_call_target="tpu_custom_call" | custom-call | flops 13421772800 | bytes 16384000 | tf_op jit(solution)/shard_map/cond/branch_1_fun/add_grads/pallas_call | solution.py:580
  427.7 0.0 copy-start.1
  427.7 0.7 copy-done.1
  (34 shorter events, 0.1 us)
Async XLA Ops:
  0.0 1.6 copy-start
  8.1 14.9 %all-to-all-start.8 = ((s32[32,1,640]{2,1,0:T(1,128)}), s32[32,1,640]{2,1,0:T(1,128)S(1)}, u32[]{:S(2)}, u32[]{:S(2)}) async-start(s32[32,1,640]{2,1,0:T(1,128)} %copy.12), calls=%async_computation.8 | async-start | bytes 163840 | tf_op jit(solution)/shard_map/all_to_all | solution.py:626
  15.4 3.3 copy-start.22
  30.6 23.6 %copy-start.16 = (s32[32,128]{1,0:T(8,128)}, s32[32,128]{1,0:T(8,128)S(1)}, u32[]{:S(2)}) copy-start(s32[32,128]{1,0:T(8,128)S(1)} %get-tuple-element.67.refs_1_.refs_2_) | copy-start | bytes 49156 | tf_op jit(solution)/shard_map/cond
  30.6 23.6 %copy-start.20 = (s32[32,128]{1,0:T(8,128)}, s32[32,128]{1,0:T(8,128)S(1)}, u32[]{:S(2)}) copy-start(s32[32,128]{1,0:T(8,128)S(1)} %get-tuple-element.66.refs_0_.refs_1_) | copy-start | bytes 49156 | tf_op jit(solution)/shard_map/cond
  54.3 97.4 %all-to-all-start.5 = ((bf16[32,512,128]{2,1,0:T(8,128)(2,1)}), bf16[32,512,128]{2,1,0:T(8,128)(2,1)}, u32[]{:S(2)}, u32[]{:S(2)}) async-start(bf16[32,512,128]{2,1,0:T(8,128)(2,1)} %gather_rows.5), calls=%async_computation.5 | async-start | bytes 8388608 | tf_op jit(solution)/shard_map/cond/branch_1_fun/all_to_all | solution.py:626
  71.5 13.6 %collective-permute-start.6 = (bf16[32,256,128]{2,1,0:T(8,128)(2,1)}, bf16[32,256,128]{2,1,0:T(8,128)(2,1)}, u32[]{:S(2)}, u32[]{:S(2)}) collective-permute-start(bf16[32,256,128]{2,1,0:T(8,128)(2,1)} %gather_pool.3), channel_id=1, source_target_pairs={{0,1},{1,0},{2,3},{3,2},{4,5},{5,4},{6,7},{7,6},{8,9},{9,8},{10,11... | collective-permute-start | bytes 6291464 | tf_op jit(solution)/shard_map/cond/branch_1_fun/ppermute | solution.py:631
  151.7 53.2 %all-to-all-start.4 = ((bf16[32,256,128]{2,1,0:T(8,128)(2,1)}), bf16[32,256,128]{2,1,0:T(8,128)(2,1)S(1)}, u32[]{:S(2)}, u32[]{:S(2)}) async-start(bf16[32,256,128]{2,1,0:T(8,128)(2,1)} %add.8), calls=%async_computation.4 | async-start | bytes 4194304 | tf_op jit(solution)/shard_map/cond/branch_1_fun/all_to_all | solution.py:626
  160.5 59.0 %collective-permute-start.9 = (bf16[2,256,400]{2,1,0:T(8,128)(2,1)}, bf16[2,256,400]{2,1,0:T(8,128)(2,1)S(1)}, u32[]{:S(2)}, u32[]{:S(2)}) collective-permute-start(bf16[2,256,400]{2,1,0:T(8,128)(2,1)} %spread_negatives.3.refs_4_), channel_id=1, source_target_pairs={{0,3},{1,2},{2,1},{3,0},{4,7},{5,6},{6,5},{7,4},{8,11},{9,10},{10,... | collective-permute-start | bytes 1228808 | tf_op jit(solution)/shard_map/cond/branch_1_fun/ppermute | solution.py:631
  162.2 57.4 %collective-permute-start.8 = (bf16[2,256,400]{2,1,0:T(8,128)(2,1)}, bf16[2,256,400]{2,1,0:T(8,128)(2,1)}, u32[]{:S(2)}, u32[]{:S(2)}) collective-permute-start(bf16[2,256,400]{2,1,0:T(8,128)(2,1)} %spread_negatives.3.refs_4_), channel_id=1, source_target_pairs={{0,2},{1,3},{2,0},{3,1},{4,6},{5,7},{6,4},{7,5},{8,10},{9,11},{10,... | collective-permute-start | bytes 1228808 | tf_op jit(solution)/shard_map/cond/branch_1_fun/ppermute | solution.py:631
  162.5 57.0 %collective-permute-start.7 = (bf16[2,256,400]{2,1,0:T(8,128)(2,1)}, bf16[2,256,400]{2,1,0:T(8,128)(2,1)}, u32[]{:S(2)}, u32[]{:S(2)}) collective-permute-start(bf16[2,256,400]{2,1,0:T(8,128)(2,1)} %spread_negatives.3.refs_4_), channel_id=1, source_target_pairs={{0,1},{1,0},{2,3},{3,2},{4,5},{5,4},{6,7},{7,6},{8,9},{9,8},{10,11... | collective-permute-start | bytes 1228808 | tf_op jit(solution)/shard_map/cond/branch_1_fun/ppermute | solution.py:631
  181.8 38.5 %copy-start.13 = (f32[400,64]{1,0:T(8,128)S(1)}, f32[400,64]{1,0:T(8,128)}, u32[]{:S(2)}) copy-start(f32[400,64]{1,0:T(8,128)} %get-tuple-element.70.refs_3_) | copy-start | bytes 307204 | tf_op jit(solution)/shard_map/cond
  204.9 1.3 copy-start.5
  219.5 0.8 copy-start.23
  248.6 4.2 copy-start.25
  248.6 5.9 %copy-start.24 = (bf16[2,256,400]{2,1,0:T(8,128)(2,1)S(1)}, bf16[2,256,400]{2,1,0:T(8,128)(2,1)}, u32[]{:S(2)}) copy-start(bf16[2,256,400]{2,1,0:T(8,128)(2,1)} %get-tuple-element.77) | copy-start | bytes 1228804 | tf_op jit(solution)/shard_map/cond
  248.6 55.7 %all-to-all-start.7 = ((bf16[32,256,128]{2,1,0:T(8,128)(2,1)}), bf16[32,256,128]{2,1,0:T(8,128)(2,1)S(1)}, u32[]{:S(2)}, u32[]{:S(2)}) async-start(bf16[32,256,128]{2,1,0:T(8,128)(2,1)} %collect_pool.1), calls=%async_computation.7 | async-start | bytes 4194304 | tf_op jit(solution)/shard_map/cond/branch_1_fun/all_to_all | solution.py:626
  252.5 20.0 %collective-permute-start.10 = (bf16[2,256,400]{2,1,0:T(8,128)(2,1)}, bf16[2,256,400]{2,1,0:T(8,128)(2,1)S(1)}, u32[]{:S(2)}, u32[]{:S(2)}) collective-permute-start(bf16[2,256,400]{2,1,0:T(8,128)(2,1)} %get-tuple-element.75), channel_id=1, source_target_pairs={{0,1},{1,0},{2,3},{3,2},{4,5},{5,4},{6,7},{7,6},{8,9},{9,8},{10,11... | collective-permute-start | bytes 1228808 | tf_op jit(solution)/shard_map/cond/branch_1_fun/ppermute | solution.py:631
  252.8 33.9 %collective-permute-start.11 = (bf16[2,256,400]{2,1,0:T(8,128)(2,1)S(1)}, bf16[2,256,400]{2,1,0:T(8,128)(2,1)S(1)}, u32[]{:S(2)}, u32[]{:S(2)}) collective-permute-start(bf16[2,256,400]{2,1,0:T(8,128)(2,1)S(1)} %copy-done.25), channel_id=1, source_target_pairs={{0,2},{1,3},{2,0},{3,1},{4,6},{5,7},{6,4},{7,5},{8,10},{9,11},{10,... | collective-permute-start | bytes 1228808 | tf_op jit(solution)/shard_map/cond/branch_1_fun/ppermute | solution.py:631
  254.5 45.3 %collective-permute-start.12 = (bf16[2,256,400]{2,1,0:T(8,128)(2,1)S(1)}, bf16[2,256,400]{2,1,0:T(8,128)(2,1)S(1)}, u32[]{:S(2)}, u32[]{:S(2)}) collective-permute-start(bf16[2,256,400]{2,1,0:T(8,128)(2,1)S(1)} %copy-done.24), channel_id=1, source_target_pairs={{0,3},{1,2},{2,1},{3,0},{4,7},{5,6},{6,5},{7,4},{8,11},{9,10},{10,... | collective-permute-start | bytes 1228808 | tf_op jit(solution)/shard_map/cond/branch_1_fun/ppermute | solution.py:631
  272.5 27.4 %copy-start.7 = (bf16[2,256,400]{2,1,0:T(8,128)(2,1)}, bf16[2,256,400]{2,1,0:T(8,128)(2,1)S(1)}, u32[]{:S(2)}) copy-start(bf16[2,256,400]{2,1,0:T(8,128)(2,1)S(1)} %collective-permute-done.10.refs_1_) | copy-start | bytes 1228804 | tf_op jit(solution)/shard_map/cond
  286.7 13.1 %copy-start.9 = (bf16[2,256,400]{2,1,0:T(8,128)(2,1)}, bf16[2,256,400]{2,1,0:T(8,128)(2,1)S(1)}, u32[]{:S(2)}) copy-start(bf16[2,256,400]{2,1,0:T(8,128)(2,1)S(1)} %collective-permute-done.11.refs_2_) | copy-start | bytes 1228804 | tf_op jit(solution)/shard_map/cond
  299.8 0.8 copy-start.11
  304.3 5.4 %copy-start.4 = (bf16[32,256,128]{2,1,0:T(8,128)(2,1)}, bf16[32,256,128]{2,1,0:T(8,128)(2,1)S(1)}, u32[]{:S(2)}) copy-start(bf16[32,256,128]{2,1,0:T(8,128)(2,1)S(1)} %all-to-all-done.7.near_ref) | copy-start | bytes 6291460 | tf_op jit(solution)/shard_map/cond
  304.3 99.3 %all-to-all-start.6 = ((bf16[32,512,128]{2,1,0:T(8,128)(2,1)}), bf16[32,512,128]{2,1,0:T(8,128)(2,1)}, u32[]{:S(2)}, u32[]{:S(2)}) async-start(bf16[32,512,128]{2,1,0:T(8,128)(2,1)} %collect_negatives.3), calls=%async_computation.6 | async-start | bytes 8388608 | tf_op jit(solution)/shard_map/cond/branch_1_fun/all_to_all | solution.py:626
  309.7 4.4 %collective-permute-start.13 = (bf16[32,256,128]{2,1,0:T(8,128)(2,1)S(1)}, bf16[32,256,128]{2,1,0:T(8,128)(2,1)}, u32[]{:S(2)}, u32[]{:S(2)}) collective-permute-start(bf16[32,256,128]{2,1,0:T(8,128)(2,1)S(1)} %all-to-all-done.7.near_ref), channel_id=1, source_target_pairs={{0,1},{1,0},{2,3},{3,2},{4,5},{5,4},{6,7},{7,6},{8,9},{9,8},{10,11... | collective-permute-start | bytes 6291464 | tf_op jit(solution)/shard_map/cond/branch_1_fun/ppermute | solution.py:631
  311.5 92.1 %copy-start.17 = (s32[32,128]{1,0:T(8,128)S(1)}, s32[32,128]{1,0:T(8,128)}, u32[]{:S(2)}) copy-start(s32[32,128]{1,0:T(8,128)} %copy-done.16) | copy-start | bytes 49156 | tf_op jit(solution)/shard_map/cond
  311.5 92.1 %copy-start.21 = (s32[32,128]{1,0:T(8,128)S(1)}, s32[32,128]{1,0:T(8,128)}, u32[]{:S(2)}) copy-start(s32[32,128]{1,0:T(8,128)} %copy-done.20) | copy-start | bytes 49156 | tf_op jit(solution)/shard_map/cond
  427.7 0.7 copy-start.1

commit v5 on v4

--- a/solution.py
+++ b/solution.py
@@ -64,7 +64,13 @@
     return (LANES * sums[:groups] + sums[groups:]).astype(jnp.int32) - 1
 
 
-def slots_kernel(ends_ref, own_ref, *refs, rows_dev, devices, chunks, neg_cap):
+def slots_kernel(me_ref, ends_ref, own_ref, *refs, rows_dev, devices, chunks, neg_cap):
+    me = me_ref[0, 0]
+
+    def position(device):
+        offset = device ^ me
+        return offset % (devices // 2) * 2 + offset // (devices // 2)
+
     msg_ref = refs[0]
     slot_refs = refs[1 : 1 + chunks]
     pool_ref = refs[1 + chunks] if chunks > 1 else None
@@ -93,7 +99,9 @@
         for at, owner, rank in zip(where, holder, found):
             place = rank - chunk * LANES
             place = jnp.where((owner >= 0) & (place >= 0) & (place < LANES), place, -1)
-            slot_refs[chunk][at] = jnp.where(place >= 0, owner * LANES + place, -1)
+            slot_refs[chunk][at] = jnp.where(
+                place >= 0, position(owner) * LANES + place, -1
+            )
             places.append(place)
         msg_ref[:, chunk * LANES : (chunk + 1) * LANES] = fill(members, codes, places, LANES)
     offset = chunks * LANES
@@ -111,7 +119,8 @@
         places = []
         for at, owner, rank, place in zip(where, holder, found, pooled):
             inside = (owner >= 0) & (rank >= LANES) & (place < room)
-            pool_ref[at] = jnp.where(inside, owner // RELAYS * room + place, -1)
+            relay = owner // RELAYS * RELAYS + place // POOL
+            pool_ref[at] = jnp.where(inside, position(relay) * POOL + place % POOL, -1)
             places.append(jnp.where(inside, place, -1))
         listed = fill(spilled, spill_codes, places, 2 * LANES)
         for chip in range(chips):
@@ -124,14 +133,14 @@
 
     where, holder, codes, members, found = prepare(own_ref)
     for at, owner, rank in zip(where, holder, found):
-        neg_ref[at] = jnp.where(owner >= 0, owner * neg_cap + rank, -1)
+        neg_ref[at] = jnp.where(owner >= 0, position(owner) * neg_cap + rank, -1)
     places = [jnp.where(owner >= 0, rank, -1) for owner, rank in zip(holder, found)]
     listed = fill(members, codes, places, LANES)
     lanes = lax.broadcasted_iota(jnp.int32, listed.shape, 1)
     msg_ref[:, offset:] = jnp.where(lanes == LANES - 1, flag, listed)
 
 
-def make_slots(ends, own, rows_dev, devices, chunks, neg_cap):
+def make_slots(me, ends, own, rows_dev, devices, chunks, neg_cap):
     pooled = chunks > 1
     width = (chunks + 1 + 2 * pooled) * LANES
     return call(
@@ -145,47 +154,55 @@
         "slots",
         16 * devices * LANES * ends.size,
         8 * ends.size,
+        in_specs=[
+            pl.BlockSpec(memory_space=pltpu.SMEM),
+            pl.BlockSpec(ends.shape, lambda: (0, 0)),
+            pl.BlockSpec(own.shape, lambda: (0, 0)),
+        ],
         out_shape=[jax.ShapeDtypeStruct((devices, width), jnp.int32)]
         + [jax.ShapeDtypeStruct(ends.shape, jnp.int32)] * (chunks + pooled)
         + [jax.ShapeDtypeStruct(own.shape, jnp.int32)],
-    )(ends, own)
+    )(me.reshape(1, 1), ends, own)
 
 
 def packed_height(count, feature):
     return feature // LANES * count + feature % LANES
 
 
-def pack(out_ref, at, start, rows, tail):
+def pack(out_ref, start, rows, tail):
     count, feature = rows.shape
     for piece in range(feature // LANES):
-        out_ref[at, start + piece * count : start + (piece + 1) * count, :] = rows[
+        out_ref[start + piece * count : start + (piece + 1) * count, :] = rows[
             :, piece * LANES : (piece + 1) * LANES
         ].astype(out_ref.dtype)
     tail = jnp.concatenate([tail, jnp.zeros((tail.shape[0], LANES - count), tail.dtype)], axis=1)
     end = start + packed_height(count, feature)
-    out_ref[at, end - tail.shape[0] : end, :] = tail.astype(out_ref.dtype)
-
-
-def pack_all(out_ref, start, count, rows, turned):
+    out_ref[end - tail.shape[0] : end, :] = tail.astype(out_ref.dtype)
+
+
+def blocks_of(ref):
+    return [ref.at[i] for i in range(ref.shape[0])]
+
+
+def pack_all(out_refs, start, count, rows, turned):
     feature = rows.shape[1]
     first = feature // LANES * LANES
-    for i in range(out_ref.shape[0]):
+    for i, out_ref in enumerate(out_refs):
         at = slice(i * count, (i + 1) * count)
-        pack(out_ref, i, start, rows[at], turned[first:, at])
-
-
-def unpack_all(in_ref, start, count, rows_ref, flat_ref):
+        pack(out_ref, start, rows[at], turned[first:, at])
+
+
+def unpack_all(in_refs, start, count, rows_ref, flat_ref):
     feature = flat_ref.shape[0]
     pieces = feature // LANES
     end = start + packed_height(count, feature)
-    devices = in_ref.shape[0]
-    for d in range(devices):
+    for d, in_ref in enumerate(in_refs):
         for piece in range(pieces):
             rows_ref[d * count : (d + 1) * count, piece * LANES : (piece + 1) * LANES] = in_ref[
-                d, start + piece * count : start + (piece + 1) * count, :
+                start + piece * count : start + (piece + 1) * count, :
             ]
     tails = [
-        in_ref[d, end - feature % LANES : end, :].astype(F32)[:, :count] for d in range(devices)
+        in_ref[end - feature % LANES : end, :].astype(F32)[:, :count] for in_ref in in_refs
     ]
     flat_ref[: pieces * LANES] = rows_ref[...].astype(F32).T.astype(BF16)
     flat_ref[pieces * LANES :] = jnp.concatenate(tails, axis=1).astype(BF16)
@@ -211,7 +228,7 @@
         out_ref[i, start:] = rows[:, i * LANES : (i + 1) * LANES].astype(BF16)
     if neg_cap:
         neg = rows[:, group * LANES :]
-        pack_all(out_ref, 0, neg_cap, neg.T, neg)
+        pack_all(blocks_of(out_ref), 0, neg_cap, neg.T, neg)
 
 
 def gather(table, requests, neg_requests=None, neg_cap=0):
@@ -238,7 +255,7 @@
     rows_dev = table_ref.shape[1]
     row = req_ref[...].reshape(1, group * POOL)
     rows = dot(table_ref[...], one_hot(rows_dev, row), NN)
-    pack_all(out_ref, 0, POOL, rows.T, rows)
+    pack_all(blocks_of(out_ref), 0, POOL, rows.T, rows)
 
 
 def gather_pool(table, requests, devices):
@@ -262,7 +279,7 @@
 
 
 def spread_neg_kernel(back_ref, slot_ref, out_ref, rows, flat, *, cap):
-    unpack_all(back_ref, 0, cap, rows, flat)
+    unpack_all(blocks_of(back_ref), 0, cap, rows, flat)
     for part in range(slot_ref.shape[0]):
         hot = one_hot(flat.shape[1], slot_ref[part : part + 1, :])
         out_ref[part] = dot(flat[...], hot, NN).T.astype(BF16)
@@ -288,7 +305,7 @@
     )(back, slot)
 
 
-def spread_kernel(*refs, first, pooled):
+def spread_kernel(*refs, first):
     back_ref, slot_ref = refs[:2]
     so_far_ref = None if first else refs[2]
     out_ref, flat = refs[2 + (not first)], refs[-1]
@@ -297,12 +314,9 @@
 
     @pl.when(pl.program_id(0) == 0)
     def _():
-        if pooled:
-            unpack_all(back_ref, 0, POOL, refs[-2], flat)
-        else:
-            start = back_ref.shape[1] - feature
-            for d in range(devices):
-                flat[:, d * LANES : (d + 1) * LANES] = back_ref[d, start:]
+        start = back_ref.shape[1] - feature
+        for d in range(devices):
+            flat[:, d * LANES : (d + 1) * LANES] = back_ref[d, start:]
 
     row = slot_ref[...].reshape(1, slot_ref.shape[-1])
     rows = dot(flat[...], one_hot(flat.shape[1], row), NN)
@@ -311,21 +325,17 @@
     out_ref[...] = rows.astype(BF16)
 
 
-def spread(back, slot, so_far, feature, pooled=False):
+def spread(back, slot, so_far, feature):
     devices = back.shape[0]
     segments, width = slot.shape
-    slots = devices * (POOL if pooled else LANES)
+    slots = devices * LANES
     tile = 512 if slots <= 4096 else 128
     steps = width // tile
     rows_spec = pl.BlockSpec((feature, tile), lambda i: (0, i))
     extra = [] if so_far is None else [so_far]
-    if pooled:
-        scratch = unpack_scratch(devices, POOL, feature)
-    else:
-        scratch = [pltpu.VMEM((feature, slots), BF16)]
-    return call(
-        functools.partial(spread_kernel, first=so_far is None, pooled=pooled),
-        "spread_pool" if pooled else "spread_rows",
+    return call(
+        functools.partial(spread_kernel, first=so_far is None),
+        "spread_rows",
         2 * feature * slots * slot.size,
         2 * feature * (slots + slot.size),
         grid=(segments * steps,),
@@ -336,8 +346,141 @@
         + [rows_spec] * len(extra),
         out_specs=rows_spec,
         out_shape=jax.ShapeDtypeStruct((feature, slot.size), BF16),
+        scratch_shapes=[pltpu.VMEM((feature, slots), BF16)],
+    )(back, slot.reshape(segments, 1, width), *extra)
+
+
+def gather_blocks_kernel(table_ref, req_ref, neg_req_ref, *out_refs, first, neg_cap):
+    feature, rows_dev = table_ref.shape
+    group = len(out_refs)
+    row = [req_ref[first + i : first + i + 1, :] for i in range(group)]
+    row += [neg_req_ref[first + i : first + i + 1, :neg_cap] for i in range(group)]
+    rows = dot(table_ref[...], one_hot(rows_dev, jnp.concatenate(row, axis=1)), NN)
+    for i, out_ref in enumerate(out_refs):
+        out_ref[out_ref.shape[0] - feature :] = rows[:, i * LANES : (i + 1) * LANES].astype(BF16)
+    neg = rows[:, group * LANES :]
+    pack_all(out_refs, 0, neg_cap, neg.T, neg)
+
+
+def gather_blocks(table, requests, neg_requests, first, group, neg_cap):
+    feature, rows_dev = table.shape
+    slots = group * (LANES + neg_cap)
+    block = jax.ShapeDtypeStruct((packed_height(neg_cap, feature) + feature, LANES), BF16)
+    return call(
+        functools.partial(gather_blocks_kernel, first=first, neg_cap=neg_cap),
+        "gather_blocks",
+        2 * feature * rows_dev * slots,
+        2 * feature * (rows_dev + slots),
+        out_shape=[block] * group,
+    )(table, requests, neg_requests)
+
+
+def relay_blocks_kernel(table_ref, req_ref, far_ref, *out_refs):
+    row = req_ref[...].reshape(1, req_ref.shape[-1])
+    rows = dot(table_ref[...], one_hot(table_ref.shape[1], row), NN)
+    pack_all(out_refs, 0, POOL, rows.T, rows)
+    for i, out_ref in enumerate(out_refs):
+        out_ref[...] = out_ref[...] + far_ref[i]
+
+
+def relay_blocks(table, requests, far, first, group):
+    feature, rows_dev = table.shape
+    devices, height, _ = far.shape
+    step = first // group
+    slots = group * POOL
+    return call(
+        relay_blocks_kernel,
+        "relay_blocks",
+        2 * feature * rows_dev * slots,
+        2 * feature * (rows_dev + 2 * slots),
+        grid=(1,),
+        in_specs=[
+            pl.BlockSpec((feature, rows_dev), lambda i: (0, 0)),
+            pl.BlockSpec((1, 1, slots), lambda i: (step, 0, 0)),
+            pl.BlockSpec((group, height, LANES), lambda i: (step, 0, 0)),
+        ],
+        out_specs=[pl.BlockSpec((height, LANES), lambda i: (0, 0))] * group,
+        out_shape=[jax.ShapeDtypeStruct((height, LANES), BF16)] * group,
+    )(table, requests.reshape(devices // group, 1, slots), far)
+
+
+def spread_neg_blocks_kernel(*refs, blocks, cap):
+    slot_ref, out_ref, rows, flat = refs[blocks:]
+    unpack_all(refs[:blocks], 0, cap, rows, flat)
+    for part in range(slot_ref.shape[0]):
+        hot = one_hot(flat.shape[1], slot_ref[part : part + 1, :])
+        out_ref[part] = dot(flat[...], hot, NN).T.astype(BF16)
+
+
+def spread_neg_blocks(back, slot, cap, feature):
+    devices = len(back)
+    parts, width = slot.shape
+    height = packed_height(cap, feature)
+    return call(
+        functools.partial(spread_neg_blocks_kernel, blocks=devices, cap=cap),
+        "spread_negatives",
+        2 * devices * cap * feature * slot.size,
+        2 * devices * cap * feature,
+        grid=(1,),
+        in_specs=[pl.BlockSpec((height, LANES), lambda i: (0, 0))] * devices
+        + [pl.BlockSpec(slot.shape, lambda i: (0, 0))],
+        out_specs=pl.BlockSpec((parts, width, feature), lambda i: (0, 0, 0)),
+        out_shape=jax.ShapeDtypeStruct((parts, width, feature), BF16),
+        scratch_shapes=unpack_scratch(devices, cap, feature),
+    )(*back, slot)
+
+
+def spread_blocks_kernel(*refs, blocks, base, pooled, first):
+    back_refs, slot_ref = refs[:blocks], refs[blocks]
+    out_ref, flat = refs[blocks + 1 + (not first)], refs[-1]
+    feature = flat.shape[0]
+
+    @pl.when(pl.program_id(0) == 0)
+    def _():
+        if pooled:
+            unpack_all(back_refs, 0, POOL, refs[-2], flat)
+        else:
+            for d, back_ref in enumerate(back_refs):
+                flat[:, d * LANES : (d + 1) * LANES] = back_ref[back_ref.shape[0] - feature :]
+
+    row = slot_ref[...].reshape(1, slot_ref.shape[-1])
+    rows = dot(flat[...], one_hot(flat.shape[1], row, base), NN)
+    if not first:
+        rows = rows + refs[blocks + 1][...].astype(F32)
+    out_ref[...] = rows.astype(BF16)
+
+
+def spread_blocks(back, slot, so_far, feature, first, pooled=False):
+    blocks = len(back)
+    segments, width = slot.shape
+    each = POOL if pooled else LANES
+    tile = width
+    steps = width // tile
+    rows_spec = pl.BlockSpec((feature, tile), lambda i: (0, i))
+    extra = [] if so_far is None else [so_far]
+    if pooled:
+        scratch = unpack_scratch(blocks, POOL, feature)
+    else:
+        scratch = [pltpu.VMEM((feature, blocks * each), BF16)]
+    return call(
+        functools.partial(
+            spread_blocks_kernel,
+            blocks=blocks,
+            base=first * each,
+            pooled=pooled,
+            first=so_far is None,
+        ),
+        "spread_pool" if pooled else "spread_blocks",
+        2 * feature * blocks * each * slot.size,
+        4 * feature * slot.size,
+        grid=(segments * steps,),
+        in_specs=[pl.BlockSpec(back[0].shape, lambda i: (0, 0))] * blocks
+        + [pl.BlockSpec((1, 1, tile), lambda i: (i // steps, 0, i % steps))]
+        + [rows_spec] * len(extra),
+        out_specs=rows_spec,
+        out_shape=jax.ShapeDtypeStruct((feature, slot.size), BF16),
         scratch_shapes=scratch,
-    )(back, slot.reshape(segments, 1, width), *extra)
+    )(*back, slot.reshape(segments, 1, width), *extra)
 
 
 def edges_kernel(*refs, parts):
@@ -472,7 +615,7 @@
     for part in range(slot_ref.shape[0]):
         hot = one_hot(group * cap, slot_ref[part : part + 1, :], step * group * cap)
         rows = rows + dot(hot, sums[part], NN)
-    pack_all(out_ref, 0, cap, rows, rows.T)
+    pack_all(blocks_of(out_ref), 0, cap, rows, rows.T)
 
 
 def collect_neg(sent, slot, grads, cap):
@@ -498,34 +641,109 @@
     )(sent, slot, *grads)
 
 
-def collect_pool_kernel(src_ref, dst_ref, slot_ref, out_ref, *, group):
+def collect_blocks_kernel(src_ref, dst_ref, slot_ref, neg_slot_ref, *refs, first, neg_cap, group):
     segments, width = slot_ref.shape
-    count = group * POOL
+    feature = src_ref.shape[0]
+    grad_refs, out_refs = refs[:-group], refs[-group:]
+    total = jnp.zeros((feature, group * LANES), F32)
+    for segment in range(segments):
+        grads = src_ref if segment < segments // 2 else dst_ref
+        start = segment % (segments // 2) * width
+        hot = one_hot(group * LANES, slot_ref[segment : segment + 1, :], first * LANES)
+        total = total + dot(grads[:, start : start + width], hot, NT)
+    total = total.astype(BF16)
+    for i, out_ref in enumerate(out_refs):
+        out_ref[out_ref.shape[0] - feature :] = total[:, i * LANES : (i + 1) * LANES]
+    rows = jnp.zeros((group * neg_cap, feature), F32)
+    for part in range(neg_slot_ref.shape[0]):
+        value = grad_refs[0][part].astype(F32)
+        for grad_ref in grad_refs[1:]:
+            value = value + grad_ref[part].astype(F32)
+        hot = one_hot(group * neg_cap, neg_slot_ref[part : part + 1, :], first * neg_cap)
+        rows = rows + dot(hot, value.astype(BF16), NN)
+    pack_all(out_refs, 0, neg_cap, rows, rows.T)
+
+
+def collect_blocks(src_grad, dst_grad, slot, neg_slot, neg_grads, first, group, neg_cap):
+    feature = src_grad.shape[0]
+    block = jax.ShapeDtypeStruct((packed_height(neg_cap, feature) + feature, LANES), BF16)
+    return call(
+        functools.partial(collect_blocks_kernel, first=first, neg_cap=neg_cap, group=group),
+        "collect_blocks",
+        2 * feature * group * LANES * slot.size,
+        2 * feature * slot.size,
+        out_shape=[block] * group,
+    )(src_grad, dst_grad, slot, neg_slot, *neg_grads)
+
+
+def collect_pool_kernel(src_ref, dst_ref, slot_ref, *out_refs, first):
+    segments, width = slot_ref.shape
+    count = len(out_refs) * POOL
     rows = jnp.zeros((count, src_ref.shape[0]), F32)
     for segment in range(segments):
         grads = src_ref if segment < segments // 2 else dst_ref
         start = segment % (segments // 2) * width
-        hot = one_hot(count, slot_ref[segment : segment + 1, :], pl.program_id(0) * count)
+        hot = one_hot(count, slot_ref[segment : segment + 1, :], first * POOL)
         rows = rows + dot(hot, grads[:, start : start + width], NT)
-    pack_all(out_ref, 0, POOL, rows, rows.T)
-
-
-def collect_pool(src_grad, dst_grad, slot, devices):
+    pack_all(out_refs, 0, POOL, rows, rows.T)
+
+
+def collect_pool(src_grad, dst_grad, slot, first, group):
     feature = src_grad.shape[0]
-    group = 8
-    slots = devices * POOL
-    height = packed_height(POOL, feature)
-    whole = pl.BlockSpec(src_grad.shape, lambda i: (0, 0))
-    return call(
-        functools.partial(collect_pool_kernel, group=group),
+    block = jax.ShapeDtypeStruct((packed_height(POOL, feature), LANES), BF16)
+    return call(
+        functools.partial(collect_pool_kernel, first=first),
         "collect_pool",
-        2 * feature * slots * slot.size,
-        2 * feature * (slots + slot.size),
-        grid=(devices // group,),
-        in_specs=[whole, whole, pl.BlockSpec(slot.shape, lambda i: (0, 0))],
-        out_specs=pl.BlockSpec((group, height, LANES), lambda i: (i, 0, 0)),
-        out_shape=jax.ShapeDtypeStruct((devices, height, LANES), BF16),
+        2 * feature * group * POOL * slot.size,
+        2 * feature * slot.size,
+        out_shape=[block] * group,
     )(src_grad, dst_grad, slot)
+
+
+def add_blocks_kernel(*refs, blocks, first, neg_cap, rows):
+    recv_refs = refs[:blocks]
+    req_ref, neg_req_ref, so_far_ref, out_ref, flat, neg_rows, neg_flat = refs[blocks:]
+    feature = flat.shape[0]
+    step = pl.program_id(0)
+
+    @pl.when(step == 0)
+    def _():
+        for d, recv_ref in enumerate(recv_refs):
+            flat[:, d * LANES : (d + 1) * LANES] = recv_ref[recv_ref.shape[0] - feature :]
+        unpack_all(recv_refs, 0, neg_cap, neg_rows, neg_flat)
+
+    base = step * rows
+    row = jnp.concatenate([req_ref[first + d : first + d + 1, :] for d in range(blocks)], axis=1)
+    total = dot(flat[...], one_hot(rows, row, base), NT)
+    row = jnp.concatenate(
+        [neg_req_ref[first + d : first + d + 1, :neg_cap] for d in range(blocks)], axis=1
+    )
+    total = total + dot(neg_flat[...], one_hot(rows, row, base), NT)
+    out_ref[...] = total + so_far_ref[...]
+
+
+def add_blocks(recv, requests, neg_requests, so_far, first, neg_cap):
+    feature, rows_dev = so_far.shape
+    blocks = len(recv)
+    rows = 1024
+    slots = blocks * LANES
+    req_spec = pl.BlockSpec(requests.shape, lambda i: (0, 0))
+    rows_spec = pl.BlockSpec((feature, rows), lambda i: (0, i))
+    return call(
+        functools.partial(
+            add_blocks_kernel, blocks=blocks, first=first, neg_cap=neg_cap, rows=rows
+        ),
+        "add_blocks",
+        2 * feature * slots * rows_dev,
+        8 * feature * rows_dev,
+        grid=(rows_dev // rows,),
+        in_specs=[pl.BlockSpec(recv[0].shape, lambda i: (0, 0))] * blocks
+        + [req_spec, req_spec, rows_spec],
+        out_specs=rows_spec,
+        out_shape=jax.ShapeDtypeStruct((feature, rows_dev), F32),
+        scratch_shapes=[pltpu.VMEM((feature, slots), BF16)]
+        + unpack_scratch(blocks, neg_cap, feature),
+    )(*recv, requests, neg_requests, so_far)
 
 
 def add_kernel(*refs, rows, neg_cap, first):
@@ -548,7 +766,7 @@
         for d in range(devices):
             flat[:, d * LANES : (d + 1) * LANES] = recv_ref[d, start:]
         if neg_cap:
-            unpack_all(recv_ref, 0, neg_cap, neg_rows, neg_flat)
+            unpack_all(blocks_of(recv_ref), 0, neg_cap, neg_rows, neg_flat)
 
     base = step * rows
     row = jnp.concatenate([req_ref[d : d + 1, :] for d in range(devices)], axis=1)
@@ -596,7 +814,7 @@
     @pl.when(step == 0)
     def _():
         for recv_ref, flat in zip((near_ref, far_ref), flats):
-            unpack_all(recv_ref, 0, POOL, packed, flat)
+            unpack_all(blocks_of(recv_ref), 0, POOL, packed, flat)
 
     total = dot(flats[0][...], one_hot(rows, near_req_ref[...], step * rows), NT)
     out_ref[...] = total + dot(flats[1][...], one_hot(rows, far_req_ref[...], step * rows), NT)
@@ -622,8 +840,26 @@
     )(near, far, requests[0][None], requests[1][None])
 
 
+def mixed(devices):
+    return [p // 2 + p % 2 * (devices // 2) for p in range(devices)]
+
+
 def exchange(value):
-    return lax.all_to_all(value, ("shard", "grp"), split_axis=0, concat_axis=0, tiled=True)
+    axes = ("shard", "grp")
+    devices = value.shape[0]
+    me = lax.axis_index(axes)
+    offsets = me ^ jnp.arange(devices, dtype=jnp.int32)
+    value = value[offsets % (devices // 2) * 2 + offsets // (devices // 2)]
+    value = lax.all_to_all(value, axes, split_axis=0, concat_axis=0, tiled=True)
+    return value[me ^ jnp.array(mixed(devices), jnp.int32)]
+
+
+def trade_blocks(blocks, first, devices):
+    offsets = mixed(devices)[first : first + len(blocks)]
+    return [
+        lax.ppermute(block, ("shard", "grp"), [(i, i ^ k) for i in range(devices)]) if k else block
+        for k, block in zip(offsets, blocks)
+    ]
 
 
 def swap(value, bit):
@@ -657,6 +893,7 @@
     width = round_up(block_len, 512)
     part = round_up(part_width, LANES)
     me = lax.axis_index("grp")
+    device = lax.axis_index(("shard", "grp"))
 
     table = entity_table.T.astype(BF16)
     relations = rel_diag.T
@@ -665,6 +902,7 @@
         [src_ids.reshape(spans, block_len), dst_ids.reshape(spans, block_len)]
     )
     message, *slots = make_slots(
+        device,
         pad_lanes(ends, width, -1),
         pad_lanes(own_ids, part, -1),
         rows_dev,
@@ -674,7 +912,8 @@
     )
     neg_slot = slots[-1]
     rel_rows = pad_lanes(rel_ids.reshape(spans, block_len), width, -1)
-    asked = exchange(message)
+    asked = lax.all_to_all(message, ("shard", "grp"), split_axis=0, concat_axis=0, tiled=True)
+    asked = asked[device ^ jnp.array(mixed(devices), jnp.int32)]
     direct = [asked[:, c * LANES : (c + 1) * LANES] for c in range(chunks)]
     neg_asked = asked[:, -LANES:]
 
@@ -704,19 +943,43 @@
         start = chunks * LANES
         core = me % RELAYS
         listed = asked[:, start : start + RELAYS * POOL].reshape(devices, RELAYS, POOL)
-        listed = listed.transpose(1, 0, 2).reshape(RELAYS, devices * POOL) - core * rows_dev
-        listed = [jnp.where(core == k, listed[0], listed[1]) for k in range(RELAYS)]
-        back = exchange(gather(table, direct[0], neg_asked, neg_cap))
-        far = swap(gather_pool(table, listed[1], devices), 1)
-        relayed = gather_pool(table, listed[0], devices) + far
-        negatives = negatives_of(back)
-        rows = spread(back, slots[0], None, feature)
-        rows = spread(exchange(relayed), slots[chunks], rows, feature, True)
+        listed = listed.transpose(1, 0, 2) - core * rows_dev
+        near_list = jnp.where(core == 0, listed[0], listed[1])
+        far_list = jnp.where(core == 0, listed[1], listed[0])
+        far_list = far_list.reshape(-1, 2, 2, POOL)[:, ::-1]
+        near_list, far_list = near_list.reshape(1, -1), far_list.reshape(1, -1)
+        small, large = 4, 8
+        back = []
+        for p in range(0, devices, small):
+            sent = gather_blocks(table, direct[0], neg_asked, p, small, neg_cap)
+            back += trade_blocks(sent, p, devices)
+        far = swap(gather_pool(table, far_list, devices), 1)
+        pool = []
+        for p in range(0, devices, large):
+            pool += trade_blocks(relay_blocks(table, near_list, far, p, large), p, devices)
+        rows = None
+        for p in range(0, devices, large):
+            rows = spread_blocks(back[p : p + large], slots[0], rows, feature, p)
+        negatives = share_out(spread_neg_blocks(back, neg_slot, neg_cap, feature))
+        for p in range(0, devices, large):
+            rows = spread_blocks(pool[p : p + large], slots[chunks], rows, feature, p, True)
         src_grad, dst_grad, neg_grads = edges(rows, rel_rows, relations, negatives)
-        near = exchange(collect_pool(src_grad, dst_grad, slots[chunks], devices))
-        sent = direct_sent(src_grad, dst_grad, neg_grads)
-        grad = add_pool(near, swap(near, 1), listed, feature, rows_dev)
-        return add_rows(sent, direct[0], grad, feature, rows_dev, neg_asked, neg_cap)
+        neg_grads = trade(neg_grads)
+        near = []
+        for p in range(0, devices, large):
+            sent = collect_pool(src_grad, dst_grad, slots[chunks], p, large)
+            near += trade_blocks(sent, p, devices)
+        recv = []
+        for p in range(0, devices, small):
+            sent = collect_blocks(
+                src_grad, dst_grad, slots[0], neg_slot, neg_grads, p, small, neg_cap
+            )
+            recv += trade_blocks(sent, p, devices)
+        near = jnp.stack(near)
+        grad = add_pool(near, swap(near, 1), [near_list[0], far_list[0]], feature, rows_dev)
+        for p in range(0, devices, large):
+            grad = add_blocks(recv[p : p + large], direct[0], neg_asked, grad, p, neg_cap)
+        return grad
 
     if chunks == 1 or sharers % RELAYS:
         return chunked().T

time: 435 us -> 637 us (1.46)
  starting transfers between devices: 28.8 us -> 180 us
  Pallas kernels: 186 us -> 263 us
  waiting for transfers between devices: 184 us -> 150 us
    ppermute x0 -> x124, starting transfers between devices: none -> 166 us  [trade_blocks(): lax.ppermute(block, ('shard', 'grp'), [(i, i ^ k) for i in range(devices)])]
    all_to_all x5 -> x1, waiting for transfers between devices: 154 us -> 2.4 us  [body(): lax.all_to_all(message, ('shard', 'grp'), split_axis=0, concat_axis=0, ti...]
    ppermute x0 -> x124, waiting for transfers between devices: none -> 126 us  [trade_blocks(): lax.ppermute(block, ('shard', 'grp'), [(i, i ^ k) for i in range(devices)])]
    pallas_call x8 -> x37, Pallas kernels: 119 us -> 209 us  [the longest x8 54.9 us: spread_blocks(): call(functools.partial(spread_blocks_kernel, blocks=blocks, base=first *...]
    all_to_all x5 -> x1, starting transfers between devices: 24.2 us -> 7.3 us  [body(): lax.all_to_all(message, ('shard', 'grp'), split_axis=0, concat_axis=0, ti...]
    pallas_call x2 -> x1, Pallas kernels: 25.7 us -> 12.8 us  [gather_pool(): call(functools.partial(gather_pool_kernel, group=group), 'gather_pool', 2...]
    ppermute x8, waiting for transfers between devices: 29.9 us -> 21.8 us  [swap(): return lax.ppermute(value, 'grp', [(i, i ^ bit) for i in range(sharers)])]
  transfers between devices with their start and end apart: 13 -> 133, of which waited for: 7 -> 38; matrix products, arithmetic and copies ran while one was open for 3% -> 2% of each run, Pallas kernels for 25% -> 33%
where the time goes in v5:
time: 637 us; the launch traced here: 629 us
  Pallas kernels  263 us (41%)
  starting transfers between devices  180 us (28%)
  waiting for transfers between devices  150 us (24%)
  local copies, waits for them, and re-layouts  18.1 us (3%)
  loops' own time  12.9 us (2%)
    ppermute x124, starting transfers between devices, trade_blocks(): lax.ppermute(block, ('shard', 'grp'), [(i, i ^ k) for i in range(devices)])  166 us
    ppermute x124, waiting for transfers between devices, trade_blocks(): lax.ppermute(block, ('shard', 'grp'), [(i, i ^ k) for i in range(devices)])  126 us
    pallas_call x8, Pallas kernels, spread_blocks(): call(functools.partial(spread_blocks_kernel, blocks=blocks, base=first *...  54.9 us
    pallas_call x8, Pallas kernels, collect_blocks(): call(functools.partial(collect_blocks_kernel, first=first, neg_cap=neg_ca...  43 us
    pallas_call x4, Pallas kernels, add_blocks(): call(functools.partial(add_blocks_kernel, blocks=blocks, first=first, neg...  37.4 us
    pallas_call x8, Pallas kernels, gather_blocks(): call(functools.partial(gather_blocks_kernel, first=first, neg_cap=neg_cap...  29.1 us
    pallas_call x1, Pallas kernels, add_pool(): call(functools.partial(add_pool_kernel, rows=rows), 'add_pool', 4 * featu...  23.4 us
    pallas_call x4, Pallas kernels, collect_pool(): call(functools.partial(collect_pool_kernel, first=first), 'collect_pool',...  22.8 us
  transfers between devices with their start and end apart: 133, of which 38 were waited for; matrix products, arithmetic and copies ran while one was open for 2% of the time, Pallas kernels for 33%

profile of v5, /device:TPU:0, one launch (start us, length us, event | category | flops | bytes accessed | tf_op | source)
XLA Modules:
  0.0 628.8 jit_solution(3825180075478408220)
XLA Ops:
  2.9 3.9 slots.1
  8.4 7.3 %all-to-all-start.4 = ((s32[32,1,640]{2,1,0:T(1,128)}), s32[32,1,640]{2,1,0:T(1,128)S(1)}, u32[]{:S(2)}, u32[]{:S(2)}) async-start(s32[32,1,640]{2,1,0:T(1,128)} %copy.16), calls=%async_computation.4 | async-start | bytes 163840 | tf_op jit(solution)/shard_map/all_to_all | solution.py:915
  25.3 602.5 %conditional.1 = (f32[400,4096]{1,0:T(8,128)}) conditional(s32[]{:T(128)} %convert_element_type.9, (s32[32,640]{1,0:T(8,128)S(1)}, bf16[400,4096]{1,0:T(8,128)(2,1)S(1)}, s32[32]{0:T(128)S(1)}, s32[4,1024]{1,0:T(4,128)S(1)}, s32[32,128]{1,0:T(8,128)S(1)}, /*index=5*/s32[32,128]{1,0:T(8,128)S(1)}, s32[32]{0:T(128)S(1)}, s32[4,1024]{1,0:T(4,128)S(1)}, ...), branch_computations={%region_1.2_spmd, %region_2.3_spmd} | conditional | flops 116601651200 | bytes 394197312 | solution.py:987
  36.5 12.8 %gather_pool.1 = bf16[32,256,128]{2,1,0:T(8,128)(2,1)} custom-call(bf16[400,4096]{1,0:T(8,128)(2,1)S(1)} %get-tuple-element.74.table_ref, s32[4,1,640]{2,1,0:T(1,128)} %reshape.172.req_ref), custom_call_target="tpu_custom_call" | custom-call | flops 8388608000 | bytes 5324800 | tf_op jit(solution)/shard_map/cond/branch_1_fun/gather_pool/pallas_call | solution.py:266
  78.8 3.8 gather_blocks.10
  83.3 4.3 collective-permute-done.56.refs_1_
  108.4 4.0 collective-permute-start.44
  116.7 6.7 %spread_blocks.4.refs_9_ = bf16[400,4096]{1,0:T(8,128)(2,1)} custom-call(bf16[512,128]{1,0:T(8,128)(2,1)} %get-tuple-element.137.refs_0_, bf16[512,128]{1,0:T(8,128)(2,1)} %copy-done.40, bf16[512,128]{1,0:T(8,128)(2,1)} %copy-done.41, bf16[512,128]{1,0:T(8,128)(2,1)} %copy-done.42, bf16[512,128]{1,0:T(8,128)(2,1)} %collective-permute-done.59.refs_4_, ...), custom_call_target="tpu_custom_call" | custom-call | flops 3355443200 | bytes 6553600 | tf_op jit(solution)/shard_map/cond/branch_1_fun/spread_blocks/pallas_call | solution.py:465
  128.5 7.4 %spread_blocks.5.refs_9_ = bf16[400,4096]{1,0:T(8,128)(2,1)} custom-call(bf16[512,128]{1,0:T(8,128)(2,1)} %copy-done.47, bf16[512,128]{1,0:T(8,128)(2,1)} %copy-done.48, bf16[512,128]{1,0:T(8,128)(2,1)} %copy-done.49, bf16[512,128]{1,0:T(8,128)(2,1)} %copy-done.50, bf16[512,128]{1,0:T(8,128)(2,1)} %copy-done.43, bf16[512,128]{1,0:T(8,128)(2,1)} %copy-done.44, ...), custom_call_target="tpu_custom_call" | custom-call | flops 3355443200 | bytes 6553600 | tf_op jit(solution)/shard_map/cond/branch_1_fun/spread_blocks/pallas_call | solution.py:465
  140.3 4.3 collective-permute-start.39
  146.7 4.7 relay_blocks.7
  156.9 7.2 %spread_blocks.6.refs_9_ = bf16[400,4096]{1,0:T(8,128)(2,1)} custom-call(bf16[512,128]{1,0:T(8,128)(2,1)} %copy-done.55, bf16[512,128]{1,0:T(8,128)(2,1)} %copy-done.56, bf16[512,128]{1,0:T(8,128)(2,1)} %copy-done.57, bf16[512,128]{1,0:T(8,128)(2,1)} %copy-done.58, bf16[512,128]{1,0:T(8,128)(2,1)} %copy-done.51, bf16[512,128]{1,0:T(8,128)(2,1)} %copy-done.52, ...), custom_call_target="tpu_custom_call" | custom-call | flops 3355443200 | bytes 6553600 | tf_op jit(solution)/shard_map/cond/branch_1_fun/spread_blocks/pallas_call | solution.py:465
  173.9 4.7 relay_blocks.6
  185.9 4.7 relay_blocks.5
  198.8 7.6 %spread_blocks.7.refs_9_ = bf16[400,4096]{1,0:T(8,128)(2,1)} custom-call(bf16[512,128]{1,0:T(8,128)(2,1)} %copy-done.63, bf16[512,128]{1,0:T(8,128)(2,1)} %copy-done.64, bf16[512,128]{1,0:T(8,128)(2,1)} %copy-done.65, bf16[512,128]{1,0:T(8,128)(2,1)} %copy-done.66, bf16[512,128]{1,0:T(8,128)(2,1)} %copy-done.59, bf16[512,128]{1,0:T(8,128)(2,1)} %copy-done.60, ...), custom_call_target="tpu_custom_call" | custom-call | flops 3355443200 | bytes 6553600 | tf_op jit(solution)/shard_map/cond/branch_1_fun/spread_blocks/pallas_call | solution.py:465
  216.0 4.7 relay_blocks.4
  230.3 6.6 %spread_pool.4.refs_9_ = bf16[400,4096]{1,0:T(8,128)(2,1)} custom-call(bf16[256,128]{1,0:T(8,128)(2,1)} %get-tuple-element.102.refs_0_, bf16[256,128]{1,0:T(8,128)(2,1)} %copy-done.141, bf16[256,128]{1,0:T(8,128)(2,1)} %copy-done.143, bf16[256,128]{1,0:T(8,128)(2,1)} %copy-done.145, bf16[256,128]{1,0:T(8,128)(2,1)} %copy-done.147, ...), custom_call_target="tpu_custom_call" | custom-call | flops 2097152000 | bytes 6553600 | tf_op jit(solution)/shard_map/cond/branch_1_fun/spread_pool/pallas_call | solution.py:465
  242.9 6.4 %spread_pool.5.refs_9_ = bf16[400,4096]{1,0:T(8,128)(2,1)} custom-call(bf16[256,128]{1,0:T(8,128)(2,1)} %copy-done.146, bf16[256,128]{1,0:T(8,128)(2,1)} %copy-done.148, bf16[256,128]{1,0:T(8,128)(2,1)} %copy-done.151, bf16[256,128]{1,0:T(8,128)(2,1)} %copy-done.154, bf16[256,128]{1,0:T(8,128)(2,1)} %copy-done.157, bf16[256,128]{1,0:T(8,128)(2,1)} %copy-done.159, ...), custom_call_target="tpu_custom_call" | custom-call | flops 2097152000 | bytes 6553600 | tf_op jit(solution)/shard_map/cond/branch_1_fun/spread_pool/pallas_call | solution.py:465
  254.3 6.4 %spread_pool.6.refs_9_ = bf16[400,4096]{1,0:T(8,128)(2,1)} custom-call(bf16[256,128]{1,0:T(8,128)(2,1)} %copy-done.160, bf16[256,128]{1,0:T(8,128)(2,1)} %copy-done.163, bf16[256,128]{1,0:T(8,128)(2,1)} %copy-done.166, bf16[256,128]{1,0:T(8,128)(2,1)} %copy-done.168, bf16[256,128]{1,0:T(8,128)(2,1)} %copy-done.170, bf16[256,128]{1,0:T(8,128)(2,1)} %copy-done.172, ...), custom_call_target="tpu_custom_call" | custom-call | flops 2097152000 | bytes 6553600 | tf_op jit(solution)/shard_map/cond/branch_1_fun/spread_pool/pallas_call | solution.py:465
  261.9 6.4 %spread_pool.7.refs_0_.refs_1_ = bf16[400,4096]{1,0:T(8,128)(2,1)} custom-call(bf16[256,128]{1,0:T(8,128)(2,1)} %copy-done.182, bf16[256,128]{1,0:T(8,128)(2,1)} %copy-done.186, bf16[256,128]{1,0:T(8,128)(2,1)} %copy-done.189, bf16[256,128]{1,0:T(8,128)(2,1)} %copy-done.191, bf16[256,128]{1,0:T(8,128)(2,1)} %copy-done.197, bf16[256,128]{1,0:T(8,128)(2,1)} %copy-done.199, ...), custom_call_target="tpu_custom_call" | custom-call | flops 2097152000 | bytes 6553600 | tf_op jit(solution)/shard_map/cond/branch_1_fun/spread_pool/pallas_call | solution.py:465
  269.5 13.6 %edges.3 = (bf16[400,2048]{1,0:T(8,128)(2,1)}, bf16[400,2048]{1,0:T(8,128)(2,1)}, bf16[2,256,400]{2,1,0:T(8,128)(2,1)}, bf16[2,256,400]{2,1,0:T(8,128)(2,1)}, bf...) custom-call(bf16[400,4096]{1,0:T(8,128)(2,1)} %spread_pool.7.refs_0_.refs_1_, ...), custom_call_target="tpu_custom_call" | custom-call | flops 5033164800 | bytes 9830400 | tf_op jit(solution)/shard_map/cond/branch_1_fun/edges/pallas_call | solution.py:544
  283.1 5.7 collect_pool.7
  288.8 5.7 collect_pool.6
  294.4 5.7 collect_pool.4
  302.9 3.8 collective-permute-start.126
  307.9 5.8 collect_pool.5
  317.5 4.2 collective-permute-done.102
  321.8 4.2 collective-permute-done.103
  328.2 4.6 collective-permute-done.104
  336.7 7.3 %collective-permute-done.106 = bf16[256,128]{1,0:T(8,128)(2,1)S(1)} collective-permute-done((bf16[256,128]{1,0:T(8,128)(2,1)S(1)}, bf16[256,128]{1,0:T(8,128)(2,1)S(1)}, u32[]{:S(2)}, u32[]{:S(2)}) %collective-permute-start.106) | collective-permute-done | bytes 65568 | tf_op jit(solution)/shard_map/cond/branch_1_fun/ppermute | solution.py:860
  344.7 3.7 collective-permute-done.107
  348.5 6.3 collective-permute-done.108
  354.7 3.9 collective-permute-done.109
  358.6 6.7 %collective-permute-done.110 = bf16[256,128]{1,0:T(8,128)(2,1)S(1)} collective-permute-done((bf16[256,128]{1,0:T(8,128)(2,1)}, bf16[256,128]{1,0:T(8,128)(2,1)S(1)}, u32[]{:S(2)}, u32[]{:S(2)}) %collective-permute-start.110) | collective-permute-done | bytes 65568 | tf_op jit(solution)/shard_map/cond/branch_1_fun/ppermute | solution.py:860
  366.7 4.0 collective-permute-done.111
  370.7 7.2 %collective-permute-done.112 = bf16[256,128]{1,0:T(8,128)(2,1)S(1)} collective-permute-done((bf16[256,128]{1,0:T(8,128)(2,1)}, bf16[256,128]{1,0:T(8,128)(2,1)S(1)}, u32[]{:S(2)}, u32[]{:S(2)}) %collective-permute-start.112) | collective-permute-done | bytes 65568 | tf_op jit(solution)/shard_map/cond/branch_1_fun/ppermute | solution.py:860
  377.9 4.8 collective-permute-done.113
  382.7 7.1 %collective-permute-done.114 = bf16[256,128]{1,0:T(8,128)(2,1)S(1)} collective-permute-done((bf16[256,128]{1,0:T(8,128)(2,1)}, bf16[256,128]{1,0:T(8,128)(2,1)S(1)}, u32[]{:S(2)}, u32[]{:S(2)}) %collective-permute-start.114) | collective-permute-done | bytes 65568 | tf_op jit(solution)/shard_map/cond/branch_1_fun/ppermute | solution.py:860
  389.8 4.2 collective-permute-done.115
  395.8 4.3 collective-permute-done.116
  403.9 5.5 collective-permute-done.118
  409.4 5.1 collective-permute-done.119
  416.8 4.7 collective-permute-done.120
  421.5 4.6 collective-permute-done.121
  426.1 6.4 %collective-permute-done.122 = bf16[256,128]{1,0:T(8,128)(2,1)S(1)} collective-permute-done((bf16[256,128]{1,0:T(8,128)(2,1)S(1)}, bf16[256,128]{1,0:T(8,128)(2,1)S(1)}, u32[]{:S(2)}, u32[]{:S(2)}) %collective-permute-start.122) | collective-permute-done | bytes 65568 | tf_op jit(solution)/shard_map/cond/branch_1_fun/ppermute | solution.py:860
  435.3 5.7 collective-permute-start.130
  450.5 10.2 %collective-permute-done.67.refs_2_ = bf16[2,256,400]{2,1,0:T(8,128)(2,1)} collective-permute-done((bf16[2,256,400]{2,1,0:T(8,128)(2,1)S(1)}, bf16[2,256,400]{2,1,0:T(8,128)(2,1)}, u32[]{:S(2)}, u32[]{:S(2)}) %collective-permute-start.67) | collective-permute-done | bytes 409632 | tf_op jit(solution)/shard_map/cond/branch_1_fun/ppermute | solution.py:867
  460.7 10.3 %collective-permute-done.68.refs_3_ = bf16[2,256,400]{2,1,0:T(8,128)(2,1)} collective-permute-done((bf16[2,256,400]{2,1,0:T(8,128)(2,1)S(1)}, bf16[2,256,400]{2,1,0:T(8,128)(2,1)}, u32[]{:S(2)}, u32[]{:S(2)}) %collective-permute-start.68) | collective-permute-done | bytes 409632 | tf_op jit(solution)/shard_map/cond/branch_1_fun/ppermute | solution.py:867
  471.0 5.4 collect_blocks.15
  478.0 3.9 collective-permute-start.99
  481.9 5.4 collect_blocks.14
  487.3 5.4 collect_blocks.13
  492.7 5.3 collect_blocks.12
  498.0 5.4 collect_blocks.11
  503.4 5.4 collect_blocks.10
  512.1 5.4 collect_blocks.9
  522.7 3.8 collective-permute-start.92
  526.5 5.4 collect_blocks.8
  538.5 23.4 %add_pool.1.refs_10_ = f32[400,4096]{1,0:T(8,128)} custom-call(bf16[32,256,128]{2,1,0:T(8,128)(2,1)} %copy-done.69, bf16[32,256,128]{2,1,0:T(8,128)(2,1)} %collective-permute-done.131.far_ref, s32[1,2560]{1,0:T(1,128)} %select_n.105.near_req_ref, s32[1,2560]{1,0:T(1,128)} %reshape.176.far_req_ref), custom_call_target="tpu_custom_call" | custom-call | flops 16777216000 | bytes 10649600 | tf_op jit(solution)/shard_map/cond/branch_1_fun/add_pool/pallas_call | solution.py:830
  570.1 9.4 %add_blocks.4.refs_10_ = f32[400,4096]{1,0:T(8,128)} custom-call(bf16[512,128]{1,0:T(8,128)(2,1)} %get-tuple-element.178.refs_0_, bf16[512,128]{1,0:T(8,128)(2,1)} %copy-done.16, bf16[512,128]{1,0:T(8,128)(2,1)} %copy-done.18, bf16[512,128]{1,0:T(8,128)(2,1)} %copy-done.20, bf16[512,128]{1,0:T(8,128)(2,1)} %copy-done.9, bf16[512,128]{1,0:T(8,128)(2,1)} %copy-done.10, ...), custom_call_target="tpu_custom_call" | custom-call | flops 3355443200 | bytes 13107200 | tf_op jit(solution)/shard_map/cond/branch_1_fun/add_blocks/pallas_call | solution.py:732
  587.0 9.3 %add_blocks.5.refs_10_ = f32[400,4096]{1,0:T(8,128)} custom-call(bf16[512,128]{1,0:T(8,128)(2,1)} %copy-done.22, bf16[512,128]{1,0:T(8,128)(2,1)} %copy-done.24, bf16[512,128]{1,0:T(8,128)(2,1)} %copy-done.26, bf16[512,128]{1,0:T(8,128)(2,1)} %copy-done.28, bf16[512,128]{1,0:T(8,128)(2,1)} %copy-done.13, bf16[512,128]{1,0:T(8,128)(2,1)} %copy-done.14, ...), custom_call_target="tpu_custom_call" | custom-call | flops 3355443200 | bytes 13107200 | tf_op jit(solution)/shard_map/cond/branch_1_fun/add_blocks/pallas_call | solution.py:732
  596.3 4.1 collective-permute-start.76
  607.2 9.3 %add_blocks.6.refs_10_ = f32[400,4096]{1,0:T(8,128)} custom-call(bf16[512,128]{1,0:T(8,128)(2,1)} %copy-done.27, bf16[512,128]{1,0:T(8,128)(2,1)} %copy-done.29, bf16[512,128]{1,0:T(8,128)(2,1)} %copy-done.31, bf16[512,128]{1,0:T(8,128)(2,1)} %copy-done.34, bf16[512,128]{1,0:T(8,128)(2,1)} %copy-done.19, bf16[512,128]{1,0:T(8,128)(2,1)} %copy-done.21, ...), custom_call_target="tpu_custom_call" | custom-call | flops 3355443200 | bytes 13107200 | tf_op jit(solution)/shard_map/cond/branch_1_fun/add_blocks/pallas_call | solution.py:732
  618.1 9.3 %add_blocks.7 = f32[400,4096]{1,0:T(8,128)} custom-call(bf16[512,128]{1,0:T(8,128)(2,1)} %copy-done.36, bf16[512,128]{1,0:T(8,128)(2,1)} %copy-done.37, bf16[512,128]{1,0:T(8,128)(2,1)} %copy-done.38, bf16[512,128]{1,0:T(8,128)(2,1)} %copy-done.39, bf16[512,128]{1,0:T(8,128)(2,1)} %copy-done.30, bf16[512,128]{1,0:T(8,128)(2,1)} %copy-done.32, ...), custom_call_target="tpu_custom_call" | custom-call | flops 3355443200 | bytes 13107200 | tf_op jit(solution)/shard_map/cond/branch_1_fun/add_blocks/pallas_call | solution.py:732
  (695 shorter events, 219.9 us)
Async XLA Ops:
  8.4 14.9 %all-to-all-start.4 = ((s32[32,1,640]{2,1,0:T(1,128)}), s32[32,1,640]{2,1,0:T(1,128)S(1)}, u32[]{:S(2)}, u32[]{:S(2)}) async-start(s32[32,1,640]{2,1,0:T(1,128)} %copy.16), calls=%async_computation.4 | async-start | bytes 163840 | tf_op jit(solution)/shard_map/all_to_all | solution.py:915
  49.3 95.2 %collective-permute-start = (bf16[32,256,128]{2,1,0:T(8,128)(2,1)}, bf16[32,256,128]{2,1,0:T(8,128)(2,1)}, u32[]{:S(2)}, u32[]{:S(2)}) collective-permute-start(bf16[32,256,128]{2,1,0:T(8,128)(2,1)} %gather_pool.1), channel_id=1, source_target_pairs={{0,1},{1,0},{2,3},{3,2},{4,5},{5,4},{6,7},{7,6},{8,9},{9,8},{10,11... | collective-permute-start | bytes 6291464 | tf_op jit(solution)/shard_map/cond/branch_1_fun/ppermute | solution.py:867
  53.0 22.6 %collective-permute-start.59 = (bf16[512,128]{1,0:T(8,128)(2,1)}, bf16[512,128]{1,0:T(8,128)(2,1)}, u32[]{:S(2)}, u32[]{:S(2)}) collective-permute-start(bf16[512,128]{1,0:T(8,128)(2,1)} %get-tuple-element.141), channel_id=1, source_target_pairs={{0,2},{1,3},{2,0},{3,1},{4,6},{5,7},{6,4},{7,5},{8,10},{9,11},{10,... | collective-permute-start | bytes 393224 | tf_op jit(solution)/shard_map/cond/branch_1_fun/ppermute | solution.py:860
  53.5 22.7 %collective-permute-start.60 = (bf16[512,128]{1,0:T(8,128)(2,1)}, bf16[512,128]{1,0:T(8,128)(2,1)}, u32[]{:S(2)}, u32[]{:S(2)}) collective-permute-start(bf16[512,128]{1,0:T(8,128)(2,1)} %get-tuple-element.142), channel_id=1, source_target_pairs={{0,18},{1,19},{2,16},{3,17},{4,22},{5,23},{6,20},{7,21},{8,26},{9,... | collective-permute-start | bytes 393224 | tf_op jit(solution)/shard_map/cond/branch_1_fun/ppermute | solution.py:860
  55.1 21.1 %collective-permute-start.61 = (bf16[512,128]{1,0:T(8,128)(2,1)}, bf16[512,128]{1,0:T(8,128)(2,1)}, u32[]{:S(2)}, u32[]{:S(2)}) collective-permute-start(bf16[512,128]{1,0:T(8,128)(2,1)} %get-tuple-element.143), channel_id=1, source_target_pairs={{0,3},{1,2},{2,1},{3,0},{4,7},{5,6},{6,5},{7,4},{8,11},{9,10},{10,... | collective-permute-start | bytes 393224 | tf_op jit(solution)/shard_map/cond/branch_1_fun/ppermute | solution.py:860
  55.7 27.0 %collective-permute-start.62 = (bf16[512,128]{1,0:T(8,128)(2,1)}, bf16[512,128]{1,0:T(8,128)(2,1)}, u32[]{:S(2)}, u32[]{:S(2)}) collective-permute-start(bf16[512,128]{1,0:T(8,128)(2,1)} %get-tuple-element.144), channel_id=1, source_target_pairs={{0,19},{1,18},{2,17},{3,16},{4,23},{5,22},{6,21},{7,20},{8,27},{9,... | collective-permute-start | bytes 393224 | tf_op jit(solution)/shard_map/cond/branch_1_fun/ppermute | solution.py:860
  82.6 14.3 %collective-permute-start.52 = (bf16[512,128]{1,0:T(8,128)(2,1)S(1)}, bf16[512,128]{1,0:T(8,128)(2,1)S(1)}, u32[]{:S(2)}, u32[]{:S(2)}) collective-permute-start(bf16[512,128]{1,0:T(8,128)(2,1)S(1)} %copy-done.125), channel_id=1, source_target_pairs={{0,6},{1,7},{2,4},{3,5},{4,2},{5,3},{6,0},{7,1},{8,14},{9,15},{10,... | collective-permute-start | bytes 393224 | tf_op jit(solution)/shard_map/cond/branch_1_fun/ppermute | solution.py:860
  97.8 14.6 %collective-permute-start.49 = (bf16[512,128]{1,0:T(8,128)(2,1)S(1)}, bf16[512,128]{1,0:T(8,128)(2,1)S(1)}, u32[]{:S(2)}, u32[]{:S(2)}) collective-permute-start(bf16[512,128]{1,0:T(8,128)(2,1)S(1)} %copy-done.116), channel_id=1, source_target_pairs={{0,20},{1,21},{2,22},{3,23},{4,16},{5,17},{6,18},{7,19},{8,28},{9,... | collective-permute-start | bytes 393224 | tf_op jit(solution)/shard_map/cond/branch_1_fun/ppermute | solution.py:860
  98.1 14.8 %collective-permute-start.50 = (bf16[512,128]{1,0:T(8,128)(2,1)S(1)}, bf16[512,128]{1,0:T(8,128)(2,1)S(1)}, u32[]{:S(2)}, u32[]{:S(2)}) collective-permute-start(bf16[512,128]{1,0:T(8,128)(2,1)S(1)} %copy-done.115), channel_id=1, source_target_pairs={{0,5},{1,4},{2,7},{3,6},{4,1},{5,0},{6,3},{7,2},{8,13},{9,12},{10,... | collective-permute-start | bytes 393224 | tf_op jit(solution)/shard_map/cond/branch_1_fun/ppermute | solution.py:860
  108.4 15.1 %collective-permute-start.44 = (bf16[512,128]{1,0:T(8,128)(2,1)S(1)}, bf16[512,128]{1,0:T(8,128)(2,1)S(1)}, u32[]{:S(2)}, u32[]{:S(2)}) collective-permute-start(bf16[512,128]{1,0:T(8,128)(2,1)S(1)} %copy-done.111), channel_id=1, source_target_pairs={{0,10},{1,11},{2,8},{3,9},{4,14},{5,15},{6,12},{7,13},{8,2},{9,3},... | collective-permute-start | bytes 393224 | tf_op jit(solution)/shard_map/cond/branch_1_fun/ppermute | solution.py:860
  124.3 14.1 %collective-permute-start.41 = (bf16[512,128]{1,0:T(8,128)(2,1)S(1)}, bf16[512,128]{1,0:T(8,128)(2,1)S(1)}, u32[]{:S(2)}, u32[]{:S(2)}) collective-permute-start(bf16[512,128]{1,0:T(8,128)(2,1)S(1)} %copy-done.105), channel_id=1, source_target_pairs={{0,24},{1,25},{2,26},{3,27},{4,28},{5,29},{6,30},{7,31},{8,16},{9,... | collective-permute-start | bytes 393224 | tf_op jit(solution)/shard_map/cond/branch_1_fun/ppermute | solution.py:860
  125.7 14.3 %collective-permute-start.42 = (bf16[512,128]{1,0:T(8,128)(2,1)S(1)}, bf16[512,128]{1,0:T(8,128)(2,1)S(1)}, u32[]{:S(2)}, u32[]{:S(2)}) collective-permute-start(bf16[512,128]{1,0:T(8,128)(2,1)S(1)} %copy-done.101), channel_id=1, source_target_pairs={{0,9},{1,8},{2,11},{3,10},{4,13},{5,12},{6,15},{7,14},{8,1},{9,0},... | collective-permute-start | bytes 393224 | tf_op jit(solution)/shard_map/cond/branch_1_fun/ppermute | solution.py:860
  136.0 15.4 %collective-permute-start.36 = (bf16[512,128]{1,0:T(8,128)(2,1)S(1)}, bf16[512,128]{1,0:T(8,128)(2,1)S(1)}, u32[]{:S(2)}, u32[]{:S(2)}) collective-permute-start(bf16[512,128]{1,0:T(8,128)(2,1)S(1)} %copy-done.102), channel_id=1, source_target_pairs={{0,14},{1,15},{2,12},{3,13},{4,10},{5,11},{6,8},{7,9},{8,6},{9,7},... | collective-permute-start | bytes 393224 | tf_op jit(solution)/shard_map/cond/branch_1_fun/ppermute | solution.py:860
  138.4 14.1 %collective-permute-start.37 = (bf16[512,128]{1,0:T(8,128)(2,1)S(1)}, bf16[512,128]{1,0:T(8,128)(2,1)S(1)}, u32[]{:S(2)}, u32[]{:S(2)}) collective-permute-start(bf16[512,128]{1,0:T(8,128)(2,1)S(1)} %copy-done.98), channel_id=1, source_target_pairs={{0,30},{1,31},{2,28},{3,29},{4,26},{5,27},{6,24},{7,25},{8,22},{9,... | collective-permute-start | bytes 393224 | tf_op jit(solution)/shard_map/cond/branch_1_fun/ppermute | solution.py:860
  140.3 15.8 %collective-permute-start.39 = (bf16[512,128]{1,0:T(8,128)(2,1)S(1)}, bf16[512,128]{1,0:T(8,128)(2,1)S(1)}, u32[]{:S(2)}, u32[]{:S(2)}) collective-permute-start(bf16[512,128]{1,0:T(8,128)(2,1)S(1)} %copy-done.92), channel_id=1, source_target_pairs={{0,31},{1,30},{2,29},{3,28},{4,27},{5,26},{6,25},{7,24},{8,23},{9,... | collective-permute-start | bytes 393224 | tf_op jit(solution)/shard_map/cond/branch_1_fun/ppermute | solution.py:860
  152.5 14.1 %collective-permute-start.34 = (bf16[512,128]{1,0:T(8,128)(2,1)S(1)}, bf16[512,128]{1,0:T(8,128)(2,1)S(1)}, u32[]{:S(2)}, u32[]{:S(2)}) collective-permute-start(bf16[512,128]{1,0:T(8,128)(2,1)S(1)} %copy-done.96), channel_id=1, source_target_pairs={{0,13},{1,12},{2,15},{3,14},{4,9},{5,8},{6,11},{7,10},{8,5},{9,4},... | collective-permute-start | bytes 393224 | tf_op jit(solution)/shard_map/cond/branch_1_fun/ppermute | solution.py:860
  153.0 17.1 %collective-permute-start.35 = (bf16[512,128]{1,0:T(8,128)(2,1)S(1)}, bf16[512,128]{1,0:T(8,128)(2,1)S(1)}, u32[]{:S(2)}, u32[]{:S(2)}) collective-permute-start(bf16[512,128]{1,0:T(8,128)(2,1)S(1)} %copy-done.93), channel_id=1, source_target_pairs={{0,29},{1,28},{2,31},{3,30},{4,25},{5,24},{6,27},{7,26},{8,21},{9,... | collective-permute-start | bytes 393224 | tf_op jit(solution)/shard_map/cond/branch_1_fun/ppermute | solution.py:860
  156.1 14.1 %collective-permute-start.25 = (bf16[256,128]{1,0:T(8,128)(2,1)}, bf16[256,128]{1,0:T(8,128)(2,1)S(1)}, u32[]{:S(2)}, u32[]{:S(2)}) collective-permute-start(bf16[256,128]{1,0:T(8,128)(2,1)} %get-tuple-element.103), channel_id=1, source_target_pairs={{0,16},{1,17},{2,18},{3,19},{4,20},{5,21},{6,22},{7,23},{8,24},{9,... | collective-permute-start | bytes 196616 | tf_op jit(solution)/shard_map/cond/branch_1_fun/ppermute | solution.py:860
  156.8 14.4 %collective-permute-start.26 = (bf16[256,128]{1,0:T(8,128)(2,1)}, bf16[256,128]{1,0:T(8,128)(2,1)S(1)}, u32[]{:S(2)}, u32[]{:S(2)}) collective-permute-start(bf16[256,128]{1,0:T(8,128)(2,1)} %get-tuple-element.104), channel_id=1, source_target_pairs={{0,1},{1,0},{2,3},{3,2},{4,5},{5,4},{6,7},{7,6},{8,9},{9,8},{10,11... | collective-permute-start | bytes 196616 | tf_op jit(solution)/shard_map/cond/branch_1_fun/ppermute | solution.py:860
  164.2 14.4 %collective-permute-start.27 = (bf16[256,128]{1,0:T(8,128)(2,1)S(1)}, bf16[256,128]{1,0:T(8,128)(2,1)S(1)}, u32[]{:S(2)}, u32[]{:S(2)}) collective-permute-start(bf16[256,128]{1,0:T(8,128)(2,1)S(1)} %copy-done.192), channel_id=1, source_target_pairs={{0,17},{1,16},{2,19},{3,18},{4,21},{5,20},{6,23},{7,22},{8,25},{9,... | collective-permute-start | bytes 196616 | tf_op jit(solution)/shard_map/cond/branch_1_fun/ppermute | solution.py:860
  181.2 15.5 %collective-permute-start.20 = (bf16[256,128]{1,0:T(8,128)(2,1)}, bf16[256,128]{1,0:T(8,128)(2,1)S(1)}, u32[]{:S(2)}, u32[]{:S(2)}) collective-permute-start(bf16[256,128]{1,0:T(8,128)(2,1)} %get-tuple-element.97), channel_id=1, source_target_pairs={{0,21},{1,20},{2,23},{3,22},{4,17},{5,16},{6,19},{7,18},{8,29},{9,... | collective-permute-start | bytes 196616 | tf_op jit(solution)/shard_map/cond/branch_1_fun/ppermute | solution.py:860
  184.3 14.3 %collective-permute-start.21 = (bf16[256,128]{1,0:T(8,128)(2,1)}, bf16[256,128]{1,0:T(8,128)(2,1)S(1)}, u32[]{:S(2)}, u32[]{:S(2)}) collective-permute-start(bf16[256,128]{1,0:T(8,128)(2,1)} %get-tuple-element.98), channel_id=1, source_target_pairs={{0,6},{1,7},{2,4},{3,5},{4,2},{5,3},{6,0},{7,1},{8,14},{9,15},{10,... | collective-permute-start | bytes 196616 | tf_op jit(solution)/shard_map/cond/branch_1_fun/ppermute | solution.py:860
  190.7 18.8 %collective-permute-start.22 = (bf16[256,128]{1,0:T(8,128)(2,1)S(1)}, bf16[256,128]{1,0:T(8,128)(2,1)S(1)}, u32[]{:S(2)}, u32[]{:S(2)}) collective-permute-start(bf16[256,128]{1,0:T(8,128)(2,1)S(1)} %copy-done.180), channel_id=1, source_target_pairs={{0,22},{1,23},{2,20},{3,21},{4,18},{5,19},{6,16},{7,17},{8,30},{9,... | collective-permute-start | bytes 196616 | tf_op jit(solution)/shard_map/cond/branch_1_fun/ppermute | solution.py:860
  192.1 17.4 %collective-permute-start.23 = (bf16[256,128]{1,0:T(8,128)(2,1)S(1)}, bf16[256,128]{1,0:T(8,128)(2,1)S(1)}, u32[]{:S(2)}, u32[]{:S(2)}) collective-permute-start(bf16[256,128]{1,0:T(8,128)(2,1)S(1)} %copy-done.176), channel_id=1, source_target_pairs={{0,7},{1,6},{2,5},{3,4},{4,3},{5,2},{6,1},{7,0},{8,15},{9,14},{10,... | collective-permute-start | bytes 196616 | tf_op jit(solution)/shard_map/cond/branch_1_fun/ppermute | solution.py:860
  193.1 19.2 %collective-permute-start.24 = (bf16[256,128]{1,0:T(8,128)(2,1)S(1)}, bf16[256,128]{1,0:T(8,128)(2,1)S(1)}, u32[]{:S(2)}, u32[]{:S(2)}) collective-permute-start(bf16[256,128]{1,0:T(8,128)(2,1)S(1)} %copy-done.173), channel_id=1, source_target_pairs={{0,23},{1,22},{2,21},{3,20},{4,19},{5,18},{6,17},{7,16},{8,31},{9,... | collective-permute-start | bytes 196616 | tf_op jit(solution)/shard_map/cond/branch_1_fun/ppermute | solution.py:860
  196.7 17.1 %collective-permute-start.9 = (bf16[256,128]{1,0:T(8,128)(2,1)}, bf16[256,128]{1,0:T(8,128)(2,1)S(1)}, u32[]{:S(2)}, u32[]{:S(2)}) collective-permute-start(bf16[256,128]{1,0:T(8,128)(2,1)} %get-tuple-element.86), channel_id=1, source_target_pairs={{0,8},{1,9},{2,10},{3,11},{4,12},{5,13},{6,14},{7,15},{8,0},{9,1},... | collective-permute-start | bytes 196616 | tf_op jit(solution)/shard_map/cond/branch_1_fun/ppermute | solution.py:860
  198.6 16.7 %collective-permute-start.10 = (bf16[256,128]{1,0:T(8,128)(2,1)}, bf16[256,128]{1,0:T(8,128)(2,1)S(1)}, u32[]{:S(2)}, u32[]{:S(2)}) collective-permute-start(bf16[256,128]{1,0:T(8,128)(2,1)} %get-tuple-element.87), channel_id=1, source_target_pairs={{0,24},{1,25},{2,26},{3,27},{4,28},{5,29},{6,30},{7,31},{8,16},{9,... | collective-permute-start | bytes 196616 | tf_op jit(solution)/shard_map/cond/branch_1_fun/ppermute | solution.py:860
  209.6 14.2 %collective-permute-start.12 = (bf16[256,128]{1,0:T(8,128)(2,1)S(1)}, bf16[256,128]{1,0:T(8,128)(2,1)S(1)}, u32[]{:S(2)}, u32[]{:S(2)}) collective-permute-start(bf16[256,128]{1,0:T(8,128)(2,1)S(1)} %copy-done.174), channel_id=1, source_target_pairs={{0,25},{1,24},{2,27},{3,26},{4,29},{5,28},{6,31},{7,30},{8,17},{9,... | collective-permute-start | bytes 196616 | tf_op jit(solution)/shard_map/cond/branch_1_fun/ppermute | solution.py:860
  220.8 16.2 %collective-permute-start.16 = (bf16[256,128]{1,0:T(8,128)(2,1)S(1)}, bf16[256,128]{1,0:T(8,128)(2,1)S(1)}, u32[]{:S(2)}, u32[]{:S(2)}) collective-permute-start(bf16[256,128]{1,0:T(8,128)(2,1)S(1)} %copy-done.165), channel_id=1, source_target_pairs={{0,27},{1,26},{2,25},{3,24},{4,31},{5,30},{6,29},{7,28},{8,19},{9,... | collective-permute-start | bytes 196616 | tf_op jit(solution)/shard_map/cond/branch_1_fun/ppermute | solution.py:860
  223.8 14.2 %collective-permute-start.1 = (bf16[256,128]{1,0:T(8,128)(2,1)}, bf16[256,128]{1,0:T(8,128)(2,1)S(1)}, u32[]{:S(2)}, u32[]{:S(2)}) collective-permute-start(bf16[256,128]{1,0:T(8,128)(2,1)} %get-tuple-element.77), channel_id=1, source_target_pairs={{0,12},{1,13},{2,14},{3,15},{4,8},{5,9},{6,10},{7,11},{8,4},{9,5},... | collective-permute-start | bytes 196616 | tf_op jit(solution)/shard_map/cond/branch_1_fun/ppermute | solution.py:860
  227.1 14.2 %collective-permute-start.4 = (bf16[256,128]{1,0:T(8,128)(2,1)}, bf16[256,128]{1,0:T(8,128)(2,1)S(1)}, u32[]{:S(2)}, u32[]{:S(2)}) collective-permute-start(bf16[256,128]{1,0:T(8,128)(2,1)} %get-tuple-element.80), channel_id=1, source_target_pairs={{0,29},{1,28},{2,31},{3,30},{4,25},{5,24},{6,27},{7,26},{8,21},{9,... | collective-permute-start | bytes 196616 | tf_op jit(solution)/shard_map/cond/branch_1_fun/ppermute | solution.py:860
  237.0 31.4 %collective-permute-start.65 = (bf16[2,256,400]{2,1,0:T(8,128)(2,1)S(1)}, bf16[2,256,400]{2,1,0:T(8,128)(2,1)S(1)}, u32[]{:S(2)}, u32[]{:S(2)}) collective-permute-start(bf16[2,256,400]{2,1,0:T(8,128)(2,1)S(1)} %copy-done.3), channel_id=1, source_target_pairs={{0,3},{1,2},{2,1},{3,0},{4,7},{5,6},{6,5},{7,4},{8,11},{9,10},{10,... | collective-permute-start | bytes 1228808 | tf_op jit(solution)/shard_map/cond/branch_1_fun/ppermute | solution.py:867
  238.0 30.3 %collective-permute-start.64 = (bf16[2,256,400]{2,1,0:T(8,128)(2,1)S(1)}, bf16[2,256,400]{2,1,0:T(8,128)(2,1)S(1)}, u32[]{:S(2)}, u32[]{:S(2)}) collective-permute-start(bf16[2,256,400]{2,1,0:T(8,128)(2,1)S(1)} %copy-done.3), channel_id=1, source_target_pairs={{0,2},{1,3},{2,0},{3,1},{4,6},{5,7},{6,4},{7,5},{8,10},{9,11},{10,... | collective-permute-start | bytes 1228808 | tf_op jit(solution)/shard_map/cond/branch_1_fun/ppermute | solution.py:867
  239.1 29.3 %collective-permute-start.63 = (bf16[2,256,400]{2,1,0:T(8,128)(2,1)S(1)}, bf16[2,256,400]{2,1,0:T(8,128)(2,1)S(1)}, u32[]{:S(2)}, u32[]{:S(2)}) collective-permute-start(bf16[2,256,400]{2,1,0:T(8,128)(2,1)S(1)} %copy-done.3), channel_id=1, source_target_pairs={{0,1},{1,0},{2,3},{3,2},{4,5},{5,4},{6,7},{7,6},{8,9},{9,8},{10,11... | collective-permute-start | bytes 1228808 | tf_op jit(solution)/shard_map/cond/branch_1_fun/ppermute | solution.py:867
  300.2 132.3 %collective-permute-start.123 = (bf16[256,128]{1,0:T(8,128)(2,1)S(1)}, bf16[256,128]{1,0:T(8,128)(2,1)S(1)}, u32[]{:S(2)}, u32[]{:S(2)}) collective-permute-start(bf16[256,128]{1,0:T(8,128)(2,1)S(1)} %copy-done.139), channel_id=1, source_target_pairs={{0,12},{1,13},{2,14},{3,15},{4,8},{5,9},{6,10},{7,11},{8,4},{9,5},... | collective-permute-start | bytes 196616 | tf_op jit(solution)/shard_map/cond/branch_1_fun/ppermute | solution.py:860
  301.6 133.6 %collective-permute-start.124 = (bf16[256,128]{1,0:T(8,128)(2,1)S(1)}, bf16[256,128]{1,0:T(8,128)(2,1)S(1)}, u32[]{:S(2)}, u32[]{:S(2)}) collective-permute-start(bf16[256,128]{1,0:T(8,128)(2,1)S(1)} %copy-done.138), channel_id=1, source_target_pairs={{0,28},{1,29},{2,30},{3,31},{4,24},{5,25},{6,26},{7,27},{8,20},{9,... | collective-permute-start | bytes 196616 | tf_op jit(solution)/shard_map/cond/branch_1_fun/ppermute | solution.py:860
  302.9 132.4 %collective-permute-start.125 = (bf16[256,128]{1,0:T(8,128)(2,1)S(1)}, bf16[256,128]{1,0:T(8,128)(2,1)S(1)}, u32[]{:S(2)}, u32[]{:S(2)}) collective-permute-start(bf16[256,128]{1,0:T(8,128)(2,1)S(1)} %copy-done.137), channel_id=1, source_target_pairs={{0,13},{1,12},{2,15},{3,14},{4,9},{5,8},{6,11},{7,10},{8,5},{9,4},... | collective-permute-start | bytes 196616 | tf_op jit(solution)/shard_map/cond/branch_1_fun/ppermute | solution.py:860
  302.9 138.2 %collective-permute-start.126 = (bf16[256,128]{1,0:T(8,128)(2,1)S(1)}, bf16[256,128]{1,0:T(8,128)(2,1)S(1)}, u32[]{:S(2)}, u32[]{:S(2)}) collective-permute-start(bf16[256,128]{1,0:T(8,128)(2,1)S(1)} %copy-done.136), channel_id=1, source_target_pairs={{0,29},{1,28},{2,31},{3,30},{4,25},{5,24},{6,27},{7,26},{8,21},{9,... | collective-permute-start | bytes 196616 | tf_op jit(solution)/shard_map/cond/branch_1_fun/ppermute | solution.py:860
  443.7 94.1 %collective-permute-start.131 = (bf16[32,256,128]{2,1,0:T(8,128)(2,1)S(1)}, bf16[32,256,128]{2,1,0:T(8,128)(2,1)}, u32[]{:S(2)}, u32[]{:S(2)}) collective-permute-start(bf16[32,256,128]{2,1,0:T(8,128)(2,1)S(1)} %constant_dynamic-update-slice_fusion.near_ref), channel_id=1, source_target_pairs={{0,1},{1,0},{2,3},{3,2},{4,5},{5,4},{6,7},{7,6},{8,9},{9,8},{10,11... | collective-permute-start | bytes 6291464 | tf_op jit(solution)/shard_map/cond/branch_1_fun/ppermute | solution.py:867
  445.8 14.8 %collective-permute-start.67 = (bf16[2,256,400]{2,1,0:T(8,128)(2,1)S(1)}, bf16[2,256,400]{2,1,0:T(8,128)(2,1)}, u32[]{:S(2)}, u32[]{:S(2)}) collective-permute-start(bf16[2,256,400]{2,1,0:T(8,128)(2,1)S(1)} %copy-done.71), channel_id=1, source_target_pairs={{0,2},{1,3},{2,0},{3,1},{4,6},{5,7},{6,4},{7,5},{8,10},{9,11},{10,... | collective-permute-start | bytes 1228808 | tf_op jit(solution)/shard_map/cond/branch_1_fun/ppermute | solution.py:867
  447.0 24.0 %collective-permute-start.68 = (bf16[2,256,400]{2,1,0:T(8,128)(2,1)S(1)}, bf16[2,256,400]{2,1,0:T(8,128)(2,1)}, u32[]{:S(2)}, u32[]{:S(2)}) collective-permute-start(bf16[2,256,400]{2,1,0:T(8,128)(2,1)S(1)} %copy-done.70), channel_id=1, source_target_pairs={{0,3},{1,2},{2,1},{3,0},{4,7},{5,6},{6,5},{7,4},{8,11},{9,10},{10,... | collective-permute-start | bytes 1228808 | tf_op jit(solution)/shard_map/cond/branch_1_fun/ppermute | solution.py:867
  476.3 32.5 %collective-permute-start.96 = (bf16[512,128]{1,0:T(8,128)(2,1)}, bf16[512,128]{1,0:T(8,128)(2,1)S(1)}, u32[]{:S(2)}, u32[]{:S(2)}) collective-permute-start(bf16[512,128]{1,0:T(8,128)(2,1)} %get-tuple-element.182), channel_id=1, source_target_pairs={{0,2},{1,3},{2,0},{3,1},{4,6},{5,7},{6,4},{7,5},{8,10},{9,11},{10,... | collective-permute-start | bytes 393224 | tf_op jit(solution)/shard_map/cond/branch_1_fun/ppermute | solution.py:860
  477.5 31.4 %collective-permute-start.97 = (bf16[512,128]{1,0:T(8,128)(2,1)}, bf16[512,128]{1,0:T(8,128)(2,1)S(1)}, u32[]{:S(2)}, u32[]{:S(2)}) collective-permute-start(bf16[512,128]{1,0:T(8,128)(2,1)} %get-tuple-element.183), channel_id=1, source_target_pairs={{0,18},{1,19},{2,16},{3,17},{4,22},{5,23},{6,20},{7,21},{8,26},{9,... | collective-permute-start | bytes 393224 | tf_op jit(solution)/shard_map/cond/branch_1_fun/ppermute | solution.py:860
  477.5 31.5 %collective-permute-start.98 = (bf16[512,128]{1,0:T(8,128)(2,1)}, bf16[512,128]{1,0:T(8,128)(2,1)S(1)}, u32[]{:S(2)}, u32[]{:S(2)}) collective-permute-start(bf16[512,128]{1,0:T(8,128)(2,1)} %get-tuple-element.184), channel_id=1, source_target_pairs={{0,3},{1,2},{2,1},{3,0},{4,7},{5,6},{6,5},{7,4},{8,11},{9,10},{10,... | collective-permute-start | bytes 393224 | tf_op jit(solution)/shard_map/cond/branch_1_fun/ppermute | solution.py:860
  478.0 39.6 %collective-permute-start.99 = (bf16[512,128]{1,0:T(8,128)(2,1)}, bf16[512,128]{1,0:T(8,128)(2,1)S(1)}, u32[]{:S(2)}, u32[]{:S(2)}) collective-permute-start(bf16[512,128]{1,0:T(8,128)(2,1)} %get-tuple-element.185), channel_id=1, source_target_pairs={{0,19},{1,18},{2,17},{3,16},{4,23},{5,22},{6,21},{7,20},{8,27},{9,... | collective-permute-start | bytes 393224 | tf_op jit(solution)/shard_map/cond/branch_1_fun/ppermute | solution.py:860
  517.6 14.4 %collective-permute-start.89 = (bf16[512,128]{1,0:T(8,128)(2,1)S(1)}, bf16[512,128]{1,0:T(8,128)(2,1)S(1)}, u32[]{:S(2)}, u32[]{:S(2)}) collective-permute-start(bf16[512,128]{1,0:T(8,128)(2,1)S(1)} %copy-done.123), channel_id=1, source_target_pairs={{0,6},{1,7},{2,4},{3,5},{4,2},{5,3},{6,0},{7,1},{8,14},{9,15},{10,... | collective-permute-start | bytes 393224 | tf_op jit(solution)/shard_map/cond/branch_1_fun/ppermute | solution.py:860
  532.0 30.0 %collective-permute-start.85 = (bf16[512,128]{1,0:T(8,128)(2,1)S(1)}, bf16[512,128]{1,0:T(8,128)(2,1)S(1)}, u32[]{:S(2)}, u32[]{:S(2)}) collective-permute-start(bf16[512,128]{1,0:T(8,128)(2,1)S(1)} %copy-done.114), channel_id=1, source_target_pairs={{0,4},{1,5},{2,6},{3,7},{4,0},{5,1},{6,2},{7,3},{8,12},{9,13},{10,... | collective-permute-start | bytes 393224 | tf_op jit(solution)/shard_map/cond/branch_1_fun/ppermute | solution.py:860
  533.0 31.3 %collective-permute-start.86 = (bf16[512,128]{1,0:T(8,128)(2,1)S(1)}, bf16[512,128]{1,0:T(8,128)(2,1)S(1)}, u32[]{:S(2)}, u32[]{:S(2)}) collective-permute-start(bf16[512,128]{1,0:T(8,128)(2,1)S(1)} %copy-done.112), channel_id=1, source_target_pairs={{0,20},{1,21},{2,22},{3,23},{4,16},{5,17},{6,18},{7,19},{8,28},{9,... | collective-permute-start | bytes 393224 | tf_op jit(solution)/shard_map/cond/branch_1_fun/ppermute | solution.py:860
  533.6 30.8 %collective-permute-start.87 = (bf16[512,128]{1,0:T(8,128)(2,1)S(1)}, bf16[512,128]{1,0:T(8,128)(2,1)S(1)}, u32[]{:S(2)}, u32[]{:S(2)}) collective-permute-start(bf16[512,128]{1,0:T(8,128)(2,1)S(1)} %copy-done.110), channel_id=1, source_target_pairs={{0,5},{1,4},{2,7},{3,6},{4,1},{5,0},{6,3},{7,2},{8,13},{9,12},{10,... | collective-permute-start | bytes 393224 | tf_op jit(solution)/shard_map/cond/branch_1_fun/ppermute | solution.py:860
  535.5 32.6 %collective-permute-start.88 = (bf16[512,128]{1,0:T(8,128)(2,1)S(1)}, bf16[512,128]{1,0:T(8,128)(2,1)S(1)}, u32[]{:S(2)}, u32[]{:S(2)}) collective-permute-start(bf16[512,128]{1,0:T(8,128)(2,1)S(1)} %copy-done.107), channel_id=1, source_target_pairs={{0,21},{1,20},{2,23},{3,22},{4,17},{5,16},{6,19},{7,18},{8,29},{9,... | collective-permute-start | bytes 393224 | tf_op jit(solution)/shard_map/cond/branch_1_fun/ppermute | solution.py:860
  537.9 30.4 %collective-permute-start.81 = (bf16[512,128]{1,0:T(8,128)(2,1)S(1)}, bf16[512,128]{1,0:T(8,128)(2,1)S(1)}, u32[]{:S(2)}, u32[]{:S(2)}) collective-permute-start(bf16[512,128]{1,0:T(8,128)(2,1)S(1)} %copy-done.103), channel_id=1, source_target_pairs={{0,10},{1,11},{2,8},{3,9},{4,14},{5,15},{6,12},{7,13},{8,2},{9,3},... | collective-permute-start | bytes 393224 | tf_op jit(solution)/shard_map/cond/branch_1_fun/ppermute | solution.py:860
  562.0 17.6 %collective-permute-start.82 = (bf16[512,128]{1,0:T(8,128)(2,1)S(1)}, bf16[512,128]{1,0:T(8,128)(2,1)S(1)}, u32[]{:S(2)}, u32[]{:S(2)}) collective-permute-start(bf16[512,128]{1,0:T(8,128)(2,1)S(1)} %copy-done.94), channel_id=1, source_target_pairs={{0,26},{1,27},{2,24},{3,25},{4,30},{5,31},{6,28},{7,29},{8,18},{9,... | collective-permute-start | bytes 393224 | tf_op jit(solution)/shard_map/cond/branch_1_fun/ppermute | solution.py:860
  564.3 15.4 %collective-permute-start.83 = (bf16[512,128]{1,0:T(8,128)(2,1)S(1)}, bf16[512,128]{1,0:T(8,128)(2,1)S(1)}, u32[]{:S(2)}, u32[]{:S(2)}) collective-permute-start(bf16[512,128]{1,0:T(8,128)(2,1)S(1)} %copy-done.91), channel_id=1, source_target_pairs={{0,11},{1,10},{2,9},{3,8},{4,15},{5,14},{6,13},{7,12},{8,3},{9,2},... | collective-permute-start | bytes 393224 | tf_op jit(solution)/shard_map/cond/branch_1_fun/ppermute | solution.py:860
  564.4 18.1 %collective-permute-start.84 = (bf16[512,128]{1,0:T(8,128)(2,1)S(1)}, bf16[512,128]{1,0:T(8,128)(2,1)S(1)}, u32[]{:S(2)}, u32[]{:S(2)}) collective-permute-start(bf16[512,128]{1,0:T(8,128)(2,1)S(1)} %copy-done.90), channel_id=1, source_target_pairs={{0,27},{1,26},{2,25},{3,24},{4,31},{5,30},{6,29},{7,28},{8,19},{9,... | collective-permute-start | bytes 393224 | tf_op jit(solution)/shard_map/cond/branch_1_fun/ppermute | solution.py:860
  568.0 15.5 %collective-permute-start.77 = (bf16[512,128]{1,0:T(8,128)(2,1)S(1)}, bf16[512,128]{1,0:T(8,128)(2,1)S(1)}, u32[]{:S(2)}, u32[]{:S(2)}) collective-permute-start(bf16[512,128]{1,0:T(8,128)(2,1)S(1)} %copy-done.89), channel_id=1, source_target_pairs={{0,8},{1,9},{2,10},{3,11},{4,12},{5,13},{6,14},{7,15},{8,0},{9,1},... | collective-permute-start | bytes 393224 | tf_op jit(solution)/shard_map/cond/branch_1_fun/ppermute | solution.py:860
  568.3 18.1 %collective-permute-start.78 = (bf16[512,128]{1,0:T(8,128)(2,1)S(1)}, bf16[512,128]{1,0:T(8,128)(2,1)S(1)}, u32[]{:S(2)}, u32[]{:S(2)}) collective-permute-start(bf16[512,128]{1,0:T(8,128)(2,1)S(1)} %copy-done.88), channel_id=1, source_target_pairs={{0,24},{1,25},{2,26},{3,27},{4,28},{5,29},{6,30},{7,31},{8,16},{9,... | collective-permute-start | bytes 393224 | tf_op jit(solution)/shard_map/cond/branch_1_fun/ppermute | solution.py:860
  579.6 16.7 %collective-permute-start.79 = (bf16[512,128]{1,0:T(8,128)(2,1)S(1)}, bf16[512,128]{1,0:T(8,128)(2,1)S(1)}, u32[]{:S(2)}, u32[]{:S(2)}) collective-permute-start(bf16[512,128]{1,0:T(8,128)(2,1)S(1)} %copy-done.81), channel_id=1, source_target_pairs={{0,9},{1,8},{2,11},{3,10},{4,13},{5,12},{6,15},{7,14},{8,1},{9,0},... | collective-permute-start | bytes 393224 | tf_op jit(solution)/shard_map/cond/branch_1_fun/ppermute | solution.py:860
  579.7 20.7 %collective-permute-start.80 = (bf16[512,128]{1,0:T(8,128)(2,1)S(1)}, bf16[512,128]{1,0:T(8,128)(2,1)S(1)}, u32[]{:S(2)}, u32[]{:S(2)}) collective-permute-start(bf16[512,128]{1,0:T(8,128)(2,1)S(1)} %copy-done.79), channel_id=1, source_target_pairs={{0,25},{1,24},{2,27},{3,26},{4,29},{5,28},{6,31},{7,30},{8,17},{9,... | collective-permute-start | bytes 393224 | tf_op jit(solution)/shard_map/cond/branch_1_fun/ppermute | solution.py:860
  582.5 18.6 %collective-permute-start.73 = (bf16[512,128]{1,0:T(8,128)(2,1)S(1)}, bf16[512,128]{1,0:T(8,128)(2,1)S(1)}, u32[]{:S(2)}, u32[]{:S(2)}) collective-permute-start(bf16[512,128]{1,0:T(8,128)(2,1)S(1)} %copy-done.87), channel_id=1, source_target_pairs={{0,14},{1,15},{2,12},{3,13},{4,10},{5,11},{6,8},{7,9},{8,6},{9,7},... | collective-permute-start | bytes 393224 | tf_op jit(solution)/shard_map/cond/branch_1_fun/ppermute | solution.py:860
  583.6 19.9 %collective-permute-start.74 = (bf16[512,128]{1,0:T(8,128)(2,1)S(1)}, bf16[512,128]{1,0:T(8,128)(2,1)S(1)}, u32[]{:S(2)}, u32[]{:S(2)}) collective-permute-start(bf16[512,128]{1,0:T(8,128)(2,1)S(1)} %copy-done.83), channel_id=1, source_target_pairs={{0,30},{1,31},{2,28},{3,29},{4,26},{5,27},{6,24},{7,25},{8,22},{9,... | collective-permute-start | bytes 393224 | tf_op jit(solution)/shard_map/cond/branch_1_fun/ppermute | solution.py:860
  586.4 17.1 %collective-permute-start.75 = (bf16[512,128]{1,0:T(8,128)(2,1)S(1)}, bf16[512,128]{1,0:T(8,128)(2,1)S(1)}, u32[]{:S(2)}, u32[]{:S(2)}) collective-permute-start(bf16[512,128]{1,0:T(8,128)(2,1)S(1)} %copy-done.80), channel_id=1, source_target_pairs={{0,15},{1,14},{2,13},{3,12},{4,11},{5,10},{6,9},{7,8},{8,7},{9,6},... | collective-permute-start | bytes 393224 | tf_op jit(solution)/shard_map/cond/branch_1_fun/ppermute | solution.py:860
  596.3 20.2 %collective-permute-start.76 = (bf16[512,128]{1,0:T(8,128)(2,1)S(1)}, bf16[512,128]{1,0:T(8,128)(2,1)S(1)}, u32[]{:S(2)}, u32[]{:S(2)}) collective-permute-start(bf16[512,128]{1,0:T(8,128)(2,1)S(1)} %copy-done.78), channel_id=1, source_target_pairs={{0,31},{1,30},{2,29},{3,28},{4,27},{5,26},{6,25},{7,24},{8,23},{9,... | collective-permute-start | bytes 393224 | tf_op jit(solution)/shard_map/cond/branch_1_fun/ppermute | solution.py:860
  600.5 16.1 %collective-permute-start.69 = (bf16[512,128]{1,0:T(8,128)(2,1)S(1)}, bf16[512,128]{1,0:T(8,128)(2,1)S(1)}, u32[]{:S(2)}, u32[]{:S(2)}) collective-permute-start(bf16[512,128]{1,0:T(8,128)(2,1)S(1)} %copy-done.86), channel_id=1, source_target_pairs={{0,12},{1,13},{2,14},{3,15},{4,8},{5,9},{6,10},{7,11},{8,4},{9,5},... | collective-permute-start | bytes 393224 | tf_op jit(solution)/shard_map/cond/branch_1_fun/ppermute | solution.py:860
  601.1 15.5 %collective-permute-start.70 = (bf16[512,128]{1,0:T(8,128)(2,1)S(1)}, bf16[512,128]{1,0:T(8,128)(2,1)S(1)}, u32[]{:S(2)}, u32[]{:S(2)}) collective-permute-start(bf16[512,128]{1,0:T(8,128)(2,1)S(1)} %copy-done.85), channel_id=1, source_target_pairs={{0,28},{1,29},{2,30},{3,31},{4,24},{5,25},{6,26},{7,27},{8,20},{9,... | collective-permute-start | bytes 393224 | tf_op jit(solution)/shard_map/cond/branch_1_fun/ppermute | solution.py:860
  (264 other events, 4126.2 us)

commit v6 on v4

--- a/solution.py
+++ b/solution.py
@@ -8,8 +8,9 @@
 from jax.sharding import PartitionSpec as P
 
 LANES = 128
-POOL = 80
-RELAYS = 2
+POOL = 48
+RELAYS = 4
+SMALL = 32
 VMEM_BYTES = 56 << 20
 F32 = jnp.float32
 BF16 = jnp.bfloat16
@@ -67,7 +68,7 @@
 def slots_kernel(ends_ref, own_ref, *refs, rows_dev, devices, chunks, neg_cap):
     msg_ref = refs[0]
     slot_refs = refs[1 : 1 + chunks]
-    pool_ref = refs[1 + chunks] if chunks > 1 else None
+    pool_ref, busy_ref = refs[1 + chunks : 3 + chunks] if chunks > 1 else (None, None)
     neg_ref = refs[-1]
     row = lax.broadcasted_iota(jnp.int32, (LANES, 2 * LANES), 0)
     lane = lax.broadcasted_iota(jnp.int32, (LANES, 2 * LANES), 1)
@@ -99,28 +100,36 @@
     offset = chunks * LANES
     flag = jnp.full((1, 1), -1, jnp.int32)
     if chunks > 1:
-        chips = devices // RELAYS
+        shards = devices // RELAYS
         room = RELAYS * POOL
-        chip_rows = lax.broadcasted_iota(jnp.int32, (chips, LANES), 0)
+        shard_rows = lax.broadcasted_iota(jnp.int32, (shards, LANES), 0)
         spilled, spill_codes = [], []
         for owner, code, rank in zip(holder, codes, found):
-            chip = jnp.where(rank >= LANES, owner // RELAYS, -1)
-            spilled.append(jnp.where(chip_rows == chip, 1.0, 0.0))
+            shard = jnp.where(rank >= LANES, owner // RELAYS, -1)
+            spilled.append(jnp.where(shard_rows == shard, 1.0, 0.0))
             spill_codes.append(code + (owner % RELAYS) * rows_dev)
         pooled, taken = ranks(spilled, mixer)
         places = []
         for at, owner, rank, place in zip(where, holder, found, pooled):
             inside = (owner >= 0) & (rank >= LANES) & (place < room)
-            pool_ref[at] = jnp.where(inside, owner // RELAYS * room + place, -1)
+            compact = jnp.where(
+                place < SMALL, owner // RELAYS * SMALL + place, (shards - 1) * SMALL + place
+            )
+            pool_ref[at] = jnp.where(inside, compact, -1)
             places.append(jnp.where(inside, place, -1))
         listed = fill(spilled, spill_codes, places, 2 * LANES)
-        for chip in range(chips):
-            msg_ref[chip * RELAYS : (chip + 1) * RELAYS, offset : offset + 2 * LANES] = (
-                jnp.broadcast_to(listed[chip : chip + 1], (RELAYS, 2 * LANES))
+        for shard in range(shards):
+            msg_ref[shard * RELAYS : (shard + 1) * RELAYS, offset : offset + 2 * LANES] = (
+                jnp.broadcast_to(listed[shard : shard + 1], (RELAYS, 2 * LANES))
             )
         offset += 2 * LANES
-        most = jnp.max(jnp.max(taken, axis=1, keepdims=True), axis=0, keepdims=True)
-        flag = jnp.where(most > room, 1, -1)
+        most = jnp.max(taken, axis=0, keepdims=True)
+        busy = jnp.where(taken > SMALL, 1.0, 0.0)
+        crowded = jnp.sum(busy, axis=0, keepdims=True) > 1.0
+        flag = jnp.where((most > room) | crowded, 1, -1)[:, :1]
+        busy_ref[...] = jnp.sum(busy * shard_rows.astype(F32), axis=0, keepdims=True).astype(
+            jnp.int32
+        )[:, :1]
 
     where, holder, codes, members, found = prepare(own_ref)
     for at, owner, rank in zip(where, holder, found):
@@ -147,6 +156,7 @@
         8 * ends.size,
         out_shape=[jax.ShapeDtypeStruct((devices, width), jnp.int32)]
         + [jax.ShapeDtypeStruct(ends.shape, jnp.int32)] * (chunks + pooled)
+        + [jax.ShapeDtypeStruct((1, 1), jnp.int32)] * pooled
         + [jax.ShapeDtypeStruct(own.shape, jnp.int32)],
     )(ends, own)
 
@@ -288,7 +298,7 @@
     )(back, slot)
 
 
-def spread_kernel(*refs, first, pooled):
+def spread_kernel(*refs, first):
     back_ref, slot_ref = refs[:2]
     so_far_ref = None if first else refs[2]
     out_ref, flat = refs[2 + (not first)], refs[-1]
@@ -297,12 +307,9 @@
 
     @pl.when(pl.program_id(0) == 0)
     def _():
-        if pooled:
-            unpack_all(back_ref, 0, POOL, refs[-2], flat)
-        else:
-            start = back_ref.shape[1] - feature
-            for d in range(devices):
-                flat[:, d * LANES : (d + 1) * LANES] = back_ref[d, start:]
+        start = back_ref.shape[1] - feature
+        for d in range(devices):
+            flat[:, d * LANES : (d + 1) * LANES] = back_ref[d, start:]
 
     row = slot_ref[...].reshape(1, slot_ref.shape[-1])
     rows = dot(flat[...], one_hot(flat.shape[1], row), NN)
@@ -311,21 +318,17 @@
     out_ref[...] = rows.astype(BF16)
 
 
-def spread(back, slot, so_far, feature, pooled=False):
+def spread(back, slot, so_far, feature):
     devices = back.shape[0]
     segments, width = slot.shape
-    slots = devices * (POOL if pooled else LANES)
+    slots = devices * LANES
     tile = 512 if slots <= 4096 else 128
     steps = width // tile
     rows_spec = pl.BlockSpec((feature, tile), lambda i: (0, i))
     extra = [] if so_far is None else [so_far]
-    if pooled:
-        scratch = unpack_scratch(devices, POOL, feature)
-    else:
-        scratch = [pltpu.VMEM((feature, slots), BF16)]
-    return call(
-        functools.partial(spread_kernel, first=so_far is None, pooled=pooled),
-        "spread_pool" if pooled else "spread_rows",
+    return call(
+        functools.partial(spread_kernel, first=so_far is None),
+        "spread_rows",
         2 * feature * slots * slot.size,
         2 * feature * (slots + slot.size),
         grid=(segments * steps,),
@@ -336,18 +339,92 @@
         + [rows_spec] * len(extra),
         out_specs=rows_spec,
         out_shape=jax.ShapeDtypeStruct((feature, slot.size), BF16),
-        scratch_shapes=scratch,
+        scratch_shapes=[pltpu.VMEM((feature, slots), BF16)],
     )(back, slot.reshape(segments, 1, width), *extra)
 
 
-def edges_kernel(*refs, parts):
+def compact_places(shards):
+    places = [(shard, 0, 0, SMALL, shard * SMALL) for shard in range(shards)]
+    to = shards * SMALL
+    for relay in range(RELAYS):
+        first = 0 if relay else SMALL
+        places.append((None, relay, first, POOL - first, to))
+        to += POOL - first
+    return places
+
+
+def compact_size(shards):
+    return shards * SMALL + RELAYS * POOL - SMALL
+
+
+def compact_pool(back_ref, busy, rows_ref, flat_ref):
+    feature = flat_ref.shape[0]
+    pieces = feature // LANES
+    tails = []
+    for shard, relay, first, count, to in compact_places(back_ref.shape[0] // RELAYS):
+        at = (busy if shard is None else shard) * RELAYS + relay
+        for piece in range(pieces):
+            start = piece * POOL + first
+            rows_ref[to : to + count, piece * LANES : (piece + 1) * LANES] = back_ref[
+                at, start : start + count, :
+            ]
+        tail = back_ref[at, pieces * POOL :, :].astype(F32)
+        tails.append(tail[:, first : first + count])
+    flat_ref[: pieces * LANES] = rows_ref[...].astype(F32).T.astype(BF16)
+    flat_ref[pieces * LANES :] = jnp.concatenate(tails, axis=1).astype(BF16)
+
+
+def expand_pool(rows, busy, out_ref):
+    feature = rows.shape[1]
+    pieces = feature // LANES
+    turned = rows.T
+    out_ref[...] = jnp.zeros(out_ref.shape, out_ref.dtype)
+    shards = out_ref.shape[0] // RELAYS
+    for shard, relay, first, count, to in compact_places(shards):
+        at = (busy if shard is None else shard) * RELAYS + relay
+        for piece in range(pieces):
+            start = piece * POOL + first
+            out_ref[at, start : start + count, :] = rows[
+                to : to + count, piece * LANES : (piece + 1) * LANES
+            ].astype(BF16)
+        if shard is not None:
+            tail = turned[pieces * LANES :, to : to + count]
+        else:
+            small = turned[pieces * LANES :, : shards * SMALL]
+            tail = turned[pieces * LANES :, to : to + count]
+            if first:
+                kept = jnp.zeros((feature % LANES, first), F32)
+                for other in range(shards):
+                    part = small[:, other * SMALL : (other + 1) * SMALL]
+                    kept = jnp.where(busy == other, part, kept)
+                tail = jnp.concatenate([kept, tail], axis=1)
+        blank = jnp.zeros((tail.shape[0], LANES - tail.shape[1]), F32)
+        out_ref[at, pieces * POOL :, :] = jnp.concatenate([tail, blank], axis=1).astype(BF16)
+
+
+def edges_kernel(*refs, parts, pooled):
+    refs = list(refs)
     src_ref, dst_ref, rel_ids_ref, rel_ref = refs[:4]
     neg_refs = refs[4 : 4 + parts]
-    src_grad_ref, dst_grad_ref = refs[4 + parts : 6 + parts]
-    neg_grad_refs = refs[6 + parts : 6 + 2 * parts]
-    negatives, turned, sums = refs[6 + 2 * parts :]
-    step = pl.program_id(1)
+    refs = refs[4 + parts :]
+    if pooled:
+        back_ref, src_slot_ref, dst_slot_ref, busy_ref = refs[:4]
+        refs = refs[4:]
+        pool_out_ref = refs.pop(2 + parts)
+        pool_rows, pool_flat, pool_sums = refs[-3:]
+    src_grad_ref, dst_grad_ref = refs[:2]
+    neg_grad_refs = refs[2 : 2 + parts]
+    negatives, turned, sums = refs[2 + parts : 5 + parts]
+    block, step = pl.program_id(0), pl.program_id(1)
+    last = step == pl.num_programs(1) - 1
     part = neg_refs[0].shape[1]
+
+    if pooled:
+
+        @pl.when((block == 0) & (step == 0))
+        def _():
+            compact_pool(back_ref, busy_ref[0, 0], pool_rows, pool_flat)
+            pool_sums[...] = jnp.zeros(pool_sums.shape, F32)
 
     @pl.when(step == 0)
     def _():
@@ -364,15 +441,25 @@
         table = table - piece.astype(F32)
     source = src_ref[...].astype(F32)
     target = dst_ref[...].astype(F32)
+    if pooled:
+        count = pool_flat.shape[1]
+        src_hot = one_hot(count, src_slot_ref[...].reshape(1, src_slot_ref.shape[-1]))
+        dst_hot = one_hot(count, dst_slot_ref[...].reshape(1, dst_slot_ref.shape[-1]))
+        source = source + dot(pool_flat[...], src_hot, NN)
+        target = target + dot(pool_flat[...], dst_hot, NN)
     product = source * relation
     positive = jnp.sum(product * target, axis=0, keepdims=True)
     pos_weight = -jax.nn.sigmoid(-positive)
     query = product.astype(BF16)
     weight = jax.nn.sigmoid(dot(negatives[...], query, NN)).astype(BF16)
     gathered = dot(turned[...], weight, NN)
-    src_grad_ref[...] = (relation * (pos_weight * target + gathered)).astype(BF16)
-    dst_grad_ref[...] = (pos_weight * product).astype(BF16)
+    src_grad = (relation * (pos_weight * target + gathered)).astype(BF16)
+    dst_grad = (pos_weight * product).astype(BF16)
+    src_grad_ref[...] = src_grad
+    dst_grad_ref[...] = dst_grad
     neg_grad = dot(weight, query, NT)
+    if pooled:
+        pool_sums[...] += dot(src_hot, src_grad, NT) + dot(dst_hot, dst_grad, NT)
 
     @pl.when(step == 0)
     def _():
@@ -382,13 +469,19 @@
     def _():
         sums[...] += neg_grad
 
-    @pl.when(step == pl.num_programs(1) - 1)
+    @pl.when(last)
     def _():
         for k in range(parts):
             neg_grad_refs[k][0] = sums[k * part : (k + 1) * part].astype(BF16)
 
-
-def edges(rows, rel_ids, relations, negatives):
+    if pooled:
+
+        @pl.when(last & (block == pl.num_programs(0) - 1))
+        def _():
+            expand_pool(pool_sums[...], busy_ref[0, 0], pool_out_ref)
+
+
+def edges(rows, rel_ids, relations, negatives, pool=None, pool_slot=None, busy=None):
     feature, endpoints = rows.shape
     parts = len(negatives)
     spans, part, _ = negatives[0].shape
@@ -398,29 +491,51 @@
     blocks = spans * steps
     edge_spec = pl.BlockSpec((feature, tile), lambda b, i: (0, b * steps + i))
     neg_spec = pl.BlockSpec((1, part, feature), lambda b, i: (b, 0, 0))
-    src_grad, dst_grad, *neg_grads = call(
-        functools.partial(edges_kernel, parts=parts),
+    operands = [rows, rows, rel_ids.reshape(spans, 1, width), relations, *negatives]
+    specs = [
+        edge_spec,
+        pl.BlockSpec((feature, tile), lambda b, i: (0, blocks + b * steps + i)),
+        pl.BlockSpec((1, 1, tile), lambda b, i: (b, 0, i)),
+        pl.BlockSpec(relations.shape, lambda b, i: (0, 0)),
+    ] + [neg_spec] * parts
+    out_specs = [edge_spec, edge_spec] + [neg_spec] * parts
+    out_shape = [jax.ShapeDtypeStruct((feature, endpoints // 2), BF16)] * 2
+    out_shape += [jax.ShapeDtypeStruct((spans, part, feature), BF16)] * parts
+    scratch = [
+        pltpu.VMEM((parts * part, feature), BF16),
+        pltpu.VMEM((feature, parts * part), BF16),
+        pltpu.VMEM((parts * part, feature), F32),
+    ]
+    if pool is not None:
+        slot = pool_slot.reshape(2 * spans, 1, width)
+        pool_spec = pl.BlockSpec(pool.shape, lambda b, i: (0, 0, 0))
+        operands += [pool, slot, slot, busy]
+        specs += [
+            pool_spec,
+            pl.BlockSpec((1, 1, tile), lambda b, i: (b, 0, i)),
+            pl.BlockSpec((1, 1, tile), lambda b, i: (spans + b, 0, i)),
+            pl.BlockSpec(memory_space=pltpu.SMEM),
+        ]
+        out_specs.append(pool_spec)
+        out_shape.append(jax.ShapeDtypeStruct(pool.shape, BF16))
+        count = compact_size(pool.shape[0] // RELAYS)
+        scratch += [
+            pltpu.VMEM((count, feature // LANES * LANES), BF16),
+            pltpu.VMEM((feature, count), BF16),
+            pltpu.VMEM((count, feature), F32),
+        ]
+    src_grad, dst_grad, *rest = call(
+        functools.partial(edges_kernel, parts=parts, pooled=pool is not None),
         "edges",
         6 * feature * parts * part * spans * width,
         4 * (rows.size + parts * negatives[0].size),
         grid=(spans, steps),
-        in_specs=[
-            edge_spec,
-            pl.BlockSpec((feature, tile), lambda b, i: (0, blocks + b * steps + i)),
-            pl.BlockSpec((1, 1, tile), lambda b, i: (b, 0, i)),
-            pl.BlockSpec(relations.shape, lambda b, i: (0, 0)),
-        ]
-        + [neg_spec] * parts,
-        out_specs=[edge_spec, edge_spec] + [neg_spec] * parts,
-        out_shape=[jax.ShapeDtypeStruct((feature, endpoints // 2), BF16)] * 2
-        + [jax.ShapeDtypeStruct((spans, part, feature), BF16)] * parts,
-        scratch_shapes=[
-            pltpu.VMEM((parts * part, feature), BF16),
-            pltpu.VMEM((feature, parts * part), BF16),
-            pltpu.VMEM((parts * part, feature), F32),
-        ],
-    )(rows, rows, rel_ids.reshape(spans, 1, width), relations, *negatives)
-    return src_grad, dst_grad, neg_grads
+        in_specs=specs,
+        out_specs=out_specs,
+        out_shape=out_shape,
+        scratch_shapes=scratch,
+    )(*operands)
+    return src_grad, dst_grad, rest
 
 
 def collect_kernel(src_ref, dst_ref, slot_ref, out_ref, *, group):
@@ -496,36 +611,6 @@
         scratch_shapes=[pltpu.VMEM(grads[0].shape, BF16)],
         input_output_aliases={0: 0},
     )(sent, slot, *grads)
-
-
-def collect_pool_kernel(src_ref, dst_ref, slot_ref, out_ref, *, group):
-    segments, width = slot_ref.shape
-    count = group * POOL
-    rows = jnp.zeros((count, src_ref.shape[0]), F32)
-    for segment in range(segments):
-        grads = src_ref if segment < segments // 2 else dst_ref
-        start = segment % (segments // 2) * width
-        hot = one_hot(count, slot_ref[segment : segment + 1, :], pl.program_id(0) * count)
-        rows = rows + dot(hot, grads[:, start : start + width], NT)
-    pack_all(out_ref, 0, POOL, rows, rows.T)
-
-
-def collect_pool(src_grad, dst_grad, slot, devices):
-    feature = src_grad.shape[0]
-    group = 8
-    slots = devices * POOL
-    height = packed_height(POOL, feature)
-    whole = pl.BlockSpec(src_grad.shape, lambda i: (0, 0))
-    return call(
-        functools.partial(collect_pool_kernel, group=group),
-        "collect_pool",
-        2 * feature * slots * slot.size,
-        2 * feature * (slots + slot.size),
-        grid=(devices // group,),
-        in_specs=[whole, whole, pl.BlockSpec(slot.shape, lambda i: (0, 0))],
-        out_specs=pl.BlockSpec((group, height, LANES), lambda i: (i, 0, 0)),
-        out_shape=jax.ShapeDtypeStruct((devices, height, LANES), BF16),
-    )(src_grad, dst_grad, slot)
 
 
 def add_kernel(*refs, rows, neg_cap, first):
@@ -590,36 +675,57 @@
     )(*operands)
 
 
-def add_pool_kernel(near_ref, far_ref, near_req_ref, far_req_ref, out_ref, packed, *flats, rows):
+def add_pool_kernel(*refs, rows, first):
+    one_ref, two_ref, one_req_ref, two_req_ref = refs[:4]
+    out_ref, packed, *flats = refs[4 + (not first) :]
     step = pl.program_id(0)
 
     @pl.when(step == 0)
     def _():
-        for recv_ref, flat in zip((near_ref, far_ref), flats):
+        for recv_ref, flat in zip((one_ref, two_ref), flats):
             unpack_all(recv_ref, 0, POOL, packed, flat)
 
-    total = dot(flats[0][...], one_hot(rows, near_req_ref[...], step * rows), NT)
-    out_ref[...] = total + dot(flats[1][...], one_hot(rows, far_req_ref[...], step * rows), NT)
-
-
-def add_pool(near, far, requests, feature, rows_dev):
+    total = dot(flats[0][...], one_hot(rows, one_req_ref[...], step * rows), NT)
+    total = total + dot(flats[1][...], one_hot(rows, two_req_ref[...], step * rows), NT)
+    if not first:
+        total = total + refs[4][...]
+    out_ref[...] = total
+
+
+def add_pool(one, two, requests, so_far, feature, rows_dev):
     rows = 512
-    devices = near.shape[0]
+    devices = one.shape[0]
     slots = devices * POOL
-    recv_spec = pl.BlockSpec(near.shape, lambda i: (0, 0, 0))
+    recv_spec = pl.BlockSpec(one.shape, lambda i: (0, 0, 0))
     req_spec = pl.BlockSpec((1, slots), lambda i: (0, 0))
+    rows_spec = pl.BlockSpec((feature, rows), lambda i: (0, i))
     packed, flat = unpack_scratch(devices, POOL, feature)
-    return call(
-        functools.partial(add_pool_kernel, rows=rows),
+    extra = [] if so_far is None else [so_far]
+    return call(
+        functools.partial(add_pool_kernel, rows=rows, first=so_far is None),
         "add_pool",
         4 * feature * slots * rows_dev,
         4 * feature * slots + 4 * feature * rows_dev,
         grid=(rows_dev // rows,),
-        in_specs=[recv_spec, recv_spec, req_spec, req_spec],
-        out_specs=pl.BlockSpec((feature, rows), lambda i: (0, i)),
+        in_specs=[recv_spec, recv_spec, req_spec, req_spec] + [rows_spec] * len(extra),
+        out_specs=rows_spec,
         out_shape=jax.ShapeDtypeStruct((feature, rows_dev), F32),
         scratch_shapes=[packed, flat, flat],
-    )(near, far, requests[0][None], requests[1][None])
+    )(one, two, requests[0][None], requests[1][None], *extra)
+
+
+def after(value, other):
+    anywhere = pl.BlockSpec(memory_space=pl.ANY)
+    return call(
+        lambda value_ref, other_ref, out_ref: None,
+        "after",
+        0,
+        0,
+        in_specs=[anywhere, anywhere],
+        out_specs=anywhere,
+        out_shape=jax.ShapeDtypeStruct(value.shape, value.dtype),
+        input_output_aliases={0: 0},
+    )(value, other)
 
 
 def exchange(value):
@@ -673,6 +779,7 @@
         neg_cap,
     )
     neg_slot = slots[-1]
+    busy = slots[-2]
     rel_rows = pad_lanes(rel_ids.reshape(spans, block_len), width, -1)
     asked = exchange(message)
     direct = [asked[:, c * LANES : (c + 1) * LANES] for c in range(chunks)]
@@ -702,23 +809,29 @@
 
     def pooled():
         start = chunks * LANES
-        core = me % RELAYS
         listed = asked[:, start : start + RELAYS * POOL].reshape(devices, RELAYS, POOL)
-        listed = listed.transpose(1, 0, 2).reshape(RELAYS, devices * POOL) - core * rows_dev
-        listed = [jnp.where(core == k, listed[0], listed[1]) for k in range(RELAYS)]
+        listed = listed.transpose(1, 0, 2).reshape(RELAYS, devices * POOL) - me * rows_dev
+        listed = listed[me ^ jnp.arange(RELAYS, dtype=jnp.int32)]
         back = exchange(gather(table, direct[0], neg_asked, neg_cap))
-        far = swap(gather_pool(table, listed[1], devices), 1)
-        relayed = gather_pool(table, listed[0], devices) + far
+        far = swap(gather_pool(table, listed[3], devices), 1)
+        far = swap(gather_pool(table, listed[2], devices) + far, 2)
+        near = swap(gather_pool(table, listed[1], devices), 1)
+        near = gather_pool(table, listed[0], devices) + near
         negatives = negatives_of(back)
         rows = spread(back, slots[0], None, feature)
-        rows = spread(exchange(relayed), slots[chunks], rows, feature, True)
-        src_grad, dst_grad, neg_grads = edges(rows, rel_rows, relations, negatives)
-        near = exchange(collect_pool(src_grad, dst_grad, slots[chunks], devices))
+        src_grad, dst_grad, rest = edges(
+            rows, rel_rows, relations, negatives, exchange(near + far), slots[chunks], busy
+        )
+        neg_grads, pool = rest[:-1], rest[-1]
+        near = exchange(pool)
+        far = swap(near, 2)
         sent = direct_sent(src_grad, dst_grad, neg_grads)
-        grad = add_pool(near, swap(near, 1), listed, feature, rows_dev)
+        grad = add_pool(near, swap(near, 1), listed[:2], None, feature, rows_dev)
+        far = after(far, grad)
+        grad = add_pool(far, swap(far, 1), listed[2:], grad, feature, rows_dev)
         return add_rows(sent, direct[0], grad, feature, rows_dev, neg_asked, neg_cap)
 
-    if chunks == 1 or sharers % RELAYS:
+    if chunks == 1 or sharers != RELAYS:
         return chunked().T
     fits = jnp.max(neg_asked[:, -1]) < 0
     return lax.cond(fits, pooled, chunked).T

time: 435 us -> 395 us (0.908)
  waiting for transfers between devices: 184 us -> 141 us
  starting transfers between devices: 28.8 us -> 33.4 us
    all_to_all x5, waiting for transfers between devices: 154 us -> 27.3 us  [exchange(): lax.all_to_all(value, ('shard', 'grp'), split_axis=0, concat_axis=0, tile...]
    ppermute x8 -> x12, waiting for transfers between devices: 29.9 us -> 113 us  [swap(): return lax.ppermute(value, 'grp', [(i, i ^ bit) for i in range(sharers)])]
    pallas_call x5, Pallas kernels: 84.3 us -> 70 us  [the longest x2 31.5 us: add_pool(): call(functools.partial(add_pool_kernel, rows=rows, first=so_far is None),...]
    pallas_call x2 -> x4, Pallas kernels: 25.7 us -> 37.1 us  [gather_pool(): call(functools.partial(gather_pool_kernel, group=group), 'gather_pool', 2...]
  transfers between devices with their start and end apart: 13 -> 17, of which waited for: 7 -> 11; matrix products, arithmetic and copies ran while one was open for 3% -> 3% of each run, Pallas kernels for 25% -> 29%
where the time goes in v6:
time: 395 us; the launch traced here: 388 us
  Pallas kernels  183 us (46%)
  waiting for transfers between devices  141 us (36%)
  starting transfers between devices  33.4 us (8%)
  local copies, waits for them, and re-layouts  15.2 us (4%)
  other arithmetic  8.51 us (2%)
  loops' own time  6.85 us (2%)
    ppermute x12, waiting for transfers between devices, swap(): return lax.ppermute(value, 'grp', [(i, i ^ bit) for i in range(sharers)])  113 us
    pallas_call x4, Pallas kernels, gather_pool(): call(functools.partial(gather_pool_kernel, group=group), 'gather_pool', 2...  37.1 us
    pallas_call x2, Pallas kernels, add_pool(): call(functools.partial(add_pool_kernel, rows=rows, first=so_far is None),...  31.5 us
    all_to_all x5, waiting for transfers between devices, exchange(): lax.all_to_all(value, ('shard', 'grp'), split_axis=0, concat_axis=0, tile...  27.3 us
    all_to_all x5, starting transfers between devices, exchange(): lax.all_to_all(value, ('shard', 'grp'), split_axis=0, concat_axis=0, tile...  25 us
    pallas_call x1, Pallas kernels, add_rows(): call(functools.partial(add_kernel, rows=rows, neg_cap=neg_cap, first=so_f...  23.9 us
    pallas_call x1, Pallas kernels, gather(): call(functools.partial(gather_kernel, group=group, neg_cap=neg_cap), 'gat...  23.6 us
    pallas_call x1, Pallas kernels, edges(): call(functools.partial(edges_kernel, parts=parts, pooled=pool is not None...  19.3 us
  transfers between devices with their start and end apart: 17, of which 11 were waited for; matrix products, arithmetic and copies ran while one was open for 3% of the time, Pallas kernels for 29%

profile of v6, /device:TPU:0, one launch (start us, length us, event | category | flops | bytes accessed | tf_op | source)
XLA Modules:
  0.0 388.5 jit_solution(11899312569561358111)
XLA Ops:
  0.0 0.8 reshape.51
  0.8 0.8 reshape.52
  1.6 0.6 pad.13.own_ref
  2.2 0.6 pad.12.ends_ref
  2.8 3.5 slots.1
  6.4 1.6 copy.21
  8.0 7.3 %all-to-all-start.8 = ((s32[32,1,640]{2,1,0:T(1,128)}), s32[32,1,640]{2,1,0:T(1,128)S(1)}, u32[]{:S(2)}, u32[]{:S(2)}) async-start(s32[32,1,640]{2,1,0:T(1,128)} %copy.21), calls=%async_computation.8 | async-start | bytes 163840 | tf_op jit(solution)/shard_map/all_to_all | solution.py:732
  15.3 3.3 convert_bitcast_fusion
  18.7 1.7 copy.22
  20.4 2.4 all-to-all-done.8
  22.9 0.7 slice_reduce_fusion
  24.3 363.2 %conditional.1 = (f32[400,4096]{1,0:T(8,128)}) conditional(s32[]{:T(128)} %convert_element_type.9, (s32[32,640]{1,0:T(8,128)S(1)}, bf16[400,4096]{1,0:T(8,128)(2,1)S(1)}, s32[4,1024]{1,0:T(4,128)S(1)}, s32[32,128]{1,0:T(8,128)S(1)}, s32[32,128]{1,0:T(8,128)S(1)}, /*index=5*/s32[4,1024]{1,0:T(4,128)S(1)}, s32[2,1024]{1,0:T(2,128)S(1)}, ...), branch_computations={%region_1.2_spmd, %region_2.3_spmd} | conditional | flops 116601651200 | bytes 207426656 | solution.py:837
  30.8 23.6 %gather_rows.5 = bf16[32,512,128]{2,1,0:T(8,128)(2,1)} custom-call(bf16[400,4096]{1,0:T(8,128)(2,1)S(1)} %get-tuple-element.64.table_ref, s32[32,128]{1,0:T(8,128)S(1)} %get-tuple-element.65.refs_0_.refs_1_, s32[32,128]{1,0:T(8,128)S(1)} %get-tuple-element.66.refs_1_.refs_2_), custom_call_target="tpu_custom_call" | custom-call | flops 16777216000 | bytes 7372800 | tf_op jit(solution)/shard_map/cond/branch_1_fun/gather_rows/pallas_call | solution.py:234
  54.4 3.6 all-to-all-start.4
  58.0 0.1 sub.12
  58.1 0.1 sub.14
  58.2 0.6 gather_fusion
  58.8 0.6 fusion.1
  59.4 9.3 %gather_pool.7 = bf16[32,160,128]{2,1,0:T(8,128)(2,1)} custom-call(bf16[400,4096]{1,0:T(8,128)(2,1)S(1)} %get-tuple-element.64.table_ref, s32[4,1,384]{2,1,0:T(1,128)} %bitcast.26), custom_call_target="tpu_custom_call" | custom-call | flops 5033164800 | bytes 4505600 | tf_op jit(solution)/shard_map/cond/branch_1_fun/gather_pool/pallas_call | solution.py:259
  68.7 0.1 collective-permute-start.10
  68.8 9.3 %gather_pool.5 = bf16[32,160,128]{2,1,0:T(8,128)(2,1)} custom-call(bf16[400,4096]{1,0:T(8,128)(2,1)S(1)} %get-tuple-element.64.table_ref, s32[4,1,384]{2,1,0:T(1,128)} %bitcast.27), custom_call_target="tpu_custom_call" | custom-call | flops 5033164800 | bytes 4505600 | tf_op jit(solution)/shard_map/cond/branch_1_fun/gather_pool/pallas_call | solution.py:259
  78.1 0.4 collective-permute-start.9
  78.5 9.3 %gather_pool.6 = bf16[32,160,128]{2,1,0:T(8,128)(2,1)} custom-call(bf16[400,4096]{1,0:T(8,128)(2,1)S(1)} %get-tuple-element.64.table_ref, s32[4,1,384]{2,1,0:T(1,128)} %bitcast.25), custom_call_target="tpu_custom_call" | custom-call | flops 5033164800 | bytes 4505600 | tf_op jit(solution)/shard_map/cond/branch_1_fun/gather_pool/pallas_call | solution.py:259
  87.8 1.7 add.19
  89.6 1.7 collective-permute-start.11
  91.3 9.2 %gather_pool.4 = bf16[32,160,128]{2,1,0:T(8,128)(2,1)} custom-call(bf16[400,4096]{1,0:T(8,128)(2,1)S(1)} %get-tuple-element.64.table_ref, s32[4,1,384]{2,1,0:T(1,128)} %bitcast.28), custom_call_target="tpu_custom_call" | custom-call | flops 5033164800 | bytes 4505600 | tf_op jit(solution)/shard_map/cond/branch_1_fun/gather_pool/pallas_call | solution.py:259
  100.5 32.7 %collective-permute-done.11 = bf16[32,160,128]{2,1,0:T(8,128)(2,1)S(1)} collective-permute-done((bf16[32,160,128]{2,1,0:T(8,128)(2,1)S(1)}, bf16[32,160,128]{2,1,0:T(8,128)(2,1)S(1)}, u32[]{:S(2)}, u32[]{:S(2)}) %collective-permute-start.11) | collective-permute-done | bytes 1310752 | tf_op jit(solution)/shard_map/cond/branch_1_fun/ppermute | solution.py:737
  133.2 2.7 add_add_fusion
  135.9 16.0 %all-to-all-done.4.refs_0_.back_ref = bf16[32,512,128]{2,1,0:T(8,128)(2,1)} async-done(((bf16[32,512,128]{2,1,0:T(8,128)(2,1)}), bf16[32,512,128]{2,1,0:T(8,128)(2,1)}, u32[]{:S(2)}, u32[]{:S(2)}) %all-to-all-start.4) | async-done | bytes 4194336 | tf_op jit(solution)/shard_map/cond/branch_1_fun/all_to_all | solution.py:732
  151.9 4.3 %all-to-all-start.5 = ((bf16[32,160,128]{2,1,0:T(8,128)(2,1)}), bf16[32,160,128]{2,1,0:T(8,128)(2,1)S(1)}, u32[]{:S(2)}, u32[]{:S(2)}) async-start(bf16[32,160,128]{2,1,0:T(8,128)(2,1)} %add_add_fusion), calls=%async_computation.5 | async-start | bytes 2621440 | tf_op jit(solution)/shard_map/cond/branch_1_fun/all_to_all | solution.py:732
  156.2 0.6 reshape.46.refs_2_
  156.8 0.6 reshape.47.refs_9_.refs_10_
  157.5 0.6 reshape.45.refs_1_
  158.1 2.9 spread_negatives.3.refs_4_
  161.0 1.6 collective-permute-start.8
  162.6 0.4 collective-permute-start.7
  163.0 19.3 %spread_rows.5.refs_0_.refs_1_ = bf16[400,4096]{1,0:T(8,128)(2,1)} custom-call(bf16[32,512,128]{2,1,0:T(8,128)(2,1)} %all-to-all-done.4.refs_0_.back_ref, s32[4,1,1024]{2,1,0:T(1,128)} %reshape.45.refs_1_), custom_call_target="tpu_custom_call" | custom-call | flops 13421772800 | bytes 6553600 | tf_op jit(solution)/shard_map/cond/branch_1_fun/spread_rows/pallas_call | solution.py:329
  182.3 6.2 %all-to-all-done.5.refs_8_ = bf16[32,160,128]{2,1,0:T(8,128)(2,1)S(1)} async-done(((bf16[32,160,128]{2,1,0:T(8,128)(2,1)}), bf16[32,160,128]{2,1,0:T(8,128)(2,1)S(1)}, u32[]{:S(2)}, u32[]{:S(2)}) %all-to-all-start.5) | async-done | bytes 1310752 | tf_op jit(solution)/shard_map/cond/branch_1_fun/all_to_all | solution.py:732
  188.5 7.1 %collective-permute-done.7.refs_6_ = bf16[2,256,400]{2,1,0:T(8,128)(2,1)S(1)} collective-permute-done((bf16[2,256,400]{2,1,0:T(8,128)(2,1)}, bf16[2,256,400]{2,1,0:T(8,128)(2,1)S(1)}, u32[]{:S(2)}, u32[]{:S(2)}) %collective-permute-start.7) | collective-permute-done | bytes 409632 | tf_op jit(solution)/shard_map/cond/branch_1_fun/ppermute | solution.py:737
  195.6 0.8 copy-done.27
  196.4 0.2 copy-done.28
  196.6 19.3 %edges.3 = (bf16[400,2048]{1,0:T(8,128)(2,1)}, bf16[400,2048]{1,0:T(8,128)(2,1)}, bf16[2,256,400]{2,1,0:T(8,128)(2,1)}, bf16[2,256,400]{2,1,0:T(8,128)(2,1)}, bf...) custom-call(bf16[400,4096]{1,0:T(8,128)(2,1)} %spread_rows.5.refs_0_.refs_1_, ...), custom_call_target="tpu_custom_call" | custom-call | flops 5033164800 | bytes 9830400 | tf_op jit(solution)/shard_map/cond/branch_1_fun/edges/pallas_call | solution.py:527
  215.9 4.6 %all-to-all-start.7 = ((bf16[32,160,128]{2,1,0:T(8,128)(2,1)}), bf16[32,160,128]{2,1,0:T(8,128)(2,1)S(1)}, u32[]{:S(2)}, u32[]{:S(2)}) async-start(bf16[32,160,128]{2,1,0:T(8,128)(2,1)} %get-tuple-element.81), calls=%async_computation.7 | async-start | bytes 2621440 | tf_op jit(solution)/shard_map/cond/branch_1_fun/all_to_all | solution.py:732
  220.5 0.3 collective-permute-start.12
  220.8 1.7 collective-permute-start.13
  222.5 18.0 %collect_grads.5.sent_ref = bf16[32,512,128]{2,1,0:T(8,128)(2,1)} custom-call(bf16[400,2048]{1,0:T(8,128)(2,1)} %get-tuple-element.75.src_ref, bf16[400,2048]{1,0:T(8,128)(2,1)} %get-tuple-element.76.dst_ref, s32[4,1024]{1,0:T(4,128)S(1)} %get-tuple-element.67.slot_ref), custom_call_target="tpu_custom_call" | custom-call | flops 13421772800 | bytes 6553600 | tf_op jit(solution)/shard_map/cond/branch_1_fun/collect_grads/pallas_call | solution.py:563
  240.5 6.9 %collective-permute-done.13.refs_2_ = bf16[2,256,400]{2,1,0:T(8,128)(2,1)S(1)} collective-permute-done((bf16[2,256,400]{2,1,0:T(8,128)(2,1)}, bf16[2,256,400]{2,1,0:T(8,128)(2,1)S(1)}, u32[]{:S(2)}, u32[]{:S(2)}) %collective-permute-start.13) | collective-permute-done | bytes 409632 | tf_op jit(solution)/shard_map/cond/branch_1_fun/ppermute | solution.py:737
  247.4 12.0 %collective-permute-done.14.refs_3_ = bf16[2,256,400]{2,1,0:T(8,128)(2,1)S(1)} collective-permute-done((bf16[2,256,400]{2,1,0:T(8,128)(2,1)}, bf16[2,256,400]{2,1,0:T(8,128)(2,1)S(1)}, u32[]{:S(2)}, u32[]{:S(2)}) %collective-permute-start.14) | collective-permute-done | bytes 409632 | tf_op jit(solution)/shard_map/cond/branch_1_fun/ppermute | solution.py:737
  259.4 0.8 copy-done.12
  260.2 3.8 collect_negatives.3
  264.0 5.2 %all-to-all-start.6 = ((bf16[32,512,128]{2,1,0:T(8,128)(2,1)}), bf16[32,512,128]{2,1,0:T(8,128)(2,1)}, u32[]{:S(2)}, u32[]{:S(2)}) async-start(bf16[32,512,128]{2,1,0:T(8,128)(2,1)} %collect_negatives.3), calls=%async_computation.6 | async-start | bytes 8388608 | tf_op jit(solution)/shard_map/cond/branch_1_fun/all_to_all | solution.py:732
  269.2 0.4 collective-permute-start.16
  269.6 1.7 collective-permute-start.15
  271.3 1.0 collective-permute-done.16.refs_1_
  272.3 1.1 copy-done.24
  273.4 15.5 %add_pool.2.other_ref.refs_4_ = f32[400,4096]{1,0:T(8,128)} custom-call(bf16[32,160,128]{2,1,0:T(8,128)(2,1)} %copy-done.5, bf16[32,160,128]{2,1,0:T(8,128)(2,1)} %copy-done.24, s32[1,1536]{1,0:T(1,128)} %get-tuple-element.96.refs_2_, s32[1,1536]{1,0:T(1,128)} %get-tuple-element.94.refs_3_), custom_call_target="tpu_custom_call" | custom-call | flops 10066329600 | bytes 9011200 | tf_op jit(solution)/shard_map/cond/branch_1_fun/add_pool/pallas_call | solution.py:704
  288.9 50.4 %collective-permute-done.15.value_ref = bf16[32,160,128]{2,1,0:T(8,128)(2,1)S(1)} collective-permute-done((bf16[32,160,128]{2,1,0:T(8,128)(2,1)S(1)}, bf16[32,160,128]{2,1,0:T(8,128)(2,1)S(1)}, u32[]{:S(2)}, u32[]{:S(2)}) %collective-permute-start.15) | collective-permute-done | bytes 1310752 | tf_op jit(solution)/shard_map/cond/branch_1_fun/ppermute | solution.py:737
  339.3 1.1 copy-done.4
  340.4 3.2 collective-permute-done.17.refs_1_
  343.7 1.0 copy-done.25
  344.7 16.0 %add_pool.3.refs_3_ = f32[400,4096]{1,0:T(8,128)} custom-call(bf16[32,160,128]{2,1,0:T(8,128)(2,1)} %after.1.refs_0_, bf16[32,160,128]{2,1,0:T(8,128)(2,1)} %copy-done.25, s32[1,1536]{1,0:T(1,128)} %get-tuple-element.95.refs_2_, s32[1,1536]{1,0:T(1,128)} %get-tuple-element.97.refs_3_, f32[400,4096]{1,0:T(8,128)} %add_pool.2.other_ref.refs_4_), custom_call_target="tpu_custom_call" | custom-call | flops 10066329600 | bytes 9011200 | tf_op jit(solution)/shard_map/cond/branch_1_fun/add_pool/pallas_call | solution.py:704
  360.7 2.7 all-to-all-done.6.refs_0_
  363.4 23.9 %add_grads.5 = f32[400,4096]{1,0:T(8,128)} custom-call(bf16[32,512,128]{2,1,0:T(8,128)(2,1)} %all-to-all-done.6.refs_0_, s32[32,128]{1,0:T(8,128)S(1)} %copy-done.22, s32[32,128]{1,0:T(8,128)S(1)} %copy-done.18, f32[400,4096]{1,0:T(8,128)} %add_pool.3.refs_3_), custom_call_target="tpu_custom_call" | custom-call | flops 13421772800 | bytes 16384000 | tf_op jit(solution)/shard_map/cond/branch_1_fun/add_grads/pallas_call | solution.py:665
  387.4 0.7 copy-done.1
  (51 shorter events, 0.3 us)
Async XLA Ops:
  0.0 1.6 copy-start
  8.0 14.9 %all-to-all-start.8 = ((s32[32,1,640]{2,1,0:T(1,128)}), s32[32,1,640]{2,1,0:T(1,128)S(1)}, u32[]{:S(2)}, u32[]{:S(2)}) async-start(s32[32,1,640]{2,1,0:T(1,128)} %copy.21), calls=%async_computation.8 | async-start | bytes 163840 | tf_op jit(solution)/shard_map/all_to_all | solution.py:732
  15.3 3.3 copy-start.23
  30.8 23.6 %copy-start.17 = (s32[32,128]{1,0:T(8,128)}, s32[32,128]{1,0:T(8,128)S(1)}, u32[]{:S(2)}) copy-start(s32[32,128]{1,0:T(8,128)S(1)} %get-tuple-element.66.refs_1_.refs_2_) | copy-start | bytes 49156 | tf_op jit(solution)/shard_map/cond
  30.8 23.6 %copy-start.21 = (s32[32,128]{1,0:T(8,128)}, s32[32,128]{1,0:T(8,128)S(1)}, u32[]{:S(2)}) copy-start(s32[32,128]{1,0:T(8,128)S(1)} %get-tuple-element.65.refs_0_.refs_1_) | copy-start | bytes 49156 | tf_op jit(solution)/shard_map/cond
  54.4 97.5 %all-to-all-start.4 = ((bf16[32,512,128]{2,1,0:T(8,128)(2,1)}), bf16[32,512,128]{2,1,0:T(8,128)(2,1)}, u32[]{:S(2)}, u32[]{:S(2)}) async-start(bf16[32,512,128]{2,1,0:T(8,128)(2,1)} %gather_rows.5), calls=%async_computation.4 | async-start | bytes 8388608 | tf_op jit(solution)/shard_map/cond/branch_1_fun/all_to_all | solution.py:732
  68.7 19.1 %collective-permute-start.10 = (bf16[32,160,128]{2,1,0:T(8,128)(2,1)}, bf16[32,160,128]{2,1,0:T(8,128)(2,1)S(1)}, u32[]{:S(2)}, u32[]{:S(2)}) collective-permute-start(bf16[32,160,128]{2,1,0:T(8,128)(2,1)} %gather_pool.7), channel_id=1, source_target_pairs={{0,1},{1,0},{2,3},{3,2},{4,5},{5,4},{6,7},{7,6},{8,9},{9,8},{10,11... | collective-permute-start | bytes 3932168 | tf_op jit(solution)/shard_map/cond/branch_1_fun/ppermute | solution.py:737
  78.1 22.4 %collective-permute-start.9 = (bf16[32,160,128]{2,1,0:T(8,128)(2,1)}, bf16[32,160,128]{2,1,0:T(8,128)(2,1)S(1)}, u32[]{:S(2)}, u32[]{:S(2)}) collective-permute-start(bf16[32,160,128]{2,1,0:T(8,128)(2,1)} %gather_pool.5), channel_id=1, source_target_pairs={{0,1},{1,0},{2,3},{3,2},{4,5},{5,4},{6,7},{7,6},{8,9},{9,8},{10,11... | collective-permute-start | bytes 3932168 | tf_op jit(solution)/shard_map/cond/branch_1_fun/ppermute | solution.py:737
  89.6 43.7 %collective-permute-start.11 = (bf16[32,160,128]{2,1,0:T(8,128)(2,1)S(1)}, bf16[32,160,128]{2,1,0:T(8,128)(2,1)S(1)}, u32[]{:S(2)}, u32[]{:S(2)}) collective-permute-start(bf16[32,160,128]{2,1,0:T(8,128)(2,1)S(1)} %add.19), channel_id=1, source_target_pairs={{0,2},{1,3},{2,0},{3,1},{4,6},{5,7},{6,4},{7,5},{8,10},{9,11},{10,... | collective-permute-start | bytes 3932168 | tf_op jit(solution)/shard_map/cond/branch_1_fun/ppermute | solution.py:737
  151.9 36.6 %all-to-all-start.5 = ((bf16[32,160,128]{2,1,0:T(8,128)(2,1)}), bf16[32,160,128]{2,1,0:T(8,128)(2,1)S(1)}, u32[]{:S(2)}, u32[]{:S(2)}) async-start(bf16[32,160,128]{2,1,0:T(8,128)(2,1)} %add_add_fusion), calls=%async_computation.5 | async-start | bytes 2621440 | tf_op jit(solution)/shard_map/cond/branch_1_fun/all_to_all | solution.py:732
  161.0 35.6 %copy-start.14 = (f32[400,64]{1,0:T(8,128)S(1)}, f32[400,64]{1,0:T(8,128)}, u32[]{:S(2)}) copy-start(f32[400,64]{1,0:T(8,128)} %get-tuple-element.69.refs_3_) | copy-start | bytes 307204 | tf_op jit(solution)/shard_map/cond
  161.0 27.5 %collective-permute-start.8 = (bf16[2,256,400]{2,1,0:T(8,128)(2,1)}, bf16[2,256,400]{2,1,0:T(8,128)(2,1)S(1)}, u32[]{:S(2)}, u32[]{:S(2)}) collective-permute-start(bf16[2,256,400]{2,1,0:T(8,128)(2,1)} %spread_negatives.3.refs_4_), channel_id=1, source_target_pairs={{0,3},{1,2},{2,1},{3,0},{4,7},{5,6},{6,5},{7,4},{8,11},{9,10},{10,... | collective-permute-start | bytes 1228808 | tf_op jit(solution)/shard_map/cond/branch_1_fun/ppermute | solution.py:737
  162.6 33.0 %collective-permute-start.7 = (bf16[2,256,400]{2,1,0:T(8,128)(2,1)}, bf16[2,256,400]{2,1,0:T(8,128)(2,1)S(1)}, u32[]{:S(2)}, u32[]{:S(2)}) collective-permute-start(bf16[2,256,400]{2,1,0:T(8,128)(2,1)} %spread_negatives.3.refs_4_), channel_id=1, source_target_pairs={{0,2},{1,3},{2,0},{3,1},{4,6},{5,7},{6,4},{7,5},{8,10},{9,11},{10,... | collective-permute-start | bytes 1228808 | tf_op jit(solution)/shard_map/cond/branch_1_fun/ppermute | solution.py:737
  163.0 32.6 %collective-permute-start.6 = (bf16[2,256,400]{2,1,0:T(8,128)(2,1)}, bf16[2,256,400]{2,1,0:T(8,128)(2,1)S(1)}, u32[]{:S(2)}, u32[]{:S(2)}) collective-permute-start(bf16[2,256,400]{2,1,0:T(8,128)(2,1)} %spread_negatives.3.refs_4_), channel_id=1, source_target_pairs={{0,1},{1,0},{2,3},{3,2},{4,5},{5,4},{6,7},{7,6},{8,9},{9,8},{10,11... | collective-permute-start | bytes 1228808 | tf_op jit(solution)/shard_map/cond/branch_1_fun/ppermute | solution.py:737
  188.5 7.2 %copy-start.6 = (bf16[32,160,128]{2,1,0:T(8,128)(2,1)}, bf16[32,160,128]{2,1,0:T(8,128)(2,1)S(1)}, u32[]{:S(2)}) copy-start(bf16[32,160,128]{2,1,0:T(8,128)(2,1)S(1)} %all-to-all-done.5.refs_8_) | copy-start | bytes 3932164 | tf_op jit(solution)/shard_map/cond
  188.5 7.2 %copy-start.26 = (bf16[2,256,400]{2,1,0:T(8,128)(2,1)}, bf16[2,256,400]{2,1,0:T(8,128)(2,1)S(1)}, u32[]{:S(2)}) copy-start(bf16[2,256,400]{2,1,0:T(8,128)(2,1)S(1)} %collective-permute-done.8.refs_7_) | copy-start | bytes 1228804 | tf_op jit(solution)/shard_map/cond
  195.6 0.8 copy-start.27
  195.6 1.0 copy-start.28
  215.9 48.1 %all-to-all-start.7 = ((bf16[32,160,128]{2,1,0:T(8,128)(2,1)}), bf16[32,160,128]{2,1,0:T(8,128)(2,1)S(1)}, u32[]{:S(2)}, u32[]{:S(2)}) async-start(bf16[32,160,128]{2,1,0:T(8,128)(2,1)} %get-tuple-element.81), calls=%async_computation.7 | async-start | bytes 2621440 | tf_op jit(solution)/shard_map/cond/branch_1_fun/all_to_all | solution.py:732
  220.5 20.0 %collective-permute-start.12 = (bf16[2,256,400]{2,1,0:T(8,128)(2,1)}, bf16[2,256,400]{2,1,0:T(8,128)(2,1)S(1)}, u32[]{:S(2)}, u32[]{:S(2)}) collective-permute-start(bf16[2,256,400]{2,1,0:T(8,128)(2,1)} %get-tuple-element.78), channel_id=1, source_target_pairs={{0,1},{1,0},{2,3},{3,2},{4,5},{5,4},{6,7},{7,6},{8,9},{9,8},{10,11... | collective-permute-start | bytes 1228808 | tf_op jit(solution)/shard_map/cond/branch_1_fun/ppermute | solution.py:737
  220.8 26.5 %collective-permute-start.13 = (bf16[2,256,400]{2,1,0:T(8,128)(2,1)}, bf16[2,256,400]{2,1,0:T(8,128)(2,1)S(1)}, u32[]{:S(2)}, u32[]{:S(2)}) collective-permute-start(bf16[2,256,400]{2,1,0:T(8,128)(2,1)} %get-tuple-element.79), channel_id=1, source_target_pairs={{0,2},{1,3},{2,0},{3,1},{4,6},{5,7},{6,4},{7,5},{8,10},{9,11},{10,... | collective-permute-start | bytes 1228808 | tf_op jit(solution)/shard_map/cond/branch_1_fun/ppermute | solution.py:737
  222.5 36.9 %collective-permute-start.14 = (bf16[2,256,400]{2,1,0:T(8,128)(2,1)}, bf16[2,256,400]{2,1,0:T(8,128)(2,1)S(1)}, u32[]{:S(2)}, u32[]{:S(2)}) collective-permute-start(bf16[2,256,400]{2,1,0:T(8,128)(2,1)} %get-tuple-element.80), channel_id=1, source_target_pairs={{0,3},{1,2},{2,1},{3,0},{4,7},{5,6},{6,5},{7,4},{8,11},{9,10},{10,... | collective-permute-start | bytes 1228808 | tf_op jit(solution)/shard_map/cond/branch_1_fun/ppermute | solution.py:737
  240.5 18.9 %copy-start.8 = (bf16[2,256,400]{2,1,0:T(8,128)(2,1)}, bf16[2,256,400]{2,1,0:T(8,128)(2,1)S(1)}, u32[]{:S(2)}) copy-start(bf16[2,256,400]{2,1,0:T(8,128)(2,1)S(1)} %collective-permute-done.12.refs_1_) | copy-start | bytes 1228804 | tf_op jit(solution)/shard_map/cond
  247.4 12.0 %copy-start.10 = (bf16[2,256,400]{2,1,0:T(8,128)(2,1)}, bf16[2,256,400]{2,1,0:T(8,128)(2,1)S(1)}, u32[]{:S(2)}) copy-start(bf16[2,256,400]{2,1,0:T(8,128)(2,1)S(1)} %collective-permute-done.13.refs_2_) | copy-start | bytes 1228804 | tf_op jit(solution)/shard_map/cond
  259.4 0.8 copy-start.12
  264.0 5.7 %copy-start.5 = (bf16[32,160,128]{2,1,0:T(8,128)(2,1)}, bf16[32,160,128]{2,1,0:T(8,128)(2,1)S(1)}, u32[]{:S(2)}) copy-start(bf16[32,160,128]{2,1,0:T(8,128)(2,1)S(1)} %all-to-all-done.7.refs_0_) | copy-start | bytes 3932164 | tf_op jit(solution)/shard_map/cond
  264.0 99.4 %all-to-all-start.6 = ((bf16[32,512,128]{2,1,0:T(8,128)(2,1)}), bf16[32,512,128]{2,1,0:T(8,128)(2,1)}, u32[]{:S(2)}, u32[]{:S(2)}) async-start(bf16[32,512,128]{2,1,0:T(8,128)(2,1)} %collect_negatives.3), calls=%async_computation.6 | async-start | bytes 8388608 | tf_op jit(solution)/shard_map/cond/branch_1_fun/all_to_all | solution.py:732
  269.2 3.1 collective-permute-start.16
  269.6 69.7 %collective-permute-start.15 = (bf16[32,160,128]{2,1,0:T(8,128)(2,1)S(1)}, bf16[32,160,128]{2,1,0:T(8,128)(2,1)S(1)}, u32[]{:S(2)}, u32[]{:S(2)}) collective-permute-start(bf16[32,160,128]{2,1,0:T(8,128)(2,1)S(1)} %all-to-all-done.7.refs_0_), channel_id=1, source_target_pairs={{0,2},{1,3},{2,0},{3,1},{4,6},{5,7},{6,4},{7,5},{8,10},{9,11},{10,... | collective-permute-start | bytes 3932168 | tf_op jit(solution)/shard_map/cond/branch_1_fun/ppermute | solution.py:737
  272.3 1.1 copy-start.24
  339.3 1.1 copy-start.4
  340.4 23.0 %copy-start.18 = (s32[32,128]{1,0:T(8,128)S(1)}, s32[32,128]{1,0:T(8,128)}, u32[]{:S(2)}) copy-start(s32[32,128]{1,0:T(8,128)} %copy-done.17) | copy-start | bytes 49156 | tf_op jit(solution)/shard_map/cond
  340.4 23.0 %copy-start.22 = (s32[32,128]{1,0:T(8,128)S(1)}, s32[32,128]{1,0:T(8,128)}, u32[]{:S(2)}) copy-start(s32[32,128]{1,0:T(8,128)} %copy-done.21) | copy-start | bytes 49156 | tf_op jit(solution)/shard_map/cond
  340.4 3.2 collective-permute-start.17
  343.7 1.0 copy-start.25
  387.4 0.7 copy-start.1

commit v7 on v6

--- a/solution.py
+++ b/solution.py
@@ -738,11 +738,28 @@
 
 
 def share_out(value):
-    return [value] + [swap(value, k) for k in range(1, lax.axis_size("grp"))]
+    sharers = lax.axis_size("grp")
+    blocks = {0: value}
+    bit = sharers // 2
+    while bit:
+        for k in list(blocks):
+            blocks[k ^ bit] = swap(blocks[k], bit)
+        bit //= 2
+    return [blocks[k] for k in range(sharers)]
 
 
 def trade(blocks):
-    return blocks[:1] + [swap(block, k) for k, block in enumerate(blocks) if k]
+    sharers = len(blocks)
+    terms = [[block] for block in blocks]
+    bit = 1
+    while bit < sharers:
+        for k in range(0, sharers, 2 * bit):
+            total = terms[k ^ bit][0].astype(F32)
+            for term in terms[k ^ bit][1:]:
+                total = total + term.astype(F32)
+            terms[k].append(swap(total.astype(BF16), bit))
+        bit *= 2
+    return terms[0]
 
 
 def pad_lanes(value, width, fill):
@@ -785,6 +802,8 @@
     direct = [asked[:, c * LANES : (c + 1) * LANES] for c in range(chunks)]
     neg_asked = asked[:, -LANES:]
 
+    sent_rows = gather(table, direct[0], neg_asked, neg_cap)
+
     def negatives_of(back):
         return share_out(spread_neg(back, neg_slot, neg_cap, feature))
 
@@ -793,7 +812,7 @@
         return exchange(collect_neg(sent, neg_slot, trade(neg_grads), neg_cap))
 
     def chunked():
-        back = [exchange(gather(table, direct[0], neg_asked, neg_cap))]
+        back = [exchange(sent_rows)]
         back += [exchange(gather(table, direct[c])) for c in range(1, chunks)]
         negatives = negatives_of(back[0])
         rows = None
@@ -812,7 +831,7 @@
         listed = asked[:, start : start + RELAYS * POOL].reshape(devices, RELAYS, POOL)
         listed = listed.transpose(1, 0, 2).reshape(RELAYS, devices * POOL) - me * rows_dev
         listed = listed[me ^ jnp.arange(RELAYS, dtype=jnp.int32)]
-        back = exchange(gather(table, direct[0], neg_asked, neg_cap))
+        back = exchange(sent_rows)
         far = swap(gather_pool(table, listed[3], devices), 1)
         far = swap(gather_pool(table, listed[2], devices) + far, 2)
         near = swap(gather_pool(table, listed[1], devices), 1)

time: 395 us -> 391 us (0.990)
  waiting for transfers between devices: 141 us -> 135 us
    all_to_all x5, waiting for transfers between devices: 27.3 us -> 22.5 us  [exchange(): lax.all_to_all(value, ('shard', 'grp'), split_axis=0, concat_axis=0, tile...]
  transfers between devices with their start and end apart: 17 -> 17, of which waited for: 11 -> 11; matrix products, arithmetic and copies ran while one was open for 3% -> 4% of each run, Pallas kernels for 29% -> 29%
where the time goes in v7:
time: 391 us; the launch traced here: 384 us
  Pallas kernels  183 us (47%)
  waiting for transfers between devices  135 us (35%)
  starting transfers between devices  34.2 us (9%)
  local copies, waits for them, and re-layouts  16.2 us (4%)
  other arithmetic  9.74 us (2%)
  loops' own time  5.76 us (1%)
    ppermute x12, waiting for transfers between devices, swap(): return lax.ppermute(value, 'grp', [(i, i ^ bit) for i in range(sharers)])  112 us
    pallas_call x4, Pallas kernels, gather_pool(): call(functools.partial(gather_pool_kernel, group=group), 'gather_pool', 2...  37.1 us
    pallas_call x2, Pallas kernels, add_pool(): call(functools.partial(add_pool_kernel, rows=rows, first=so_far is None),...  31.5 us
    all_to_all x5, starting transfers between devices, exchange(): lax.all_to_all(value, ('shard', 'grp'), split_axis=0, concat_axis=0, tile...  25.9 us
    pallas_call x1, Pallas kernels, add_rows(): call(functools.partial(add_kernel, rows=rows, neg_cap=neg_cap, first=so_f...  23.8 us
    pallas_call x1, Pallas kernels, gather(): call(functools.partial(gather_kernel, group=group, neg_cap=neg_cap), 'gat...  23.6 us
    all_to_all x5, waiting for transfers between devices, exchange(): lax.all_to_all(value, ('shard', 'grp'), split_axis=0, concat_axis=0, tile...  22.5 us
    pallas_call x1, Pallas kernels, spread(): call(functools.partial(spread_kernel, first=so_far is None), 'spread_rows...  19.5 us
  transfers between devices with their start and end apart: 17, of which 11 were waited for; matrix products, arithmetic and copies ran while one was open for 4% of the time, Pallas kernels for 29%

profile of v7, /device:TPU:0, one launch (start us, length us, event | category | flops | bytes accessed | tf_op | source)
XLA Modules:
  0.0 384.3 jit_solution(4923210287728626230)
XLA Ops:
  0.0 0.8 reshape.51
  0.8 0.8 reshape.52
  1.6 0.6 pad.13.own_ref
  2.2 0.6 pad.12.ends_ref
  2.8 3.5 slots.1
  6.4 1.6 copy.21
  8.0 7.3 %all-to-all-start.8 = ((s32[32,1,640]{2,1,0:T(1,128)}), s32[32,1,640]{2,1,0:T(1,128)S(1)}, u32[]{:S(2)}, u32[]{:S(2)}) async-start(s32[32,1,640]{2,1,0:T(1,128)} %copy.21), calls=%async_computation.8 | async-start | bytes 163840 | tf_op jit(solution)/shard_map/all_to_all | solution.py:732
  15.3 3.3 convert_bitcast_fusion.table_ref
  18.7 1.7 copy.22
  20.4 2.4 all-to-all-done.8
  22.9 0.7 slice_reduce_fusion
  24.2 23.6 %gather_rows.3 = bf16[32,512,128]{2,1,0:T(8,128)(2,1)} custom-call(bf16[400,4096]{1,0:T(8,128)(2,1)S(1)} %convert_bitcast_fusion.table_ref, s32[32,128]{1,0:T(8,128)S(1)} %get-tuple-element.105.refs_0_, s32[32,128]{1,0:T(8,128)S(1)} %get-tuple-element.104.refs_1_), custom_call_target="tpu_custom_call" | custom-call | flops 16777216000 | bytes 7372800 | tf_op jit(solution)/shard_map/gather_rows/pallas_call | solution.py:234
  47.8 335.3 %conditional.1 = (f32[400,4096]{1,0:T(8,128)}) conditional(s32[]{:T(128)} %convert_element_type.34, (s32[32,640]{1,0:T(8,128)S(1)}, bf16[400,4096]{1,0:T(8,128)(2,1)S(1)}, s32[4,1024]{1,0:T(4,128)S(1)}, bf16[32,512,128]{2,1,0:T(8,128)(2,1)}, s32[4,1024]{1,0:T(4,128)S(1)}, /*index=5*/s32[2,1024]{1,0:T(2,128)S(1)}, s32[2,256]{1,0:T(2,128)S(1)}, ...), branch_computations={%region_1.2_spmd, %region_2.3_spmd} | conditional | flops 99825254400 | bytes 198825024 | solution.py:856
  53.2 0.6 copy-done.15
  53.7 3.6 all-to-all-start.4
  57.6 0.6 gather_fusion
  58.2 0.6 fusion.1
  58.8 9.3 %gather_pool.7 = bf16[32,160,128]{2,1,0:T(8,128)(2,1)} custom-call(bf16[400,4096]{1,0:T(8,128)(2,1)S(1)} %get-tuple-element.74.table_ref, s32[4,1,384]{2,1,0:T(1,128)} %bitcast.26), custom_call_target="tpu_custom_call" | custom-call | flops 5033164800 | bytes 4505600 | tf_op jit(solution)/shard_map/cond/branch_1_fun/gather_pool/pallas_call | solution.py:259
  68.2 9.3 %gather_pool.5 = bf16[32,160,128]{2,1,0:T(8,128)(2,1)} custom-call(bf16[400,4096]{1,0:T(8,128)(2,1)S(1)} %get-tuple-element.74.table_ref, s32[4,1,384]{2,1,0:T(1,128)} %bitcast.27), custom_call_target="tpu_custom_call" | custom-call | flops 5033164800 | bytes 4505600 | tf_op jit(solution)/shard_map/cond/branch_1_fun/gather_pool/pallas_call | solution.py:259
  77.5 0.4 collective-permute-start.9
  77.9 9.3 %gather_pool.6 = bf16[32,160,128]{2,1,0:T(8,128)(2,1)} custom-call(bf16[400,4096]{1,0:T(8,128)(2,1)S(1)} %get-tuple-element.74.table_ref, s32[4,1,384]{2,1,0:T(1,128)} %bitcast.25), custom_call_target="tpu_custom_call" | custom-call | flops 5033164800 | bytes 4505600 | tf_op jit(solution)/shard_map/cond/branch_1_fun/gather_pool/pallas_call | solution.py:259
  87.1 1.7 add.24
  88.9 1.7 collective-permute-start.11
  90.6 9.3 %gather_pool.4 = bf16[32,160,128]{2,1,0:T(8,128)(2,1)} custom-call(bf16[400,4096]{1,0:T(8,128)(2,1)S(1)} %get-tuple-element.74.table_ref, s32[4,1,384]{2,1,0:T(1,128)} %bitcast.28), custom_call_target="tpu_custom_call" | custom-call | flops 5033164800 | bytes 4505600 | tf_op jit(solution)/shard_map/cond/branch_1_fun/gather_pool/pallas_call | solution.py:259
  99.9 32.7 %collective-permute-done.11 = bf16[32,160,128]{2,1,0:T(8,128)(2,1)S(1)} collective-permute-done((bf16[32,160,128]{2,1,0:T(8,128)(2,1)S(1)}, bf16[32,160,128]{2,1,0:T(8,128)(2,1)S(1)}, u32[]{:S(2)}, u32[]{:S(2)}) %collective-permute-start.11) | collective-permute-done | bytes 1310752 | tf_op jit(solution)/shard_map/cond/branch_1_fun/ppermute | solution.py:737
  132.6 2.8 add_add_fusion
  135.3 15.9 %all-to-all-done.4.refs_0_.back_ref = bf16[32,512,128]{2,1,0:T(8,128)(2,1)} async-done(((bf16[32,512,128]{2,1,0:T(8,128)(2,1)}), bf16[32,512,128]{2,1,0:T(8,128)(2,1)}, u32[]{:S(2)}, u32[]{:S(2)}) %all-to-all-start.4) | async-done | bytes 4194336 | tf_op jit(solution)/shard_map/cond/branch_1_fun/all_to_all | solution.py:732
  151.2 4.2 %all-to-all-start.5 = ((bf16[32,160,128]{2,1,0:T(8,128)(2,1)}), bf16[32,160,128]{2,1,0:T(8,128)(2,1)S(1)}, u32[]{:S(2)}, u32[]{:S(2)}) async-start(bf16[32,160,128]{2,1,0:T(8,128)(2,1)} %add_add_fusion), calls=%async_computation.5 | async-start | bytes 2621440 | tf_op jit(solution)/shard_map/cond/branch_1_fun/all_to_all | solution.py:732
  155.4 2.9 spread_negatives.3.refs_4_
  158.3 1.6 collective-permute-start.7
  159.9 0.6 reshape.46.refs_2_
  160.5 0.6 reshape.47.refs_9_.refs_10_
  161.1 0.6 reshape.45.refs_1_
  161.7 19.9 %collective-permute-done.7.refs_6_ = bf16[2,256,400]{2,1,0:T(8,128)(2,1)S(1)} collective-permute-done((bf16[2,256,400]{2,1,0:T(8,128)(2,1)}, bf16[2,256,400]{2,1,0:T(8,128)(2,1)S(1)}, u32[]{:S(2)}, u32[]{:S(2)}) %collective-permute-start.7) | collective-permute-done | bytes 409632 | tf_op jit(solution)/shard_map/cond/branch_1_fun/ppermute | solution.py:737
  181.6 19.5 %spread_rows.5.refs_0_.refs_1_ = bf16[400,4096]{1,0:T(8,128)(2,1)} custom-call(bf16[32,512,128]{2,1,0:T(8,128)(2,1)} %all-to-all-done.4.refs_0_.back_ref, s32[4,1,1024]{2,1,0:T(1,128)} %reshape.45.refs_1_), custom_call_target="tpu_custom_call" | custom-call | flops 13421772800 | bytes 6553600 | tf_op jit(solution)/shard_map/cond/branch_1_fun/spread_rows/pallas_call | solution.py:329
  201.1 1.0 copy-done.6
  202.1 0.2 copy-done.25
  202.3 0.2 copy-done.26
  202.5 19.2 %edges.3 = (bf16[400,2048]{1,0:T(8,128)(2,1)}, bf16[400,2048]{1,0:T(8,128)(2,1)}, bf16[2,256,400]{2,1,0:T(8,128)(2,1)}, bf16[2,256,400]{2,1,0:T(8,128)(2,1)}, bf...) custom-call(bf16[400,4096]{1,0:T(8,128)(2,1)} %spread_rows.5.refs_0_.refs_1_, ...), custom_call_target="tpu_custom_call" | custom-call | flops 5033164800 | bytes 9830400 | tf_op jit(solution)/shard_map/cond/branch_1_fun/edges/pallas_call | solution.py:527
  221.7 6.0 %all-to-all-start.7 = ((bf16[32,160,128]{2,1,0:T(8,128)(2,1)}), bf16[32,160,128]{2,1,0:T(8,128)(2,1)S(1)}, u32[]{:S(2)}, u32[]{:S(2)}) async-start(bf16[32,160,128]{2,1,0:T(8,128)(2,1)} %get-tuple-element.87), calls=%async_computation.7 | async-start | bytes 2621440 | tf_op jit(solution)/shard_map/cond/branch_1_fun/all_to_all | solution.py:732
  227.7 0.3 collective-permute-start.13
  228.1 0.3 collective-permute-start.12
  228.3 1.6 collective-permute-done.13
  229.9 1.2 add_convert_fusion.1
  231.1 1.8 collective-permute-start.14
  232.9 17.9 %collect_grads.5.sent_ref = bf16[32,512,128]{2,1,0:T(8,128)(2,1)} custom-call(bf16[400,2048]{1,0:T(8,128)(2,1)} %get-tuple-element.79.src_ref, bf16[400,2048]{1,0:T(8,128)(2,1)} %get-tuple-element.80.dst_ref, s32[4,1024]{1,0:T(4,128)S(1)} %get-tuple-element.70.slot_ref), custom_call_target="tpu_custom_call" | custom-call | flops 13421772800 | bytes 6553600 | tf_op jit(solution)/shard_map/cond/branch_1_fun/collect_grads/pallas_call | solution.py:563
  250.9 3.2 collective-permute-done.14.refs_2_
  254.1 0.8 copy-done.10
  254.9 3.5 collect_negatives.3
  258.4 1.5 all-to-all-done.7.refs_0_
  260.0 4.9 %all-to-all-start.6 = ((bf16[32,512,128]{2,1,0:T(8,128)(2,1)}), bf16[32,512,128]{2,1,0:T(8,128)(2,1)}, u32[]{:S(2)}, u32[]{:S(2)}) async-start(bf16[32,512,128]{2,1,0:T(8,128)(2,1)} %collect_negatives.3), calls=%async_computation.6 | async-start | bytes 8388608 | tf_op jit(solution)/shard_map/cond/branch_1_fun/all_to_all | solution.py:732
  264.8 0.4 collective-permute-start.16
  265.3 1.7 collective-permute-start.15
  267.0 1.0 collective-permute-done.16.refs_1_
  267.9 1.1 copy-done.22
  269.0 15.5 %add_pool.2.other_ref.refs_4_ = f32[400,4096]{1,0:T(8,128)} custom-call(bf16[32,160,128]{2,1,0:T(8,128)(2,1)} %copy-done.5, bf16[32,160,128]{2,1,0:T(8,128)(2,1)} %copy-done.22, s32[1,1536]{1,0:T(1,128)} %get-tuple-element.102.refs_2_, s32[1,1536]{1,0:T(1,128)} %get-tuple-element.100.refs_3_), custom_call_target="tpu_custom_call" | custom-call | flops 10066329600 | bytes 9011200 | tf_op jit(solution)/shard_map/cond/branch_1_fun/add_pool/pallas_call | solution.py:704
  284.5 50.4 %collective-permute-done.15.value_ref = bf16[32,160,128]{2,1,0:T(8,128)(2,1)S(1)} collective-permute-done((bf16[32,160,128]{2,1,0:T(8,128)(2,1)S(1)}, bf16[32,160,128]{2,1,0:T(8,128)(2,1)S(1)}, u32[]{:S(2)}, u32[]{:S(2)}) %collective-permute-start.15) | collective-permute-done | bytes 1310752 | tf_op jit(solution)/shard_map/cond/branch_1_fun/ppermute | solution.py:737
  335.0 1.1 copy-done.4
  336.1 3.2 collective-permute-done.17.refs_1_
  339.4 1.1 copy-done.23
  340.4 15.9 %add_pool.3.refs_3_ = f32[400,4096]{1,0:T(8,128)} custom-call(bf16[32,160,128]{2,1,0:T(8,128)(2,1)} %after.1.refs_0_, bf16[32,160,128]{2,1,0:T(8,128)(2,1)} %copy-done.23, s32[1,1536]{1,0:T(1,128)} %get-tuple-element.101.refs_2_, s32[1,1536]{1,0:T(1,128)} %get-tuple-element.103.refs_3_, f32[400,4096]{1,0:T(8,128)} %add_pool.2.other_ref.refs_4_), custom_call_target="tpu_custom_call" | custom-call | flops 10066329600 | bytes 9011200 | tf_op jit(solution)/shard_map/cond/branch_1_fun/add_pool/pallas_call | solution.py:704
  356.4 2.6 all-to-all-done.6.refs_0_
  359.0 23.8 %add_grads.5 = f32[400,4096]{1,0:T(8,128)} custom-call(bf16[32,512,128]{2,1,0:T(8,128)(2,1)} %all-to-all-done.6.refs_0_, s32[32,128]{1,0:T(8,128)S(1)} %copy-done.20, s32[32,128]{1,0:T(8,128)S(1)} %copy-done.16, f32[400,4096]{1,0:T(8,128)} %add_pool.3.refs_3_), custom_call_target="tpu_custom_call" | custom-call | flops 13421772800 | bytes 16384000 | tf_op jit(solution)/shard_map/cond/branch_1_fun/add_grads/pallas_call | solution.py:665
  383.1 0.7 copy-done.1
  (50 shorter events, 0.6 us)
Async XLA Ops:
  0.0 1.6 copy-start
  8.0 14.9 %all-to-all-start.8 = ((s32[32,1,640]{2,1,0:T(1,128)}), s32[32,1,640]{2,1,0:T(1,128)S(1)}, u32[]{:S(2)}, u32[]{:S(2)}) async-start(s32[32,1,640]{2,1,0:T(1,128)} %copy.21), calls=%async_computation.8 | async-start | bytes 163840 | tf_op jit(solution)/shard_map/all_to_all | solution.py:732
  15.3 3.3 copy-start.21
  53.1 0.6 copy-start.15
  53.1 0.6 copy-start.19
  53.7 97.5 %all-to-all-start.4 = ((bf16[32,512,128]{2,1,0:T(8,128)(2,1)}), bf16[32,512,128]{2,1,0:T(8,128)(2,1)}, u32[]{:S(2)}, u32[]{:S(2)}) async-start(bf16[32,512,128]{2,1,0:T(8,128)(2,1)} %get-tuple-element.69), calls=%async_computation.4 | async-start | bytes 8388608 | tf_op jit(solution)/shard_map/cond/branch_1_fun/all_to_all | solution.py:732
  68.1 19.1 %collective-permute-start.10 = (bf16[32,160,128]{2,1,0:T(8,128)(2,1)}, bf16[32,160,128]{2,1,0:T(8,128)(2,1)S(1)}, u32[]{:S(2)}, u32[]{:S(2)}) collective-permute-start(bf16[32,160,128]{2,1,0:T(8,128)(2,1)} %gather_pool.7), channel_id=1, source_target_pairs={{0,1},{1,0},{2,3},{3,2},{4,5},{5,4},{6,7},{7,6},{8,9},{9,8},{10,11... | collective-permute-start | bytes 3932168 | tf_op jit(solution)/shard_map/cond/branch_1_fun/ppermute | solution.py:737
  77.5 22.4 %collective-permute-start.9 = (bf16[32,160,128]{2,1,0:T(8,128)(2,1)}, bf16[32,160,128]{2,1,0:T(8,128)(2,1)S(1)}, u32[]{:S(2)}, u32[]{:S(2)}) collective-permute-start(bf16[32,160,128]{2,1,0:T(8,128)(2,1)} %gather_pool.5), channel_id=1, source_target_pairs={{0,1},{1,0},{2,3},{3,2},{4,5},{5,4},{6,7},{7,6},{8,9},{9,8},{10,11... | collective-permute-start | bytes 3932168 | tf_op jit(solution)/shard_map/cond/branch_1_fun/ppermute | solution.py:737
  88.9 43.7 %collective-permute-start.11 = (bf16[32,160,128]{2,1,0:T(8,128)(2,1)S(1)}, bf16[32,160,128]{2,1,0:T(8,128)(2,1)S(1)}, u32[]{:S(2)}, u32[]{:S(2)}) collective-permute-start(bf16[32,160,128]{2,1,0:T(8,128)(2,1)S(1)} %add.24), channel_id=1, source_target_pairs={{0,2},{1,3},{2,0},{3,1},{4,6},{5,7},{6,4},{7,5},{8,10},{9,11},{10,... | collective-permute-start | bytes 3932168 | tf_op jit(solution)/shard_map/cond/branch_1_fun/ppermute | solution.py:737
  151.2 49.9 %all-to-all-start.5 = ((bf16[32,160,128]{2,1,0:T(8,128)(2,1)}), bf16[32,160,128]{2,1,0:T(8,128)(2,1)S(1)}, u32[]{:S(2)}, u32[]{:S(2)}) async-start(bf16[32,160,128]{2,1,0:T(8,128)(2,1)} %add_add_fusion), calls=%async_computation.5 | async-start | bytes 2621440 | tf_op jit(solution)/shard_map/cond/branch_1_fun/all_to_all | solution.py:732
  158.3 23.3 %collective-permute-start.7 = (bf16[2,256,400]{2,1,0:T(8,128)(2,1)}, bf16[2,256,400]{2,1,0:T(8,128)(2,1)S(1)}, u32[]{:S(2)}, u32[]{:S(2)}) collective-permute-start(bf16[2,256,400]{2,1,0:T(8,128)(2,1)} %spread_negatives.3.refs_4_), channel_id=1, source_target_pairs={{0,2},{1,3},{2,0},{3,1},{4,6},{5,7},{6,4},{7,5},{8,10},{9,11},{10,... | collective-permute-start | bytes 1228808 | tf_op jit(solution)/shard_map/cond/branch_1_fun/ppermute | solution.py:737
  161.7 40.8 %copy-start.12 = (f32[400,64]{1,0:T(8,128)S(1)}, f32[400,64]{1,0:T(8,128)}, u32[]{:S(2)}) copy-start(f32[400,64]{1,0:T(8,128)} %get-tuple-element.72.refs_3_) | copy-start | bytes 307204 | tf_op jit(solution)/shard_map/cond
  161.7 39.4 %collective-permute-start.6 = (bf16[2,256,400]{2,1,0:T(8,128)(2,1)}, bf16[2,256,400]{2,1,0:T(8,128)(2,1)S(1)}, u32[]{:S(2)}, u32[]{:S(2)}) collective-permute-start(bf16[2,256,400]{2,1,0:T(8,128)(2,1)} %spread_negatives.3.refs_4_), channel_id=1, source_target_pairs={{0,1},{1,0},{2,3},{3,2},{4,5},{5,4},{6,7},{7,6},{8,9},{9,8},{10,11... | collective-permute-start | bytes 1228808 | tf_op jit(solution)/shard_map/cond/branch_1_fun/ppermute | solution.py:737
  181.6 19.5 %copy-start.24 = (bf16[2,256,400]{2,1,0:T(8,128)(2,1)}, bf16[2,256,400]{2,1,0:T(8,128)(2,1)S(1)}, u32[]{:S(2)}) copy-start(bf16[2,256,400]{2,1,0:T(8,128)(2,1)S(1)} %collective-permute-done.7.refs_6_) | copy-start | bytes 1228804 | tf_op jit(solution)/shard_map/cond
  181.6 19.5 %collective-permute-start.8 = (bf16[2,256,400]{2,1,0:T(8,128)(2,1)S(1)}, bf16[2,256,400]{2,1,0:T(8,128)(2,1)S(1)}, u32[]{:S(2)}, u32[]{:S(2)}) collective-permute-start(bf16[2,256,400]{2,1,0:T(8,128)(2,1)S(1)} %collective-permute-done.7.refs_6_), channel_id=1, source_target_pairs={{0,1},{1,0},{2,3},{3,2},{4,5},{5,4},{6,7},{7,6},{8,9},{9,8},{10,11... | collective-permute-start | bytes 1228808 | tf_op jit(solution)/shard_map/cond/branch_1_fun/ppermute | solution.py:737
  201.1 1.1 copy-start.6
  201.1 1.2 copy-start.25
  201.1 1.4 copy-start.26
  221.7 38.2 %all-to-all-start.7 = ((bf16[32,160,128]{2,1,0:T(8,128)(2,1)}), bf16[32,160,128]{2,1,0:T(8,128)(2,1)S(1)}, u32[]{:S(2)}, u32[]{:S(2)}) async-start(bf16[32,160,128]{2,1,0:T(8,128)(2,1)} %get-tuple-element.87), calls=%async_computation.7 | async-start | bytes 2621440 | tf_op jit(solution)/shard_map/cond/branch_1_fun/all_to_all | solution.py:732
  227.7 2.2 collective-permute-start.13
  228.1 22.8 %collective-permute-start.12 = (bf16[2,256,400]{2,1,0:T(8,128)(2,1)}, bf16[2,256,400]{2,1,0:T(8,128)(2,1)S(1)}, u32[]{:S(2)}, u32[]{:S(2)}) collective-permute-start(bf16[2,256,400]{2,1,0:T(8,128)(2,1)} %get-tuple-element.82), channel_id=1, source_target_pairs={{0,1},{1,0},{2,3},{3,2},{4,5},{5,4},{6,7},{7,6},{8,9},{9,8},{10,11... | collective-permute-start | bytes 1228808 | tf_op jit(solution)/shard_map/cond/branch_1_fun/ppermute | solution.py:737
  231.1 23.0 %collective-permute-start.14 = (bf16[2,256,400]{2,1,0:T(8,128)(2,1)S(1)}, bf16[2,256,400]{2,1,0:T(8,128)(2,1)S(1)}, u32[]{:S(2)}, u32[]{:S(2)}) collective-permute-start(bf16[2,256,400]{2,1,0:T(8,128)(2,1)S(1)} %add_convert_fusion.1), channel_id=1, source_target_pairs={{0,2},{1,3},{2,0},{3,1},{4,6},{5,7},{6,4},{7,5},{8,10},{9,11},{10,... | collective-permute-start | bytes 1228808 | tf_op jit(solution)/shard_map/cond/branch_1_fun/ppermute | solution.py:737
  250.9 3.3 copy-start.8
  254.1 0.8 copy-start.10
  260.0 5.3 %copy-start.5 = (bf16[32,160,128]{2,1,0:T(8,128)(2,1)}, bf16[32,160,128]{2,1,0:T(8,128)(2,1)S(1)}, u32[]{:S(2)}) copy-start(bf16[32,160,128]{2,1,0:T(8,128)(2,1)S(1)} %all-to-all-done.7.refs_0_) | copy-start | bytes 3932164 | tf_op jit(solution)/shard_map/cond
  260.0 99.0 %all-to-all-start.6 = ((bf16[32,512,128]{2,1,0:T(8,128)(2,1)}), bf16[32,512,128]{2,1,0:T(8,128)(2,1)}, u32[]{:S(2)}, u32[]{:S(2)}) async-start(bf16[32,512,128]{2,1,0:T(8,128)(2,1)} %collect_negatives.3), calls=%async_computation.6 | async-start | bytes 8388608 | tf_op jit(solution)/shard_map/cond/branch_1_fun/all_to_all | solution.py:732
  264.8 3.1 collective-permute-start.16
  265.3 69.7 %collective-permute-start.15 = (bf16[32,160,128]{2,1,0:T(8,128)(2,1)S(1)}, bf16[32,160,128]{2,1,0:T(8,128)(2,1)S(1)}, u32[]{:S(2)}, u32[]{:S(2)}) collective-permute-start(bf16[32,160,128]{2,1,0:T(8,128)(2,1)S(1)} %all-to-all-done.7.refs_0_), channel_id=1, source_target_pairs={{0,2},{1,3},{2,0},{3,1},{4,6},{5,7},{6,4},{7,5},{8,10},{9,11},{10,... | collective-permute-start | bytes 3932168 | tf_op jit(solution)/shard_map/cond/branch_1_fun/ppermute | solution.py:737
  267.9 1.1 copy-start.22
  335.0 1.1 copy-start.4
  336.1 22.9 %copy-start.16 = (s32[32,128]{1,0:T(8,128)S(1)}, s32[32,128]{1,0:T(8,128)}, u32[]{:S(2)}) copy-start(s32[32,128]{1,0:T(8,128)} %copy-done.15) | copy-start | bytes 49156 | tf_op jit(solution)/shard_map/cond
  336.1 22.9 %copy-start.20 = (s32[32,128]{1,0:T(8,128)S(1)}, s32[32,128]{1,0:T(8,128)}, u32[]{:S(2)}) copy-start(s32[32,128]{1,0:T(8,128)} %copy-done.19) | copy-start | bytes 49156 | tf_op jit(solution)/shard_map/cond
  336.1 3.2 collective-permute-start.17
  339.3 1.1 copy-start.23
  383.1 0.7 copy-start.1

commit v8 on v7

--- a/solution.py
+++ b/solution.py
@@ -127,9 +127,8 @@
         busy = jnp.where(taken > SMALL, 1.0, 0.0)
         crowded = jnp.sum(busy, axis=0, keepdims=True) > 1.0
         flag = jnp.where((most > room) | crowded, 1, -1)[:, :1]
-        busy_ref[...] = jnp.sum(busy * shard_rows.astype(F32), axis=0, keepdims=True).astype(
-            jnp.int32
-        )[:, :1]
+        place = jnp.sum(busy * shard_rows.astype(F32), axis=0, keepdims=True).astype(jnp.int32)
+        busy_ref[...] = jnp.minimum(place, shards - 1)[:, :1]
 
     where, holder, codes, members, found = prepare(own_ref)
     for at, owner, rank in zip(where, holder, found):
@@ -737,13 +736,13 @@
     return lax.ppermute(value, "grp", [(i, i ^ bit) for i in range(sharers)])
 
 
-def share_out(value):
+def share_out(value, wait=lambda block: block):
     sharers = lax.axis_size("grp")
     blocks = {0: value}
     bit = sharers // 2
     while bit:
         for k in list(blocks):
-            blocks[k ^ bit] = swap(blocks[k], bit)
+            blocks[k ^ bit] = swap(wait(blocks[k]) if k else blocks[k], bit)
         bit //= 2
     return [blocks[k] for k in range(sharers)]
 
@@ -804,16 +803,16 @@
 
     sent_rows = gather(table, direct[0], neg_asked, neg_cap)
 
-    def negatives_of(back):
-        return share_out(spread_neg(back, neg_slot, neg_cap, feature))
+    def negatives_of(back, *wait):
+        return share_out(spread_neg(back, neg_slot, neg_cap, feature), *wait)
 
     def direct_sent(src_grad, dst_grad, neg_grads):
         sent = collect(src_grad, dst_grad, slots[0], devices, neg_cap)
         return exchange(collect_neg(sent, neg_slot, trade(neg_grads), neg_cap))
 
-    def chunked():
+    def chunked(zero=0):
         back = [exchange(sent_rows)]
-        back += [exchange(gather(table, direct[c])) for c in range(1, chunks)]
+        back += [exchange(gather(table, direct[c] + zero)) for c in range(1, chunks)]
         negatives = negatives_of(back[0])
         rows = None
         for c in range(chunks):
@@ -836,8 +835,8 @@
         far = swap(gather_pool(table, listed[2], devices) + far, 2)
         near = swap(gather_pool(table, listed[1], devices), 1)
         near = gather_pool(table, listed[0], devices) + near
-        negatives = negatives_of(back)
         rows = spread(back, slots[0], None, feature)
+        negatives = negatives_of(back, lambda block: after(block, rows))
         src_grad, dst_grad, rest = edges(
             rows, rel_rows, relations, negatives, exchange(near + far), slots[chunks], busy
         )
@@ -852,8 +851,12 @@
 
     if chunks == 1 or sharers != RELAYS:
         return chunked().T
-    fits = jnp.max(neg_asked[:, -1]) < 0
-    return lax.cond(fits, pooled, chunked).T
+    flag = jnp.max(neg_asked[:, -1])
+    return lax.while_loop(
+        lambda state: state[1] > 0,
+        lambda state: (chunked(jnp.minimum(state[1], 0)), -state[1]),
+        (pooled(), flag),
+    )[0].T
 
 
 def solution(mesh):

time: 391 us -> 378 us (0.967); the launches traced: 384 us -> 376 us
  waiting for transfers between devices: 135 us -> 118 us
  starting transfers between devices: 34.2 us -> 48.7 us
  loops' own time: 5.76 us -> 0.57 us
    ppermute x12 -> x13, waiting for transfers between devices: 112 us -> 92.4 us  [swap(): return lax.ppermute(value, 'grp', [(i, i ^ bit) for i in range(sharers)])]
    all_to_all x5, starting transfers between devices: 25.9 us -> 39.6 us  [exchange(): lax.all_to_all(value, ('shard', 'grp'), split_axis=0, concat_axis=0, tile...]
    cond x30 -> x0, local copies, waits for them, and re-layouts: 6.03 us -> none
    another operation x1, loops' own time: 5.76 us -> 0.57 us  [body(): lax.while_loop(lambda state: state[1] > 0, lambda state: (chunked(jnp.min...]
    unnamed x8 -> x33, local copies, waits for them, and re-layouts: 2.44 us -> 7.47 us
    ppermute x12 -> x13, starting transfers between devices: 8.35 us -> 9.08 us  [swap(): return lax.ppermute(value, 'grp', [(i, i ^ bit) for i in range(sharers)])]
  transfers between devices with their start and end apart: 17 -> 18, of which waited for: 11 -> 12; matrix products, arithmetic and copies ran while one was open for 4% -> 5% of each run, Pallas kernels for 29% -> 36%
where the time goes in v8:
time: 378 us; the launch traced here: 376 us
  Pallas kernels  182 us (48%)
  waiting for transfers between devices  118 us (31%)
  starting transfers between devices  48.7 us (13%)
  local copies, waits for them, and re-layouts  16.6 us (4%)
  other arithmetic  9.76 us (3%)
    ppermute x13, waiting for transfers between devices, swap(): return lax.ppermute(value, 'grp', [(i, i ^ bit) for i in range(sharers)])  92.4 us
    all_to_all x5, starting transfers between devices, exchange(): lax.all_to_all(value, ('shard', 'grp'), split_axis=0, concat_axis=0, tile...  39.6 us
    pallas_call x4, Pallas kernels, gather_pool(): call(functools.partial(gather_pool_kernel, group=group), 'gather_pool', 2...  37.1 us
    pallas_call x2, Pallas kernels, add_pool(): call(functools.partial(add_pool_kernel, rows=rows, first=so_far is None),...  31.5 us
    all_to_all x5, waiting for transfers between devices, exchange(): lax.all_to_all(value, ('shard', 'grp'), split_axis=0, concat_axis=0, tile...  25.8 us
    pallas_call x1, Pallas kernels, add_rows(): call(functools.partial(add_kernel, rows=rows, neg_cap=neg_cap, first=so_f...  23.9 us
    pallas_call x1, Pallas kernels, gather(): call(functools.partial(gather_kernel, group=group, neg_cap=neg_cap), 'gat...  23.6 us
    pallas_call x1, Pallas kernels, edges(): call(functools.partial(edges_kernel, parts=parts, pooled=pool is not None...  19.4 us
  transfers between devices with their start and end apart: 18, of which 12 were waited for; matrix products, arithmetic and copies ran while one was open for 5% of the time, Pallas kernels for 36%

profile of v8, /device:TPU:0, one launch (start us, length us, event | category | flops | bytes accessed | tf_op | source)
XLA Modules:
  0.0 376.1 jit_solution(14830903117877983632)
XLA Ops:
  0.0 0.8 reshape.50
  0.8 0.8 reshape.49
  1.6 0.6 pad.12.ends_ref
  2.3 0.6 pad.13.own_ref
  2.9 3.5 slots.1
  6.4 1.6 copy.17
  8.0 7.3 %all-to-all-start.3 = ((s32[32,1,640]{2,1,0:T(1,128)}), s32[32,1,640]{2,1,0:T(1,128)S(1)}, u32[]{:S(2)}, u32[]{:S(2)}) async-start(s32[32,1,640]{2,1,0:T(1,128)} %copy.17), calls=%async_computation.3 | async-start | bytes 163840 | tf_op jit(solution)/shard_map/all_to_all | solution.py:731
  15.3 3.3 convert_bitcast_fusion.table_ref
  18.6 4.3 %all-to-all-done.3 = s32[32,1,640]{2,1,0:T(1,128)S(1)} async-done(((s32[32,1,640]{2,1,0:T(1,128)}), s32[32,1,640]{2,1,0:T(1,128)S(1)}, u32[]{:S(2)}, u32[]{:S(2)}) %all-to-all-start.3) | async-done | bytes 81952 | tf_op jit(solution)/shard_map/all_to_all | solution.py:731
  22.9 23.6 %gather_rows.4 = bf16[32,512,128]{2,1,0:T(8,128)(2,1)} custom-call(bf16[400,4096]{1,0:T(8,128)(2,1)S(1)} %convert_bitcast_fusion.table_ref, s32[32,128]{1,0:T(8,128)S(1)} %get-tuple-element.426.refs_0_.refs_1_, s32[32,128]{1,0:T(8,128)S(1)} %get-tuple-element.427.refs_1_.refs_2_), custom_call_target="tpu_custom_call" | custom-call | flops 16777216000 | bytes 7372800 | tf_op jit(solution)/shard_map/gather_rows/pallas_call | solution.py:233
  46.5 3.6 all-to-all-start.4
  50.4 0.6 gather_fusion
  50.9 0.6 fusion.2
  51.6 9.3 %gather_pool.7 = bf16[32,160,128]{2,1,0:T(8,128)(2,1)} custom-call(bf16[400,4096]{1,0:T(8,128)(2,1)S(1)} %convert_bitcast_fusion.table_ref, s32[4,1,384]{2,1,0:T(1,128)} %bitcast.23), custom_call_target="tpu_custom_call" | custom-call | flops 5033164800 | bytes 4505600 | tf_op jit(solution)/shard_map/gather_pool/pallas_call | solution.py:258
  60.9 9.3 %gather_pool.5 = bf16[32,160,128]{2,1,0:T(8,128)(2,1)} custom-call(bf16[400,4096]{1,0:T(8,128)(2,1)S(1)} %convert_bitcast_fusion.table_ref, s32[4,1,384]{2,1,0:T(1,128)} %bitcast.24), custom_call_target="tpu_custom_call" | custom-call | flops 5033164800 | bytes 4505600 | tf_op jit(solution)/shard_map/gather_pool/pallas_call | solution.py:258
  70.2 0.5 collective-permute-start.6
  70.6 9.3 %gather_pool.6 = bf16[32,160,128]{2,1,0:T(8,128)(2,1)} custom-call(bf16[400,4096]{1,0:T(8,128)(2,1)S(1)} %convert_bitcast_fusion.table_ref, s32[4,1,384]{2,1,0:T(1,128)} %bitcast.22), custom_call_target="tpu_custom_call" | custom-call | flops 5033164800 | bytes 4505600 | tf_op jit(solution)/shard_map/gather_pool/pallas_call | solution.py:258
  79.9 1.7 add.47
  81.7 1.6 collective-permute-start.8
  83.3 9.3 %gather_pool.4 = bf16[32,160,128]{2,1,0:T(8,128)(2,1)} custom-call(bf16[400,4096]{1,0:T(8,128)(2,1)S(1)} %convert_bitcast_fusion.table_ref, s32[4,1,384]{2,1,0:T(1,128)} %bitcast.25), custom_call_target="tpu_custom_call" | custom-call | flops 5033164800 | bytes 4505600 | tf_op jit(solution)/shard_map/gather_pool/pallas_call | solution.py:258
  92.6 32.7 %collective-permute-done.8 = bf16[32,160,128]{2,1,0:T(8,128)(2,1)S(1)} collective-permute-done((bf16[32,160,128]{2,1,0:T(8,128)(2,1)S(1)}, bf16[32,160,128]{2,1,0:T(8,128)(2,1)S(1)}, u32[]{:S(2)}, u32[]{:S(2)}) %collective-permute-start.8) | collective-permute-done | bytes 1310752 | tf_op jit(solution)/shard_map/ppermute | solution.py:736
  125.2 2.8 add_add_fusion
  128.0 16.1 %all-to-all-done.4.refs_0_.back_ref = bf16[32,512,128]{2,1,0:T(8,128)(2,1)} async-done(((bf16[32,512,128]{2,1,0:T(8,128)(2,1)}), bf16[32,512,128]{2,1,0:T(8,128)(2,1)}, u32[]{:S(2)}, u32[]{:S(2)}) %all-to-all-start.4) | async-done | bytes 4194336 | tf_op jit(solution)/shard_map/all_to_all | solution.py:731
  144.2 4.1 %all-to-all-start.5 = ((bf16[32,160,128]{2,1,0:T(8,128)(2,1)}), bf16[32,160,128]{2,1,0:T(8,128)(2,1)}, u32[]{:S(2)}, u32[]{:S(2)}) async-start(bf16[32,160,128]{2,1,0:T(8,128)(2,1)} %add_add_fusion), calls=%async_computation.5 | async-start | bytes 2621440 | tf_op jit(solution)/shard_map/all_to_all | solution.py:731
  148.3 0.6 reshape.51.refs_1_
  148.9 2.9 spread_negatives.2.refs_4_
  151.8 0.4 collective-permute-start.3
  152.2 1.7 collective-permute-start.4
  153.9 18.6 %spread_rows.3.other_ref.refs_0_.refs_1_ = bf16[400,4096]{1,0:T(8,128)(2,1)S(1)} custom-call(bf16[32,512,128]{2,1,0:T(8,128)(2,1)} %all-to-all-done.4.refs_0_.back_ref, s32[4,1,1024]{2,1,0:T(1,128)} %reshape.51.refs_1_), custom_call_target="tpu_custom_call" | custom-call | flops 13421772800 | bytes 6553600 | tf_op jit(solution)/shard_map/spread_rows/pallas_call | solution.py:328
  172.5 2.1 collective-permute-done.4.refs_6_
  174.6 1.9 copy.28.value_ref
  176.8 0.6 reshape.53.refs_2_
  177.4 0.8 copy.18
  178.2 1.3 reshape.54.refs_9_.refs_10_
  179.5 1.0 all-to-all-done.5.refs_8_
  180.5 19.4 %edges.4 = (bf16[400,2048]{1,0:T(8,128)(2,1)}, bf16[400,2048]{1,0:T(8,128)(2,1)}, bf16[2,256,400]{2,1,0:T(8,128)(2,1)}, bf16[2,256,400]{2,1,0:T(8,128)(2,1)}, bf...) custom-call(bf16[400,4096]{1,0:T(8,128)(2,1)} %copy-done.7, ...), custom_call_target="tpu_custom_call" | custom-call | flops 5033164800 | bytes 9830400 | tf_op jit(solution)/shard_map/edges/pallas_call | solution.py:526
  199.9 5.2 %all-to-all-start.7 = ((bf16[32,160,128]{2,1,0:T(8,128)(2,1)}), bf16[32,160,128]{2,1,0:T(8,128)(2,1)}, u32[]{:S(2)}, u32[]{:S(2)}) async-start(bf16[32,160,128]{2,1,0:T(8,128)(2,1)} %get-tuple-element.183), calls=%async_computation.7 | async-start | bytes 2621440 | tf_op jit(solution)/shard_map/all_to_all | solution.py:731
  205.1 0.3 collective-permute-start.10
  205.4 0.3 collective-permute-start.9
  205.7 1.6 collective-permute-done.10
  207.3 1.2 add_convert_fusion.1
  208.5 1.8 collective-permute-start.11
  210.2 17.9 %collect_grads.5.sent_ref = bf16[32,512,128]{2,1,0:T(8,128)(2,1)} custom-call(bf16[400,2048]{1,0:T(8,128)(2,1)} %get-tuple-element.177.src_ref, bf16[400,2048]{1,0:T(8,128)(2,1)} %get-tuple-element.178.dst_ref, s32[4,1024]{1,0:T(4,128)S(1)} %get-tuple-element.424.slot_ref), custom_call_target="tpu_custom_call" | custom-call | flops 13421772800 | bytes 6553600 | tf_op jit(solution)/shard_map/collect_grads/pallas_call | solution.py:562
  228.2 3.2 collective-permute-done.11.refs_2_
  231.4 0.8 copy-done.11
  232.2 3.5 collect_negatives.4
  235.7 1.6 all-to-all-done.7.refs_0_
  237.3 19.4 %all-to-all-start.6 = ((bf16[32,512,128]{2,1,0:T(8,128)(2,1)}), bf16[32,512,128]{2,1,0:T(8,128)(2,1)}, u32[]{:S(2)}, u32[]{:S(2)}) async-start(bf16[32,512,128]{2,1,0:T(8,128)(2,1)} %collect_negatives.4), calls=%async_computation.6 | async-start | bytes 8388608 | tf_op jit(solution)/shard_map/all_to_all | solution.py:731
  257.0 1.7 collective-permute-start.12
  258.6 1.4 collective-permute-done.13.refs_1_
  260.1 1.1 copy-done.21
  261.1 15.5 %add_pool.2.other_ref.refs_4_ = f32[400,4096]{1,0:T(8,128)} custom-call(bf16[32,160,128]{2,1,0:T(8,128)(2,1)} %all-to-all-done.7.refs_0_, bf16[32,160,128]{2,1,0:T(8,128)(2,1)} %copy-done.21, s32[1,1536]{1,0:T(1,128)} %get-tuple-element.223.refs_2_, s32[1,1536]{1,0:T(1,128)} %get-tuple-element.221.refs_3_), custom_call_target="tpu_custom_call" | custom-call | flops 10066329600 | bytes 9011200 | tf_op jit(solution)/shard_map/add_pool/pallas_call | solution.py:703
  276.7 50.0 %collective-permute-done.12.value_ref = bf16[32,160,128]{2,1,0:T(8,128)(2,1)S(1)} collective-permute-done((bf16[32,160,128]{2,1,0:T(8,128)(2,1)}, bf16[32,160,128]{2,1,0:T(8,128)(2,1)S(1)}, u32[]{:S(2)}, u32[]{:S(2)}) %collective-permute-start.12) | collective-permute-done | bytes 1310752 | tf_op jit(solution)/shard_map/ppermute | solution.py:736
  326.7 1.1 copy-done.9
  327.8 0.6 reshape.63
  328.4 0.7 slice_reduce_fusion
  329.1 0.5 collective-permute-start.15
  329.6 1.4 collective-permute-done.14.refs_1_
  331.0 1.1 copy-done.20
  332.1 16.0 %add_pool.3.refs_3_ = f32[400,4096]{1,0:T(8,128)} custom-call(bf16[32,160,128]{2,1,0:T(8,128)(2,1)} %after.3.refs_0_, bf16[32,160,128]{2,1,0:T(8,128)(2,1)} %copy-done.20, s32[1,1536]{1,0:T(1,128)} %get-tuple-element.222.refs_2_, s32[1,1536]{1,0:T(1,128)} %get-tuple-element.224.refs_3_, f32[400,4096]{1,0:T(8,128)} %add_pool.2.other_ref.refs_4_), custom_call_target="tpu_custom_call" | custom-call | flops 10066329600 | bytes 9011200 | tf_op jit(solution)/shard_map/add_pool/pallas_call | solution.py:703
  348.0 2.8 all-to-all-done.6.refs_0_
  350.8 23.9 %add_grads.5 = f32[400,4096]{1,0:T(8,128)} custom-call(bf16[32,512,128]{2,1,0:T(8,128)(2,1)} %all-to-all-done.6.refs_0_, s32[32,128]{1,0:T(8,128)} %copy-done.18, s32[32,128]{1,0:T(8,128)} %copy-done.17, f32[400,4096]{1,0:T(8,128)} %add_pool.3.refs_3_), custom_call_target="tpu_custom_call" | custom-call | flops 13421772800 | bytes 16384000 | tf_op jit(solution)/shard_map/add_grads/pallas_call | solution.py:664
  374.7 0.6 while.13
  375.3 0.7 copy-done.1
  (50 shorter events, 0.9 us)
Async XLA Ops:
  0.0 2.2 copy-start
  8.0 14.9 %all-to-all-start.3 = ((s32[32,1,640]{2,1,0:T(1,128)}), s32[32,1,640]{2,1,0:T(1,128)S(1)}, u32[]{:S(2)}, u32[]{:S(2)}) async-start(s32[32,1,640]{2,1,0:T(1,128)} %copy.17), calls=%async_computation.3 | async-start | bytes 163840 | tf_op jit(solution)/shard_map/all_to_all | solution.py:731
  22.9 23.6 %copy-start.17 = (s32[32,128]{1,0:T(8,128)}, s32[32,128]{1,0:T(8,128)S(1)}, u32[]{:S(2)}) copy-start(s32[32,128]{1,0:T(8,128)S(1)} %get-tuple-element.427.refs_1_.refs_2_) | copy-start | bytes 49156
  22.9 23.6 %copy-start.18 = (s32[32,128]{1,0:T(8,128)}, s32[32,128]{1,0:T(8,128)S(1)}, u32[]{:S(2)}) copy-start(s32[32,128]{1,0:T(8,128)S(1)} %get-tuple-element.426.refs_0_.refs_1_) | copy-start | bytes 49156
  46.5 97.7 %all-to-all-start.4 = ((bf16[32,512,128]{2,1,0:T(8,128)(2,1)}), bf16[32,512,128]{2,1,0:T(8,128)(2,1)}, u32[]{:S(2)}, u32[]{:S(2)}) async-start(bf16[32,512,128]{2,1,0:T(8,128)(2,1)} %gather_rows.4), calls=%async_computation.4 | async-start | bytes 8388608 | tf_op jit(solution)/shard_map/all_to_all | solution.py:731
  60.8 19.1 %collective-permute-start.7 = (bf16[32,160,128]{2,1,0:T(8,128)(2,1)}, bf16[32,160,128]{2,1,0:T(8,128)(2,1)S(1)}, u32[]{:S(2)}, u32[]{:S(2)}) collective-permute-start(bf16[32,160,128]{2,1,0:T(8,128)(2,1)} %gather_pool.7), channel_id=1, source_target_pairs={{0,1},{1,0},{2,3},{3,2},{4,5},{5,4},{6,7},{7,6},{8,9},{9,8},{10,11... | collective-permute-start | bytes 3932168 | tf_op jit(solution)/shard_map/ppermute | solution.py:736
  70.2 22.4 %collective-permute-start.6 = (bf16[32,160,128]{2,1,0:T(8,128)(2,1)}, bf16[32,160,128]{2,1,0:T(8,128)(2,1)S(1)}, u32[]{:S(2)}, u32[]{:S(2)}) collective-permute-start(bf16[32,160,128]{2,1,0:T(8,128)(2,1)} %gather_pool.5), channel_id=1, source_target_pairs={{0,1},{1,0},{2,3},{3,2},{4,5},{5,4},{6,7},{7,6},{8,9},{9,8},{10,11... | collective-permute-start | bytes 3932168 | tf_op jit(solution)/shard_map/ppermute | solution.py:736
  81.7 43.6 %collective-permute-start.8 = (bf16[32,160,128]{2,1,0:T(8,128)(2,1)S(1)}, bf16[32,160,128]{2,1,0:T(8,128)(2,1)S(1)}, u32[]{:S(2)}, u32[]{:S(2)}) collective-permute-start(bf16[32,160,128]{2,1,0:T(8,128)(2,1)S(1)} %add.47), channel_id=1, source_target_pairs={{0,2},{1,3},{2,0},{3,1},{4,6},{5,7},{6,4},{7,5},{8,10},{9,11},{10,... | collective-permute-start | bytes 3932168 | tf_op jit(solution)/shard_map/ppermute | solution.py:736
  144.2 36.3 %all-to-all-start.5 = ((bf16[32,160,128]{2,1,0:T(8,128)(2,1)}), bf16[32,160,128]{2,1,0:T(8,128)(2,1)}, u32[]{:S(2)}, u32[]{:S(2)}) async-start(bf16[32,160,128]{2,1,0:T(8,128)(2,1)} %add_add_fusion), calls=%async_computation.5 | async-start | bytes 2621440 | tf_op jit(solution)/shard_map/all_to_all | solution.py:731
  151.8 28.7 %collective-permute-start.3 = (bf16[2,256,400]{2,1,0:T(8,128)(2,1)}, bf16[2,256,400]{2,1,0:T(8,128)(2,1)}, u32[]{:S(2)}, u32[]{:S(2)}) collective-permute-start(bf16[2,256,400]{2,1,0:T(8,128)(2,1)} %spread_negatives.2.refs_4_), channel_id=1, source_target_pairs={{0,1},{1,0},{2,3},{3,2},{4,5},{5,4},{6,7},{7,6},{8,9},{9,8},{10,11... | collective-permute-start | bytes 1228808 | tf_op jit(solution)/shard_map/ppermute | solution.py:736
  152.2 22.4 %collective-permute-start.4 = (bf16[2,256,400]{2,1,0:T(8,128)(2,1)}, bf16[2,256,400]{2,1,0:T(8,128)(2,1)}, u32[]{:S(2)}, u32[]{:S(2)}) collective-permute-start(bf16[2,256,400]{2,1,0:T(8,128)(2,1)} %spread_negatives.2.refs_4_), channel_id=1, source_target_pairs={{0,2},{1,3},{2,0},{3,1},{4,6},{5,7},{6,4},{7,5},{8,10},{9,11},{10,... | collective-permute-start | bytes 1228808 | tf_op jit(solution)/shard_map/ppermute | solution.py:736
  172.5 4.0 %copy-start.7 = (bf16[400,4096]{1,0:T(8,128)(2,1)}, bf16[400,4096]{1,0:T(8,128)(2,1)S(1)}, u32[]{:S(2)}) copy-start(bf16[400,4096]{1,0:T(8,128)(2,1)S(1)} %spread_rows.3.other_ref.refs_0_.refs_1_) | copy-start | bytes 9830404
  172.5 4.2 %copy-start.19 = (s32[2000]{0:T(1024)S(1)}, s32[2000]{0:T(1024)}, u32[]{:S(2)}) copy-start(s32[2000]{0:T(1024)} %param.12) | copy-start | bytes 24004
  172.5 4.9 %copy-start.13 = (f32[64,400]{1,0:T(8,128)S(1)}, f32[64,400]{1,0:T(8,128)}, u32[]{:S(2)}) copy-start(f32[64,400]{1,0:T(8,128)} %param.9) | copy-start | bytes 307204
  176.5 4.0 %collective-permute-start.5 = (bf16[2,256,400]{2,1,0:T(8,128)(2,1)}, bf16[2,256,400]{2,1,0:T(8,128)(2,1)}, u32[]{:S(2)}, u32[]{:S(2)}) collective-permute-start(bf16[2,256,400]{2,1,0:T(8,128)(2,1)} %after.2), channel_id=1, source_target_pairs={{0,1},{1,0},{2,3},{3,2},{4,5},{5,4},{6,7},{7,6},{8,9},{9,8},{10,11... | collective-permute-start | bytes 1228808 | tf_op jit(solution)/shard_map/ppermute | solution.py:736
  176.8 151.0 %copy-start.14 = (s32[2,1024]{1,0:T(2,128)}, s32[2,1024]{1,0:T(2,128)S(1)}, u32[]{:S(2)}) copy-start(s32[2,1024]{1,0:T(2,128)S(1)} %pad.14) | copy-start | bytes 24580
  199.9 37.4 %all-to-all-start.7 = ((bf16[32,160,128]{2,1,0:T(8,128)(2,1)}), bf16[32,160,128]{2,1,0:T(8,128)(2,1)}, u32[]{:S(2)}, u32[]{:S(2)}) async-start(bf16[32,160,128]{2,1,0:T(8,128)(2,1)} %get-tuple-element.183), calls=%async_computation.7 | async-start | bytes 2621440 | tf_op jit(solution)/shard_map/all_to_all | solution.py:731
  205.1 2.2 collective-permute-start.10
  205.4 22.8 %collective-permute-start.9 = (bf16[2,256,400]{2,1,0:T(8,128)(2,1)}, bf16[2,256,400]{2,1,0:T(8,128)(2,1)S(1)}, u32[]{:S(2)}, u32[]{:S(2)}) collective-permute-start(bf16[2,256,400]{2,1,0:T(8,128)(2,1)} %get-tuple-element.180), channel_id=1, source_target_pairs={{0,1},{1,0},{2,3},{3,2},{4,5},{5,4},{6,7},{7,6},{8,9},{9,8},{10,11... | collective-permute-start | bytes 1228808 | tf_op jit(solution)/shard_map/ppermute | solution.py:736
  208.5 22.9 %collective-permute-start.11 = (bf16[2,256,400]{2,1,0:T(8,128)(2,1)S(1)}, bf16[2,256,400]{2,1,0:T(8,128)(2,1)S(1)}, u32[]{:S(2)}, u32[]{:S(2)}) collective-permute-start(bf16[2,256,400]{2,1,0:T(8,128)(2,1)S(1)} %add_convert_fusion.1), channel_id=1, source_target_pairs={{0,2},{1,3},{2,0},{3,1},{4,6},{5,7},{6,4},{7,5},{8,10},{9,11},{10,... | collective-permute-start | bytes 1228808 | tf_op jit(solution)/shard_map/ppermute | solution.py:736
  228.2 3.2 copy-start.10
  231.4 0.8 copy-start.11
  237.3 113.5 %all-to-all-start.6 = ((bf16[32,512,128]{2,1,0:T(8,128)(2,1)}), bf16[32,512,128]{2,1,0:T(8,128)(2,1)}, u32[]{:S(2)}, u32[]{:S(2)}) async-start(bf16[32,512,128]{2,1,0:T(8,128)(2,1)} %collect_negatives.4), calls=%async_computation.6 | async-start | bytes 8388608 | tf_op jit(solution)/shard_map/all_to_all | solution.py:731
  256.8 3.3 collective-permute-start.13
  257.0 69.7 %collective-permute-start.12 = (bf16[32,160,128]{2,1,0:T(8,128)(2,1)}, bf16[32,160,128]{2,1,0:T(8,128)(2,1)S(1)}, u32[]{:S(2)}, u32[]{:S(2)}) collective-permute-start(bf16[32,160,128]{2,1,0:T(8,128)(2,1)} %all-to-all-done.7.refs_0_), channel_id=1, source_target_pairs={{0,2},{1,3},{2,0},{3,1},{4,6},{5,7},{6,4},{7,5},{8,10},{9,11},{10,... | collective-permute-start | bytes 3932168 | tf_op jit(solution)/shard_map/ppermute | solution.py:736
  260.1 1.1 copy-start.21
  276.7 51.1 %copy-start.15 = (s32[4,1024]{1,0:T(4,128)S(1)}, s32[4,1024]{1,0:T(4,128)}, u32[]{:S(2)}) copy-start(s32[4,1024]{1,0:T(4,128)} %get-tuple-element.416) | copy-start | bytes 49156
  326.7 1.1 copy-start.9
  327.7 3.2 collective-permute-start.14
  329.1 45.6 %collective-permute-start.15 = (bf16[2,256,400]{2,1,0:T(8,128)(2,1)}, bf16[2,256,400]{2,1,0:T(8,128)(2,1)}, u32[]{:S(2)}, u32[]{:S(2)}) collective-permute-start(bf16[2,256,400]{2,1,0:T(8,128)(2,1)} %collective-permute-done.4.refs_6_), channel_id=1, source_target_pairs={{0,1},{1,0},{2,3},{3,2},{4,5},{5,4},{6,7},{7,6},{8,9},{9,8},{10,11... | collective-permute-start | bytes 1228808 | tf_op jit(solution)/shard_map/while/body/ppermute | solution.py:736
  331.0 1.1 copy-start.20
  348.0 26.6 %copy-start.12 = (f32[64,400]{0,1:T(8,128)S(1)}, f32[64,400]{0,1:T(8,128)}, u32[]{:S(2)}) copy-start(f32[64,400]{0,1:T(8,128)} %copy.18) | copy-start | bytes 307204
  375.2 0.7 copy-start.1
